TPU v7x, 32 devices: a whole 2x2x4 slice. The times are simulated.
32 devices in a mesh: ctx: 8 (over z, y), fsdp: 4 (over x, core).
Axes of the slice: x: 2, y: 2, z: 4, core: 2. Of those that a mesh axis runs over, the one named last changes fastest.
Arguments:
- hidden_in: bfloat16 [4, 2048, 4096], P('fsdp', 'ctx'), may hold values from -40 to 40
- page_tokens: int32 [4, 8], P('fsdp'), may hold values from 1 to 1024, 2048 in all within a row
- grad_attn: bfloat16 [4, 2048, 128], P('fsdp', 'ctx'), may hold values from -6 to 6
- w_qkv: bfloat16 [4096, 384], P('fsdp'), may hold values from -1 to 1
Outputs:
- grad_hidden: bfloat16 [4, 2048, 4096], P('fsdp', 'ctx')
- grad_w_qkv: float32 [4096, 384], P('fsdp')
Inputs may be any that keep to these rules, and one draw needn't show every extreme that they name: `page_tokens`: each document's page lengths sum to 2048.
All inputs are finite; a program needn't handle non-finite values.
Results may differ from a plain program's by a relative error of at most 0.039.
Values may be sent and summed in bfloat16 or wider, within the bound.
No kernel may reach another device: no remote copies, remote signals or barrier semaphores. Data moves between devices by JAX's collectives and lax.ppermute only.
A program may use at most 128 MiB of HBM per device.

v0:
```python
import jax
import jax.numpy as jnp
from jax import lax
from jax.sharding import PartitionSpec as P


def page_limits(page_row, positions, total_len):
    page_ends = jnp.cumsum(page_row)
    return jnp.min(
        jnp.where(page_ends[None, :] > positions[:, None], page_ends[None, :], total_len), axis=1
    )


def dot_rows(left, right):
    return lax.dot_general(
        left, right, (((1,), (1,)), ((), ())), preferred_element_type=jnp.float32
    )


def dot_cols(left, right):
    return lax.dot_general(
        left, right, (((0,), (0,)), ((), ())), preferred_element_type=jnp.float32
    )


def local(hidden_in, page_tokens, grad_attn, w_qkv):
    inputs_dev = hidden_in[0]
    grad_out = grad_attn[0]
    page_row = page_tokens[0]
    tok_rows = inputs_dev.shape[0]
    head_width = grad_out.shape[1]
    seq_len = tok_rows * lax.axis_size("ctx")
    score_scale = head_width ** (-0.5)
    weights_all = lax.all_gather(w_qkv, "fsdp", axis=0, tiled=True)
    projected = jnp.dot(inputs_dev, weights_all, preferred_element_type=jnp.float32)
    projected = projected.astype(jnp.bfloat16)
    queries = projected[:, :head_width]
    keys_own = projected[:, head_width : 2 * head_width]
    values_own = projected[:, 2 * head_width :]
    keys_all, values_all = (
        lax.all_gather(keys_own, "ctx", axis=0, tiled=True),
        lax.all_gather(values_own, "ctx", axis=0, tiled=True),
    )
    first_pos = lax.axis_index("ctx") * tok_rows
    positions = first_pos + jnp.arange(tok_rows, dtype=jnp.int32)
    limits = page_limits(page_row, positions, seq_len)
    key_pos = jnp.arange(seq_len, dtype=jnp.int32)
    visible = key_pos[None, :] < limits[:, None]
    scores = jnp.where(visible, dot_rows(queries, keys_all) * score_scale, -1e30)
    row_max = jnp.max(scores, axis=1, keepdims=True)
    log_total = row_max[:, 0] + jnp.log(jnp.sum(jnp.exp(scores - row_max), axis=1))
    probs_full = jnp.exp(scores - log_total[:, None])
    probs_half = probs_full.astype(jnp.bfloat16)
    attended = jnp.dot(probs_half, values_all, preferred_element_type=jnp.float32)
    out_dot = jnp.sum(grad_out.astype(jnp.float32) * attended, axis=1)
    dprob = dot_rows(grad_out, values_all)
    dscore = (probs_full * (dprob - out_dot[:, None]) * score_scale).astype(jnp.bfloat16)
    query_grad = jnp.dot(dscore, keys_all, preferred_element_type=jnp.float32)
    q_piece = lax.all_gather(queries.astype(jnp.float32), "ctx", axis=0, tiled=True).astype(
        jnp.bfloat16
    )
    grad_piece = lax.all_gather(grad_out.astype(jnp.float32), "ctx", axis=0, tiled=True).astype(
        jnp.bfloat16
    )
    total_piece = lax.all_gather(log_total, "ctx", axis=0, tiled=True)
    dot_piece = lax.all_gather(out_dot, "ctx", axis=0, tiled=True)
    piece_rows = q_piece.shape[0]
    piece_limits = page_limits(page_row, jnp.arange(piece_rows, dtype=jnp.int32), seq_len)
    seen = positions[None, :] < piece_limits[:, None]
    piece_scores = jnp.where(seen, dot_rows(q_piece, keys_own) * score_scale, -1e30)
    piece_probs = jnp.exp(piece_scores - total_piece[:, None])
    piece_half = piece_probs.astype(jnp.bfloat16)
    piece_dprob = dot_rows(grad_piece, values_own)
    piece_dscore = (piece_probs * (piece_dprob - dot_piece[:, None]) * score_scale).astype(
        jnp.bfloat16
    )
    key_grad = dot_cols(piece_dscore, q_piece)
    value_grad = dot_cols(piece_half, grad_piece)
    grad_qkv = jnp.concatenate([query_grad, key_grad, value_grad], axis=1).astype(jnp.bfloat16)
    grad_inputs = dot_rows(grad_qkv, weights_all)
    grad_inputs = grad_inputs.astype(jnp.bfloat16)[None]
    block_term = dot_cols(inputs_dev, grad_qkv).astype(jnp.bfloat16)
    block_sum = lax.psum_scatter(
        lax.optimization_barrier(block_term).astype(jnp.float32).astype(jnp.bfloat16),
        "fsdp",
        scatter_dimension=0,
        tiled=True,
    ).astype(jnp.float32)
    grad_weights = lax.psum(block_sum, "ctx")
    return (grad_inputs, grad_weights)


def solution(mesh):
    in_specs = (P("fsdp", "ctx", None), P("fsdp", None), P("fsdp", "ctx", None), P("fsdp", None))
    out_specs = (P("fsdp", "ctx", None), P("fsdp", None))
    return jax.shard_map(local, mesh=mesh, in_specs=in_specs, out_specs=out_specs, check_vma=False)
```

profile of v0, /device:TPU:0, one launch (start us, length us, event | category | flops | bytes accessed | tf_op | source)
XLA Modules:
  0.0 318.6 jit_solution(13162329503484276652)
XLA Ops:
  7.2 0.0 copy-start
  7.2 0.0 all-gather.4.cloned.1.call-start
  7.2 0.7 all-gather.4.cloned.1.call-update
  7.9 0.0 reduce-scatter.2.cloned.1.call-start
  8.0 0.9 copy.10
  8.9 0.8 reduce-window.8
  9.8 0.0 copy-start.5
  9.8 0.1 select_reduce_fusion.1
  9.8 0.7 select_reduce_fusion
  10.5 0.0 copy-done.5
  10.5 33.0 %all_gather.26 = bf16[2048,128]{0,1:T(8,128)(2,1)S(1)} all-gather(bf16[256,128]{0,1:T(8,128)(2,1)S(1)} %bitcast.60), channel_id=1, replica_groups=mesh['ctx'=8,'fsdp'=4] {'ctx'}, dimensions={0}, use_global_device_ids=true | all-gather | bytes 589824 | tf_op jit(solution)/shard_map/all_gather | solution.py:62
  43.6 0.0 all-gather.4.cloned.1.call-done
  43.6 0.0 copy-done
  43.6 3.1 fusion.20
  46.8 31.6 %all_gather.22 = bf16[2048,128]{1,0:T(8,128)(2,1)S(1)} all-gather(bf16[256,128]{1,0:T(8,128)(2,1)S(1)} %get-tuple-element.10), channel_id=1, replica_groups=mesh['ctx'=8,'fsdp'=4] {'ctx'}, dimensions={0}, use_global_device_ids=true | all-gather | bytes 589824 | tf_op jit(solution)/shard_map/all_gather | solution.py:41
  78.3 0.0 copy-start.3
  78.3 0.6 fusion.50
  78.9 0.0 copy-start.1
  78.9 0.4 exponential_reduce_fusion
  79.4 0.0 copy-done.3
  79.4 31.4 %all_gather.23 = bf16[2048,128]{1,0:T(8,128)(2,1)S(1)} all-gather(bf16[256,128]{1,0:T(8,128)(2,1)S(1)} %get-tuple-element.8), channel_id=1, replica_groups=mesh['ctx'=8,'fsdp'=4] {'ctx'}, dimensions={0}, use_global_device_ids=true | all-gather | bytes 589824 | tf_op jit(solution)/shard_map/all_gather | solution.py:42
  110.8 0.0 copy-done.1
  110.8 0.6 fusion.25
  111.4 0.0 copy-start.4
  111.4 0.0 copy-start.6
  111.4 2.6 fusion.23
  114.0 20.3 %all-gather.1 = f32[8,1,256]{2,1,0:T(1,128)S(1)} all-gather(f32[1,1,256]{2,1,0:T(1,128)S(1)} %bitcast.64), channel_id=1, replica_groups=mesh['ctx'=8,'fsdp'=4] {'ctx'}, dimensions={0}, use_global_device_ids=true | all-gather | bytes 9216 | tf_op jit(solution)/shard_map/all_gather | solution.py:66
  134.3 16.3 %all-gather = f32[8,1,256]{2,1,0:T(1,128)S(1)} all-gather(f32[1,1,256]{2,1,0:T(1,128)S(1)} %bitcast.62), channel_id=1, replica_groups=mesh['ctx'=8,'fsdp'=4] {'ctx'}, dimensions={0}, use_global_device_ids=true | all-gather | bytes 9216 | tf_op jit(solution)/shard_map/all_gather | solution.py:65
  150.6 31.2 %all_gather.24 = bf16[2048,128]{1,0:T(8,128)(2,1)S(1)} all-gather(bf16[256,128]{1,0:T(8,128)(2,1)S(1)} %get-tuple-element.9), channel_id=1, replica_groups=mesh['ctx'=8,'fsdp'=4] {'ctx'}, dimensions={0}, use_global_device_ids=true | all-gather | bytes 589824 | tf_op jit(solution)/shard_map/all_gather | solution.py:59
  181.7 0.0 copy-done.4
  181.7 0.0 copy-done.6
  181.7 0.7 fusion.11
  182.4 0.0 copy-start.2
  182.4 1.3 copy-done.2
  183.7 0.3 convolution_convert_fusion.2
  184.0 2.4 fusion.24
  186.5 2.7 fusion
  189.2 0.0 reduce-scatter.2.cloned.1.call-update
  189.2 4.5 %fusion.1 = bf16[1,256,4096]{2,1,0:T(8,128)(2,1)} fusion(bf16[4096,384]{1,0:T(8,128)(2,1)} %all-gather.4.cloned.1.call-done, bf16[256,128]{0,1:T(8,128)(2,1)S(1)} %convolution_convert_fusion.2, bf16[256,128]{0,1:T(8,128)(2,1)S(1)} %fusion.24, bf16[256,128]{0,1:T(8,128)(2,1)S(1)} %fusion.23), kind=kOutput, calls=%fused_computation.3 | convolution fusion | flops 806944768 | bytes 5439488 | tf_op jit(solution)/shard_map/dot_general | solution.py:15
  193.7 32.6 %reduce-scatter.2.cloned.1.call-done = bf16[1024,384]{0,1:T(8,128)(2,1)} async-done(((bf16[4096,384]{0,1:T(8,128)(2,1)}), bf16[1024,384]{0,1:T(8,128)(2,1)}) %reduce-scatter.2.cloned.1.call-update) | async-done | bytes 786448 | tf_op jit(solution)/shard_map/reduce_scatter | solution.py:83
  226.3 82.5 %all-reduce.1 = f32[1024,384]{0,1:T(8,128)} all-reduce(bf16[1024,384]{0,1:T(8,128)(2,1)} %reduce-scatter.2.cloned.1.call-done), channel_id=1, replica_groups=mesh['ctx'=8,'fsdp'=4] {'ctx'}, use_global_device_ids=true, to_apply=%region_7.8 | all-reduce | flops 393216 | bytes 2359296 | tf_op jit(solution)/shard_map/psum | solution.py:89
  308.8 3.0 copy.13
  (3 shorter events, 0.0 us)
Async XLA Ops:
  7.2 36.4 %copy-start = (bf16[1,256,4096]{2,1,0:T(8,128)(2,1)S(1)}, bf16[1,256,4096]{2,1,0:T(8,128)(2,1)}, u32[]{:S(2)}) copy-start(bf16[1,256,4096]{2,1,0:T(8,128)(2,1)} %param.4) | copy-start | bytes 6291460
  7.2 36.4 %all-gather.4.cloned.1.call-start = ((), (), s32[]{:S(2)}) async-start(), calls=%async_computation.1 | async-start | bytes 3932160 | tf_op jit(solution)/shard_map/all_gather | solution.py:34
  7.9 218.4 %reduce-scatter.2.cloned.1.call-start = ((), (), s32[]{:S(2)}) async-start(), calls=%async_computation.2 | async-start | bytes 3932160 | tf_op jit(solution)/shard_map/reduce_scatter | solution.py:83
  9.8 0.8 copy-start.5
  78.3 1.0 copy-start.3
  78.9 31.8 %copy-start.1 = (f32[256,2048]{1,0:T(8,128)}, f32[256,2048]{1,0:T(8,128)S(1)}, u32[]{:S(2)}) copy-start(f32[256,2048]{1,0:T(8,128)S(1)} %get-tuple-element.12) | copy-start | bytes 6291460
  111.4 70.3 %copy-start.4 = (s32[2048]{0:T(1024)S(1)}, s32[2048]{0:T(1024)}, u32[]{:S(2)}) copy-start(s32[2048]{0:T(1024)} %select_reduce_fusion) | copy-start | bytes 24580
  111.4 70.3 %copy-start.6 = (s32[256]{0:T(256)S(1)}, s32[256]{0:T(256)}, u32[]{:S(2)}) copy-start(s32[256]{0:T(256)} %copy-done.5) | copy-start | bytes 3076
  182.4 1.3 copy-start.2
Sparse Core Ops, SparseCore 0:
  9.6 31.2 all-gather.3
  189.3 36.9 reduce-scatter.1
where the time goes:
time: 319 us
  blocking collectives  246 us (77%)
  waiting for transfers between devices  33.3 us (10%)
  matrix products  17.5 us (5%)
  between operations  14.2 us (4%)
  local copies, waits for them, and re-layouts  5.34 us (2%)
    psum x1, blocking collectives, local(): grad_weights = lax.psum(block_sum, 'ctx')  82.5 us
    all_gather x1, blocking collectives, local(): lax.all_gather(grad_out.astype(jnp.float32), 'ctx', axis=0, tiled=True)  33 us
    reduce_scatter x1, waiting for transfers between devices, local(): lax.psum_scatter(lax.optimization_barrier(block_term).astype(jnp.float32)...  32.6 us
    all_gather x1, blocking collectives, local(): lax.all_gather(keys_own, 'ctx', axis=0, tiled=True)  31.6 us
    all_gather x1, blocking collectives, local(): lax.all_gather(values_own, 'ctx', axis=0, tiled=True)  31.4 us
    all_gather x1, blocking collectives, local(): lax.all_gather(queries.astype(jnp.float32), 'ctx', axis=0, tiled=True)  31.2 us
    all_gather x1, blocking collectives, local(): dot_piece = lax.all_gather(out_dot, 'ctx', axis=0, tiled=True)  20.3 us
    all_gather x1, blocking collectives, local(): total_piece = lax.all_gather(log_total, 'ctx', axis=0, tiled=True)  16.3 us
  transfers between devices with their start and end apart: 2, of which 1 were waited for; matrix products, arithmetic and copies ran while one was open for 2% of the time, Pallas kernels for 0%

commit v1 on v0

v1 whole, which is shorter than its diff:
```python
import functools
import math

import jax
import jax.numpy as jnp
from jax import lax
from jax.experimental import pallas as pl
from jax.experimental.pallas import tpu as pltpu
from jax.sharding import PartitionSpec as P

F32 = jnp.float32
BF16 = jnp.bfloat16
VMEM = pl.BlockSpec(memory_space=pltpu.VMEM)
SMEM = pl.BlockSpec(memory_space=pltpu.SMEM)
PARAMS = pltpu.CompilerParams(vmem_limit_bytes=56 * 1024 * 1024)


def nt(left, right):
    return lax.dot_general(left, right, (((1,), (1,)), ((), ())), preferred_element_type=F32)


def nn(left, right):
    return jnp.dot(left, right, preferred_element_type=F32)


def tn(left, right):
    return lax.dot_general(left, right, (((0,), (0,)), ((), ())), preferred_element_type=F32)


def project_kernel(parts, ids_ref, hidden_ref, *refs):
    weights, out_ref = refs[:parts], refs[parts]
    rows = weights[0].shape[0]
    total = None
    for part in range(parts):
        start = pl.multiple_of(ids_ref[part] * rows, rows)
        term = nn(hidden_ref[:, pl.ds(start, rows)], weights[part][...])
        total = term if total is None else total + term
    out_ref[...] = total.astype(BF16)


def project(ids, hidden, weights):
    return pl.pallas_call(
        functools.partial(project_kernel, len(weights)),
        out_shape=jax.ShapeDtypeStruct((hidden.shape[0], weights[0].shape[1]), BF16),
        in_specs=[SMEM] + [VMEM] * (1 + len(weights)),
        out_specs=VMEM,
        compiler_params=PARAMS,
        cost_estimate=pl.CostEstimate(
            flops=2 * hidden.size * weights[0].shape[1], bytes_accessed=4 * hidden.size, transcendentals=0
        ),
        name="project",
    )(ids, hidden, *weights)


def hidden_kernel(parts, ids_ref, grad_ref, *refs):
    weights, out_ref = refs[:parts], refs[parts]
    rows = weights[0].shape[0]
    for part in range(parts):
        start = pl.multiple_of(ids_ref[part] * rows, rows)
        out_ref[:, pl.ds(start, rows)] = nt(grad_ref[...], weights[part][...]).astype(BF16)


def hidden_grad(ids, grad, weights):
    width = len(weights) * weights[0].shape[0]
    return pl.pallas_call(
        functools.partial(hidden_kernel, len(weights)),
        out_shape=jax.ShapeDtypeStruct((grad.shape[0], width), BF16),
        in_specs=[SMEM] + [VMEM] * (1 + len(weights)),
        out_specs=VMEM,
        compiler_params=PARAMS,
        cost_estimate=pl.CostEstimate(
            flops=2 * grad.size * width, bytes_accessed=4 * grad.shape[0] * width, transcendentals=0
        ),
        name="hidden_grad",
    )(ids, grad, *weights)


def attend_kernel(blocks, bq, bk, ids_ref, pages_ref, *refs):
    qkv_parts, out_parts = refs[:blocks], refs[blocks : 2 * blocks]
    grad_ref, own_ref = refs[2 * blocks : 2 * blocks + 2]
    qkv_ref, do_ref, s_ref, dp_ref, dk_ref, dv_ref, kt_ref = refs[2 * blocks + 2 :]
    seq, hd = do_ref.shape
    rows = seq // blocks
    scale = hd**-0.5
    scale2 = scale * math.log2(math.e)
    for block in range(blocks):
        start = pl.multiple_of(ids_ref[block] * rows, rows)
        qkv_ref[pl.ds(start, rows), :] = qkv_parts[block][...]
        do_ref[pl.ds(start, rows), :] = out_parts[block][:, out_parts[block].shape[1] - hd :]
    dk_ref[...] = jnp.zeros_like(dk_ref)
    dv_ref[...] = jnp.zeros_like(dv_ref)
    kt_ref[...] = qkv_ref[:, hd : 2 * hd].T
    ends, end = [], jnp.int32(0)
    for page in range(pages_ref.shape[1]):
        end = end + pages_ref[0, page]
        ends.append(end)

    def limit_of(pos):
        limit = jnp.full_like(pos, seq)
        for page_end in ends:
            limit = jnp.minimum(limit, jnp.where(page_end > pos, page_end, seq))
        return limit

    @pl.loop(0, seq // bq)
    def _(i):
        q0 = pl.multiple_of(i * bq, bq)
        limits = limit_of(q0 + lax.broadcasted_iota(jnp.int32, (1, bq), 1))
        count = lax.div(limit_of(q0 + (bq - 1)) + (bk - 1), bk)
        q = qkv_ref[pl.ds(q0, bq), :hd]
        do = do_ref[pl.ds(q0, bq), :]

        def scores(j, row_max):
            k0 = pl.multiple_of(j * bk, bk)
            s = nt(qkv_ref[pl.ds(k0, bk), hd : 2 * hd], q) * scale2
            key = k0 + lax.broadcasted_iota(jnp.int32, (bk, 1), 0)
            s = jnp.where(key < limits, s, -1e30)
            s_ref[pl.ds(k0, bk), :] = s
            dp_ref[pl.ds(k0, bk), :] = nt(qkv_ref[pl.ds(k0, bk), 2 * hd :], do)
            return jnp.maximum(row_max, jnp.max(s, axis=0, keepdims=True))

        row_max = lax.fori_loop(0, count, scores, jnp.full((1, bq), -3e38, F32))

        def sums(j, carry):
            total, dot = carry
            k0 = pl.multiple_of(j * bk, bk)
            p = jnp.exp2(s_ref[pl.ds(k0, bk), :] - row_max)
            s_ref[pl.ds(k0, bk), :] = p
            total = total + jnp.sum(p, axis=0, keepdims=True)
            dot = dot + jnp.sum(p * dp_ref[pl.ds(k0, bk), :], axis=0, keepdims=True)
            return total, dot

        zero = jnp.zeros((1, bq), F32)
        total, dot = lax.fori_loop(0, count, sums, (zero, zero))
        inv = 1.0 / total
        gain = inv * scale
        shift = dot * inv * gain

        def grads(j, dqt):
            k0 = pl.multiple_of(j * bk, bk)
            p = s_ref[pl.ds(k0, bk), :]
            half = (p * inv).astype(BF16)
            ds = (p * (dp_ref[pl.ds(k0, bk), :] * gain - shift)).astype(BF16)
            dv_ref[pl.ds(k0, bk), :] += nn(half, do)
            dk_ref[pl.ds(k0, bk), :] += nn(ds, q)
            return dqt + nn(kt_ref[:, pl.ds(k0, bk)], ds)

        dqt = lax.fori_loop(0, count, grads, jnp.zeros((hd, bq), F32))
        grad_ref[pl.ds(q0, bq), :hd] = dqt.T.astype(BF16)

    grad_ref[:, hd : 2 * hd] = dk_ref[...].astype(BF16)
    grad_ref[:, 2 * hd :] = dv_ref[...].astype(BF16)
    own = pl.multiple_of(ids_ref[0] * rows, rows)
    own_ref[...] = grad_ref[pl.ds(own, rows), :]


def attend(ids, pages, qkv_parts, out_parts, hd):
    blocks = len(qkv_parts)
    rows, width = qkv_parts[0].shape
    seq = rows * blocks
    block = 512 if seq % 512 == 0 and seq <= 4096 else rows
    return pl.pallas_call(
        functools.partial(attend_kernel, blocks, block, block),
        out_shape=(jax.ShapeDtypeStruct((seq, width), BF16), jax.ShapeDtypeStruct((rows, width), BF16)),
        in_specs=[SMEM, SMEM] + [VMEM] * (2 * blocks),
        out_specs=(VMEM, VMEM),
        scratch_shapes=[
            pltpu.VMEM((seq, width), BF16),
            pltpu.VMEM((seq, hd), BF16),
            pltpu.VMEM((seq, block), F32),
            pltpu.VMEM((seq, block), F32),
            pltpu.VMEM((seq, hd), F32),
            pltpu.VMEM((seq, hd), F32),
            pltpu.VMEM((hd, seq), BF16),
        ],
        compiler_params=PARAMS,
        cost_estimate=pl.CostEstimate(
            flops=10 * seq * seq * hd, bytes_accessed=6 * seq * width, transcendentals=seq * seq
        ),
        name="attend",
    )(ids, pages, *qkv_parts, *out_parts)


def weight_kernel(blocks, ids_ref, grad_ref, *refs):
    hidden_parts, out_ref = refs[:blocks], refs[blocks]
    rows = grad_ref.shape[0] // blocks
    total = None
    for block in range(blocks):
        start = pl.multiple_of(ids_ref[block] * rows, rows)
        term = tn(hidden_parts[block][:, : out_ref.shape[0]], grad_ref[pl.ds(start, rows), :])
        total = term if total is None else total + term
    out_ref[...] = total


def weight_grad(ids, grad, hidden_parts, columns):
    return pl.pallas_call(
        functools.partial(weight_kernel, len(hidden_parts)),
        out_shape=jax.ShapeDtypeStruct((columns, grad.shape[1]), F32),
        in_specs=[SMEM] + [VMEM] * (1 + len(hidden_parts)),
        out_specs=VMEM,
        compiler_params=PARAMS,
        cost_estimate=pl.CostEstimate(
            flops=2 * grad.size * columns, bytes_accessed=4 * grad.shape[0] * columns, transcendentals=0
        ),
        name="weight_grad",
    )(ids, grad, *hidden_parts)


def swap(array, axis, size, distance):
    return lax.ppermute(array, axis, [(i, i ^ distance) for i in range(size)])


def local(ctx_size, fsdp_size, hidden_in, page_tokens, grad_attn, w_qkv):
    hidden, grad_out = hidden_in[0], grad_attn[0]
    rows, depth = hidden.shape
    hd = grad_out.shape[1]
    f, c = lax.axis_index("fsdp"), lax.axis_index("ctx")
    fsdp_ids = f ^ jnp.arange(fsdp_size, dtype=jnp.int32)
    ctx_ids = c ^ jnp.arange(ctx_size, dtype=jnp.int32)
    piece = depth // (fsdp_size * ctx_size)
    columns = fsdp_size * piece

    weights = {0: w_qkv}
    bit = fsdp_size // 2
    while bit:
        weights.update({k ^ bit: swap(weights[k], "fsdp", fsdp_size, bit) for k in list(weights)})
        bit //= 2
    weights = [weights[k] for k in range(fsdp_size)]

    cut = hidden.reshape(rows, fsdp_size, ctx_size, piece)
    hidden_parts = []
    for k in range(ctx_size):
        chunk = lax.dynamic_index_in_dim(cut, ctx_ids[k], 2, keepdims=False).reshape(rows, columns)
        chunk = jnp.concatenate([chunk, grad_out], axis=1)
        hidden_parts.append(swap(chunk, "ctx", ctx_size, k) if k else chunk)

    projected = project(fsdp_ids, hidden, weights)
    qkv_parts = [swap(projected, "ctx", ctx_size, k) if k else projected for k in range(ctx_size)]
    grad_all, grad_own = attend(ctx_ids, page_tokens, qkv_parts, hidden_parts, hd)
    partial = weight_grad(ctx_ids, grad_all, hidden_parts, columns)
    grad_inputs = hidden_grad(fsdp_ids, grad_own, weights)

    partial = partial.reshape(fsdp_size, piece, -1)
    bit = 1
    while bit < fsdp_size:
        pairs = partial.reshape(partial.shape[0] // 2, 2, *partial.shape[1:])
        mine = (f // bit) % 2
        away = lax.dynamic_index_in_dim(pairs, 1 - mine, 1, keepdims=False).astype(BF16)
        kept = lax.dynamic_index_in_dim(pairs, mine, 1, keepdims=False)
        partial = kept + swap(away, "fsdp", fsdp_size, bit).astype(F32)
        bit *= 2
    reduced = partial[0].astype(BF16)
    copies = jnp.broadcast_to(reduced[None], (ctx_size, *reduced.shape))
    gathered = lax.all_to_all(copies, "ctx", 0, 0)
    grad_weights = gathered.reshape(ctx_size * piece, -1).astype(F32)
    return grad_inputs[None], grad_weights


def solution(mesh):
    in_specs = (P("fsdp", "ctx", None), P("fsdp", None), P("fsdp", "ctx", None), P("fsdp", None))
    out_specs = (P("fsdp", "ctx", None), P("fsdp", None))
    body = functools.partial(local, mesh.shape["ctx"], mesh.shape["fsdp"])
    return jax.shard_map(body, mesh=mesh, in_specs=in_specs, out_specs=out_specs, check_vma=False)
```

time: 319 us -> 203 us (0.64)
  blocking collectives: 246 us -> 0 us
  starting transfers between devices: 0.08 us -> 56.9 us
  waiting for transfers between devices: 33.3 us -> 71.8 us
  Pallas kernels: 0 us -> 34.6 us
  matrix products: 17.5 us -> 0 us
  local copies, waits for them, and re-layouts: 5.34 us -> 18.9 us
    all_gather x6 -> x0, blocking collectives: 164 us -> none  [the longest x1 33 us: local(): lax.all_gather(grad_out.astype(jnp.float32), 'ctx', axis=0, tiled=True)]
    psum x1 -> x0, blocking collectives: 82.5 us -> none  [local(): grad_weights = lax.psum(block_sum, 'ctx')]
    ppermute x0 -> x19, waiting for transfers between devices: none -> 56.6 us  [swap(): return lax.ppermute(array, axis, [(i, i ^ distance) for i in range(size)])]
    ppermute x0 -> x19, starting transfers between devices: none -> 45.9 us  [swap(): return lax.ppermute(array, axis, [(i, i ^ distance) for i in range(size)])]
    pallas_call x0 -> x4, Pallas kernels: none -> 34.6 us  [the longest x1 21.3 us: attend(): pl.pallas_call(functools.partial(attend_kernel, blocks, block, block), ou...]
    reduce_scatter x1 -> x0, waiting for transfers between devices: 32.6 us -> none  [local(): lax.psum_scatter(lax.optimization_barrier(block_term).astype(jnp.float32)...]
    dot_general x9 -> x0, matrix products: 17.5 us -> none  [the longest x3 5.77 us: dot_rows(): lax.dot_general(left, right, (((1,), (1,)), ((), ())), preferred_element_...]
    all_to_all x0 -> x1, waiting for transfers between devices: none -> 15.2 us  [local(): gathered = lax.all_to_all(copies, 'ctx', 0, 0)]
  transfers between devices with their start and end apart: 2 -> 20, of which waited for: 1 -> 8; matrix products, arithmetic and copies ran while one was open for 2% -> 9% of each run, Pallas kernels for 0% -> 4%
where the time goes in v1:
time: 203 us; the launch traced here: 202 us
  waiting for transfers between devices  71.8 us (35%)
  starting transfers between devices  56.9 us (28%)
  Pallas kernels  34.6 us (17%)
  local copies, waits for them, and re-layouts  18.9 us (9%)
  between operations  15.8 us (8%)
  other arithmetic  4.21 us (2%)
    ppermute x19, waiting for transfers between devices, swap(): return lax.ppermute(array, axis, [(i, i ^ distance) for i in range(size)])  56.6 us
    ppermute x19, starting transfers between devices, swap(): return lax.ppermute(array, axis, [(i, i ^ distance) for i in range(size)])  45.9 us
    pallas_call x1, Pallas kernels, attend(): pl.pallas_call(functools.partial(attend_kernel, blocks, block, block), ou...  21.3 us
    all_to_all x1, waiting for transfers between devices, local(): gathered = lax.all_to_all(copies, 'ctx', 0, 0)  15.2 us
    dynamic_slice x1, local copies, waits for them, and re-layouts, local(): lax.dynamic_index_in_dim(cut, ctx_ids[k], 2, keepdims=False)  13.2 us
    all_to_all x1, starting transfers between devices, local(): gathered = lax.all_to_all(copies, 'ctx', 0, 0)  11 us
    pallas_call x1, Pallas kernels, hidden_grad(): pl.pallas_call(functools.partial(hidden_kernel, len(weights)), out_shape=...  4.51 us
    pallas_call x1, Pallas kernels, project(): pl.pallas_call(functools.partial(project_kernel, len(weights)), out_shape...  4.45 us
  transfers between devices with their start and end apart: 20, of which 8 were waited for; matrix products, arithmetic and copies ran while one was open for 9% of the time, Pallas kernels for 4%

profile of v1, /device:TPU:0, one launch (start us, length us, event | category | flops | bytes accessed | tf_op | source)
XLA Modules:
  0.0 202.3 jit_solution(5607205642277922219)
XLA Ops:
  0.6 3.0 %collective-permute-start.1 = (bf16[1024,384]{1,0:T(8,128)(2,1)}, bf16[1024,384]{1,0:T(8,128)(2,1)S(1)}, u32[]{:S(2)}, u32[]{:S(2)}) collective-permute-start(bf16[1024,384]{1,0:T(8,128)(2,1)} %refs_0_.3), channel_id=1, source_target_pairs={{0,2},{1,3},{2,0},{3,1},{4,6},{5,7},{6,4},{7,5},{8,10},{9,11},{10,... | collective-permute-start | bytes 2359304 | tf_op jit(solution)/shard_map/ppermute | solution.py:209
  3.6 0.0 collective-permute-start
  3.6 0.7 fusion.2
  14.3 2.1 %copy.22 = bf16[32,8,32,128]{3,2,1,0:T(8,128)(2,1)S(1)} copy(bf16[32,8,32,128]{3,1,2,0:T(8,128)(2,1)} %bitcast.50) | data formatting | bytes 4194304
  16.3 0.0 copy-done.9
  21.3 13.2 %dynamic-slice_reduce_fusion = (bf16[256,4,128]{2,1,0:T(4,128)(2,1)S(1)}, bf16[256,4,128]{2,1,0:T(4,128)(2,1)S(1)}, bf16[256,4,128]{2,1,0:T(4,128)(2,1)S(1)}, bf...) fusion(bf16[256,4,8,128]{3,2,1,0:T(8,128)(2,1)S(1)} %bitcast.49, ...), kind=kLoop, calls=%fused_computation.9 | loop fusion | bytes 4194336 | tf_op jit(solution)/shard_map/jit(dynamic_index_in_dim)/dynamic_slice | solution.py:232
  34.5 0.0 copy-start.8
  34.5 0.1 copy_bitcast_fusion.2
  34.6 0.1 copy_bitcast_fusion.4
  34.6 0.1 copy_bitcast_fusion.6
  34.7 0.0 collective-permute-done.1.refs_2_
  34.7 0.0 copy-start
  34.7 0.6 collective-permute-start.2
  35.3 0.1 copy_bitcast_fusion
  35.4 0.0 copy-done.8
  35.4 1.3 pad_maximum_fusion
  36.7 1.5 collective-permute-start.10
  38.2 1.6 collective-permute-start.11
  39.8 0.4 collective-permute-start.12
  40.2 6.6 %collective-permute-done.10.refs_9_.refs_1_ = bf16[256,640]{1,0:T(8,128)(2,1)S(1)} collective-permute-done((bf16[256,640]{1,0:T(8,128)(2,1)S(1)}, bf16[256,640]{1,0:T(8,128)(2,1)S(1)}, u32[]{:S(2)}, u32[]{:S(2)}) %collective-permute-start.10) | collective-permute-done | bytes 327712 | tf_op jit(solution)/shard_map/ppermute | solution.py:209
  46.7 2.6 %collective-permute-start.13 = (bf16[256,640]{1,0:T(8,128)(2,1)}, bf16[256,640]{1,0:T(8,128)(2,1)S(1)}, u32[]{:S(2)}, u32[]{:S(2)}) collective-permute-start(bf16[256,640]{1,0:T(8,128)(2,1)} %get-tuple-element.18), channel_id=1, source_target_pairs={{0,16},{4,20},{8,24},{12,28},{16,0},{20,4},{24,8},{28,12},{1,17},{... | collective-permute-start | bytes 983048 | tf_op jit(solution)/shard_map/ppermute | solution.py:209
  49.3 0.0 collective-permute-done.11.refs_10_.refs_2_
  49.3 1.9 collective-permute-start.14
  51.3 0.0 collective-permute-done.refs_1_
  51.3 2.9 %collective-permute-start.15 = (bf16[256,640]{1,0:T(8,128)(2,1)}, bf16[256,640]{1,0:T(8,128)(2,1)}, u32[]{:S(2)}, u32[]{:S(2)}) collective-permute-start(bf16[256,640]{1,0:T(8,128)(2,1)} %get-tuple-element.20), channel_id=1, source_target_pairs={{0,24},{4,28},{8,16},{12,20},{16,8},{20,12},{24,0},{28,4},{1,25},{... | collective-permute-start | bytes 983048 | tf_op jit(solution)/shard_map/ppermute | solution.py:209
  54.2 0.0 collective-permute-done.2.refs_3_
  54.2 1.8 collective-permute-start.16
  56.1 0.5 iota_xor_fusion.1.ids_ref
  56.6 4.4 %project.1.refs_0_ = bf16[256,384]{1,0:T(8,128)(2,1)} custom-call(s32[4]{0:T(128)} %iota_xor_fusion.1.ids_ref, bf16[256,4096]{1,0:T(8,128)(2,1)} %bitcast.51, bf16[1024,384]{1,0:T(8,128)(2,1)} %refs_0_.3, bf16[1024,384]{1,0:T(8,128)(2,1)} %collective-permute-done.refs_1_, bf16[1024,384]{1,0:T(8,128)(2,1)} %copy-done, bf16[1024,384]{1,0:T(8,128)(2,1)} %copy-done.1), custom_call_target="tpu_custom_call" | custom-call | flops 805306368 | bytes 4194304 | tf_op jit(solution)/shard_map/project/pallas_call | solution.py:42
  61.0 0.0 collective-permute-done.12.refs_11_.refs_3_
  61.1 2.4 %collective-permute-start.3 = (bf16[256,384]{1,0:T(8,128)(2,1)}, bf16[256,384]{1,0:T(8,128)(2,1)S(1)}, u32[]{:S(2)}, u32[]{:S(2)}) collective-permute-start(bf16[256,384]{1,0:T(8,128)(2,1)} %project.1.refs_0_), channel_id=1, source_target_pairs={{0,4},{4,0},{8,12},{12,8},{16,20},{20,16},{24,28},{28,24},{1,5},{5... | collective-permute-start | bytes 589832 | tf_op jit(solution)/shard_map/ppermute | solution.py:209
  63.4 23.2 %collective-permute-done.13.refs_12_.refs_4_ = bf16[256,640]{1,0:T(8,128)(2,1)S(1)} collective-permute-done((bf16[256,640]{1,0:T(8,128)(2,1)}, bf16[256,640]{1,0:T(8,128)(2,1)S(1)}, u32[]{:S(2)}, u32[]{:S(2)}) %collective-permute-start.13) | collective-permute-done | bytes 327712 | tf_op jit(solution)/shard_map/ppermute | solution.py:209
  86.6 0.8 collective-permute-start.4
  87.5 7.1 %collective-permute-done.14.refs_13_.refs_5_ = bf16[256,640]{1,0:T(8,128)(2,1)S(1)} collective-permute-done((bf16[256,640]{1,0:T(8,128)(2,1)}, bf16[256,640]{1,0:T(8,128)(2,1)S(1)}, u32[]{:S(2)}, u32[]{:S(2)}) %collective-permute-start.14) | collective-permute-done | bytes 327712 | tf_op jit(solution)/shard_map/ppermute | solution.py:209
  94.6 0.9 collective-permute-start.5
  95.5 0.0 collective-permute-done.15.refs_14_.refs_6_
  95.5 8.0 %collective-permute-start.6 = (bf16[256,384]{1,0:T(8,128)(2,1)}, bf16[256,384]{1,0:T(8,128)(2,1)S(1)}, u32[]{:S(2)}, u32[]{:S(2)}) collective-permute-start(bf16[256,384]{1,0:T(8,128)(2,1)} %project.1.refs_0_), channel_id=1, source_target_pairs={{0,16},{4,20},{8,24},{12,28},{16,0},{20,4},{24,8},{28,12},{1,17},{... | collective-permute-start | bytes 589832 | tf_op jit(solution)/shard_map/ppermute | solution.py:209
  103.5 0.0 collective-permute-done.16.refs_15_.refs_7_
  103.5 12.5 %collective-permute-start.7 = (bf16[256,384]{1,0:T(8,128)(2,1)}, bf16[256,384]{1,0:T(8,128)(2,1)S(1)}, u32[]{:S(2)}, u32[]{:S(2)}) collective-permute-start(bf16[256,384]{1,0:T(8,128)(2,1)} %project.1.refs_0_), channel_id=1, source_target_pairs={{0,20},{4,16},{8,28},{12,24},{16,4},{20,0},{24,12},{28,8},{1,21},{... | collective-permute-start | bytes 589832 | tf_op jit(solution)/shard_map/ppermute | solution.py:209
  116.0 0.0 collective-permute-done.3.refs_1_
  116.0 0.4 collective-permute-start.8
  116.4 0.0 collective-permute-done.4.refs_2_
  116.4 3.9 %collective-permute-start.9 = (bf16[256,384]{1,0:T(8,128)(2,1)}, bf16[256,384]{1,0:T(8,128)(2,1)S(1)}, u32[]{:S(2)}, u32[]{:S(2)}) collective-permute-start(bf16[256,384]{1,0:T(8,128)(2,1)} %project.1.refs_0_), channel_id=1, source_target_pairs={{0,28},{4,24},{8,20},{12,16},{16,12},{20,8},{24,4},{28,0},{1,29},{... | collective-permute-start | bytes 589832 | tf_op jit(solution)/shard_map/ppermute | solution.py:209
  120.3 0.0 collective-permute-done.5.refs_3_
  120.3 9.1 %collective-permute-done.6.refs_4_ = bf16[256,384]{1,0:T(8,128)(2,1)S(1)} collective-permute-done((bf16[256,384]{1,0:T(8,128)(2,1)}, bf16[256,384]{1,0:T(8,128)(2,1)S(1)}, u32[]{:S(2)}, u32[]{:S(2)}) %collective-permute-start.6) | collective-permute-done | bytes 196640 | tf_op jit(solution)/shard_map/ppermute | solution.py:209
  129.4 4.9 %collective-permute-done.7.refs_5_ = bf16[256,384]{1,0:T(8,128)(2,1)S(1)} collective-permute-done((bf16[256,384]{1,0:T(8,128)(2,1)}, bf16[256,384]{1,0:T(8,128)(2,1)S(1)}, u32[]{:S(2)}, u32[]{:S(2)}) %collective-permute-start.7) | collective-permute-done | bytes 196640 | tf_op jit(solution)/shard_map/ppermute | solution.py:209
  134.3 0.0 collective-permute-done.8.refs_6_
  134.3 0.0 collective-permute-done.9.refs_7_
  134.4 0.6 copy-done.14
  135.0 0.1 copy-done.15
  135.0 0.1 copy-done.16
  135.1 21.3 %attend.1 = (bf16[2048,384]{1,0:T(8,128)(2,1)}, bf16[256,384]{1,0:T(8,128)(2,1)}) custom-call(s32[8]{0:T(128)} %copy-done.9, s32[1,8]{1,0:T(1,128)} %pages_ref.1, bf16[256,384]{1,0:T(8,128)(2,1)} %project.1.refs_0_, bf16[256,384]{1,0:T(8,128)(2,1)} %copy-done.10, bf16[256,384]{1,0:T(8,128)(2,1)} %copy-done.11, bf16[256,384]{1,0:T(8,128)(2,1)} %copy-done.12, ...), custom_call_target="tpu_custom_call" | custom-call | flops 5368709120 | bytes 4718592 | tf_op jit(solution)/shard_map/attend/pallas_call | solution.py:161
  156.4 4.3 %weight_grad.1 = f32[512,384]{1,0:T(8,128)} custom-call(s32[8]{0:T(128)} %copy-done.9, bf16[2048,384]{1,0:T(8,128)(2,1)} %get-tuple-element.5.grad_ref, bf16[256,640]{1,0:T(8,128)(2,1)} %get-tuple-element.21.refs_8_.refs_0_, bf16[256,640]{1,0:T(8,128)(2,1)} %copy-done.2, bf16[256,640]{1,0:T(8,128)(2,1)} %copy-done.3, bf16[256,640]{1,0:T(8,128)(2,1)} %copy-done.4, ...), custom_call_target="tpu_custom_call" | custom-call | flops 805306368 | bytes 4194304 | tf_op jit(solution)/shard_map/weight_grad/pallas_call | solution.py:195
  160.8 1.0 fusion
  161.8 0.1 collective-permute-start.17
  161.9 1.4 collective-permute-done.17
  163.3 1.0 bitcast_add_fusion
  164.3 0.6 collective-permute-start.18
  164.9 4.3 %collective-permute-done.18 = bf16[1,128,384]{2,1,0:T(8,128)(2,1)S(1)} collective-permute-done((bf16[1,128,384]{2,1,0:T(8,128)(2,1)S(1)}, bf16[1,128,384]{2,1,0:T(8,128)(2,1)S(1)}, u32[]{:S(2)}, u32[]{:S(2)}) %collective-permute-start.18) | collective-permute-done | bytes 98336 | tf_op jit(solution)/shard_map/ppermute | solution.py:209
  169.3 1.0 broadcast_in_dim.13
  170.2 11.0 %all-to-all-start = ((bf16[8,128,384]{2,1,0:T(8,128)(2,1)}), bf16[8,128,384]{2,1,0:T(8,128)(2,1)S(1)}, u32[]{:S(2)}, u32[]{:S(2)}) async-start(bf16[8,128,384]{2,1,0:T(8,128)(2,1)} %broadcast_in_dim.13), calls=%async_computation | async-start | bytes 1572864 | tf_op jit(solution)/shard_map/all_to_all | solution.py:253
  181.2 4.5 %hidden_grad.1 = bf16[256,4096]{1,0:T(8,128)(2,1)} custom-call(s32[4]{0:T(128)} %iota_xor_fusion.1.ids_ref, bf16[256,384]{1,0:T(8,128)(2,1)} %get-tuple-element.4.grad_ref, bf16[1024,384]{1,0:T(8,128)(2,1)} %refs_0_.3, bf16[1024,384]{1,0:T(8,128)(2,1)} %collective-permute-done.refs_1_, bf16[1024,384]{1,0:T(8,128)(2,1)} %copy-done, bf16[1024,384]{1,0:T(8,128)(2,1)} %copy-done.1), custom_call_target="tpu_custom_call" | custom-call | flops 805306368 | bytes 4194304 | tf_op jit(solution)/shard_map/hidden_grad/pallas_call | solution.py:65
  185.7 15.2 %all-to-all-done = bf16[8,128,384]{2,1,0:T(8,128)(2,1)S(1)} async-done(((bf16[8,128,384]{2,1,0:T(8,128)(2,1)}), bf16[8,128,384]{2,1,0:T(8,128)(2,1)S(1)}, u32[]{:S(2)}, u32[]{:S(2)}) %all-to-all-start) | async-done | bytes 786464 | tf_op jit(solution)/shard_map/all_to_all | solution.py:253
  200.9 1.3 bitcast_convert_fusion
  (30 shorter events, 0.1 us)
Async XLA Ops:
  0.6 34.1 %collective-permute-start.1 = (bf16[1024,384]{1,0:T(8,128)(2,1)}, bf16[1024,384]{1,0:T(8,128)(2,1)S(1)}, u32[]{:S(2)}, u32[]{:S(2)}) collective-permute-start(bf16[1024,384]{1,0:T(8,128)(2,1)} %refs_0_.3), channel_id=1, source_target_pairs={{0,2},{1,3},{2,0},{3,1},{4,6},{5,7},{6,4},{7,5},{8,10},{9,11},{10,... | collective-permute-start | bytes 2359304 | tf_op jit(solution)/shard_map/ppermute | solution.py:209
  3.6 47.7 %collective-permute-start = (bf16[1024,384]{1,0:T(8,128)(2,1)}, bf16[1024,384]{1,0:T(8,128)(2,1)}, u32[]{:S(2)}, u32[]{:S(2)}) collective-permute-start(bf16[1024,384]{1,0:T(8,128)(2,1)} %refs_0_.3), channel_id=1, source_target_pairs={{0,1},{1,0},{2,3},{3,2},{4,5},{5,4},{6,7},{7,6},{8,9},{9,8},{10,11... | collective-permute-start | bytes 2359304 | tf_op jit(solution)/shard_map/ppermute | solution.py:209
  3.6 12.7 %copy-start.9 = (s32[8]{0:T(128)}, s32[8]{0:T(128)S(1)}, u32[]{:S(2)}) copy-start(s32[8]{0:T(128)S(1)} %iota_xor_fusion.ids_ref) | copy-start | bytes 100
  34.5 0.9 copy-start.8
  34.7 2.0 copy-start
  34.7 19.5 %collective-permute-start.2 = (bf16[1024,384]{1,0:T(8,128)(2,1)S(1)}, bf16[1024,384]{1,0:T(8,128)(2,1)S(1)}, u32[]{:S(2)}, u32[]{:S(2)}) collective-permute-start(bf16[1024,384]{1,0:T(8,128)(2,1)S(1)} %collective-permute-done.1.refs_2_), channel_id=1, source_target_pairs={{0,1},{1,0},{2,3},{3,2},{4,5},{5,4},{6,7},{7,6},{8,9},{9,8},{10,11... | collective-permute-start | bytes 2359304 | tf_op jit(solution)/shard_map/ppermute | solution.py:209
  36.7 10.1 %collective-permute-start.10 = (bf16[256,640]{1,0:T(8,128)(2,1)S(1)}, bf16[256,640]{1,0:T(8,128)(2,1)S(1)}, u32[]{:S(2)}, u32[]{:S(2)}) collective-permute-start(bf16[256,640]{1,0:T(8,128)(2,1)S(1)} %get-tuple-element.15), channel_id=1, source_target_pairs={{0,4},{4,0},{8,12},{12,8},{16,20},{20,16},{24,28},{28,24},{1,5},{5... | collective-permute-start | bytes 983048 | tf_op jit(solution)/shard_map/ppermute | solution.py:209
  38.2 11.1 %collective-permute-start.11 = (bf16[256,640]{1,0:T(8,128)(2,1)S(1)}, bf16[256,640]{1,0:T(8,128)(2,1)S(1)}, u32[]{:S(2)}, u32[]{:S(2)}) collective-permute-start(bf16[256,640]{1,0:T(8,128)(2,1)S(1)} %get-tuple-element.16), channel_id=1, source_target_pairs={{0,8},{4,12},{8,0},{12,4},{16,24},{20,28},{24,16},{28,20},{1,9},{5... | collective-permute-start | bytes 983048 | tf_op jit(solution)/shard_map/ppermute | solution.py:209
  39.8 21.3 %collective-permute-start.12 = (bf16[256,640]{1,0:T(8,128)(2,1)}, bf16[256,640]{1,0:T(8,128)(2,1)S(1)}, u32[]{:S(2)}, u32[]{:S(2)}) collective-permute-start(bf16[256,640]{1,0:T(8,128)(2,1)} %get-tuple-element.17), channel_id=1, source_target_pairs={{0,12},{4,8},{8,4},{12,0},{16,28},{20,24},{24,20},{28,16},{1,13},{... | collective-permute-start | bytes 983048 | tf_op jit(solution)/shard_map/ppermute | solution.py:209
  46.7 87.6 %copy-start.2 = (bf16[256,640]{1,0:T(8,128)(2,1)}, bf16[256,640]{1,0:T(8,128)(2,1)S(1)}, u32[]{:S(2)}) copy-start(bf16[256,640]{1,0:T(8,128)(2,1)S(1)} %collective-permute-done.10.refs_9_.refs_1_) | copy-start | bytes 983044
  46.7 39.9 %collective-permute-start.13 = (bf16[256,640]{1,0:T(8,128)(2,1)}, bf16[256,640]{1,0:T(8,128)(2,1)S(1)}, u32[]{:S(2)}, u32[]{:S(2)}) collective-permute-start(bf16[256,640]{1,0:T(8,128)(2,1)} %get-tuple-element.18), channel_id=1, source_target_pairs={{0,16},{4,20},{8,24},{12,28},{16,0},{20,4},{24,8},{28,12},{1,17},{... | collective-permute-start | bytes 983048 | tf_op jit(solution)/shard_map/ppermute | solution.py:209
  49.3 85.0 %copy-start.3 = (bf16[256,640]{1,0:T(8,128)(2,1)}, bf16[256,640]{1,0:T(8,128)(2,1)S(1)}, u32[]{:S(2)}) copy-start(bf16[256,640]{1,0:T(8,128)(2,1)S(1)} %collective-permute-done.11.refs_10_.refs_2_) | copy-start | bytes 983044
  49.3 45.3 %collective-permute-start.14 = (bf16[256,640]{1,0:T(8,128)(2,1)}, bf16[256,640]{1,0:T(8,128)(2,1)S(1)}, u32[]{:S(2)}, u32[]{:S(2)}) collective-permute-start(bf16[256,640]{1,0:T(8,128)(2,1)} %get-tuple-element.19), channel_id=1, source_target_pairs={{0,20},{4,16},{8,28},{12,24},{16,4},{20,0},{24,12},{28,8},{1,21},{... | collective-permute-start | bytes 983048 | tf_op jit(solution)/shard_map/ppermute | solution.py:209
  51.3 44.2 %collective-permute-start.15 = (bf16[256,640]{1,0:T(8,128)(2,1)}, bf16[256,640]{1,0:T(8,128)(2,1)}, u32[]{:S(2)}, u32[]{:S(2)}) collective-permute-start(bf16[256,640]{1,0:T(8,128)(2,1)} %get-tuple-element.20), channel_id=1, source_target_pairs={{0,24},{4,28},{8,16},{12,20},{16,8},{20,12},{24,0},{28,4},{1,25},{... | collective-permute-start | bytes 983048 | tf_op jit(solution)/shard_map/ppermute | solution.py:209
  54.2 2.4 %copy-start.1 = (bf16[1024,384]{1,0:T(8,128)(2,1)}, bf16[1024,384]{1,0:T(8,128)(2,1)S(1)}, u32[]{:S(2)}) copy-start(bf16[1024,384]{1,0:T(8,128)(2,1)S(1)} %collective-permute-done.2.refs_3_) | copy-start | bytes 2359300
  54.2 49.2 %collective-permute-start.16 = (bf16[256,640]{1,0:T(8,128)(2,1)S(1)}, bf16[256,640]{1,0:T(8,128)(2,1)S(1)}, u32[]{:S(2)}, u32[]{:S(2)}) collective-permute-start(bf16[256,640]{1,0:T(8,128)(2,1)S(1)} %get-tuple-element.14), channel_id=1, source_target_pairs={{0,28},{4,24},{8,20},{12,16},{16,12},{20,8},{24,4},{28,0},{1,29},{... | collective-permute-start | bytes 983048 | tf_op jit(solution)/shard_map/ppermute | solution.py:209
  61.1 73.3 %copy-start.4 = (bf16[256,640]{1,0:T(8,128)(2,1)}, bf16[256,640]{1,0:T(8,128)(2,1)S(1)}, u32[]{:S(2)}) copy-start(bf16[256,640]{1,0:T(8,128)(2,1)S(1)} %collective-permute-done.12.refs_11_.refs_3_) | copy-start | bytes 983044
  61.1 54.9 %collective-permute-start.3 = (bf16[256,384]{1,0:T(8,128)(2,1)}, bf16[256,384]{1,0:T(8,128)(2,1)S(1)}, u32[]{:S(2)}, u32[]{:S(2)}) collective-permute-start(bf16[256,384]{1,0:T(8,128)(2,1)} %project.1.refs_0_), channel_id=1, source_target_pairs={{0,4},{4,0},{8,12},{12,8},{16,20},{20,16},{24,28},{28,24},{1,5},{5... | collective-permute-start | bytes 589832 | tf_op jit(solution)/shard_map/ppermute | solution.py:209
  86.6 47.7 %copy-start.5 = (bf16[256,640]{1,0:T(8,128)(2,1)}, bf16[256,640]{1,0:T(8,128)(2,1)S(1)}, u32[]{:S(2)}) copy-start(bf16[256,640]{1,0:T(8,128)(2,1)S(1)} %collective-permute-done.13.refs_12_.refs_4_) | copy-start | bytes 983044
  86.6 29.7 %collective-permute-start.4 = (bf16[256,384]{1,0:T(8,128)(2,1)}, bf16[256,384]{1,0:T(8,128)(2,1)S(1)}, u32[]{:S(2)}, u32[]{:S(2)}) collective-permute-start(bf16[256,384]{1,0:T(8,128)(2,1)} %project.1.refs_0_), channel_id=1, source_target_pairs={{0,8},{4,12},{8,0},{12,4},{16,24},{20,28},{24,16},{28,20},{1,9},{5... | collective-permute-start | bytes 589832 | tf_op jit(solution)/shard_map/ppermute | solution.py:209
  94.6 39.8 %copy-start.6 = (bf16[256,640]{1,0:T(8,128)(2,1)}, bf16[256,640]{1,0:T(8,128)(2,1)S(1)}, u32[]{:S(2)}) copy-start(bf16[256,640]{1,0:T(8,128)(2,1)S(1)} %collective-permute-done.14.refs_13_.refs_5_) | copy-start | bytes 983044
  94.6 25.7 %collective-permute-start.5 = (bf16[256,384]{1,0:T(8,128)(2,1)}, bf16[256,384]{1,0:T(8,128)(2,1)S(1)}, u32[]{:S(2)}, u32[]{:S(2)}) collective-permute-start(bf16[256,384]{1,0:T(8,128)(2,1)} %project.1.refs_0_), channel_id=1, source_target_pairs={{0,12},{4,8},{8,4},{12,0},{16,28},{20,24},{24,20},{28,16},{1,13},{... | collective-permute-start | bytes 589832 | tf_op jit(solution)/shard_map/ppermute | solution.py:209
  95.5 33.9 %collective-permute-start.6 = (bf16[256,384]{1,0:T(8,128)(2,1)}, bf16[256,384]{1,0:T(8,128)(2,1)S(1)}, u32[]{:S(2)}, u32[]{:S(2)}) collective-permute-start(bf16[256,384]{1,0:T(8,128)(2,1)} %project.1.refs_0_), channel_id=1, source_target_pairs={{0,16},{4,20},{8,24},{12,28},{16,0},{20,4},{24,8},{28,12},{1,17},{... | collective-permute-start | bytes 589832 | tf_op jit(solution)/shard_map/ppermute | solution.py:209
  103.5 30.9 %copy-start.7 = (bf16[256,640]{1,0:T(8,128)(2,1)}, bf16[256,640]{1,0:T(8,128)(2,1)S(1)}, u32[]{:S(2)}) copy-start(bf16[256,640]{1,0:T(8,128)(2,1)S(1)} %collective-permute-done.16.refs_15_.refs_7_) | copy-start | bytes 983044
  103.5 30.8 %collective-permute-start.7 = (bf16[256,384]{1,0:T(8,128)(2,1)}, bf16[256,384]{1,0:T(8,128)(2,1)S(1)}, u32[]{:S(2)}, u32[]{:S(2)}) collective-permute-start(bf16[256,384]{1,0:T(8,128)(2,1)} %project.1.refs_0_), channel_id=1, source_target_pairs={{0,20},{4,16},{8,28},{12,24},{16,4},{20,0},{24,12},{28,8},{1,21},{... | collective-permute-start | bytes 589832 | tf_op jit(solution)/shard_map/ppermute | solution.py:209
  116.0 18.4 %copy-start.10 = (bf16[256,384]{1,0:T(8,128)(2,1)}, bf16[256,384]{1,0:T(8,128)(2,1)S(1)}, u32[]{:S(2)}) copy-start(bf16[256,384]{1,0:T(8,128)(2,1)S(1)} %collective-permute-done.3.refs_1_) | copy-start | bytes 589828
  116.0 18.3 %collective-permute-start.8 = (bf16[256,384]{1,0:T(8,128)(2,1)}, bf16[256,384]{1,0:T(8,128)(2,1)S(1)}, u32[]{:S(2)}, u32[]{:S(2)}) collective-permute-start(bf16[256,384]{1,0:T(8,128)(2,1)} %project.1.refs_0_), channel_id=1, source_target_pairs={{0,24},{4,28},{8,16},{12,20},{16,8},{20,12},{24,0},{28,4},{1,25},{... | collective-permute-start | bytes 589832 | tf_op jit(solution)/shard_map/ppermute | solution.py:209
  116.4 18.0 %copy-start.11 = (bf16[256,384]{1,0:T(8,128)(2,1)}, bf16[256,384]{1,0:T(8,128)(2,1)S(1)}, u32[]{:S(2)}) copy-start(bf16[256,384]{1,0:T(8,128)(2,1)S(1)} %collective-permute-done.4.refs_2_) | copy-start | bytes 589828
  116.4 17.9 %collective-permute-start.9 = (bf16[256,384]{1,0:T(8,128)(2,1)}, bf16[256,384]{1,0:T(8,128)(2,1)S(1)}, u32[]{:S(2)}, u32[]{:S(2)}) collective-permute-start(bf16[256,384]{1,0:T(8,128)(2,1)} %project.1.refs_0_), channel_id=1, source_target_pairs={{0,28},{4,24},{8,20},{12,16},{16,12},{20,8},{24,4},{28,0},{1,29},{... | collective-permute-start | bytes 589832 | tf_op jit(solution)/shard_map/ppermute | solution.py:209
  120.3 14.1 %copy-start.12 = (bf16[256,384]{1,0:T(8,128)(2,1)}, bf16[256,384]{1,0:T(8,128)(2,1)S(1)}, u32[]{:S(2)}) copy-start(bf16[256,384]{1,0:T(8,128)(2,1)S(1)} %collective-permute-done.5.refs_3_) | copy-start | bytes 589828
  129.4 5.0 %copy-start.13 = (bf16[256,384]{1,0:T(8,128)(2,1)}, bf16[256,384]{1,0:T(8,128)(2,1)S(1)}, u32[]{:S(2)}) copy-start(bf16[256,384]{1,0:T(8,128)(2,1)S(1)} %collective-permute-done.6.refs_4_) | copy-start | bytes 589828
  134.3 0.7 copy-start.14
  134.3 0.7 copy-start.15
  134.3 0.8 copy-start.16
  161.8 1.5 collective-permute-start.17
  164.3 4.9 %collective-permute-start.18 = (bf16[1,128,384]{2,1,0:T(8,128)(2,1)S(1)}, bf16[1,128,384]{2,1,0:T(8,128)(2,1)S(1)}, u32[]{:S(2)}, u32[]{:S(2)}) collective-permute-start(bf16[1,128,384]{2,1,0:T(8,128)(2,1)S(1)} %dynamic-slice_convert_fusion.1), channel_id=1, source_target_pairs={{0,2},{1,3},{2,0},{3,1},{4,6},{5,7},{6,4},{7,5},{8,10},{9,11},{10,... | collective-permute-start | bytes 294920 | tf_op jit(solution)/shard_map/ppermute | solution.py:209
  170.2 30.7 %all-to-all-start = ((bf16[8,128,384]{2,1,0:T(8,128)(2,1)}), bf16[8,128,384]{2,1,0:T(8,128)(2,1)S(1)}, u32[]{:S(2)}, u32[]{:S(2)}) async-start(bf16[8,128,384]{2,1,0:T(8,128)(2,1)} %broadcast_in_dim.13), calls=%async_computation | async-start | bytes 1572864 | tf_op jit(solution)/shard_map/all_to_all | solution.py:253

commit v2 on v1

v2 whole, which is shorter than its diff:
```python
import functools
import math

import jax
import jax.numpy as jnp
from jax import lax
from jax.experimental import pallas as pl
from jax.experimental.pallas import tpu as pltpu
from jax.sharding import PartitionSpec as P

F32 = jnp.float32
BF16 = jnp.bfloat16
VMEM = pl.BlockSpec(memory_space=pltpu.VMEM)
SMEM = pl.BlockSpec(memory_space=pltpu.SMEM)
PARAMS = pltpu.CompilerParams(vmem_limit_bytes=56 * 1024 * 1024)


def nt(left, right):
    return lax.dot_general(left, right, (((1,), (1,)), ((), ())), preferred_element_type=F32)


def nn(left, right):
    return jnp.dot(left, right, preferred_element_type=F32)


def tn(left, right):
    return lax.dot_general(left, right, (((0,), (0,)), ((), ())), preferred_element_type=F32)


def pallas(kernel, out_shape, scalars, arrays, name, flops, scratch=()):
    outs = out_shape if isinstance(out_shape, tuple) else (out_shape,)
    moved = sum(a.size * a.dtype.itemsize for a in (*arrays, *outs))
    return pl.pallas_call(
        kernel,
        out_shape=out_shape,
        in_specs=[SMEM] * len(scalars) + [VMEM] * len(arrays),
        out_specs=jax.tree.map(lambda _: VMEM, out_shape),
        scratch_shapes=scratch,
        compiler_params=PARAMS,
        cost_estimate=pl.CostEstimate(flops=flops, bytes_accessed=moved, transcendentals=0),
        name=name,
    )(*scalars, *arrays)


def shape(dims, dtype=BF16):
    return jax.ShapeDtypeStruct(dims, dtype)


def cut_kernel(group, fsdp_size, ctx_size, piece, ids_ref, hidden_ref, *outs):
    for k, out in enumerate(outs):
        for block in range(fsdp_size * ctx_size // group):
            start = pl.multiple_of((block * group + ids_ref[k]) * piece, piece)
            out[:, block * piece : (block + 1) * piece] = hidden_ref[:, pl.ds(start, piece)]


def cut(ids, hidden, group, fsdp_size, ctx_size):
    rows, depth = hidden.shape
    piece = depth // (fsdp_size * ctx_size)
    if piece % 128:
        pieces = hidden.reshape(rows, depth // (piece * group), group, piece)
        return [
            lax.dynamic_index_in_dim(pieces, ids[k], 2, keepdims=False).reshape(rows, depth // group)
            for k in range(group)
        ]
    return pallas(
        functools.partial(cut_kernel, group, fsdp_size, ctx_size, piece),
        tuple(shape((rows, depth // group)) for _ in range(group)),
        [ids],
        [hidden],
        "cut",
        0,
    )


def project_kernel(columns, width, ids_ref, hidden_ref, *refs):
    out_ref = refs[len(columns)]
    total = None
    for part, first in enumerate(columns):
        weight = refs[part]
        rows = weight.shape[0]
        start = pl.multiple_of(ids_ref[part] * rows, rows)
        term = nn(hidden_ref[:, pl.ds(start, rows)], weight[:, first : first + width])
        total = term if total is None else total + term
    out_ref[...] = total.astype(BF16)


def project(ids, hidden, parts, width):
    return pallas(
        functools.partial(project_kernel, [first for _, first in parts], width),
        shape((hidden.shape[0], width)),
        [ids],
        [hidden] + [array for array, _ in parts],
        "project",
        2 * hidden.size * width,
    )


def hidden_kernel(layout, ids_ref, grad_ref, *refs):
    out_ref = refs[len(refs) - 1]
    at = 0
    for part, pieces in enumerate(layout):
        total = None
        for first, count in pieces:
            weight = refs[at]
            at += 1
            rows = weight.shape[0]
            term = nt(grad_ref[:, first : first + count], weight[...])
            total = term if total is None else total + term
        start = pl.multiple_of(ids_ref[part] * rows, rows)
        out_ref[:, pl.ds(start, rows)] = total.astype(BF16)


def hidden_grad(ids, grad, layout, weights, depth):
    return pallas(
        functools.partial(hidden_kernel, layout),
        shape((grad.shape[0], depth)),
        [ids],
        [grad, *weights],
        "hidden_grad",
        2 * grad.size * depth,
    )


def attend_kernel(blocks, group, bq, bk, ids_ref, pages_ref, *refs):
    q_parts, k_parts, v_parts, g_parts = (refs[i * blocks : (i + 1) * blocks] for i in range(4))
    grad_ref, own_ref = refs[4 * blocks : 4 * blocks + 2]
    q_ref, k_ref, v_ref, do_ref, s_ref, dp_ref, dk_ref, dv_ref, kt_ref = refs[4 * blocks + 2 :]
    seq, hd = do_ref.shape
    rows = seq // blocks
    near = rows * group
    scale = hd**-0.5
    scale2 = scale * math.log2(math.e)
    for block in range(blocks):
        here = pl.ds(pl.multiple_of(ids_ref[block] * rows, rows), rows)
        q_ref[here, :] = q_parts[block][...]
        k_ref[here, :] = k_parts[block][...]
        v_ref[here, :] = v_parts[block][...]
        do_ref[here, :] = g_parts[block][...]
    dk_ref[...] = jnp.zeros_like(dk_ref)
    dv_ref[...] = jnp.zeros_like(dv_ref)
    kt_ref[...] = k_ref[...].T
    ends, end = [], jnp.int32(0)
    for page in range(pages_ref.shape[1]):
        end = end + pages_ref[0, page]
        ends.append(end)
    low = lax.div(ids_ref[0], group) * near
    near_first, near_last = lax.div(low, bk), lax.div(low, bk) + near // bk

    def limit_of(pos):
        limit = jnp.full_like(pos, seq)
        for page_end in ends:
            limit = jnp.minimum(limit, jnp.where(page_end > pos, page_end, seq))
        return limit

    @pl.loop(0, seq // bq)
    def _(i):
        q0 = pl.multiple_of(i * bq, bq)
        limits = limit_of(q0 + lax.broadcasted_iota(jnp.int32, (1, bq), 1))
        count = lax.div(limit_of(q0 + (bq - 1)) + (bk - 1), bk)
        q = q_ref[pl.ds(q0, bq), :]
        do = do_ref[pl.ds(q0, bq), :]

        def scores(j, row_max):
            k0 = pl.multiple_of(j * bk, bk)
            s = nt(k_ref[pl.ds(k0, bk), :], q) * scale2
            key = k0 + lax.broadcasted_iota(jnp.int32, (bk, 1), 0)
            s = jnp.where(key < limits, s, -1e30)
            s_ref[pl.ds(k0, bk), :] = s
            dp_ref[pl.ds(k0, bk), :] = nt(v_ref[pl.ds(k0, bk), :], do)
            return jnp.maximum(row_max, jnp.max(s, axis=0, keepdims=True))

        row_max = lax.fori_loop(0, count, scores, jnp.full((1, bq), -3e38, F32))

        def sums(j, carry):
            total, dot = carry
            k0 = pl.multiple_of(j * bk, bk)
            p = jnp.exp2(s_ref[pl.ds(k0, bk), :] - row_max)
            s_ref[pl.ds(k0, bk), :] = p
            total = total + jnp.sum(p, axis=0, keepdims=True)
            dot = dot + jnp.sum(p * dp_ref[pl.ds(k0, bk), :], axis=0, keepdims=True)
            return total, dot

        zero = jnp.zeros((1, bq), F32)
        total, dot = lax.fori_loop(0, count, sums, (zero, zero))
        inv = 1.0 / total
        gain = inv * scale
        shift = dot * inv * gain

        def dscore(j):
            k0 = pl.multiple_of(j * bk, bk)
            p = s_ref[pl.ds(k0, bk), :]
            return k0, p, (p * (dp_ref[pl.ds(k0, bk), :] * gain - shift)).astype(BF16)

        def key_grads(j, carry):
            k0, p, ds = dscore(j)
            dv_ref[pl.ds(k0 - low, bk), :] += nn((p * inv).astype(BF16), do)
            dk_ref[pl.ds(k0 - low, bk), :] += nn(ds, q)
            return carry

        def query_grads(j, dqt):
            k0, _, ds = dscore(j)
            return dqt + nn(kt_ref[:, pl.ds(k0, bk)], ds)

        def all_grads(j, dqt):
            k0, p, ds = dscore(j)
            dv_ref[pl.ds(k0 - low, bk), :] += nn((p * inv).astype(BF16), do)
            dk_ref[pl.ds(k0 - low, bk), :] += nn(ds, q)
            return dqt + nn(kt_ref[:, pl.ds(k0, bk)], ds)

        first, last = jnp.minimum(near_first, count), jnp.minimum(near_last, count)
        is_near = (q0 >= low) & (q0 < low + near)

        @pl.when(is_near)
        def _():
            dqt = lax.fori_loop(0, first, query_grads, jnp.zeros((hd, bq), F32))
            dqt = lax.fori_loop(first, last, all_grads, dqt)
            dqt = lax.fori_loop(last, count, query_grads, dqt)
            grad_ref[pl.ds(pl.multiple_of(q0 - low, bq), bq), :hd] = dqt.T.astype(BF16)

        @pl.when(jnp.logical_not(is_near))
        def _():
            lax.fori_loop(first, last, key_grads, 0)

    grad_ref[:, hd : 2 * hd] = dk_ref[...].astype(BF16)
    grad_ref[:, 2 * hd :] = dv_ref[...].astype(BF16)
    own = pl.multiple_of(lax.rem(ids_ref[0], group) * rows, rows)
    own_ref[...] = grad_ref[pl.ds(own, rows), :]


def attend(ids, pages, q, k, v, g, group):
    blocks = len(q)
    rows, hd = q[0].shape
    seq = rows * blocks
    near = rows * group
    block = 512 if near % 512 == 0 and seq <= 4096 else rows
    return pallas(
        functools.partial(attend_kernel, blocks, group, block, block),
        (shape((near, 3 * hd)), shape((rows, 3 * hd))),
        [ids, pages],
        [*q, *k, *v, *g],
        "attend",
        10 * seq * seq * hd,
        [pltpu.VMEM((seq, hd), BF16)] * 4
        + [pltpu.VMEM((seq, block), F32)] * 2
        + [pltpu.VMEM((near, hd), F32)] * 2
        + [pltpu.VMEM((hd, seq), BF16)],
    )


def weight_kernel(group, fsdp_size, ids_ref, fsdp_ref, grad_ref, *refs):
    parts, (kept_ref, away_ref) = refs[:group], refs[group:]
    rows = grad_ref.shape[0] // group
    size = parts[0].shape[1] // fsdp_size
    for j in range(fsdp_size):
        columns = pl.ds(pl.multiple_of(fsdp_ref[j] * size, size), size)
        total = None
        for k in range(group):
            here = pl.ds(pl.multiple_of(ids_ref[k] * rows, rows), rows)
            term = tn(parts[k][:, columns], grad_ref[here, :])
            total = term if total is None else total + term
        out = away_ref if j % 2 else kept_ref
        out[j // 2] = total.astype(out.dtype)


def weight_grad(ids, fsdp_ids, grad, parts):
    group, fsdp_size, width = len(parts), fsdp_ids.shape[0], grad.shape[1]
    size = parts[0].shape[1] // fsdp_size
    rows = parts[0].shape[0]
    if size % 128:
        total = sum(
            tn(parts[k], lax.dynamic_slice_in_dim(grad, ids[k] * rows, rows, 0)) for k in range(group)
        ).reshape(fsdp_size, size, width)
        both = jnp.take(total, fsdp_ids, axis=0).reshape(fsdp_size // 2, 2, size, width)
        return both[:, 0], both[:, 1].astype(BF16)
    half = (fsdp_size // 2, size, width)
    return pallas(
        functools.partial(weight_kernel, group, fsdp_size),
        (shape(half, F32), shape(half)),
        [ids, fsdp_ids],
        [grad, *parts],
        "weight_grad",
        2 * grad.size * fsdp_size * size,
    )


def swap(array, axis, size, distance):
    return lax.ppermute(array, axis, [(i, i ^ distance) for i in range(size)])


def gather_blocks(block, size):
    even = [swap(block, "ctx", size, k) if k else block for k in range(0, size, 2)]
    odd = swap(jnp.concatenate(even, axis=0), "ctx", size, 1)
    rows = block.shape[0]
    return even + [odd[i * rows : (i + 1) * rows] for i in range(size // 2)]


def local(ctx_size, fsdp_size, hidden_in, page_tokens, grad_attn, w_qkv):
    hidden, grad_out = hidden_in[0], grad_attn[0]
    rows, depth = hidden.shape
    hd = grad_out.shape[1]
    f, c = lax.axis_index("fsdp"), lax.axis_index("ctx")
    fsdp_ids = f ^ jnp.arange(fsdp_size, dtype=jnp.int32)
    order = jnp.array([*range(0, ctx_size, 2), *range(1, ctx_size, 2)], jnp.int32)
    ctx_ids = c ^ order
    group = min(4, ctx_size)
    group_ids = (c % group) ^ jnp.arange(group, dtype=jnp.int32)

    firsts = [hd, 2 * hd, 0]
    top = fsdp_size // 2
    parts = {0: [(w_qkv, first) for first in firsts]}
    parts[top] = [(swap(w_qkv[:, first : first + hd], "fsdp", fsdp_size, top), 0) for first in firsts]
    bit = top // 2
    while bit:
        for k in list(parts):
            moved = {}
            for array, _ in parts[k]:
                if id(array) not in moved:
                    moved[id(array)] = swap(array, "fsdp", fsdp_size, bit)
            parts[k ^ bit] = [(moved[id(array)], first) for array, first in parts[k]]
        bit //= 2

    g_parts = gather_blocks(grad_out, ctx_size)
    chunks = cut(group_ids, hidden, group, fsdp_size, ctx_size)
    hidden_parts = [swap(chunks[k], "ctx", ctx_size, k) if k else chunks[k] for k in range(group)]

    gathered = []
    for number in range(3):
        weights = [parts[k][number] for k in range(fsdp_size)]
        gathered.append(gather_blocks(project(fsdp_ids, hidden, weights, hd), ctx_size))
    k_parts, v_parts, q_parts = gathered
    grad_near, grad_own = attend(ctx_ids, page_tokens, q_parts, k_parts, v_parts, g_parts, group)

    layout, weights = [], []
    for k in range(fsdp_size):
        if parts[k][0][0] is parts[k][1][0]:
            layout.append([(0, 3 * hd)])
            weights.append(parts[k][0][0])
        else:
            layout.append([(first, hd) for first in firsts])
            weights.extend(array for array, _ in parts[k])
    grad_inputs = hidden_grad(fsdp_ids, grad_own, layout, weights, depth)

    kept, away = weight_grad(group_ids, fsdp_ids, grad_near, hidden_parts)
    bit = 1
    while bit < fsdp_size:
        total = kept + swap(away, "fsdp", fsdp_size, bit).astype(F32)
        bit *= 2
        if bit < fsdp_size:
            kept, away = total[0::2], total[1::2].astype(BF16)
    total = total[0]
    bit = group
    while bit < ctx_size:
        half = total.astype(BF16)
        total = half.astype(F32) + swap(half, "ctx", ctx_size, bit).astype(F32)
        bit *= 2
    total = total.astype(BF16)
    gathered = jnp.stack([swap(total, "ctx", ctx_size, k) if k else total for k in range(group)])
    gathered = jnp.take(gathered, group_ids, axis=0)
    size = total.shape[0] // (ctx_size // group)
    grad_weights = gathered.reshape(group, ctx_size // group, size, -1).swapaxes(0, 1)
    return grad_inputs[None], grad_weights.reshape(ctx_size * size, -1).astype(F32)


def solution(mesh):
    in_specs = (P("fsdp", "ctx", None), P("fsdp", None), P("fsdp", "ctx", None), P("fsdp", None))
    out_specs = (P("fsdp", "ctx", None), P("fsdp", None))
    body = functools.partial(local, mesh.shape["ctx"], mesh.shape["fsdp"])
    return jax.shard_map(body, mesh=mesh, in_specs=in_specs, out_specs=out_specs, check_vma=False)
```

time: 203 us -> 138 us (0.68)
  waiting for transfers between devices: 71.8 us -> 50.4 us
  starting transfers between devices: 56.9 us -> 36.1 us
  between operations: 15.8 us -> 0.97 us
  local copies, waits for them, and re-layouts: 18.9 us -> 8.86 us
  Pallas kernels: 34.6 us -> 37.6 us
    all_to_all x1 -> x0, waiting for transfers between devices: 15.2 us -> none  [local(): gathered = lax.all_to_all(copies, 'ctx', 0, 0)]
    dynamic_slice x1 -> x0, local copies, waits for them, and re-layouts: 13.2 us -> none  [local(): lax.dynamic_index_in_dim(cut, ctx_ids[k], 2, keepdims=False)]
    all_to_all x1 -> x0, starting transfers between devices: 11 us -> none  [local(): gathered = lax.all_to_all(copies, 'ctx', 0, 0)]
    ppermute x19 -> x32, starting transfers between devices: 45.9 us -> 36.1 us  [swap(): return lax.ppermute(array, axis, [(i, i ^ distance) for i in range(size)])]
    ppermute x19 -> x32, waiting for transfers between devices: 56.6 us -> 50.4 us  [swap(): return lax.ppermute(array, axis, [(i, i ^ distance) for i in range(size)])]
    slice x1 -> x6, local copies, waits for them, and re-layouts: 0.66 us -> 4.06 us  [the longest x4 2.88 us: gather_blocks(): return even + [odd[i * rows:(i + 1) * rows] for i in range(size // 2)]]
    pallas_call x4 -> x7, Pallas kernels: 34.6 us -> 37.6 us  [pallas(): pl.pallas_call(kernel, out_shape=out_shape, in_specs=[SMEM] * len(scalars...]
  transfers between devices with their start and end apart: 20 -> 32, of which waited for: 8 -> 15; matrix products, arithmetic and copies ran while one was open for 9% -> 5% of each run, Pallas kernels for 4% -> 24%
where the time goes in v2:
time: 138 us
  waiting for transfers between devices  50.4 us (37%)
  Pallas kernels  37.6 us (27%)
  starting transfers between devices  36.1 us (26%)
  local copies, waits for them, and re-layouts  8.86 us (6%)
  other arithmetic  4.15 us (3%)
    ppermute x32, waiting for transfers between devices, swap(): return lax.ppermute(array, axis, [(i, i ^ distance) for i in range(size)])  50.4 us
    pallas_call x7, Pallas kernels, pallas(): pl.pallas_call(kernel, out_shape=out_shape, in_specs=[SMEM] * len(scalars...  37.6 us
    ppermute x32, starting transfers between devices, swap(): return lax.ppermute(array, axis, [(i, i ^ distance) for i in range(size)])  36.1 us
    slice x4, local copies, waits for them, and re-layouts, gather_blocks(): return even + [odd[i * rows:(i + 1) * rows] for i in range(size // 2)]  2.88 us
    unnamed x58, local copies, waits for them, and re-layouts  2.82 us
  transfers between devices with their start and end apart: 32, of which 15 were waited for; matrix products, arithmetic and copies ran while one was open for 5% of the time, Pallas kernels for 24%

profile of v2, /device:TPU:0, one launch (start us, length us, event | category | flops | bytes accessed | tf_op | source)
XLA Modules:
  0.0 138.0 jit_solution(14538185579819673327)
XLA Ops:
  0.7 0.5 collective-permute-start
  1.2 1.2 fusion.3
  2.3 2.6 %collective-permute-start.1 = (bf16[1024,128]{1,0:T(8,128)(2,1)S(1)}, bf16[1024,128]{1,0:T(8,128)(2,1)S(1)}, u32[]{:S(2)}, u32[]{:S(2)}) collective-permute-start(bf16[1024,128]{1,0:T(8,128)(2,1)S(1)} %get-tuple-element.20), channel_id=1, source_target_pairs={{0,2},{1,3},{2,0},{3,1},{4,6},{5,7},{6,4},{7,5},{8,10},{9,11},{10,... | collective-permute-start | bytes 786440 | tf_op jit(solution)/shard_map/ppermute | solution.py:287
  4.9 1.6 %collective-permute-start.19 = (bf16[256,128]{1,0:T(8,128)(2,1)S(1)}, bf16[256,128]{1,0:T(8,128)(2,1)S(1)}, u32[]{:S(2)}, u32[]{:S(2)}) collective-permute-start(bf16[256,128]{1,0:T(8,128)(2,1)S(1)} %bitcast.27), channel_id=1, source_target_pairs={{0,8},{4,12},{8,0},{12,4},{16,24},{20,28},{24,16},{28,20},{1,9},{5... | collective-permute-start | bytes 196616 | tf_op jit(solution)/shard_map/ppermute | solution.py:287
  6.5 2.6 %collective-permute-start.20 = (bf16[256,128]{1,0:T(8,128)(2,1)S(1)}, bf16[256,128]{1,0:T(8,128)(2,1)S(1)}, u32[]{:S(2)}, u32[]{:S(2)}) collective-permute-start(bf16[256,128]{1,0:T(8,128)(2,1)S(1)} %bitcast.28), channel_id=1, source_target_pairs={{0,16},{4,20},{8,24},{12,28},{16,0},{20,4},{24,8},{28,12},{1,17},{... | collective-permute-start | bytes 196616 | tf_op jit(solution)/shard_map/ppermute | solution.py:287
  9.1 0.2 collective-permute-start.21
  9.3 0.4 collective-permute-start.7
  9.7 4.4 %collective-permute-done.20.refs_26_ = bf16[256,128]{1,0:T(8,128)(2,1)S(1)} collective-permute-done((bf16[256,128]{1,0:T(8,128)(2,1)S(1)}, bf16[256,128]{1,0:T(8,128)(2,1)S(1)}, u32[]{:S(2)}, u32[]{:S(2)}) %collective-permute-start.20) | collective-permute-done | bytes 65568 | tf_op jit(solution)/shard_map/ppermute | solution.py:287
  14.1 0.5 collective-permute-start.13
  14.6 0.6 collective-permute-done.21.refs_27_
  15.3 1.6 %collective-permute-start.22 = (bf16[1024,128]{1,0:T(8,128)(2,1)S(1)}, bf16[1024,128]{1,0:T(8,128)(2,1)S(1)}, u32[]{:S(2)}, u32[]{:S(2)}) collective-permute-start(bf16[1024,128]{1,0:T(8,128)(2,1)S(1)} %pad_maximum_fusion.4), channel_id=1, source_target_pairs={{0,4},{4,0},{8,12},{12,8},{16,20},{20,16},{24,28},{28,24},{1,5},{5... | collective-permute-start | bytes 786440 | tf_op jit(solution)/shard_map/ppermute | solution.py:287
  16.9 0.6 broadcast_xor_fusion.ids_ref
  17.4 0.5 iota_xor_fusion.1.ids_ref.fsdp_ref
  18.0 0.6 collective-permute-done.7.refs_2_
  18.6 0.5 iota_xor_fusion.ids_ref
  19.1 3.4 %cut.1 = (bf16[256,1024]{1,0:T(8,128)(2,1)}, bf16[256,1024]{1,0:T(8,128)(2,1)}, bf16[256,1024]{1,0:T(8,128)(2,1)}, bf16[256,1024]{1,0:T(8,128)(2,1)}) custom-call(s32[4]{0:T(128)} %iota_xor_fusion.ids_ref, bf16[256,4096]{1,0:T(8,128)(2,1)} %bitcast.15), custom_call_target="tpu_custom_call" | custom-call | bytes 4194304 | tf_op jit(solution)/shard_map/cut/pallas_call | solution.py:33
  22.4 0.7 collective-permute-done.13.refs_2_.refs_3_
  23.1 0.7 copy-done.4
  23.9 0.9 copy-done
  24.8 3.5 %project.3.refs_0_ = bf16[256,128]{1,0:T(8,128)(2,1)} custom-call(s32[4]{0:T(128)} %iota_xor_fusion.1.ids_ref.fsdp_ref, bf16[256,4096]{1,0:T(8,128)(2,1)} %bitcast.16, bf16[1024,384]{1,0:T(8,128)(2,1)} %refs_0_.7, bf16[1024,384]{1,0:T(8,128)(2,1)} %copy-done, bf16[1024,128]{1,0:T(8,128)(2,1)} %copy-done.1, bf16[1024,128]{1,0:T(8,128)(2,1)} %copy-done.4), custom_call_target="tpu_custom_call" | custom-call | flops 268435456 | bytes 4259840 | tf_op jit(solution)/shard_map/project/pallas_call | solution.py:33
  28.3 1.9 %collective-permute-start.3 = (bf16[256,128]{1,0:T(8,128)(2,1)}, bf16[256,128]{1,0:T(8,128)(2,1)S(1)}, u32[]{:S(2)}, u32[]{:S(2)}) collective-permute-start(bf16[256,128]{1,0:T(8,128)(2,1)} %project.3.refs_0_), channel_id=1, source_target_pairs={{0,8},{4,12},{8,0},{12,4},{16,24},{20,28},{24,16},{28,20},{1,9},{5... | collective-permute-start | bytes 196616 | tf_op jit(solution)/shard_map/ppermute | solution.py:287
  30.2 2.8 %collective-permute-start.4 = (bf16[256,128]{1,0:T(8,128)(2,1)}, bf16[256,128]{1,0:T(8,128)(2,1)S(1)}, u32[]{:S(2)}, u32[]{:S(2)}) collective-permute-start(bf16[256,128]{1,0:T(8,128)(2,1)} %project.3.refs_0_), channel_id=1, source_target_pairs={{0,16},{4,20},{8,24},{12,28},{16,0},{20,4},{24,8},{28,12},{1,17},{... | collective-permute-start | bytes 196616 | tf_op jit(solution)/shard_map/ppermute | solution.py:287
  33.0 0.7 fusion.4
  33.7 1.6 %collective-permute-start.23 = (bf16[256,1024]{1,0:T(8,128)(2,1)S(1)}, bf16[256,1024]{1,0:T(8,128)(2,1)S(1)}, u32[]{:S(2)}, u32[]{:S(2)}) collective-permute-start(bf16[256,1024]{1,0:T(8,128)(2,1)S(1)} %copy-done.24), channel_id=1, source_target_pairs={{0,4},{4,0},{8,12},{12,8},{16,20},{20,16},{24,28},{28,24},{1,5},{5... | collective-permute-start | bytes 1572872 | tf_op jit(solution)/shard_map/ppermute | solution.py:287
  35.3 3.5 %project.4.refs_8_ = bf16[256,128]{1,0:T(8,128)(2,1)} custom-call(s32[4]{0:T(128)} %iota_xor_fusion.1.ids_ref.fsdp_ref, bf16[256,4096]{1,0:T(8,128)(2,1)} %bitcast.17, bf16[1024,384]{1,0:T(8,128)(2,1)} %refs_0_.7, bf16[1024,384]{1,0:T(8,128)(2,1)} %copy-done, bf16[1024,128]{1,0:T(8,128)(2,1)} %copy-done.2, bf16[1024,128]{1,0:T(8,128)(2,1)} %copy-done.5), custom_call_target="tpu_custom_call" | custom-call | flops 268435456 | bytes 4259840 | tf_op jit(solution)/shard_map/project/pallas_call | solution.py:33
  38.8 0.7 collective-permute-start.9
  39.5 3.7 %collective-permute-start.10 = (bf16[256,128]{1,0:T(8,128)(2,1)}, bf16[256,128]{1,0:T(8,128)(2,1)S(1)}, u32[]{:S(2)}, u32[]{:S(2)}) collective-permute-start(bf16[256,128]{1,0:T(8,128)(2,1)} %project.4.refs_8_), channel_id=1, source_target_pairs={{0,16},{4,20},{8,24},{12,28},{16,0},{20,4},{24,8},{28,12},{1,17},{... | collective-permute-start | bytes 196616 | tf_op jit(solution)/shard_map/ppermute | solution.py:287
  43.3 0.7 collective-permute-start.6
  44.0 3.5 %project.5.refs_16_ = bf16[256,128]{1,0:T(8,128)(2,1)} custom-call(s32[4]{0:T(128)} %iota_xor_fusion.1.ids_ref.fsdp_ref, bf16[256,4096]{1,0:T(8,128)(2,1)} %bitcast.18, bf16[1024,384]{1,0:T(8,128)(2,1)} %refs_0_.7, bf16[1024,384]{1,0:T(8,128)(2,1)} %copy-done, bf16[1024,128]{1,0:T(8,128)(2,1)} %copy-done.3, bf16[1024,128]{1,0:T(8,128)(2,1)} %copy-done.6), custom_call_target="tpu_custom_call" | custom-call | flops 268435456 | bytes 4259840 | tf_op jit(solution)/shard_map/project/pallas_call | solution.py:33
  47.5 0.7 collective-permute-start.15
  48.2 3.7 %collective-permute-start.16 = (bf16[256,128]{1,0:T(8,128)(2,1)}, bf16[256,128]{1,0:T(8,128)(2,1)S(1)}, u32[]{:S(2)}, u32[]{:S(2)}) collective-permute-start(bf16[256,128]{1,0:T(8,128)(2,1)} %project.5.refs_16_), channel_id=1, source_target_pairs={{0,16},{4,20},{8,24},{12,28},{16,0},{20,4},{24,8},{28,12},{1,17},{... | collective-permute-start | bytes 196616 | tf_op jit(solution)/shard_map/ppermute | solution.py:287
  52.0 0.3 collective-permute-done.15.refs_17_
  52.3 0.5 collective-permute-start.24
  52.7 3.2 %collective-permute-done.16.refs_18_ = bf16[256,128]{1,0:T(8,128)(2,1)S(1)} collective-permute-done((bf16[256,128]{1,0:T(8,128)(2,1)}, bf16[256,128]{1,0:T(8,128)(2,1)S(1)}, u32[]{:S(2)}, u32[]{:S(2)}) %collective-permute-start.16) | collective-permute-done | bytes 65568 | tf_op jit(solution)/shard_map/ppermute | solution.py:287
  55.9 0.6 collective-permute-start.25
  56.6 2.5 %collective-permute-done.17.refs_19_ = bf16[256,128]{1,0:T(8,128)(2,1)S(1)} collective-permute-done((bf16[256,128]{1,0:T(8,128)(2,1)}, bf16[256,128]{1,0:T(8,128)(2,1)S(1)}, u32[]{:S(2)}, u32[]{:S(2)}) %collective-permute-start.17) | collective-permute-done | bytes 65568 | tf_op jit(solution)/shard_map/ppermute | solution.py:287
  59.0 1.4 collective-permute-start.12
  60.4 0.9 pad_maximum_fusion.3
  61.3 0.7 collective-permute-start.18
  62.0 0.7 fusion.7
  62.7 5.6 %collective-permute-done.12 = bf16[1024,128]{1,0:T(8,128)(2,1)S(1)} collective-permute-done((bf16[1024,128]{1,0:T(8,128)(2,1)S(1)}, bf16[1024,128]{1,0:T(8,128)(2,1)S(1)}, u32[]{:S(2)}, u32[]{:S(2)}) %collective-permute-start.12) | collective-permute-done | bytes 262176 | tf_op jit(solution)/shard_map/ppermute | solution.py:287
  68.3 0.7 fusion.6
  69.0 11.3 %collective-permute-done.18 = bf16[1024,128]{1,0:T(8,128)(2,1)S(1)} collective-permute-done((bf16[1024,128]{1,0:T(8,128)(2,1)S(1)}, bf16[1024,128]{1,0:T(8,128)(2,1)S(1)}, u32[]{:S(2)}, u32[]{:S(2)}) %collective-permute-start.18) | collective-permute-done | bytes 262176 | tf_op jit(solution)/shard_map/ppermute | solution.py:287
  80.3 0.7 fusion.5
  81.1 15.2 %attend.1 = (bf16[1024,384]{1,0:T(8,128)(2,1)}, bf16[256,384]{1,0:T(8,128)(2,1)}) custom-call(s32[8]{0:T(128)} %broadcast_xor_fusion.ids_ref, s32[1,8]{1,0:T(1,128)} %pages_ref.1, bf16[256,128]{1,0:T(8,128)(2,1)} %project.3.refs_0_, bf16[256,128]{1,0:T(8,128)(2,1)} %copy-done.13, bf16[256,128]{1,0:T(8,128)(2,1)} %copy-done.14, bf16[256,128]{1,0:T(8,128)(2,1)} %copy-done.15, ...), custom_call_target="tpu_custom_call" | custom-call | flops 5368709120 | bytes 3080192 | tf_op jit(solution)/shard_map/attend/pallas_call | solution.py:33
  96.3 0.7 copy-done.25
  97.0 0.2 copy-done.26
  97.2 0.2 copy-done.27
  97.4 3.8 %weight_grad.1 = (f32[2,256,384]{2,1,0:T(8,128)}, bf16[2,256,384]{2,1,0:T(8,128)(2,1)}) custom-call(s32[4]{0:T(128)} %iota_xor_fusion.ids_ref, s32[4]{0:T(128)} %iota_xor_fusion.1.ids_ref.fsdp_ref, bf16[1024,384]{1,0:T(8,128)(2,1)} %get-tuple-element.11.grad_ref, bf16[256,1024]{1,0:T(8,128)(2,1)} %get-tuple-element.12.refs_0_, bf16[256,1024]{1,0:T(8,128)(2,1)} %copy-done.25, ...), custom_call_target="tpu_custom_call" | custom-call | flops 805306368 | bytes 4063232 | tf_op jit(solution)/shard_map/weight_grad/pallas_call | solution.py:33
  101.2 1.9 %collective-permute-done.26 = bf16[2,256,384]{2,1,0:T(8,128)(2,1)S(1)} collective-permute-done((bf16[2,256,384]{2,1,0:T(8,128)(2,1)}, bf16[2,256,384]{2,1,0:T(8,128)(2,1)S(1)}, u32[]{:S(2)}, u32[]{:S(2)}) %collective-permute-start.26) | collective-permute-done | bytes 393248 | tf_op jit(solution)/shard_map/ppermute | solution.py:287
  103.2 1.2 convert_add_fusion
  104.4 3.4 %collective-permute-start.27 = (bf16[1,256,384]{2,1,0:T(8,128)(2,1)S(1)}, bf16[1,256,384]{2,1,0:T(8,128)(2,1)S(1)}, u32[]{:S(2)}, u32[]{:S(2)}) collective-permute-start(bf16[1,256,384]{2,1,0:T(8,128)(2,1)S(1)} %slice.113), channel_id=1, source_target_pairs={{0,2},{1,3},{2,0},{3,1},{4,6},{5,7},{6,4},{7,5},{8,10},{9,11},{10,... | collective-permute-start | bytes 589832 | tf_op jit(solution)/shard_map/ppermute | solution.py:287
  107.8 5.2 %collective-permute-done.27 = bf16[1,256,384]{2,1,0:T(8,128)(2,1)S(1)} collective-permute-done((bf16[1,256,384]{2,1,0:T(8,128)(2,1)S(1)}, bf16[1,256,384]{2,1,0:T(8,128)(2,1)S(1)}, u32[]{:S(2)}, u32[]{:S(2)}) %collective-permute-start.27) | collective-permute-done | bytes 196640 | tf_op jit(solution)/shard_map/ppermute | solution.py:287
  113.2 10.5 %collective-permute-done.28 = bf16[256,384]{1,0:T(8,128)(2,1)S(1)} collective-permute-done((bf16[256,384]{1,0:T(8,128)(2,1)S(1)}, bf16[256,384]{1,0:T(8,128)(2,1)S(1)}, u32[]{:S(2)}, u32[]{:S(2)}) %collective-permute-start.28) | collective-permute-done | bytes 196640 | tf_op jit(solution)/shard_map/ppermute | solution.py:287
  123.8 2.3 %collective-permute-start.30 = (bf16[256,384]{1,0:T(8,128)(2,1)S(1)}, bf16[256,384]{1,0:T(8,128)(2,1)S(1)}, u32[]{:S(2)}, u32[]{:S(2)}) collective-permute-start(bf16[256,384]{1,0:T(8,128)(2,1)S(1)} %add_convert_fusion), channel_id=1, source_target_pairs={{0,8},{4,12},{8,0},{12,4},{16,24},{20,28},{24,16},{28,20},{1,9},{5... | collective-permute-start | bytes 589832 | tf_op jit(solution)/shard_map/ppermute | solution.py:287
  126.1 1.2 collective-permute-start.29
  127.3 4.8 %hidden_grad.1 = bf16[256,4096]{1,0:T(8,128)(2,1)} custom-call(s32[4]{0:T(128)} %iota_xor_fusion.1.ids_ref.fsdp_ref, bf16[256,384]{1,0:T(8,128)(2,1)} %get-tuple-element.10.grad_ref, bf16[1024,384]{1,0:T(8,128)(2,1)} %refs_0_.7, bf16[1024,384]{1,0:T(8,128)(2,1)} %copy-done, bf16[1024,128]{1,0:T(8,128)(2,1)} %copy-done.2, bf16[1024,128]{1,0:T(8,128)(2,1)} %copy-done.3, ...), custom_call_target="tpu_custom_call" | custom-call | flops 805306368 | bytes 5439488 | tf_op jit(solution)/shard_map/hidden_grad/pallas_call | solution.py:33
  132.1 0.4 collective-permute-done.31
  132.5 2.6 %collective-permute-done.30 = bf16[256,384]{1,0:T(8,128)(2,1)S(1)} collective-permute-done((bf16[256,384]{1,0:T(8,128)(2,1)S(1)}, bf16[256,384]{1,0:T(8,128)(2,1)S(1)}, u32[]{:S(2)}, u32[]{:S(2)}) %collective-permute-start.30) | collective-permute-done | bytes 196640 | tf_op jit(solution)/shard_map/ppermute | solution.py:287
  135.1 0.6 collective-permute-done.29
  135.7 0.1 pad_maximum_fusion
  135.9 0.7 gather_fusion
  136.6 0.2 convert_bitcast_fusion
  136.8 1.3 copy.7
  (88 shorter events, 0.6 us)
Async XLA Ops:
  0.6 16.2 %copy-start.28 = (s32[8]{0:T(128)S(1)}, s32[8]{0:T(128)}, u32[]{:S(2)}) copy-start(s32[8]{0:T(128)} %constant.37.clone) | copy-start | bytes 100
  0.6 4.3 %copy-start.9 = (bf16[1,256,128]{2,1,0:T(8,128)(2,1)S(1)}, bf16[1,256,128]{2,1,0:T(8,128)(2,1)}, u32[]{:S(2)}) copy-start(bf16[1,256,128]{2,1,0:T(8,128)(2,1)} %param.7) | copy-start | bytes 196612
  0.7 22.5 %collective-permute-start = (bf16[1024,384]{1,0:T(8,128)(2,1)}, bf16[1024,384]{1,0:T(8,128)(2,1)S(1)}, u32[]{:S(2)}, u32[]{:S(2)}) collective-permute-start(bf16[1024,384]{1,0:T(8,128)(2,1)} %refs_0_.7), channel_id=1, source_target_pairs={{0,1},{1,0},{2,3},{3,2},{4,5},{5,4},{6,7},{7,6},{8,9},{9,8},{10,11... | collective-permute-start | bytes 2359304 | tf_op jit(solution)/shard_map/ppermute | solution.py:287
  2.3 14.5 %collective-permute-start.1 = (bf16[1024,128]{1,0:T(8,128)(2,1)S(1)}, bf16[1024,128]{1,0:T(8,128)(2,1)S(1)}, u32[]{:S(2)}, u32[]{:S(2)}) collective-permute-start(bf16[1024,128]{1,0:T(8,128)(2,1)S(1)} %get-tuple-element.20), channel_id=1, source_target_pairs={{0,2},{1,3},{2,0},{3,1},{4,6},{5,7},{6,4},{7,5},{8,10},{9,11},{10,... | collective-permute-start | bytes 786440 | tf_op jit(solution)/shard_map/ppermute | solution.py:287
  4.9 4.4 %collective-permute-start.19 = (bf16[256,128]{1,0:T(8,128)(2,1)S(1)}, bf16[256,128]{1,0:T(8,128)(2,1)S(1)}, u32[]{:S(2)}, u32[]{:S(2)}) collective-permute-start(bf16[256,128]{1,0:T(8,128)(2,1)S(1)} %bitcast.27), channel_id=1, source_target_pairs={{0,8},{4,12},{8,0},{12,4},{16,24},{20,28},{24,16},{28,20},{1,9},{5... | collective-permute-start | bytes 196616 | tf_op jit(solution)/shard_map/ppermute | solution.py:287
  6.5 7.6 %collective-permute-start.20 = (bf16[256,128]{1,0:T(8,128)(2,1)S(1)}, bf16[256,128]{1,0:T(8,128)(2,1)S(1)}, u32[]{:S(2)}, u32[]{:S(2)}) collective-permute-start(bf16[256,128]{1,0:T(8,128)(2,1)S(1)} %bitcast.28), channel_id=1, source_target_pairs={{0,16},{4,20},{8,24},{12,28},{16,0},{20,4},{24,8},{28,12},{1,17},{... | collective-permute-start | bytes 196616 | tf_op jit(solution)/shard_map/ppermute | solution.py:287
  9.1 6.2 %collective-permute-start.21 = (bf16[256,128]{1,0:T(8,128)(2,1)S(1)}, bf16[256,128]{1,0:T(8,128)(2,1)S(1)}, u32[]{:S(2)}, u32[]{:S(2)}) collective-permute-start(bf16[256,128]{1,0:T(8,128)(2,1)S(1)} %bitcast.29), channel_id=1, source_target_pairs={{0,24},{4,28},{8,16},{12,20},{16,8},{20,12},{24,0},{28,4},{1,25},{... | collective-permute-start | bytes 196616 | tf_op jit(solution)/shard_map/ppermute | solution.py:287
  9.3 19.0 %copy-start.10 = (bf16[256,128]{1,0:T(8,128)(2,1)}, bf16[256,128]{1,0:T(8,128)(2,1)S(1)}, u32[]{:S(2)}) copy-start(bf16[256,128]{1,0:T(8,128)(2,1)S(1)} %collective-permute-done.19.refs_25_) | copy-start | bytes 196612
  9.3 9.2 %collective-permute-start.7 = (bf16[1024,128]{1,0:T(8,128)(2,1)S(1)}, bf16[1024,128]{1,0:T(8,128)(2,1)S(1)}, u32[]{:S(2)}, u32[]{:S(2)}) collective-permute-start(bf16[1024,128]{1,0:T(8,128)(2,1)S(1)} %get-tuple-element.19), channel_id=1, source_target_pairs={{0,2},{1,3},{2,0},{3,1},{4,6},{5,7},{6,4},{7,5},{8,10},{9,11},{10,... | collective-permute-start | bytes 786440 | tf_op jit(solution)/shard_map/ppermute | solution.py:287
  14.1 14.2 %copy-start.11 = (bf16[256,128]{1,0:T(8,128)(2,1)}, bf16[256,128]{1,0:T(8,128)(2,1)S(1)}, u32[]{:S(2)}) copy-start(bf16[256,128]{1,0:T(8,128)(2,1)S(1)} %collective-permute-done.20.refs_26_) | copy-start | bytes 196612
  14.1 9.0 %collective-permute-start.13 = (bf16[1024,128]{1,0:T(8,128)(2,1)S(1)}, bf16[1024,128]{1,0:T(8,128)(2,1)S(1)}, u32[]{:S(2)}, u32[]{:S(2)}) collective-permute-start(bf16[1024,128]{1,0:T(8,128)(2,1)S(1)} %get-tuple-element.18), channel_id=1, source_target_pairs={{0,2},{1,3},{2,0},{3,1},{4,6},{5,7},{6,4},{7,5},{8,10},{9,11},{10,... | collective-permute-start | bytes 786440 | tf_op jit(solution)/shard_map/ppermute | solution.py:287
  15.2 13.0 %copy-start.12 = (bf16[256,128]{1,0:T(8,128)(2,1)}, bf16[256,128]{1,0:T(8,128)(2,1)S(1)}, u32[]{:S(2)}) copy-start(bf16[256,128]{1,0:T(8,128)(2,1)S(1)} %collective-permute-done.21.refs_27_) | copy-start | bytes 196612
  15.3 17.7 %collective-permute-start.22 = (bf16[1024,128]{1,0:T(8,128)(2,1)S(1)}, bf16[1024,128]{1,0:T(8,128)(2,1)S(1)}, u32[]{:S(2)}, u32[]{:S(2)}) collective-permute-start(bf16[1024,128]{1,0:T(8,128)(2,1)S(1)} %pad_maximum_fusion.4), channel_id=1, source_target_pairs={{0,4},{4,0},{8,12},{12,8},{16,20},{20,16},{24,28},{28,24},{1,5},{5... | collective-permute-start | bytes 786440 | tf_op jit(solution)/shard_map/ppermute | solution.py:287
  16.9 6.3 %copy-start.1 = (bf16[1024,128]{1,0:T(8,128)(2,1)}, bf16[1024,128]{1,0:T(8,128)(2,1)S(1)}, u32[]{:S(2)}) copy-start(bf16[1024,128]{1,0:T(8,128)(2,1)S(1)} %collective-permute-done.1.refs_2_.refs_4_) | copy-start | bytes 786436
  16.9 6.3 %collective-permute-start.2 = (bf16[1024,128]{1,0:T(8,128)(2,1)S(1)}, bf16[1024,128]{1,0:T(8,128)(2,1)S(1)}, u32[]{:S(2)}, u32[]{:S(2)}) collective-permute-start(bf16[1024,128]{1,0:T(8,128)(2,1)S(1)} %collective-permute-done.1.refs_2_.refs_4_), channel_id=1, source_target_pairs={{0,1},{1,0},{2,3},{3,2},{4,5},{5,4},{6,7},{7,6},{8,9},{9,8},{10,11... | collective-permute-start | bytes 786440 | tf_op jit(solution)/shard_map/ppermute | solution.py:287
  18.5 9.7 %copy-start.2 = (bf16[1024,128]{1,0:T(8,128)(2,1)}, bf16[1024,128]{1,0:T(8,128)(2,1)S(1)}, u32[]{:S(2)}) copy-start(bf16[1024,128]{1,0:T(8,128)(2,1)S(1)} %collective-permute-done.7.refs_2_) | copy-start | bytes 786436
  18.6 15.1 %collective-permute-start.8 = (bf16[1024,128]{1,0:T(8,128)(2,1)S(1)}, bf16[1024,128]{1,0:T(8,128)(2,1)S(1)}, u32[]{:S(2)}, u32[]{:S(2)}) collective-permute-start(bf16[1024,128]{1,0:T(8,128)(2,1)S(1)} %collective-permute-done.7.refs_2_), channel_id=1, source_target_pairs={{0,1},{1,0},{2,3},{3,2},{4,5},{5,4},{6,7},{7,6},{8,9},{9,8},{10,11... | collective-permute-start | bytes 786440 | tf_op jit(solution)/shard_map/ppermute | solution.py:287
  22.4 11.3 %copy-start.24 = (bf16[256,1024]{1,0:T(8,128)(2,1)S(1)}, bf16[256,1024]{1,0:T(8,128)(2,1)}, u32[]{:S(2)}) copy-start(bf16[256,1024]{1,0:T(8,128)(2,1)} %get-tuple-element.13) | copy-start | bytes 1572868
  23.1 20.2 %copy-start.3 = (bf16[1024,128]{1,0:T(8,128)(2,1)}, bf16[1024,128]{1,0:T(8,128)(2,1)S(1)}, u32[]{:S(2)}) copy-start(bf16[1024,128]{1,0:T(8,128)(2,1)S(1)} %collective-permute-done.13.refs_2_.refs_3_) | copy-start | bytes 786436
  23.1 20.2 %collective-permute-start.14 = (bf16[1024,128]{1,0:T(8,128)(2,1)S(1)}, bf16[1024,128]{1,0:T(8,128)(2,1)S(1)}, u32[]{:S(2)}, u32[]{:S(2)}) collective-permute-start(bf16[1024,128]{1,0:T(8,128)(2,1)S(1)} %collective-permute-done.13.refs_2_.refs_3_), channel_id=1, source_target_pairs={{0,1},{1,0},{2,3},{3,2},{4,5},{5,4},{6,7},{7,6},{8,9},{9,8},{10,11... | collective-permute-start | bytes 786440 | tf_op jit(solution)/shard_map/ppermute | solution.py:287
  23.1 0.8 copy-start.4
  23.9 0.9 copy-start
  28.3 10.6 %collective-permute-start.3 = (bf16[256,128]{1,0:T(8,128)(2,1)}, bf16[256,128]{1,0:T(8,128)(2,1)S(1)}, u32[]{:S(2)}, u32[]{:S(2)}) collective-permute-start(bf16[256,128]{1,0:T(8,128)(2,1)} %project.3.refs_0_), channel_id=1, source_target_pairs={{0,8},{4,12},{8,0},{12,4},{16,24},{20,28},{24,16},{28,20},{1,9},{5... | collective-permute-start | bytes 196616 | tf_op jit(solution)/shard_map/ppermute | solution.py:287
  30.2 9.4 %collective-permute-start.4 = (bf16[256,128]{1,0:T(8,128)(2,1)}, bf16[256,128]{1,0:T(8,128)(2,1)S(1)}, u32[]{:S(2)}, u32[]{:S(2)}) collective-permute-start(bf16[256,128]{1,0:T(8,128)(2,1)} %project.3.refs_0_), channel_id=1, source_target_pairs={{0,16},{4,20},{8,24},{12,28},{16,0},{20,4},{24,8},{28,12},{1,17},{... | collective-permute-start | bytes 196616 | tf_op jit(solution)/shard_map/ppermute | solution.py:287
  32.9 10.3 %collective-permute-start.5 = (bf16[256,128]{1,0:T(8,128)(2,1)}, bf16[256,128]{1,0:T(8,128)(2,1)S(1)}, u32[]{:S(2)}, u32[]{:S(2)}) collective-permute-start(bf16[256,128]{1,0:T(8,128)(2,1)} %project.3.refs_0_), channel_id=1, source_target_pairs={{0,24},{4,28},{8,16},{12,20},{16,8},{20,12},{24,0},{28,4},{1,25},{... | collective-permute-start | bytes 196616 | tf_op jit(solution)/shard_map/ppermute | solution.py:287
  33.7 1.6 %copy-start.5 = (bf16[1024,128]{1,0:T(8,128)(2,1)}, bf16[1024,128]{1,0:T(8,128)(2,1)S(1)}, u32[]{:S(2)}) copy-start(bf16[1024,128]{1,0:T(8,128)(2,1)S(1)} %collective-permute-done.8.refs_3_.refs_5_) | copy-start | bytes 786436
  33.7 9.6 %copy-start.7 = (bf16[256,128]{1,0:T(8,128)(2,1)S(1)}, bf16[256,128]{1,0:T(8,128)(2,1)}, u32[]{:S(2)}) copy-start(bf16[256,128]{1,0:T(8,128)(2,1)} %project.3.refs_0_) | copy-start | bytes 196612
  33.7 62.5 %collective-permute-start.23 = (bf16[256,1024]{1,0:T(8,128)(2,1)S(1)}, bf16[256,1024]{1,0:T(8,128)(2,1)S(1)}, u32[]{:S(2)}, u32[]{:S(2)}) collective-permute-start(bf16[256,1024]{1,0:T(8,128)(2,1)S(1)} %copy-done.24), channel_id=1, source_target_pairs={{0,4},{4,0},{8,12},{12,8},{16,20},{20,16},{24,28},{28,24},{1,5},{5... | collective-permute-start | bytes 1572872 | tf_op jit(solution)/shard_map/ppermute | solution.py:287
  38.8 8.7 %copy-start.13 = (bf16[256,128]{1,0:T(8,128)(2,1)}, bf16[256,128]{1,0:T(8,128)(2,1)S(1)}, u32[]{:S(2)}) copy-start(bf16[256,128]{1,0:T(8,128)(2,1)S(1)} %collective-permute-done.3.refs_1_) | copy-start | bytes 196612
  38.8 8.7 %collective-permute-start.9 = (bf16[256,128]{1,0:T(8,128)(2,1)}, bf16[256,128]{1,0:T(8,128)(2,1)S(1)}, u32[]{:S(2)}, u32[]{:S(2)}) collective-permute-start(bf16[256,128]{1,0:T(8,128)(2,1)} %project.4.refs_8_), channel_id=1, source_target_pairs={{0,8},{4,12},{8,0},{12,4},{16,24},{20,28},{24,16},{28,20},{1,9},{5... | collective-permute-start | bytes 196616 | tf_op jit(solution)/shard_map/ppermute | solution.py:287
  39.5 8.0 %copy-start.14 = (bf16[256,128]{1,0:T(8,128)(2,1)}, bf16[256,128]{1,0:T(8,128)(2,1)S(1)}, u32[]{:S(2)}) copy-start(bf16[256,128]{1,0:T(8,128)(2,1)S(1)} %collective-permute-done.4.refs_2_) | copy-start | bytes 196612
  39.5 8.7 %collective-permute-start.10 = (bf16[256,128]{1,0:T(8,128)(2,1)}, bf16[256,128]{1,0:T(8,128)(2,1)S(1)}, u32[]{:S(2)}, u32[]{:S(2)}) collective-permute-start(bf16[256,128]{1,0:T(8,128)(2,1)} %project.4.refs_8_), channel_id=1, source_target_pairs={{0,16},{4,20},{8,24},{12,28},{16,0},{20,4},{24,8},{28,12},{1,17},{... | collective-permute-start | bytes 196616 | tf_op jit(solution)/shard_map/ppermute | solution.py:287
  43.2 4.3 %copy-start.15 = (bf16[256,128]{1,0:T(8,128)(2,1)}, bf16[256,128]{1,0:T(8,128)(2,1)S(1)}, u32[]{:S(2)}) copy-start(bf16[256,128]{1,0:T(8,128)(2,1)S(1)} %collective-permute-done.5.refs_3_) | copy-start | bytes 196612
  43.2 8.8 %collective-permute-start.11 = (bf16[256,128]{1,0:T(8,128)(2,1)}, bf16[256,128]{1,0:T(8,128)(2,1)S(1)}, u32[]{:S(2)}, u32[]{:S(2)}) collective-permute-start(bf16[256,128]{1,0:T(8,128)(2,1)} %project.4.refs_8_), channel_id=1, source_target_pairs={{0,24},{4,28},{8,16},{12,20},{16,8},{20,12},{24,0},{28,4},{1,25},{... | collective-permute-start | bytes 196616 | tf_op jit(solution)/shard_map/ppermute | solution.py:287
  43.3 8.7 %copy-start.8 = (bf16[256,128]{1,0:T(8,128)(2,1)S(1)}, bf16[256,128]{1,0:T(8,128)(2,1)}, u32[]{:S(2)}) copy-start(bf16[256,128]{1,0:T(8,128)(2,1)} %project.4.refs_8_) | copy-start | bytes 196612
  43.3 9.0 %copy-start.23 = (bf16[256,1024]{1,0:T(8,128)(2,1)S(1)}, bf16[256,1024]{1,0:T(8,128)(2,1)}, u32[]{:S(2)}) copy-start(bf16[256,1024]{1,0:T(8,128)(2,1)} %get-tuple-element.14) | copy-start | bytes 1572868
  43.3 12.6 %copy-start.22 = (bf16[256,1024]{1,0:T(8,128)(2,1)S(1)}, bf16[256,1024]{1,0:T(8,128)(2,1)}, u32[]{:S(2)}) copy-start(bf16[256,1024]{1,0:T(8,128)(2,1)} %get-tuple-element.15) | copy-start | bytes 1572868
  43.3 0.7 copy-start.6
  43.3 17.9 %collective-permute-start.6 = (bf16[1024,128]{1,0:T(8,128)(2,1)S(1)}, bf16[1024,128]{1,0:T(8,128)(2,1)S(1)}, u32[]{:S(2)}, u32[]{:S(2)}) collective-permute-start(bf16[1024,128]{1,0:T(8,128)(2,1)S(1)} %pad_maximum_fusion.1), channel_id=1, source_target_pairs={{0,4},{4,0},{8,12},{12,8},{16,20},{20,16},{24,28},{28,24},{1,5},{5... | collective-permute-start | bytes 786440 | tf_op jit(solution)/shard_map/ppermute | solution.py:287
  47.5 33.5 %copy-start.16 = (bf16[256,128]{1,0:T(8,128)(2,1)}, bf16[256,128]{1,0:T(8,128)(2,1)S(1)}, u32[]{:S(2)}) copy-start(bf16[256,128]{1,0:T(8,128)(2,1)S(1)} %collective-permute-done.9.refs_9_) | copy-start | bytes 196612
  47.5 4.7 %collective-permute-start.15 = (bf16[256,128]{1,0:T(8,128)(2,1)}, bf16[256,128]{1,0:T(8,128)(2,1)S(1)}, u32[]{:S(2)}, u32[]{:S(2)}) collective-permute-start(bf16[256,128]{1,0:T(8,128)(2,1)} %project.5.refs_16_), channel_id=1, source_target_pairs={{0,8},{4,12},{8,0},{12,4},{16,24},{20,28},{24,16},{28,20},{1,9},{5... | collective-permute-start | bytes 196616 | tf_op jit(solution)/shard_map/ppermute | solution.py:287
  48.2 32.8 %copy-start.17 = (bf16[256,128]{1,0:T(8,128)(2,1)}, bf16[256,128]{1,0:T(8,128)(2,1)S(1)}, u32[]{:S(2)}) copy-start(bf16[256,128]{1,0:T(8,128)(2,1)S(1)} %collective-permute-done.10.refs_10_) | copy-start | bytes 196612
  48.2 7.7 %collective-permute-start.16 = (bf16[256,128]{1,0:T(8,128)(2,1)}, bf16[256,128]{1,0:T(8,128)(2,1)S(1)}, u32[]{:S(2)}, u32[]{:S(2)}) collective-permute-start(bf16[256,128]{1,0:T(8,128)(2,1)} %project.5.refs_16_), channel_id=1, source_target_pairs={{0,16},{4,20},{8,24},{12,28},{16,0},{20,4},{24,8},{28,12},{1,17},{... | collective-permute-start | bytes 196616 | tf_op jit(solution)/shard_map/ppermute | solution.py:287
  52.0 29.1 %copy-start.18 = (bf16[256,128]{1,0:T(8,128)(2,1)}, bf16[256,128]{1,0:T(8,128)(2,1)S(1)}, u32[]{:S(2)}) copy-start(bf16[256,128]{1,0:T(8,128)(2,1)S(1)} %collective-permute-done.11.refs_11_) | copy-start | bytes 196612
  52.0 7.0 %collective-permute-start.17 = (bf16[256,128]{1,0:T(8,128)(2,1)}, bf16[256,128]{1,0:T(8,128)(2,1)S(1)}, u32[]{:S(2)}, u32[]{:S(2)}) collective-permute-start(bf16[256,128]{1,0:T(8,128)(2,1)} %project.5.refs_16_), channel_id=1, source_target_pairs={{0,24},{4,28},{8,16},{12,20},{16,8},{20,12},{24,0},{28,4},{1,25},{... | collective-permute-start | bytes 196616 | tf_op jit(solution)/shard_map/ppermute | solution.py:287
  52.3 28.7 %copy-start.19 = (bf16[256,128]{1,0:T(8,128)(2,1)}, bf16[256,128]{1,0:T(8,128)(2,1)S(1)}, u32[]{:S(2)}) copy-start(bf16[256,128]{1,0:T(8,128)(2,1)S(1)} %collective-permute-done.15.refs_17_) | copy-start | bytes 196612
  52.3 44.0 %collective-permute-start.24 = (bf16[256,1024]{1,0:T(8,128)(2,1)S(1)}, bf16[256,1024]{1,0:T(8,128)(2,1)S(1)}, u32[]{:S(2)}, u32[]{:S(2)}) collective-permute-start(bf16[256,1024]{1,0:T(8,128)(2,1)S(1)} %copy-done.23), channel_id=1, source_target_pairs={{0,8},{4,12},{8,0},{12,4},{16,24},{20,28},{24,16},{28,20},{1,9},{5... | collective-permute-start | bytes 1572872 | tf_op jit(solution)/shard_map/ppermute | solution.py:287
  55.9 25.1 %copy-start.20 = (bf16[256,128]{1,0:T(8,128)(2,1)}, bf16[256,128]{1,0:T(8,128)(2,1)S(1)}, u32[]{:S(2)}) copy-start(bf16[256,128]{1,0:T(8,128)(2,1)S(1)} %collective-permute-done.16.refs_18_) | copy-start | bytes 196612
  55.9 40.4 %collective-permute-start.25 = (bf16[256,1024]{1,0:T(8,128)(2,1)S(1)}, bf16[256,1024]{1,0:T(8,128)(2,1)S(1)}, u32[]{:S(2)}, u32[]{:S(2)}) collective-permute-start(bf16[256,1024]{1,0:T(8,128)(2,1)S(1)} %copy-done.22), channel_id=1, source_target_pairs={{0,12},{4,8},{8,4},{12,0},{16,28},{20,24},{24,20},{28,16},{1,13},{... | collective-permute-start | bytes 1572872 | tf_op jit(solution)/shard_map/ppermute | solution.py:287
  59.0 22.0 %copy-start.21 = (bf16[256,128]{1,0:T(8,128)(2,1)}, bf16[256,128]{1,0:T(8,128)(2,1)S(1)}, u32[]{:S(2)}) copy-start(bf16[256,128]{1,0:T(8,128)(2,1)S(1)} %collective-permute-done.17.refs_19_) | copy-start | bytes 196612
  59.0 9.3 %collective-permute-start.12 = (bf16[1024,128]{1,0:T(8,128)(2,1)S(1)}, bf16[1024,128]{1,0:T(8,128)(2,1)S(1)}, u32[]{:S(2)}, u32[]{:S(2)}) collective-permute-start(bf16[1024,128]{1,0:T(8,128)(2,1)S(1)} %pad_maximum_fusion.2), channel_id=1, source_target_pairs={{0,4},{4,0},{8,12},{12,8},{16,20},{20,16},{24,28},{28,24},{1,5},{5... | collective-permute-start | bytes 786440 | tf_op jit(solution)/shard_map/ppermute | solution.py:287
  61.3 19.0 %collective-permute-start.18 = (bf16[1024,128]{1,0:T(8,128)(2,1)S(1)}, bf16[1024,128]{1,0:T(8,128)(2,1)S(1)}, u32[]{:S(2)}, u32[]{:S(2)}) collective-permute-start(bf16[1024,128]{1,0:T(8,128)(2,1)S(1)} %pad_maximum_fusion.3), channel_id=1, source_target_pairs={{0,4},{4,0},{8,12},{12,8},{16,20},{20,16},{24,28},{28,24},{1,5},{5... | collective-permute-start | bytes 786440 | tf_op jit(solution)/shard_map/ppermute | solution.py:287
  96.2 0.8 copy-start.25
  96.3 1.0 copy-start.26
  96.3 1.1 copy-start.27
  101.2 1.9 %collective-permute-start.26 = (bf16[2,256,384]{2,1,0:T(8,128)(2,1)}, bf16[2,256,384]{2,1,0:T(8,128)(2,1)S(1)}, u32[]{:S(2)}, u32[]{:S(2)}) collective-permute-start(bf16[2,256,384]{2,1,0:T(8,128)(2,1)} %get-tuple-element.17), channel_id=1, source_target_pairs={{0,1},{1,0},{2,3},{3,2},{4,5},{5,4},{6,7},{7,6},{8,9},{9,8},{10,11... | collective-permute-start | bytes 1179656 | tf_op jit(solution)/shard_map/ppermute | solution.py:287
  104.4 8.6 %collective-permute-start.27 = (bf16[1,256,384]{2,1,0:T(8,128)(2,1)S(1)}, bf16[1,256,384]{2,1,0:T(8,128)(2,1)S(1)}, u32[]{:S(2)}, u32[]{:S(2)}) collective-permute-start(bf16[1,256,384]{2,1,0:T(8,128)(2,1)S(1)} %slice.113), channel_id=1, source_target_pairs={{0,2},{1,3},{2,0},{3,1},{4,6},{5,7},{6,4},{7,5},{8,10},{9,11},{10,... | collective-permute-start | bytes 589832 | tf_op jit(solution)/shard_map/ppermute | solution.py:287
  113.0 10.6 %collective-permute-start.28 = (bf16[256,384]{1,0:T(8,128)(2,1)S(1)}, bf16[256,384]{1,0:T(8,128)(2,1)S(1)}, u32[]{:S(2)}, u32[]{:S(2)}) collective-permute-start(bf16[256,384]{1,0:T(8,128)(2,1)S(1)} %fusion.1), channel_id=1, source_target_pairs={{0,16},{4,20},{8,24},{12,28},{16,0},{20,4},{24,8},{28,12},{1,17},{... | collective-permute-start | bytes 589832 | tf_op jit(solution)/shard_map/ppermute | solution.py:287
  123.7 8.8 %collective-permute-start.31 = (bf16[256,384]{1,0:T(8,128)(2,1)S(1)}, bf16[256,384]{1,0:T(8,128)(2,1)S(1)}, u32[]{:S(2)}, u32[]{:S(2)}) collective-permute-start(bf16[256,384]{1,0:T(8,128)(2,1)S(1)} %add_convert_fusion), channel_id=1, source_target_pairs={{0,12},{4,8},{8,4},{12,0},{16,28},{20,24},{24,20},{28,16},{1,13},{... | collective-permute-start | bytes 589832 | tf_op jit(solution)/shard_map/ppermute | solution.py:287
  123.8 11.3 %collective-permute-start.30 = (bf16[256,384]{1,0:T(8,128)(2,1)S(1)}, bf16[256,384]{1,0:T(8,128)(2,1)S(1)}, u32[]{:S(2)}, u32[]{:S(2)}) collective-permute-start(bf16[256,384]{1,0:T(8,128)(2,1)S(1)} %add_convert_fusion), channel_id=1, source_target_pairs={{0,8},{4,12},{8,0},{12,4},{16,24},{20,28},{24,16},{28,20},{1,9},{5... | collective-permute-start | bytes 589832 | tf_op jit(solution)/shard_map/ppermute | solution.py:287
  126.1 9.6 %collective-permute-start.29 = (bf16[256,384]{1,0:T(8,128)(2,1)S(1)}, bf16[256,384]{1,0:T(8,128)(2,1)S(1)}, u32[]{:S(2)}, u32[]{:S(2)}) collective-permute-start(bf16[256,384]{1,0:T(8,128)(2,1)S(1)} %add_convert_fusion), channel_id=1, source_target_pairs={{0,4},{4,0},{8,12},{12,8},{16,20},{20,16},{24,28},{28,24},{1,5},{5... | collective-permute-start | bytes 589832 | tf_op jit(solution)/shard_map/ppermute | solution.py:287

commit v3 on v2

v3 whole, which is shorter than its diff:
```python
import functools
import math

import jax
import jax.numpy as jnp
from jax import lax
from jax.experimental import pallas as pl
from jax.experimental.pallas import tpu as pltpu
from jax.sharding import PartitionSpec as P

F32 = jnp.float32
BF16 = jnp.bfloat16
VMEM = pl.BlockSpec(memory_space=pltpu.VMEM)
SMEM = pl.BlockSpec(memory_space=pltpu.SMEM)
ANY = pl.BlockSpec(memory_space=pltpu.HBM)
MIB = 1024 * 1024


def nt(left, right):
    return lax.dot_general(left, right, (((1,), (1,)), ((), ())), preferred_element_type=F32)


def nn(left, right):
    return jnp.dot(left, right, preferred_element_type=F32)


def tn(left, right):
    return lax.dot_general(left, right, (((0,), (0,)), ((), ())), preferred_element_type=F32)


def pallas(kernel, out_shape, scalars, arrays, name, flops, scratch=(), far=()):
    outs = out_shape if isinstance(out_shape, tuple) else (out_shape,)
    moved = sum(a.size * a.dtype.itemsize for a in (*arrays, *far, *outs))
    held = moved + sum(math.prod(a.shape) * jnp.dtype(a.dtype).itemsize for a in scratch)
    return pl.pallas_call(
        kernel,
        out_shape=out_shape,
        in_specs=[SMEM] * len(scalars) + [VMEM] * len(arrays) + [ANY] * len(far),
        out_specs=jax.tree.map(lambda _: VMEM, out_shape),
        scratch_shapes=[*scratch]
        + [pltpu.VMEM(a.shape, a.dtype) for a in far]
        + [pltpu.SemaphoreType.DMA] * len(far),
        compiler_params=pltpu.CompilerParams(vmem_limit_bytes=min(held + 8 * MIB, 60 * MIB)),
        cost_estimate=pl.CostEstimate(flops=flops, bytes_accessed=moved, transcendentals=0),
        name=name,
    )(*scalars, *arrays, *far)


def shape(dims, dtype=BF16):
    return jax.ShapeDtypeStruct(dims, dtype)


def cut_kernel(group, fsdp_size, ctx_size, piece, ids_ref, hidden_ref, *refs):
    blocks = fsdp_size * ctx_size // group
    outs, sems = refs[:group], refs[group]
    copies = []
    for k, out in enumerate(outs):
        for block in range(blocks):
            start = pl.multiple_of((block * group + ids_ref[k]) * piece, piece)
            copies.append(
                pltpu.make_async_copy(
                    hidden_ref.at[:, pl.ds(start, piece)],
                    out.at[:, pl.ds(block * piece, piece)],
                    sems.at[k * blocks + block],
                )
            )
    for copy in copies:
        copy.start()
    for copy in copies:
        copy.wait()


def cut(ids, hidden, group, fsdp_size, ctx_size):
    rows, depth = hidden.shape
    piece = depth // (fsdp_size * ctx_size)
    if piece % 128:
        pieces = hidden.reshape(rows, depth // (piece * group), group, piece)
        return [
            lax.dynamic_index_in_dim(pieces, ids[k], 2, keepdims=False).reshape(rows, depth // group)
            for k in range(group)
        ]
    blocks = fsdp_size * ctx_size
    return pl.pallas_call(
        functools.partial(cut_kernel, group, fsdp_size, ctx_size, piece),
        out_shape=tuple(shape((rows, depth // group)) for _ in range(group)),
        in_specs=[SMEM, ANY],
        out_specs=(VMEM,) * group,
        scratch_shapes=[pltpu.SemaphoreType.DMA((blocks,))],
        compiler_params=pltpu.CompilerParams(vmem_limit_bytes=8 * MIB),
        cost_estimate=pl.CostEstimate(flops=0, bytes_accessed=4 * hidden.size, transcendentals=0),
        name="cut",
    )(ids, hidden)


def fetch(sources, slots):
    count = len(sources)
    copies = [pltpu.make_async_copy(sources[i], slots[i], slots[count + i]) for i in range(count)]
    for copy in copies:
        copy.start()
    return copies


def project_kernel(count, ids_ref, *refs):
    slots = refs[len(refs) - 2 * (count + 1) :]
    copies = fetch(refs[: count + 1], slots)
    hidden = slots[count]
    copies[count].wait()
    total = None
    for part in range(count):
        rows = slots[part].shape[0]
        start = pl.multiple_of(ids_ref[part] * rows, rows)
        copies[part].wait()
        term = nn(hidden[:, pl.ds(start, rows)], slots[part][...])
        total = term if total is None else total + term
    first = 0
    for out in refs[count + 1 : len(refs) - 2 * (count + 1)]:
        width = out.shape[1]
        out[...] = total[:, first : first + width].astype(BF16)
        first += width


def project(ids, hidden, weights, widths):
    return pallas(
        functools.partial(project_kernel, len(weights)),
        tuple(shape((hidden.shape[0], width)) for width in widths),
        [ids],
        [],
        "project",
        2 * hidden.size * sum(widths),
        far=[*weights, hidden],
    )


def hidden_kernel(count, ids_ref, grad_ref, *refs):
    slots = refs[count + 1 :]
    copies = fetch(refs[:count], slots)
    for part in range(count):
        rows = slots[part].shape[0]
        start = pl.multiple_of(ids_ref[part] * rows, rows)
        copies[part].wait()
        refs[count][:, pl.ds(start, rows)] = nt(grad_ref[...], slots[part][...]).astype(BF16)


def hidden_grad(ids, grad, weights, depth):
    return pallas(
        functools.partial(hidden_kernel, len(weights)),
        shape((grad.shape[0], depth)),
        [ids],
        [grad],
        "hidden_grad",
        2 * grad.size * depth,
        far=weights,
    )


def attend_kernel(layouts, group, rows, bq, bk, block_ref, pages_ref, *refs):
    count = sum(len(layout) for layout in layouts)
    parts, (grad_ref, own_ref) = refs[:count], refs[count : count + 2]
    q_ref, k_ref, v_ref, do_ref, s_ref, dp_ref, dk_ref, dv_ref, kt_ref = refs[count + 2 :]
    seq, hd = do_ref.shape
    near = rows * group
    block = block_ref[0]
    scale = hd**-0.5
    scale2 = scale * math.log2(math.e)
    at = 0
    for layout, targets in zip(layouts, ((q_ref, k_ref), (v_ref,), (do_ref,))):
        for distances in layout:
            for number, distance in enumerate(distances):
                here = pl.ds(pl.multiple_of((block ^ distance) * rows, rows), rows)
                for column, target in enumerate(targets):
                    target[here, :] = parts[at][number * rows : (number + 1) * rows, column * hd : (column + 1) * hd]
            at += 1
    dk_ref[...] = jnp.zeros_like(dk_ref)
    dv_ref[...] = jnp.zeros_like(dv_ref)
    kt_ref[...] = k_ref[...].T
    ends, end = [], jnp.int32(0)
    for page in range(pages_ref.shape[1]):
        end = end + pages_ref[0, page]
        ends.append(end)
    low = lax.div(block, group) * near
    near_first, near_last = lax.div(low, bk), lax.div(low, bk) + near // bk

    def limit_of(pos):
        limit = jnp.full_like(pos, seq)
        for page_end in ends:
            limit = jnp.minimum(limit, jnp.where(page_end > pos, page_end, seq))
        return limit

    @pl.loop(0, seq // bq)
    def _(i):
        q0 = pl.multiple_of(i * bq, bq)
        limits = limit_of(q0 + lax.broadcasted_iota(jnp.int32, (1, bq), 1))
        count = lax.div(limit_of(q0 + (bq - 1)) + (bk - 1), bk)
        q = q_ref[pl.ds(q0, bq), :]
        do = do_ref[pl.ds(q0, bq), :]

        def scores(j, row_max):
            k0 = pl.multiple_of(j * bk, bk)
            s = nt(k_ref[pl.ds(k0, bk), :], q) * scale2
            key = k0 + lax.broadcasted_iota(jnp.int32, (bk, 1), 0)
            s = jnp.where(key < limits, s, -1e30)
            s_ref[pl.ds(k0, bk), :] = s
            dp_ref[pl.ds(k0, bk), :] = nt(v_ref[pl.ds(k0, bk), :], do)
            return jnp.maximum(row_max, jnp.max(s, axis=0, keepdims=True))

        row_max = lax.fori_loop(0, count, scores, jnp.full((1, bq), -3e38, F32))

        def sums(j, carry):
            total, dot = carry
            k0 = pl.multiple_of(j * bk, bk)
            p = jnp.exp2(s_ref[pl.ds(k0, bk), :] - row_max)
            s_ref[pl.ds(k0, bk), :] = p
            total = total + jnp.sum(p, axis=0, keepdims=True)
            dot = dot + jnp.sum(p * dp_ref[pl.ds(k0, bk), :], axis=0, keepdims=True)
            return total, dot

        zero = jnp.zeros((1, bq), F32)
        total, dot = lax.fori_loop(0, count, sums, (zero, zero))
        inv = 1.0 / total
        gain = inv * scale
        shift = dot * inv * gain

        def dscore(j):
            k0 = pl.multiple_of(j * bk, bk)
            p = s_ref[pl.ds(k0, bk), :]
            return k0, p, (p * (dp_ref[pl.ds(k0, bk), :] * gain - shift)).astype(BF16)

        def key_grads(j, carry):
            k0, p, ds = dscore(j)
            dv_ref[pl.ds(k0 - low, bk), :] += nn((p * inv).astype(BF16), do)
            dk_ref[pl.ds(k0 - low, bk), :] += nn(ds, q)
            return carry

        def query_grads(j, dqt):
            k0, _, ds = dscore(j)
            return dqt + nn(kt_ref[:, pl.ds(k0, bk)], ds)

        def all_grads(j, dqt):
            k0, p, ds = dscore(j)
            dv_ref[pl.ds(k0 - low, bk), :] += nn((p * inv).astype(BF16), do)
            dk_ref[pl.ds(k0 - low, bk), :] += nn(ds, q)
            return dqt + nn(kt_ref[:, pl.ds(k0, bk)], ds)

        first, last = jnp.minimum(near_first, count), jnp.minimum(near_last, count)
        is_near = (q0 >= low) & (q0 < low + near)

        @pl.when(is_near)
        def _():
            dqt = lax.fori_loop(0, first, query_grads, jnp.zeros((hd, bq), F32))
            dqt = lax.fori_loop(first, last, all_grads, dqt)
            dqt = lax.fori_loop(last, count, query_grads, dqt)
            grad_ref[pl.ds(pl.multiple_of(q0 - low, bq), bq), :hd] = dqt.T.astype(BF16)

        @pl.when(jnp.logical_not(is_near))
        def _():
            lax.fori_loop(first, last, key_grads, 0)

    grad_ref[:, hd : 2 * hd] = dk_ref[...].astype(BF16)
    grad_ref[:, 2 * hd :] = dv_ref[...].astype(BF16)
    own = pl.multiple_of(lax.rem(block, group) * rows, rows)
    own_ref[...] = grad_ref[pl.ds(own, rows), :]


def attend(block, pages, sets, blocks, group):
    rows = sets[0][0][0].shape[0] // len(sets[0][0][1])
    hd = sets[1][0][0].shape[1]
    seq, near = rows * blocks, rows * group
    tile = 512 if near % 512 == 0 and seq <= 4096 else rows
    layouts = [[distances for _, distances in parts] for parts in sets]
    return pallas(
        functools.partial(attend_kernel, layouts, group, rows, tile, tile),
        (shape((near, 3 * hd)), shape((rows, 3 * hd))),
        [block, pages],
        [array for parts in sets for array, _ in parts],
        "attend",
        10 * seq * seq * hd,
        [pltpu.VMEM((seq, hd), BF16)] * 4
        + [pltpu.VMEM((seq, tile), F32)] * 2
        + [pltpu.VMEM((near, hd), F32)] * 2
        + [pltpu.VMEM((hd, seq), BF16)],
    )


def weight_kernel(group, fsdp_size, ids_ref, fsdp_ref, grad_ref, *refs):
    parts, (kept_ref, away_ref) = refs[:group], refs[group:]
    rows = grad_ref.shape[0] // group
    size = parts[0].shape[1] // fsdp_size
    for j in range(fsdp_size):
        columns = pl.ds(pl.multiple_of(fsdp_ref[j] * size, size), size)
        total = None
        for k in range(group):
            here = pl.ds(pl.multiple_of(ids_ref[k] * rows, rows), rows)
            term = tn(parts[k][:, columns], grad_ref[here, :])
            total = term if total is None else total + term
        out = away_ref if j % 2 else kept_ref
        out[j // 2] = total.astype(out.dtype)


def weight_grad(ids, fsdp_ids, grad, parts):
    group, fsdp_size, width = len(parts), fsdp_ids.shape[0], grad.shape[1]
    size = parts[0].shape[1] // fsdp_size
    rows = parts[0].shape[0]
    if size % 128:
        total = sum(
            tn(parts[k], lax.dynamic_slice_in_dim(grad, ids[k] * rows, rows, 0)) for k in range(group)
        ).reshape(fsdp_size, size, width)
        both = jnp.take(total, fsdp_ids, axis=0).reshape(fsdp_size // 2, 2, size, width)
        return both[:, 0], both[:, 1].astype(BF16)
    half = (fsdp_size // 2, size, width)
    return pallas(
        functools.partial(weight_kernel, group, fsdp_size),
        (shape(half, F32), shape(half)),
        [ids, fsdp_ids],
        [grad, *parts],
        "weight_grad",
        2 * grad.size * fsdp_size * size,
    )


def finish_kernel(group, piece, ids_ref, *refs):
    out_ref = refs[group]
    for k in range(group):
        for half in range(refs[k].shape[0] // piece):
            start = pl.multiple_of((half * group + ids_ref[k]) * piece, piece)
            out_ref[pl.ds(start, piece), :] = refs[k][half * piece : (half + 1) * piece, :].astype(F32)


def finish(ids, blocks, piece):
    group = len(blocks)
    rows, width = blocks[0].shape
    if piece % 16:
        order = jnp.take(jnp.stack(blocks), ids, axis=0).reshape(group, rows // piece, piece, width)
        return order.swapaxes(0, 1).reshape(group * rows, width).astype(F32)
    return pallas(
        functools.partial(finish_kernel, group, piece),
        shape((group * rows, width), F32),
        [ids],
        blocks,
        "finish",
        0,
    )


def swap(array, axis, size, distance):
    return lax.ppermute(array, axis, [(i, i ^ distance) for i in range(size)])


def spread(part, size):
    array, distances = part
    return [(swap(array, "ctx", size, k), [k ^ d for d in distances]) for k in range(2, size, 2)]


def widen(parts, size):
    arrays = [array for array, _ in parts]
    whole = jnp.concatenate(arrays, axis=0) if len(arrays) > 1 else arrays[0]
    return swap(whole, "ctx", size, 1), [1 ^ d for _, distances in parts for d in distances]


def after(part, done):
    array, *_ = lax.optimization_barrier((part[0], *[other for other, _ in done]))
    return array, part[1]


def local(ctx_size, fsdp_size, hidden_in, page_tokens, grad_attn, w_qkv):
    hidden, grad_out = hidden_in[0], grad_attn[0]
    rows, depth = hidden.shape
    hd = grad_out.shape[1]
    f, c = lax.axis_index("fsdp"), lax.axis_index("ctx")
    fsdp_ids = f ^ jnp.arange(fsdp_size, dtype=jnp.int32)
    group = min(4, ctx_size)
    group_ids = (c % group) ^ jnp.arange(group, dtype=jnp.int32)

    top = fsdp_size // 2
    weights = {0: w_qkv, top: swap(w_qkv, "fsdp", fsdp_size, top)}
    chunks = list(cut(group_ids, hidden, group, fsdp_size, ctx_size))
    grads = [after((grad_out, [0]), [(chunks[1], 0)])]
    grads += spread(grads[0], ctx_size)
    hidden_parts = {0: chunks[0], **{k: swap(chunks[k], "ctx", ctx_size, k) for k in range(2, group - 1)}}
    weights[top], arrays = lax.optimization_barrier((weights[top], [array for array, _ in grads]))
    grads = [(array, distances) for array, (_, distances) in zip(arrays, grads)]
    grads.append(widen(grads, ctx_size))
    bit = top // 2
    while bit:
        weights.update({k ^ bit: swap(weights[k], "fsdp", fsdp_size, bit) for k in list(weights)})
        bit //= 2
    weights = [weights[k] for k in range(fsdp_size)]

    qk, v = project(fsdp_ids, hidden, weights, (2 * hd, hd))
    qk, late = lax.optimization_barrier((qk, grads[-1][0]))
    grads[-1] = late, grads[-1][1]
    chunks[1], _ = after((chunks[1], 0), [(qk, 0)])
    hidden_parts[1] = swap(chunks[1], "ctx", ctx_size, 1)
    qks = [(qk, [0])]
    qks += spread(qks[0], ctx_size)
    v_pair = [(v, [0]), widen([(v, [0])], ctx_size)]
    pair = jnp.concatenate([array for array, _ in v_pair], axis=0), [0, 1]
    vs = [pair, *spread(after(pair, qks[1:]), ctx_size)]
    qks.append(widen([after(qks[0], [pair, (hidden_parts[2], 0)]), *qks[1:]], ctx_size))
    late, _ = after((chunks[group - 1], 0), vs[1:])
    hidden_parts[group - 1] = swap(late, "ctx", ctx_size, group - 1)
    hidden_parts = [hidden_parts[k] for k in range(group)]
    block = c.reshape(1).astype(jnp.int32)
    grad_near, grad_own = attend(block, page_tokens, [qks, vs, grads], ctx_size, group)
    grad_inputs = hidden_grad(fsdp_ids, grad_own, weights, depth)

    kept, away = weight_grad(group_ids, fsdp_ids, grad_near, hidden_parts)
    bit = 1
    while bit < fsdp_size:
        total = kept + swap(away, "fsdp", fsdp_size, bit).astype(F32)
        bit *= 2
        if bit < fsdp_size:
            kept, away = total[0::2], total[1::2].astype(BF16)
    total = total[0]
    bit = group
    while bit < ctx_size:
        half = total.astype(BF16)
        total = half.astype(F32) + swap(half, "ctx", ctx_size, bit).astype(F32)
        bit *= 2
    total, grad_inputs = lax.optimization_barrier((total.astype(BF16), grad_inputs))
    gathered = [swap(total, "ctx", ctx_size, k) if k else total for k in range(group)]
    grad_weights = finish(group_ids, gathered, depth // (fsdp_size * ctx_size))
    return grad_inputs[None], grad_weights


def solution(mesh):
    in_specs = (P("fsdp", "ctx", None), P("fsdp", None), P("fsdp", "ctx", None), P("fsdp", None))
    out_specs = (P("fsdp", "ctx", None), P("fsdp", None))
    body = functools.partial(local, mesh.shape["ctx"], mesh.shape["fsdp"])
    return jax.shard_map(body, mesh=mesh, in_specs=in_specs, out_specs=out_specs, check_vma=False)
```

time: 138 us -> 118 us (0.86)
  Pallas kernels: 37.6 us -> 27.6 us
  local copies, waits for them, and re-layouts: 8.86 us -> 5.18 us
  other arithmetic: 4.15 us -> 1.78 us
  starting transfers between devices: 36.1 us -> 34.1 us
  waiting for transfers between devices: 50.4 us -> 48.6 us
    pallas_call x7 -> x5, Pallas kernels: 37.6 us -> 25.3 us  [pallas(): pl.pallas_call(kernel, out_shape=out_shape, in_specs=[SMEM] * len(scalars...]
    slice x5 -> x0, local copies, waits for them, and re-layouts: 4.03 us -> none  [the longest x4 2.88 us: gather_blocks(): return even + [odd[i * rows:(i + 1) * rows] for i in range(size // 2)]]
    unnamed x58 -> x25, local copies, waits for them, and re-layouts: 2.82 us -> 5.15 us
    pallas_call x0 -> x1, Pallas kernels: none -> 2.29 us  [cut(): pl.pallas_call(functools.partial(cut_kernel, group, fsdp_size, ctx_size,...]
    ppermute x32 -> x24, starting transfers between devices: 36.1 us -> 34.1 us  [swap(): return lax.ppermute(array, axis, [(i, i ^ distance) for i in range(size)])]
    ppermute x32 -> x24, waiting for transfers between devices: 50.4 us -> 48.6 us  [swap(): return lax.ppermute(array, axis, [(i, i ^ distance) for i in range(size)])]
  transfers between devices with their start and end apart: 32 -> 24, of which waited for: 15 -> 16; matrix products, arithmetic and copies ran while one was open for 5% -> 1% of each run, Pallas kernels for 24% -> 20%
where the time goes in v3:
time: 118 us
  waiting for transfers between devices  48.6 us (41%)
  starting transfers between devices  34.1 us (29%)
  Pallas kernels  27.6 us (23%)
  local copies, waits for them, and re-layouts  5.18 us (4%)
  other arithmetic  1.78 us (2%)
    ppermute x24, waiting for transfers between devices, swap(): return lax.ppermute(array, axis, [(i, i ^ distance) for i in range(size)])  48.6 us
    ppermute x24, starting transfers between devices, swap(): return lax.ppermute(array, axis, [(i, i ^ distance) for i in range(size)])  34.1 us
    pallas_call x5, Pallas kernels, pallas(): pl.pallas_call(kernel, out_shape=out_shape, in_specs=[SMEM] * len(scalars...  25.3 us
    unnamed x25, local copies, waits for them, and re-layouts  5.15 us
  transfers between devices with their start and end apart: 24, of which 16 were waited for; matrix products, arithmetic and copies ran while one was open for 1% of the time, Pallas kernels for 20%

profile of v3, /device:TPU:0, one launch (start us, length us, event | category | flops | bytes accessed | tf_op | source)
XLA Modules:
  0.0 118.0 jit_solution(7244474493998608572)
XLA Ops:
  0.6 3.0 %collective-permute-start.1 = (bf16[1024,384]{1,0:T(8,128)(2,1)}, bf16[1024,384]{1,0:T(8,128)(2,1)S(1)}, u32[]{:S(2)}, u32[]{:S(2)}) collective-permute-start(bf16[1024,384]{1,0:T(8,128)(2,1)} %refs_0_.3), channel_id=1, source_target_pairs={{0,2},{1,3},{2,0},{3,1},{4,6},{5,7},{6,4},{7,5},{8,10},{9,11},{10,... | collective-permute-start | bytes 2359304 | tf_op jit(solution)/shard_map/ppermute | solution.py:345
  3.6 1.6 %copy-done = bf16[1,256,4096]{2,1,0:T(8,128)(2,1)S(1)} copy-done((bf16[1,256,4096]{2,1,0:T(8,128)(2,1)S(1)}, bf16[1,256,4096]{2,1,0:T(8,128)(2,1)}, u32[]{:S(2)}) %copy-start) | copy-done | bytes 2097176
  5.2 2.3 %cut.1 = (bf16[256,1024]{1,0:T(8,128)(2,1)S(1)}, bf16[256,1024]{1,0:T(8,128)(2,1)S(1)}, bf16[256,1024]{1,0:T(8,128)(2,1)}, bf16[256,1024]{1,0:T(8,128)(2,1)S(1)}) custom-call(s32[4]{0:T(128)S(1)} %iota_xor_fusion.1.ids_ref, bf16[256,4096]{1,0:T(8,128)(2,1)S(1)} %bitcast.6), custom_call_target="tpu_custom_call" | custom-call | bytes 4194304 | tf_op jit(solution)/shard_map/cut/pallas_call | solution.py:83
  7.5 0.0 copy-start.5
  7.5 0.8 copy-done.5
  8.3 0.8 copy-done.7
  9.1 0.8 copy-done.9
  9.9 1.6 %collective-permute-start.2 = (bf16[256,128]{1,0:T(8,128)(2,1)}, bf16[256,128]{1,0:T(8,128)(2,1)S(1)}, u32[]{:S(2)}, u32[]{:S(2)}) collective-permute-start(bf16[256,128]{1,0:T(8,128)(2,1)} %bitcast.8), channel_id=1, source_target_pairs={{0,8},{4,12},{8,0},{12,4},{16,24},{20,28},{24,16},{28,20},{1,9},{5... | collective-permute-start | bytes 196616 | tf_op jit(solution)/shard_map/ppermute | solution.py:345
  11.5 2.6 %collective-permute-start.3 = (bf16[256,128]{1,0:T(8,128)(2,1)}, bf16[256,128]{1,0:T(8,128)(2,1)S(1)}, u32[]{:S(2)}, u32[]{:S(2)}) collective-permute-start(bf16[256,128]{1,0:T(8,128)(2,1)} %bitcast.9), channel_id=1, source_target_pairs={{0,16},{4,20},{8,24},{12,28},{16,0},{20,4},{24,8},{28,12},{1,17},{... | collective-permute-start | bytes 196616 | tf_op jit(solution)/shard_map/ppermute | solution.py:345
  14.1 0.2 collective-permute-start.4
  14.3 0.0 collective-permute-start
  14.3 0.1 collective-permute-done.2.refs_10_
  14.4 4.3 %collective-permute-done.3.refs_11_ = bf16[256,128]{1,0:T(8,128)(2,1)S(1)} collective-permute-done((bf16[256,128]{1,0:T(8,128)(2,1)}, bf16[256,128]{1,0:T(8,128)(2,1)S(1)}, u32[]{:S(2)}, u32[]{:S(2)}) %collective-permute-start.3) | collective-permute-done | bytes 65568 | tf_op jit(solution)/shard_map/ppermute | solution.py:345
  18.7 1.7 %collective-permute-done.4.refs_12_ = bf16[256,128]{1,0:T(8,128)(2,1)S(1)} collective-permute-done((bf16[256,128]{1,0:T(8,128)(2,1)}, bf16[256,128]{1,0:T(8,128)(2,1)S(1)}, u32[]{:S(2)}, u32[]{:S(2)}) %collective-permute-start.4) | collective-permute-done | bytes 65568 | tf_op jit(solution)/shard_map/ppermute | solution.py:345
  20.4 1.0 collective-permute-done.1.refs_2_
  21.4 0.0 collective-permute-start.5
  21.4 1.8 %collective-permute-start.11 = (bf16[256,1024]{1,0:T(8,128)(2,1)}, bf16[256,1024]{1,0:T(8,128)(2,1)}, u32[]{:S(2)}, u32[]{:S(2)}) collective-permute-start(bf16[256,1024]{1,0:T(8,128)(2,1)} %get-tuple-element.36), channel_id=1, source_target_pairs={{0,8},{4,12},{8,0},{12,4},{16,24},{20,28},{24,16},{28,20},{1,9},{5... | collective-permute-start | bytes 1572872 | tf_op jit(solution)/shard_map/ppermute | solution.py:345
  23.2 1.5 %pad_maximum_fusion.1 = bf16[1024,128]{1,0:T(8,128)(2,1)} fusion(bf16[256,128]{1,0:T(8,128)(2,1)S(1)} %collective-permute-done.4.refs_12_, bf16[256,128]{1,0:T(8,128)(2,1)S(1)} %collective-permute-done.3.refs_11_, bf16[256,128]{1,0:T(8,128)(2,1)S(1)} %collective-permute-done.2.refs_10_, bf16[256,128]{1,0:T(8,128)(2,1)} %bitcast.11), kind=kLoop, calls=%fused_computation.6 | loop fusion | flops 1048576 | bytes 524288 | tf_op jit(solution)/shard_map/concatenate | solution.py:355
  24.8 1.5 %collective-permute-start.6 = (bf16[1024,128]{1,0:T(8,128)(2,1)}, bf16[1024,128]{1,0:T(8,128)(2,1)S(1)}, u32[]{:S(2)}, u32[]{:S(2)}) collective-permute-start(bf16[1024,128]{1,0:T(8,128)(2,1)} %pad_maximum_fusion.1), channel_id=1, source_target_pairs={{0,4},{4,0},{8,12},{12,8},{16,20},{20,16},{24,28},{28,24},{1,5},{5... | collective-permute-start | bytes 786440 | tf_op jit(solution)/shard_map/ppermute | solution.py:345
  26.3 0.0 collective-permute-done.refs_1_
  26.3 0.0 collective-permute-done.5.refs_3_
  26.3 0.0 copy-start.2
  26.3 1.1 copy-done.2
  27.5 3.3 %project.1 = (bf16[256,256]{1,0:T(8,128)(2,1)S(1)}, bf16[256,128]{1,0:T(8,128)(2,1)S(1)}) custom-call(s32[4]{0:T(128)S(1)} %iota_xor_fusion.ids_ref.fsdp_ref, bf16[1024,384]{1,0:T(8,128)(2,1)S(1)} %copy-done.2, bf16[1024,384]{1,0:T(8,128)(2,1)} %collective-permute-done.refs_1_, bf16[1024,384]{1,0:T(8,128)(2,1)S(1)} %collective-permute-done.1.refs_2_, ...), custom_call_target="tpu_custom_call" | custom-call | flops 805306368 | bytes 5439488 | tf_op jit(solution)/shard_map/project/pallas_call | solution.py:35
  30.8 2.6 %collective-permute-done.6.refs_13_ = bf16[1024,128]{1,0:T(8,128)(2,1)S(1)} collective-permute-done((bf16[1024,128]{1,0:T(8,128)(2,1)}, bf16[1024,128]{1,0:T(8,128)(2,1)S(1)}, u32[]{:S(2)}, u32[]{:S(2)}) %collective-permute-start.6) | collective-permute-done | bytes 262176 | tf_op jit(solution)/shard_map/ppermute | solution.py:345
  33.4 0.3 collective-permute-start.7
  33.7 2.8 %collective-permute-start.8 = (bf16[256,256]{1,0:T(8,128)(2,1)S(1)}, bf16[256,256]{1,0:T(8,128)(2,1)S(1)}, u32[]{:S(2)}, u32[]{:S(2)}) collective-permute-start(bf16[256,256]{1,0:T(8,128)(2,1)S(1)} %get-tuple-element.37.refs_0_), channel_id=1, source_target_pairs={{0,16},{4,20},{8,24},{12,28},{16,0},{20,4},{24,8},{28,12},{1,17},{... | collective-permute-start | bytes 393224 | tf_op jit(solution)/shard_map/ppermute | solution.py:345
  36.5 1.3 %collective-permute-start.9 = (bf16[256,256]{1,0:T(8,128)(2,1)S(1)}, bf16[256,256]{1,0:T(8,128)(2,1)S(1)}, u32[]{:S(2)}, u32[]{:S(2)}) collective-permute-start(bf16[256,256]{1,0:T(8,128)(2,1)S(1)} %get-tuple-element.37.refs_0_), channel_id=1, source_target_pairs={{0,24},{4,28},{8,16},{12,20},{16,8},{20,12},{24,0},{28,4},{1,25},{... | collective-permute-start | bytes 393224 | tf_op jit(solution)/shard_map/ppermute | solution.py:345
  37.8 1.5 %collective-permute-start.10 = (bf16[256,128]{1,0:T(8,128)(2,1)S(1)}, bf16[256,128]{1,0:T(8,128)(2,1)S(1)}, u32[]{:S(2)}, u32[]{:S(2)}) collective-permute-start(bf16[256,128]{1,0:T(8,128)(2,1)S(1)} %get-tuple-element.35), channel_id=1, source_target_pairs={{0,4},{4,0},{8,12},{12,8},{16,20},{20,16},{24,28},{28,24},{1,5},{5... | collective-permute-start | bytes 196616 | tf_op jit(solution)/shard_map/ppermute | solution.py:345
  39.3 2.7 %collective-permute-done.10 = bf16[256,128]{1,0:T(8,128)(2,1)S(1)} collective-permute-done((bf16[256,128]{1,0:T(8,128)(2,1)S(1)}, bf16[256,128]{1,0:T(8,128)(2,1)S(1)}, u32[]{:S(2)}, u32[]{:S(2)}) %collective-permute-start.10) | collective-permute-done | bytes 65568 | tf_op jit(solution)/shard_map/ppermute | solution.py:345
  42.1 0.0 collective-permute-done.7.refs_1_
  42.1 0.0 collective-permute-done.8.refs_2_
  42.1 4.6 %collective-permute-done.9.refs_3_ = bf16[256,256]{1,0:T(8,128)(2,1)S(1)} collective-permute-done((bf16[256,256]{1,0:T(8,128)(2,1)S(1)}, bf16[256,256]{1,0:T(8,128)(2,1)S(1)}, u32[]{:S(2)}, u32[]{:S(2)}) %collective-permute-start.9) | collective-permute-done | bytes 131104 | tf_op jit(solution)/shard_map/ppermute | solution.py:345
  46.8 1.6 %collective-permute-start.12 = (bf16[1024,256]{1,0:T(8,128)(2,1)S(1)}, bf16[1024,256]{1,0:T(8,128)(2,1)S(1)}, u32[]{:S(2)}, u32[]{:S(2)}) collective-permute-start(bf16[1024,256]{1,0:T(8,128)(2,1)S(1)} %pad_maximum_fusion), channel_id=1, source_target_pairs={{0,4},{4,0},{8,12},{12,8},{16,20},{20,16},{24,28},{28,24},{1,5},{5... | collective-permute-start | bytes 1572872 | tf_op jit(solution)/shard_map/ppermute | solution.py:345
  48.4 2.0 %collective-permute-start.13 = (bf16[512,128]{1,0:T(8,128)(2,1)S(1)}, bf16[512,128]{1,0:T(8,128)(2,1)S(1)}, u32[]{:S(2)}, u32[]{:S(2)}) collective-permute-start(bf16[512,128]{1,0:T(8,128)(2,1)S(1)} %constant_dynamic-update-slice_fusion.refs_5_), channel_id=1, source_target_pairs={{0,8},{4,12},{8,0},{12,4},{16,24},{20,28},{24,16},{28,20},{1,9},{5... | collective-permute-start | bytes 393224 | tf_op jit(solution)/shard_map/ppermute | solution.py:345
  50.3 1.9 %collective-permute-start.14 = (bf16[512,128]{1,0:T(8,128)(2,1)S(1)}, bf16[512,128]{1,0:T(8,128)(2,1)S(1)}, u32[]{:S(2)}, u32[]{:S(2)}) collective-permute-start(bf16[512,128]{1,0:T(8,128)(2,1)S(1)} %constant_dynamic-update-slice_fusion.refs_5_), channel_id=1, source_target_pairs={{0,16},{4,20},{8,24},{12,28},{16,0},{20,4},{24,8},{28,12},{1,17},{... | collective-permute-start | bytes 393224 | tf_op jit(solution)/shard_map/ppermute | solution.py:345
  52.3 1.4 %collective-permute-start.15 = (bf16[512,128]{1,0:T(8,128)(2,1)S(1)}, bf16[512,128]{1,0:T(8,128)(2,1)S(1)}, u32[]{:S(2)}, u32[]{:S(2)}) collective-permute-start(bf16[512,128]{1,0:T(8,128)(2,1)S(1)} %constant_dynamic-update-slice_fusion.refs_5_), channel_id=1, source_target_pairs={{0,24},{4,28},{8,16},{12,20},{16,8},{20,12},{24,0},{28,4},{1,25},{... | collective-permute-start | bytes 393224 | tf_op jit(solution)/shard_map/ppermute | solution.py:345
  53.7 0.5 collective-permute-start.16
  54.2 0.2 collective-permute-done.13.refs_6_
  54.4 7.6 %collective-permute-done.14.refs_7_ = bf16[512,128]{1,0:T(8,128)(2,1)S(1)} collective-permute-done((bf16[512,128]{1,0:T(8,128)(2,1)S(1)}, bf16[512,128]{1,0:T(8,128)(2,1)S(1)}, u32[]{:S(2)}, u32[]{:S(2)}) %collective-permute-start.14) | collective-permute-done | bytes 131104 | tf_op jit(solution)/shard_map/ppermute | solution.py:345
  62.0 0.0 collective-permute-done.15.refs_8_
  62.0 2.1 %collective-permute-start.17 = (bf16[256,1024]{1,0:T(8,128)(2,1)S(1)}, bf16[256,1024]{1,0:T(8,128)(2,1)S(1)}, u32[]{:S(2)}, u32[]{:S(2)}) collective-permute-start(bf16[256,1024]{1,0:T(8,128)(2,1)S(1)} %copy-done.8), channel_id=1, source_target_pairs={{0,12},{4,8},{8,4},{12,0},{16,28},{20,24},{24,20},{28,16},{1,13},{... | collective-permute-start | bytes 1572872 | tf_op jit(solution)/shard_map/ppermute | solution.py:345
  64.1 0.0 collective-permute-done.12.refs_4_
  64.1 0.0 copy-start.6
  64.1 13.3 %attend.1 = (bf16[1024,384]{1,0:T(8,128)(2,1)S(1)}, bf16[256,384]{1,0:T(8,128)(2,1)S(1)}) custom-call(s32[1]{0:T(128)} %bitcast.block_ref, s32[1,8]{1,0:T(1,128)S(1)} %copy-done.11, bf16[256,256]{1,0:T(8,128)(2,1)S(1)} %get-tuple-element.37.refs_0_, bf16[256,256]{1,0:T(8,128)(2,1)S(1)} %collective-permute-done.7.refs_1_, ...), custom_call_target="tpu_custom_call" | custom-call | flops 5368709120 | bytes 3080192 | tf_op jit(solution)/shard_map/attend/pallas_call | solution.py:35
  77.5 4.9 %collective-permute-done.16.refs_1_ = bf16[256,1024]{1,0:T(8,128)(2,1)S(1)} collective-permute-done((bf16[256,1024]{1,0:T(8,128)(2,1)S(1)}, bf16[256,1024]{1,0:T(8,128)(2,1)S(1)}, u32[]{:S(2)}, u32[]{:S(2)}) %collective-permute-start.16) | collective-permute-done | bytes 524320 | tf_op jit(solution)/shard_map/ppermute | solution.py:345
  82.3 0.0 collective-permute-done.17.refs_3_
  82.3 2.4 %weight_grad.1 = (f32[2,256,384]{2,1,0:T(8,128)S(1)}, bf16[2,256,384]{2,1,0:T(8,128)(2,1)S(1)}) custom-call(s32[4]{0:T(128)S(1)} %iota_xor_fusion.1.ids_ref, s32[4]{0:T(128)S(1)} %iota_xor_fusion.ids_ref.fsdp_ref, bf16[1024,384]{1,0:T(8,128)(2,1)S(1)} %get-tuple-element.40.grad_ref, bf16[256,1024]{1,0:T(8,128)(2,1)S(1)} %copy-done.6, ...), custom_call_target="tpu_custom_call" | custom-call | flops 805306368 | bytes 4063232 | tf_op jit(solution)/shard_map/weight_grad/pallas_call | solution.py:35
  84.7 0.0 copy-start.3
  84.7 0.1 collective-permute-start.18
  84.8 1.7 %collective-permute-done.18 = bf16[2,256,384]{2,1,0:T(8,128)(2,1)S(1)} collective-permute-done((bf16[2,256,384]{2,1,0:T(8,128)(2,1)S(1)}, bf16[2,256,384]{2,1,0:T(8,128)(2,1)S(1)}, u32[]{:S(2)}, u32[]{:S(2)}) %collective-permute-start.18) | collective-permute-done | bytes 393248 | tf_op jit(solution)/shard_map/ppermute | solution.py:345
  86.5 0.1 convert_add_fusion
  86.7 1.6 %collective-permute-start.19 = (bf16[1,256,384]{2,1,0:T(8,128)(2,1)S(1)}, bf16[1,256,384]{2,1,0:T(8,128)(2,1)S(1)}, u32[]{:S(2)}, u32[]{:S(2)}) collective-permute-start(bf16[1,256,384]{2,1,0:T(8,128)(2,1)S(1)} %slice.19), channel_id=1, source_target_pairs={{0,2},{1,3},{2,0},{3,1},{4,6},{5,7},{6,4},{7,5},{8,10},{9,11},{10,... | collective-permute-start | bytes 589832 | tf_op jit(solution)/shard_map/ppermute | solution.py:345
  88.2 5.4 %collective-permute-done.19 = bf16[1,256,384]{2,1,0:T(8,128)(2,1)S(1)} collective-permute-done((bf16[1,256,384]{2,1,0:T(8,128)(2,1)S(1)}, bf16[1,256,384]{2,1,0:T(8,128)(2,1)S(1)}, u32[]{:S(2)}, u32[]{:S(2)}) %collective-permute-start.19) | collective-permute-done | bytes 196640 | tf_op jit(solution)/shard_map/ppermute | solution.py:345
  93.7 2.8 %collective-permute-start.20 = (bf16[256,384]{1,0:T(8,128)(2,1)S(1)}, bf16[256,384]{1,0:T(8,128)(2,1)S(1)}, u32[]{:S(2)}, u32[]{:S(2)}) collective-permute-start(bf16[256,384]{1,0:T(8,128)(2,1)S(1)} %fusion.1), channel_id=1, source_target_pairs={{0,16},{4,20},{8,24},{12,28},{16,0},{20,4},{24,8},{28,12},{1,17},{... | collective-permute-start | bytes 589832 | tf_op jit(solution)/shard_map/ppermute | solution.py:345
  96.5 4.5 %hidden_grad.1 = bf16[256,4096]{1,0:T(8,128)(2,1)} custom-call(s32[4]{0:T(128)S(1)} %iota_xor_fusion.ids_ref.fsdp_ref, bf16[256,384]{1,0:T(8,128)(2,1)S(1)} %get-tuple-element.47.grad_ref, bf16[1024,384]{1,0:T(8,128)(2,1)S(1)} %copy-done.3, bf16[1024,384]{1,0:T(8,128)(2,1)} %collective-permute-done.refs_1_, ...), custom_call_target="tpu_custom_call" | custom-call | flops 805306368 | bytes 5439488 | tf_op jit(solution)/shard_map/hidden_grad/pallas_call | solution.py:35
  101.0 4.1 %collective-permute-done.20 = bf16[256,384]{1,0:T(8,128)(2,1)S(1)} collective-permute-done((bf16[256,384]{1,0:T(8,128)(2,1)S(1)}, bf16[256,384]{1,0:T(8,128)(2,1)S(1)}, u32[]{:S(2)}, u32[]{:S(2)}) %collective-permute-start.20) | collective-permute-done | bytes 196640 | tf_op jit(solution)/shard_map/ppermute | solution.py:345
  105.1 0.1 add_convert_fusion.refs_0_
  105.1 1.6 %collective-permute-start.21 = (bf16[256,384]{1,0:T(8,128)(2,1)S(1)}, bf16[256,384]{1,0:T(8,128)(2,1)S(1)}, u32[]{:S(2)}, u32[]{:S(2)}) collective-permute-start(bf16[256,384]{1,0:T(8,128)(2,1)S(1)} %add_convert_fusion.refs_0_), channel_id=1, source_target_pairs={{0,4},{4,0},{8,12},{12,8},{16,20},{20,16},{24,28},{28,24},{1,5},{5... | collective-permute-start | bytes 589832 | tf_op jit(solution)/shard_map/ppermute | solution.py:345
  106.7 2.0 %collective-permute-start.23 = (bf16[256,384]{1,0:T(8,128)(2,1)S(1)}, bf16[256,384]{1,0:T(8,128)(2,1)S(1)}, u32[]{:S(2)}, u32[]{:S(2)}) collective-permute-start(bf16[256,384]{1,0:T(8,128)(2,1)S(1)} %add_convert_fusion.refs_0_), channel_id=1, source_target_pairs={{0,12},{4,8},{8,4},{12,0},{16,28},{20,24},{24,20},{28,16},{1,13},{... | collective-permute-start | bytes 589832 | tf_op jit(solution)/shard_map/ppermute | solution.py:345
  108.7 3.5 %collective-permute-done.21.refs_1_ = bf16[256,384]{1,0:T(8,128)(2,1)S(1)} collective-permute-done((bf16[256,384]{1,0:T(8,128)(2,1)S(1)}, bf16[256,384]{1,0:T(8,128)(2,1)S(1)}, u32[]{:S(2)}, u32[]{:S(2)}) %collective-permute-start.21) | collective-permute-done | bytes 196640 | tf_op jit(solution)/shard_map/ppermute | solution.py:345
  112.2 1.7 %collective-permute-done.22.refs_2_ = bf16[256,384]{1,0:T(8,128)(2,1)S(1)} collective-permute-done((bf16[256,384]{1,0:T(8,128)(2,1)S(1)}, bf16[256,384]{1,0:T(8,128)(2,1)S(1)}, u32[]{:S(2)}, u32[]{:S(2)}) %collective-permute-start.22) | collective-permute-done | bytes 196640 | tf_op jit(solution)/shard_map/ppermute | solution.py:345
  113.9 2.3 %collective-permute-done.23.refs_3_ = bf16[256,384]{1,0:T(8,128)(2,1)S(1)} collective-permute-done((bf16[256,384]{1,0:T(8,128)(2,1)S(1)}, bf16[256,384]{1,0:T(8,128)(2,1)S(1)}, u32[]{:S(2)}, u32[]{:S(2)}) %collective-permute-start.23) | collective-permute-done | bytes 196640 | tf_op jit(solution)/shard_map/ppermute | solution.py:345
  116.2 1.8 %finish.1 = f32[1024,384]{1,0:T(8,128)} custom-call(s32[4]{0:T(128)S(1)} %iota_xor_fusion.1.ids_ref, bf16[256,384]{1,0:T(8,128)(2,1)S(1)} %add_convert_fusion.refs_0_, bf16[256,384]{1,0:T(8,128)(2,1)S(1)} %collective-permute-done.21.refs_1_, bf16[256,384]{1,0:T(8,128)(2,1)S(1)} %collective-permute-done.22.refs_2_, ...), custom_call_target="tpu_custom_call" | custom-call | bytes 2359296 | tf_op jit(solution)/shard_map/finish/pallas_call | solution.py:35
  (24 shorter events, 0.2 us)
Async XLA Ops:
  0.6 20.8 %collective-permute-start.1 = (bf16[1024,384]{1,0:T(8,128)(2,1)}, bf16[1024,384]{1,0:T(8,128)(2,1)S(1)}, u32[]{:S(2)}, u32[]{:S(2)}) collective-permute-start(bf16[1024,384]{1,0:T(8,128)(2,1)} %refs_0_.3), channel_id=1, source_target_pairs={{0,2},{1,3},{2,0},{3,1},{4,6},{5,7},{6,4},{7,5},{8,10},{9,11},{10,... | collective-permute-start | bytes 2359304 | tf_op jit(solution)/shard_map/ppermute | solution.py:345
  3.6 1.6 %copy-start = (bf16[1,256,4096]{2,1,0:T(8,128)(2,1)S(1)}, bf16[1,256,4096]{2,1,0:T(8,128)(2,1)}, u32[]{:S(2)}) copy-start(bf16[1,256,4096]{2,1,0:T(8,128)(2,1)} %param.4) | copy-start | bytes 6291460
  5.2 21.1 %copy-start.1 = (bf16[1,256,4096]{2,1,0:T(8,128)(2,1)S(1)}, bf16[1,256,4096]{2,1,0:T(8,128)(2,1)}, u32[]{:S(2)}) copy-start(bf16[1,256,4096]{2,1,0:T(8,128)(2,1)} %param.4) | copy-start | bytes 6291460
  7.5 0.8 copy-start.5
  8.3 0.8 copy-start.7
  9.1 0.8 copy-start.9
  9.9 4.5 %collective-permute-start.2 = (bf16[256,128]{1,0:T(8,128)(2,1)}, bf16[256,128]{1,0:T(8,128)(2,1)S(1)}, u32[]{:S(2)}, u32[]{:S(2)}) collective-permute-start(bf16[256,128]{1,0:T(8,128)(2,1)} %bitcast.8), channel_id=1, source_target_pairs={{0,8},{4,12},{8,0},{12,4},{16,24},{20,28},{24,16},{28,20},{1,9},{5... | collective-permute-start | bytes 196616 | tf_op jit(solution)/shard_map/ppermute | solution.py:345
  11.5 7.2 %collective-permute-start.3 = (bf16[256,128]{1,0:T(8,128)(2,1)}, bf16[256,128]{1,0:T(8,128)(2,1)S(1)}, u32[]{:S(2)}, u32[]{:S(2)}) collective-permute-start(bf16[256,128]{1,0:T(8,128)(2,1)} %bitcast.9), channel_id=1, source_target_pairs={{0,16},{4,20},{8,24},{12,28},{16,0},{20,4},{24,8},{28,12},{1,17},{... | collective-permute-start | bytes 196616 | tf_op jit(solution)/shard_map/ppermute | solution.py:345
  14.1 6.3 %collective-permute-start.4 = (bf16[256,128]{1,0:T(8,128)(2,1)}, bf16[256,128]{1,0:T(8,128)(2,1)S(1)}, u32[]{:S(2)}, u32[]{:S(2)}) collective-permute-start(bf16[256,128]{1,0:T(8,128)(2,1)} %bitcast.10), channel_id=1, source_target_pairs={{0,24},{4,28},{8,16},{12,20},{16,8},{20,12},{24,0},{28,4},{1,25},{... | collective-permute-start | bytes 196616 | tf_op jit(solution)/shard_map/ppermute | solution.py:345
  14.3 12.0 %collective-permute-start = (bf16[1024,384]{1,0:T(8,128)(2,1)}, bf16[1024,384]{1,0:T(8,128)(2,1)}, u32[]{:S(2)}, u32[]{:S(2)}) collective-permute-start(bf16[1024,384]{1,0:T(8,128)(2,1)} %refs_0_.3), channel_id=1, source_target_pairs={{0,1},{1,0},{2,3},{3,2},{4,5},{5,4},{6,7},{7,6},{8,9},{9,8},{10,11... | collective-permute-start | bytes 2359304 | tf_op jit(solution)/shard_map/ppermute | solution.py:345
  21.4 4.9 %collective-permute-start.5 = (bf16[1024,384]{1,0:T(8,128)(2,1)S(1)}, bf16[1024,384]{1,0:T(8,128)(2,1)}, u32[]{:S(2)}, u32[]{:S(2)}) collective-permute-start(bf16[1024,384]{1,0:T(8,128)(2,1)S(1)} %collective-permute-done.1.refs_2_), channel_id=1, source_target_pairs={{0,1},{1,0},{2,3},{3,2},{4,5},{5,4},{6,7},{7,6},{8,9},{9,8},{10,11... | collective-permute-start | bytes 2359304 | tf_op jit(solution)/shard_map/ppermute | solution.py:345
  21.4 20.7 %collective-permute-start.11 = (bf16[256,1024]{1,0:T(8,128)(2,1)}, bf16[256,1024]{1,0:T(8,128)(2,1)}, u32[]{:S(2)}, u32[]{:S(2)}) collective-permute-start(bf16[256,1024]{1,0:T(8,128)(2,1)} %get-tuple-element.36), channel_id=1, source_target_pairs={{0,8},{4,12},{8,0},{12,4},{16,24},{20,28},{24,16},{28,20},{1,9},{5... | collective-permute-start | bytes 1572872 | tf_op jit(solution)/shard_map/ppermute | solution.py:345
  24.8 8.6 %collective-permute-start.6 = (bf16[1024,128]{1,0:T(8,128)(2,1)}, bf16[1024,128]{1,0:T(8,128)(2,1)S(1)}, u32[]{:S(2)}, u32[]{:S(2)}) collective-permute-start(bf16[1024,128]{1,0:T(8,128)(2,1)} %pad_maximum_fusion.1), channel_id=1, source_target_pairs={{0,4},{4,0},{8,12},{12,8},{16,20},{20,16},{24,28},{28,24},{1,5},{5... | collective-permute-start | bytes 786440 | tf_op jit(solution)/shard_map/ppermute | solution.py:345
  26.3 37.8 %copy-start.11 = (s32[1,8]{1,0:T(1,128)S(1)}, s32[1,8]{1,0:T(1,128)}, u32[]{:S(2)}) copy-start(s32[1,8]{1,0:T(1,128)} %pages_ref.1) | copy-start | bytes 100
  26.3 1.1 copy-start.2
  27.4 26.2 %copy-start.10 = (bf16[256,1024]{1,0:T(8,128)(2,1)S(1)}, bf16[256,1024]{1,0:T(8,128)(2,1)}, u32[]{:S(2)}) copy-start(bf16[256,1024]{1,0:T(8,128)(2,1)} %copy-done.9) | copy-start | bytes 1572868
  27.5 34.6 %copy-start.8 = (bf16[256,1024]{1,0:T(8,128)(2,1)S(1)}, bf16[256,1024]{1,0:T(8,128)(2,1)}, u32[]{:S(2)}) copy-start(bf16[256,1024]{1,0:T(8,128)(2,1)} %copy-done.7) | copy-start | bytes 1572868
  27.5 36.7 %copy-start.4 = (bf16[1,256,128]{2,1,0:T(8,128)(2,1)S(1)}, bf16[1,256,128]{2,1,0:T(8,128)(2,1)}, u32[]{:S(2)}) copy-start(bf16[1,256,128]{2,1,0:T(8,128)(2,1)} %param.6) | copy-start | bytes 196612
  33.4 8.7 %collective-permute-start.7 = (bf16[256,256]{1,0:T(8,128)(2,1)S(1)}, bf16[256,256]{1,0:T(8,128)(2,1)S(1)}, u32[]{:S(2)}, u32[]{:S(2)}) collective-permute-start(bf16[256,256]{1,0:T(8,128)(2,1)S(1)} %get-tuple-element.37.refs_0_), channel_id=1, source_target_pairs={{0,8},{4,12},{8,0},{12,4},{16,24},{20,28},{24,16},{28,20},{1,9},{5... | collective-permute-start | bytes 393224 | tf_op jit(solution)/shard_map/ppermute | solution.py:345
  33.7 8.4 %collective-permute-start.8 = (bf16[256,256]{1,0:T(8,128)(2,1)S(1)}, bf16[256,256]{1,0:T(8,128)(2,1)S(1)}, u32[]{:S(2)}, u32[]{:S(2)}) collective-permute-start(bf16[256,256]{1,0:T(8,128)(2,1)S(1)} %get-tuple-element.37.refs_0_), channel_id=1, source_target_pairs={{0,16},{4,20},{8,24},{12,28},{16,0},{20,4},{24,8},{28,12},{1,17},{... | collective-permute-start | bytes 393224 | tf_op jit(solution)/shard_map/ppermute | solution.py:345
  36.5 10.3 %collective-permute-start.9 = (bf16[256,256]{1,0:T(8,128)(2,1)S(1)}, bf16[256,256]{1,0:T(8,128)(2,1)S(1)}, u32[]{:S(2)}, u32[]{:S(2)}) collective-permute-start(bf16[256,256]{1,0:T(8,128)(2,1)S(1)} %get-tuple-element.37.refs_0_), channel_id=1, source_target_pairs={{0,24},{4,28},{8,16},{12,20},{16,8},{20,12},{24,0},{28,4},{1,25},{... | collective-permute-start | bytes 393224 | tf_op jit(solution)/shard_map/ppermute | solution.py:345
  37.8 4.3 %collective-permute-start.10 = (bf16[256,128]{1,0:T(8,128)(2,1)S(1)}, bf16[256,128]{1,0:T(8,128)(2,1)S(1)}, u32[]{:S(2)}, u32[]{:S(2)}) collective-permute-start(bf16[256,128]{1,0:T(8,128)(2,1)S(1)} %get-tuple-element.35), channel_id=1, source_target_pairs={{0,4},{4,0},{8,12},{12,8},{16,20},{20,16},{24,28},{28,24},{1,5},{5... | collective-permute-start | bytes 196616 | tf_op jit(solution)/shard_map/ppermute | solution.py:345
  46.8 17.3 %collective-permute-start.12 = (bf16[1024,256]{1,0:T(8,128)(2,1)S(1)}, bf16[1024,256]{1,0:T(8,128)(2,1)S(1)}, u32[]{:S(2)}, u32[]{:S(2)}) collective-permute-start(bf16[1024,256]{1,0:T(8,128)(2,1)S(1)} %pad_maximum_fusion), channel_id=1, source_target_pairs={{0,4},{4,0},{8,12},{12,8},{16,20},{20,16},{24,28},{28,24},{1,5},{5... | collective-permute-start | bytes 1572872 | tf_op jit(solution)/shard_map/ppermute | solution.py:345
  48.4 6.0 %collective-permute-start.13 = (bf16[512,128]{1,0:T(8,128)(2,1)S(1)}, bf16[512,128]{1,0:T(8,128)(2,1)S(1)}, u32[]{:S(2)}, u32[]{:S(2)}) collective-permute-start(bf16[512,128]{1,0:T(8,128)(2,1)S(1)} %constant_dynamic-update-slice_fusion.refs_5_), channel_id=1, source_target_pairs={{0,8},{4,12},{8,0},{12,4},{16,24},{20,28},{24,16},{28,20},{1,9},{5... | collective-permute-start | bytes 393224 | tf_op jit(solution)/shard_map/ppermute | solution.py:345
  50.3 11.7 %collective-permute-start.14 = (bf16[512,128]{1,0:T(8,128)(2,1)S(1)}, bf16[512,128]{1,0:T(8,128)(2,1)S(1)}, u32[]{:S(2)}, u32[]{:S(2)}) collective-permute-start(bf16[512,128]{1,0:T(8,128)(2,1)S(1)} %constant_dynamic-update-slice_fusion.refs_5_), channel_id=1, source_target_pairs={{0,16},{4,20},{8,24},{12,28},{16,0},{20,4},{24,8},{28,12},{1,17},{... | collective-permute-start | bytes 393224 | tf_op jit(solution)/shard_map/ppermute | solution.py:345
  52.3 9.7 %collective-permute-start.15 = (bf16[512,128]{1,0:T(8,128)(2,1)S(1)}, bf16[512,128]{1,0:T(8,128)(2,1)S(1)}, u32[]{:S(2)}, u32[]{:S(2)}) collective-permute-start(bf16[512,128]{1,0:T(8,128)(2,1)S(1)} %constant_dynamic-update-slice_fusion.refs_5_), channel_id=1, source_target_pairs={{0,24},{4,28},{8,16},{12,20},{16,8},{20,12},{24,0},{28,4},{1,25},{... | collective-permute-start | bytes 393224 | tf_op jit(solution)/shard_map/ppermute | solution.py:345
  53.7 28.7 %collective-permute-start.16 = (bf16[256,1024]{1,0:T(8,128)(2,1)S(1)}, bf16[256,1024]{1,0:T(8,128)(2,1)S(1)}, u32[]{:S(2)}, u32[]{:S(2)}) collective-permute-start(bf16[256,1024]{1,0:T(8,128)(2,1)S(1)} %copy-done.10), channel_id=1, source_target_pairs={{0,4},{4,0},{8,12},{12,8},{16,20},{20,16},{24,28},{28,24},{1,5},{5... | collective-permute-start | bytes 1572872 | tf_op jit(solution)/shard_map/ppermute | solution.py:345
  62.0 20.3 %collective-permute-start.17 = (bf16[256,1024]{1,0:T(8,128)(2,1)S(1)}, bf16[256,1024]{1,0:T(8,128)(2,1)S(1)}, u32[]{:S(2)}, u32[]{:S(2)}) collective-permute-start(bf16[256,1024]{1,0:T(8,128)(2,1)S(1)} %copy-done.8), channel_id=1, source_target_pairs={{0,12},{4,8},{8,4},{12,0},{16,28},{20,24},{24,20},{28,16},{1,13},{... | collective-permute-start | bytes 1572872 | tf_op jit(solution)/shard_map/ppermute | solution.py:345
  64.1 18.2 %copy-start.6 = (bf16[256,1024]{1,0:T(8,128)(2,1)S(1)}, bf16[256,1024]{1,0:T(8,128)(2,1)}, u32[]{:S(2)}) copy-start(bf16[256,1024]{1,0:T(8,128)(2,1)} %copy-done.5) | copy-start | bytes 1572868
  84.7 11.7 %copy-start.3 = (bf16[1024,384]{1,0:T(8,128)(2,1)S(1)}, bf16[1024,384]{1,0:T(8,128)(2,1)}, u32[]{:S(2)}) copy-start(bf16[1024,384]{1,0:T(8,128)(2,1)} %refs_0_.3) | copy-start | bytes 2359300
  84.7 1.8 %collective-permute-start.18 = (bf16[2,256,384]{2,1,0:T(8,128)(2,1)S(1)}, bf16[2,256,384]{2,1,0:T(8,128)(2,1)S(1)}, u32[]{:S(2)}, u32[]{:S(2)}) collective-permute-start(bf16[2,256,384]{2,1,0:T(8,128)(2,1)S(1)} %get-tuple-element.46), channel_id=1, source_target_pairs={{0,1},{1,0},{2,3},{3,2},{4,5},{5,4},{6,7},{7,6},{8,9},{9,8},{10,11... | collective-permute-start | bytes 1179656 | tf_op jit(solution)/shard_map/ppermute | solution.py:345
  86.7 7.0 %collective-permute-start.19 = (bf16[1,256,384]{2,1,0:T(8,128)(2,1)S(1)}, bf16[1,256,384]{2,1,0:T(8,128)(2,1)S(1)}, u32[]{:S(2)}, u32[]{:S(2)}) collective-permute-start(bf16[1,256,384]{2,1,0:T(8,128)(2,1)S(1)} %slice.19), channel_id=1, source_target_pairs={{0,2},{1,3},{2,0},{3,1},{4,6},{5,7},{6,4},{7,5},{8,10},{9,11},{10,... | collective-permute-start | bytes 589832 | tf_op jit(solution)/shard_map/ppermute | solution.py:345
  93.7 11.3 %collective-permute-start.20 = (bf16[256,384]{1,0:T(8,128)(2,1)S(1)}, bf16[256,384]{1,0:T(8,128)(2,1)S(1)}, u32[]{:S(2)}, u32[]{:S(2)}) collective-permute-start(bf16[256,384]{1,0:T(8,128)(2,1)S(1)} %fusion.1), channel_id=1, source_target_pairs={{0,16},{4,20},{8,24},{12,28},{16,0},{20,4},{24,8},{28,12},{1,17},{... | collective-permute-start | bytes 589832 | tf_op jit(solution)/shard_map/ppermute | solution.py:345
  105.1 7.1 %collective-permute-start.21 = (bf16[256,384]{1,0:T(8,128)(2,1)S(1)}, bf16[256,384]{1,0:T(8,128)(2,1)S(1)}, u32[]{:S(2)}, u32[]{:S(2)}) collective-permute-start(bf16[256,384]{1,0:T(8,128)(2,1)S(1)} %add_convert_fusion.refs_0_), channel_id=1, source_target_pairs={{0,4},{4,0},{8,12},{12,8},{16,20},{20,16},{24,28},{28,24},{1,5},{5... | collective-permute-start | bytes 589832 | tf_op jit(solution)/shard_map/ppermute | solution.py:345
  106.7 7.2 %collective-permute-start.22 = (bf16[256,384]{1,0:T(8,128)(2,1)S(1)}, bf16[256,384]{1,0:T(8,128)(2,1)S(1)}, u32[]{:S(2)}, u32[]{:S(2)}) collective-permute-start(bf16[256,384]{1,0:T(8,128)(2,1)S(1)} %add_convert_fusion.refs_0_), channel_id=1, source_target_pairs={{0,8},{4,12},{8,0},{12,4},{16,24},{20,28},{24,16},{28,20},{1,9},{5... | collective-permute-start | bytes 589832 | tf_op jit(solution)/shard_map/ppermute | solution.py:345
  106.7 9.5 %collective-permute-start.23 = (bf16[256,384]{1,0:T(8,128)(2,1)S(1)}, bf16[256,384]{1,0:T(8,128)(2,1)S(1)}, u32[]{:S(2)}, u32[]{:S(2)}) collective-permute-start(bf16[256,384]{1,0:T(8,128)(2,1)S(1)} %add_convert_fusion.refs_0_), channel_id=1, source_target_pairs={{0,12},{4,8},{8,4},{12,0},{16,28},{20,24},{24,20},{28,16},{1,13},{... | collective-permute-start | bytes 589832 | tf_op jit(solution)/shard_map/ppermute | solution.py:345

commit v4 on v3

v4 whole, which is shorter than its diff:
```python
import functools
import math

import jax
import jax.numpy as jnp
from jax import lax
from jax.experimental import pallas as pl
from jax.experimental.pallas import tpu as pltpu
from jax.sharding import PartitionSpec as P

F32 = jnp.float32
BF16 = jnp.bfloat16
VMEM = pl.BlockSpec(memory_space=pltpu.VMEM)
SMEM = pl.BlockSpec(memory_space=pltpu.SMEM)
ANY = pl.BlockSpec(memory_space=pltpu.HBM)
MIB = 1024 * 1024


def nt(left, right):
    return lax.dot_general(left, right, (((1,), (1,)), ((), ())), preferred_element_type=F32)


def nn(left, right):
    return jnp.dot(left, right, preferred_element_type=F32)


def tn(left, right):
    return lax.dot_general(left, right, (((0,), (0,)), ((), ())), preferred_element_type=F32)


def pallas(kernel, out_shape, scalars, arrays, name, flops, scratch=(), far=()):
    outs = out_shape if isinstance(out_shape, tuple) else (out_shape,)
    moved = sum(a.size * a.dtype.itemsize for a in (*arrays, *far, *outs))
    held = moved + sum(math.prod(a.shape) * jnp.dtype(a.dtype).itemsize for a in scratch)
    return pl.pallas_call(
        kernel,
        out_shape=out_shape,
        in_specs=[SMEM] * len(scalars) + [VMEM] * len(arrays) + [ANY] * len(far),
        out_specs=jax.tree.map(lambda _: VMEM, out_shape),
        scratch_shapes=[*scratch]
        + [pltpu.VMEM(a.shape, a.dtype) for a in far]
        + [pltpu.SemaphoreType.DMA] * len(far),
        compiler_params=pltpu.CompilerParams(vmem_limit_bytes=min(held + 8 * MIB, 60 * MIB)),
        cost_estimate=pl.CostEstimate(flops=flops, bytes_accessed=moved, transcendentals=0),
        name=name,
    )(*scalars, *arrays, *far)


def shape(dims, dtype=BF16):
    return jax.ShapeDtypeStruct(dims, dtype)


def cut_copies(members, outs, group, piece, ids_ref, hidden_ref, sems):
    copies = []
    for k, out in zip(members, outs):
        for block in range(out.shape[1] // piece):
            start = pl.multiple_of((block * group + ids_ref[k]) * piece, piece)
            source = hidden_ref.at[:, pl.ds(start, piece)]
            target = out.at[:, pl.ds(block * piece, piece)]
            copies.append(pltpu.make_async_copy(source, target, sems.at[len(copies)]))
            copies[len(copies) - 1].start()
    return copies


def cut_kernel(members, group, piece, ids_ref, hidden_ref, *refs):
    for copy in cut_copies(members, refs[: len(members)], group, piece, ids_ref, hidden_ref, refs[len(members)]):
        copy.wait()


def cut_plain(ids, hidden, k, group, piece):
    rows, depth = hidden.shape
    pieces = hidden.reshape(rows, depth // (group * piece), group, piece)
    return lax.dynamic_index_in_dim(pieces, ids[k], 2, keepdims=False).reshape(rows, depth // group)


def cut(ids, hidden, members, group, piece):
    rows, depth = hidden.shape
    if piece % 128:
        return [cut_plain(ids, hidden, k, group, piece) for k in members]
    count = len(members)
    return pl.pallas_call(
        functools.partial(cut_kernel, members, group, piece),
        out_shape=tuple(shape((rows, depth // group)) for _ in members),
        in_specs=[SMEM, ANY],
        out_specs=(VMEM,) * count,
        scratch_shapes=[pltpu.SemaphoreType.DMA((count * depth // (group * piece),))],
        compiler_params=pltpu.CompilerParams(vmem_limit_bytes=8 * MIB),
        cost_estimate=pl.CostEstimate(flops=0, bytes_accessed=hidden.size * count, transcendentals=0),
        name="cut",
    )(ids, hidden)


def fetch(sources, slots):
    count = len(sources)
    copies = [pltpu.make_async_copy(sources[i], slots[i], slots[count + i]) for i in range(count)]
    for copy in copies:
        copy.start()
    return copies


def project_kernel(places, ids_ref, *refs):
    count = len(places)
    slots = refs[len(refs) - 2 * (count + 1) :]
    copies = fetch(refs[: count + 1], slots)
    hidden = slots[count]
    size = sum(slots[i].shape[0] for i in range(count) if places[i][0] == 0)
    copies[count].wait()
    total = None
    for i, (part, first) in enumerate(places):
        rows = slots[i].shape[0]
        start = pl.multiple_of(ids_ref[part] * size + first, rows)
        copies[i].wait()
        term = nn(hidden[:, pl.ds(start, rows)], slots[i][...])
        total = term if total is None else total + term
    first = 0
    for out in refs[count + 1 : len(refs) - 2 * (count + 1)]:
        width = out.shape[1]
        out[...] = total[:, first : first + width].astype(BF16)
        first += width


def project(ids, hidden, weights, widths):
    return pallas(
        functools.partial(project_kernel, [place for _, *place in weights]),
        tuple(shape((hidden.shape[0], width)) for width in widths),
        [ids],
        [],
        "project",
        2 * hidden.size * sum(widths),
        far=[*[array for array, *_ in weights], hidden],
    )


def hidden_kernel(places, ids_ref, grad_ref, *refs):
    count = len(places)
    slots = refs[count + 1 :]
    copies = fetch(refs[:count], slots)
    size = sum(slots[i].shape[0] for i in range(count) if places[i][0] == 0)
    for i, (part, first) in enumerate(places):
        rows = slots[i].shape[0]
        start = pl.multiple_of(ids_ref[part] * size + first, rows)
        copies[i].wait()
        refs[count][:, pl.ds(start, rows)] = nt(grad_ref[...], slots[i][...]).astype(BF16)


def hidden_grad(ids, grad, weights, depth):
    return pallas(
        functools.partial(hidden_kernel, [place for _, *place in weights]),
        shape((grad.shape[0], depth)),
        [ids],
        [grad],
        "hidden_grad",
        2 * grad.size * depth,
        far=[array for array, *_ in weights],
    )


def attend_kernel(layouts, group, rows, bq, bk, block_ref, pages_ref, *refs):
    count = sum(len(layout) for layout in layouts)
    parts, (grad_ref, own_ref) = refs[:count], refs[count : count + 2]
    q_ref, k_ref, v_ref, do_ref, s_ref, dp_ref, dk_ref, dv_ref, kt_ref, m_ref = refs[count + 2 :]
    seq, hd = do_ref.shape
    near = rows * group
    block = block_ref[0]
    scale = hd**-0.5
    scale2 = scale * math.log2(math.e)
    at = 0
    for layout, targets in zip(layouts, ((q_ref, k_ref), (v_ref,), (do_ref,))):
        for distances in layout:
            for number, distance in enumerate(distances):
                here = pl.ds(pl.multiple_of((block ^ distance) * rows, rows), rows)
                for column, target in enumerate(targets):
                    target[here, :] = parts[at][number * rows : (number + 1) * rows, column * hd : (column + 1) * hd]
            at += 1
    dk_ref[...] = jnp.zeros_like(dk_ref)
    dv_ref[...] = jnp.zeros_like(dv_ref)
    kt_ref[...] = k_ref[...].T
    ends, end = [], jnp.int32(0)
    for page in range(pages_ref.shape[1]):
        end = end + pages_ref[0, page]
        ends.append(end)
    low = lax.div(block, group) * near
    near_first, near_last = lax.div(low, bk), lax.div(low, bk) + near // bk

    def limit_of(pos):
        limit = jnp.full_like(pos, seq)
        for page_end in ends:
            limit = jnp.minimum(limit, jnp.where(page_end > pos, page_end, seq))
        return limit

    @pl.loop(0, seq // bq)
    def _(i):
        q0 = pl.multiple_of(i * bq, bq)
        limits = limit_of(q0 + lax.broadcasted_iota(jnp.int32, (1, bq), 1))
        count = lax.div(limit_of(q0 + (bq - 1)) + (bk - 1), bk)
        first, last = jnp.minimum(near_first, count), jnp.minimum(near_last, count)
        is_near = (q0 >= low) & (q0 < low + near)

        @pl.when(is_near | (first < last))
        def _():
            q = q_ref[pl.ds(q0, bq), :]
            do = do_ref[pl.ds(q0, bq), :]
            qt, dot_t = q.T, do.T

            def scores(masked, j, carry):
                row_max, total, dot = carry
                k0 = pl.multiple_of(j * bk, bk)
                s = nn(k_ref[pl.ds(k0, bk), :], qt) * scale2
                if masked:
                    key = k0 + lax.broadcasted_iota(jnp.int32, (bk, 1), 0)
                    s = jnp.where(key < limits, s, -1e30)
                high = jnp.maximum(row_max, jnp.max(s, axis=0, keepdims=True))
                p = jnp.exp2(s - high)
                dp = nn(v_ref[pl.ds(k0, bk), :], dot_t)
                s_ref[pl.ds(k0, bk), :] = p
                dp_ref[pl.ds(k0, bk), :] = dp
                m_ref[j] = high
                fade = jnp.exp2(row_max - high)
                total = total * fade + jnp.sum(p, axis=0, keepdims=True)
                dot = dot * fade + jnp.sum(p * dp, axis=0, keepdims=True)
                return high, total, dot

            zero = jnp.zeros((1, bq), F32)
            carry = (jnp.full((1, bq), -3e38, F32), zero, zero)
            full = jnp.minimum(lax.div(q0, bk), count)
            carry = lax.fori_loop(0, full, functools.partial(scores, False), carry)
            row_max, total, dot = lax.fori_loop(full, count, functools.partial(scores, True), carry)
            inv = 1.0 / total
            dot = dot * inv

            def dscore(j):
                k0 = pl.multiple_of(j * bk, bk)
                share = jnp.exp2(m_ref[j] - row_max) * inv
                gain = share * scale
                p = s_ref[pl.ds(k0, bk), :]
                return k0, p * share, (p * (dp_ref[pl.ds(k0, bk), :] * gain - dot * gain)).astype(BF16)

            def key_grads(j, carry):
                k0, p, ds = dscore(j)
                dv_ref[pl.ds(k0 - low, bk), :] += nn(p.astype(BF16), do)
                dk_ref[pl.ds(k0 - low, bk), :] += nn(ds, q)
                return carry

            def query_grads(j, dqt):
                k0, _, ds = dscore(j)
                return dqt + nn(kt_ref[:, pl.ds(k0, bk)], ds)

            def all_grads(j, dqt):
                k0, p, ds = dscore(j)
                dv_ref[pl.ds(k0 - low, bk), :] += nn(p.astype(BF16), do)
                dk_ref[pl.ds(k0 - low, bk), :] += nn(ds, q)
                return dqt + nn(kt_ref[:, pl.ds(k0, bk)], ds)

            @pl.when(is_near)
            def _():
                dqt = lax.fori_loop(0, first, query_grads, jnp.zeros((hd, bq), F32))
                dqt = lax.fori_loop(first, last, all_grads, dqt)
                dqt = lax.fori_loop(last, count, query_grads, dqt)
                grad_ref[pl.ds(pl.multiple_of(q0 - low, bq), bq), :hd] = dqt.T.astype(BF16)

            @pl.when(jnp.logical_not(is_near))
            def _():
                lax.fori_loop(first, last, key_grads, 0)

    grad_ref[:, hd : 2 * hd] = dk_ref[...].astype(BF16)
    grad_ref[:, 2 * hd :] = dv_ref[...].astype(BF16)
    own = pl.multiple_of(lax.rem(block, group) * rows, rows)
    own_ref[...] = grad_ref[pl.ds(own, rows), :]


def attend(block, pages, sets, blocks, group):
    rows = sets[0][0][0].shape[0] // len(sets[0][0][1])
    hd = sets[1][0][0].shape[1]
    seq, near = rows * blocks, rows * group
    bq, bk = (near, 2 * rows) if seq <= 4096 else (rows, rows)
    layouts = [[distances for _, distances in parts] for parts in sets]
    return pallas(
        functools.partial(attend_kernel, layouts, group, rows, bq, bk),
        (shape((near, 3 * hd)), shape((rows, 3 * hd))),
        [block, pages],
        [array for parts in sets for array, _ in parts],
        "attend",
        10 * seq * seq * hd,
        [pltpu.VMEM((seq, hd), BF16)] * 4
        + [pltpu.VMEM((seq, bq), F32)] * 2
        + [pltpu.VMEM((near, hd), F32)] * 2
        + [pltpu.VMEM((hd, seq), BF16), pltpu.VMEM((seq // bk, 1, bq), F32)],
    )


def weight_kernel(group, piece, ids_ref, fsdp_ref, grad_ref, hidden_ref, *refs):
    parts, (kept_ref, away_ref, own_ref, sems) = refs[: group - 1], refs[group - 1 :]
    copies = cut_copies([0], [own_ref], group, piece, ids_ref, hidden_ref, sems)
    rows, width = own_ref.shape
    fsdp_size = 2 * kept_ref.shape[0]
    size = width // fsdp_size
    for copy in copies:
        copy.wait()
    for j in range(fsdp_size):
        columns = pl.ds(pl.multiple_of(fsdp_ref[j] * size, size), size)
        total = None
        for k, part in enumerate((own_ref, *parts)):
            here = pl.ds(pl.multiple_of(ids_ref[k] * rows, rows), rows)
            term = tn(part[:, columns], grad_ref[here, :])
            total = term if total is None else total + term
        out = away_ref if j % 2 else kept_ref
        out[j // 2] = total.astype(out.dtype)


def weight_grad(ids, fsdp_ids, grad, hidden, parts, piece):
    group, fsdp_size, width = len(parts) + 1, fsdp_ids.shape[0], grad.shape[1]
    rows, columns = parts[0].shape
    size = columns // fsdp_size
    half = (fsdp_size // 2, size, width)
    if piece % 128:
        parts = [cut_plain(ids, hidden, 0, group, piece), *parts]
        total = sum(tn(parts[k], lax.dynamic_slice_in_dim(grad, ids[k] * rows, rows, 0)) for k in range(group))
        both = jnp.take(total.reshape(fsdp_size, size, width), fsdp_ids, axis=0)
        both = both.reshape(fsdp_size // 2, 2, size, width)
        return both[:, 0], both[:, 1].astype(BF16)
    return pl.pallas_call(
        functools.partial(weight_kernel, group, piece),
        out_shape=(shape(half, F32), shape(half)),
        in_specs=[SMEM, SMEM, VMEM, ANY] + [VMEM] * (group - 1),
        out_specs=(VMEM, VMEM),
        scratch_shapes=[pltpu.VMEM((rows, columns), BF16), pltpu.SemaphoreType.DMA((columns // piece,))],
        compiler_params=pltpu.CompilerParams(vmem_limit_bytes=20 * MIB),
        cost_estimate=pl.CostEstimate(flops=2 * grad.size * columns, bytes_accessed=8 * MIB, transcendentals=0),
        name="weight_grad",
    )(ids, fsdp_ids, grad, hidden, *parts)


def finish_kernel(group, piece, ids_ref, *refs):
    out_ref = refs[group]
    for k in range(group):
        for half in range(refs[k].shape[0] // piece):
            start = pl.multiple_of((half * group + ids_ref[k]) * piece, piece)
            out_ref[pl.ds(start, piece), :] = refs[k][half * piece : (half + 1) * piece, :].astype(F32)


def finish(ids, blocks, piece):
    group = len(blocks)
    rows, width = blocks[0].shape
    if piece % 16:
        order = jnp.take(jnp.stack(blocks), ids, axis=0).reshape(group, rows // piece, piece, width)
        return order.swapaxes(0, 1).reshape(group * rows, width).astype(F32)
    return pallas(
        functools.partial(finish_kernel, group, piece),
        shape((group * rows, width), F32),
        [ids],
        blocks,
        "finish",
        0,
    )


def swap(array, axis, size, distance):
    return lax.ppermute(array, axis, [(i, i ^ distance) for i in range(size)])


def spread(part, size):
    array, distances = part
    return [(swap(array, "ctx", size, k), [k ^ d for d in distances]) for k in range(2, size, 2)]


def widen(parts, size):
    arrays = [array for array, _ in parts]
    whole = jnp.concatenate(arrays, axis=0) if len(arrays) > 1 else arrays[0]
    return swap(whole, "ctx", size, 1), [1 ^ d for _, distances in parts for d in distances]


def after(part, done):
    array, *_ = lax.optimization_barrier((part[0], *[other for other, _ in done]))
    return array, part[1]


def local(ctx_size, fsdp_size, hidden_in, page_tokens, grad_attn, w_qkv):
    hidden, grad_out = hidden_in[0], grad_attn[0]
    rows, depth = hidden.shape
    hd = grad_out.shape[1]
    f, c = lax.axis_index("fsdp"), lax.axis_index("ctx")
    fsdp_ids = f ^ jnp.arange(fsdp_size, dtype=jnp.int32)
    group = min(4, ctx_size)
    group_ids = (c % group) ^ jnp.arange(group, dtype=jnp.int32)

    piece = depth // (fsdp_size * ctx_size)
    top = fsdp_size // 2
    weights = {0: [w_qkv], top: [swap(w_qkv, "fsdp", fsdp_size, top)]}
    chunks = dict(zip((1, 2), cut(group_ids, hidden, (1, 2), group, piece)))
    grads = [(grad_out, [0])]
    grads += spread(grads[0], ctx_size)
    moved = {k: swap(chunks[k], "ctx", ctx_size, k) for k in (1, 2)}
    arrays, _ = lax.optimization_barrier(([array for array, _ in grads], chunks))
    grads = [(array, distances) for array, (_, distances) in zip(arrays, grads)]
    whole = jnp.concatenate([array for array, _ in grads], axis=0)
    array, distances = widen([(whole, [d for _, distances in grads for d in distances])], ctx_size)
    weights[top], array = lax.optimization_barrier((weights[top], array))
    grads.append((array, distances))
    bit = top // 2
    while bit:
        for k in list(weights):
            halves = weights[k]
            weights[k ^ bit] = [swap(half, "fsdp", fsdp_size, bit) for half in halves]
        bit //= 2
    size = w_qkv.shape[0]
    weights = [
        (array, k, number * (size // len(weights[k]))) for k in range(fsdp_size) for number, array in enumerate(weights[k])
    ]

    qk, v = project(fsdp_ids, hidden, weights, (2 * hd, hd))
    qks = [(qk, [0])]
    qks += spread(qks[0], ctx_size)
    v_pair = [(v, [0]), widen([after((v, [0]), [(moved[1], 0)])], ctx_size)]
    pair = jnp.concatenate([array for array, _ in v_pair], axis=0), [0, 1]
    vs = [pair, *spread(after(pair, qks[1:]), ctx_size)]
    qks.append(widen([after(qks[0], [pair, (moved[1], 0), (moved[2], 0)]), *qks[1:]], ctx_size))
    (late,) = cut(group_ids, after((hidden, 0), [(qk, 0)])[0], (3,), group, piece)
    moved[3] = swap(after((late, 0), vs[1:])[0], "ctx", ctx_size, 3)
    block = c.reshape(1).astype(jnp.int32)
    grad_near, grad_own = attend(block, page_tokens, [qks, vs, grads], ctx_size, group)
    grad_inputs = hidden_grad(fsdp_ids, grad_own, weights, depth)

    kept, away = weight_grad(group_ids, fsdp_ids, grad_near, hidden, [moved[k] for k in (1, 2, 3)], piece)
    bit = 1
    while bit < fsdp_size:
        total = kept + swap(away, "fsdp", fsdp_size, bit).astype(F32)
        bit *= 2
        if bit < fsdp_size:
            kept, away = total[0::2], total[1::2].astype(BF16)
    total = total[0]
    bit = group
    while bit < ctx_size:
        half = total.astype(BF16)
        total = half.astype(F32) + swap(half, "ctx", ctx_size, bit).astype(F32)
        bit *= 2
    total, grad_inputs = lax.optimization_barrier((total.astype(BF16), grad_inputs))
    gathered = [swap(total, "ctx", ctx_size, k) if k else total for k in range(group)]
    grad_weights = finish(group_ids, gathered, depth // (fsdp_size * ctx_size))
    return grad_inputs[None], grad_weights


def solution(mesh):
    in_specs = (P("fsdp", "ctx", None), P("fsdp", None), P("fsdp", "ctx", None), P("fsdp", None))
    out_specs = (P("fsdp", "ctx", None), P("fsdp", None))
    body = functools.partial(local, mesh.shape["ctx"], mesh.shape["fsdp"])
    return jax.shard_map(body, mesh=mesh, in_specs=in_specs, out_specs=out_specs, check_vma=False)
```

time: 118 us -> 113 us (0.958)
  starting transfers between devices: 34.1 us -> 29.4 us
  waiting for transfers between devices: 48.6 us -> 50.5 us
  local copies, waits for them, and re-layouts: 5.18 us -> 3.5 us
    ppermute x24, starting transfers between devices: 34.1 us -> 29.4 us  [swap(): return lax.ppermute(array, axis, [(i, i ^ distance) for i in range(size)])]
    pallas_call x1 -> x3, Pallas kernels: 2.29 us -> 5.5 us  [the longest x2 2.85 us: cut(): pl.pallas_call(functools.partial(cut_kernel, members, group, piece), out_...]
    pallas_call x5 -> x4, Pallas kernels: 25.3 us -> 22.7 us  [pallas(): pl.pallas_call(kernel, out_shape=out_shape, in_specs=[SMEM] * len(scalars...]
    ppermute x24, waiting for transfers between devices: 48.6 us -> 50.5 us  [swap(): return lax.ppermute(array, axis, [(i, i ^ distance) for i in range(size)])]
    unnamed x25 -> x21, local copies, waits for them, and re-layouts: 5.15 us -> 3.46 us
    concatenate x2 -> x1, other arithmetic: 1.58 us -> 0.03 us  [widen(): whole = jnp.concatenate(arrays, axis=0) if len(arrays) > 1 else arrays[0]]
  transfers between devices with their start and end apart: 24 -> 24, of which waited for: 16 -> 16; matrix products, arithmetic and copies ran while one was open for 1% -> 1% of each run, Pallas kernels for 20% -> 21%
where the time goes in v4:
time: 113 us; the launch traced here: 114 us
  waiting for transfers between devices  50.5 us (45%)
  starting transfers between devices  29.4 us (26%)
  Pallas kernels  28.2 us (25%)
  local copies, waits for them, and re-layouts  3.5 us (3%)
    ppermute x24, waiting for transfers between devices, swap(): return lax.ppermute(array, axis, [(i, i ^ distance) for i in range(size)])  50.5 us
    ppermute x24, starting transfers between devices, swap(): return lax.ppermute(array, axis, [(i, i ^ distance) for i in range(size)])  29.4 us
    pallas_call x4, Pallas kernels, pallas(): pl.pallas_call(kernel, out_shape=out_shape, in_specs=[SMEM] * len(scalars...  22.7 us
    unnamed x21, local copies, waits for them, and re-layouts  3.46 us
    pallas_call x2, Pallas kernels, cut(): pl.pallas_call(functools.partial(cut_kernel, members, group, piece), out_...  2.85 us
    pallas_call x1, Pallas kernels, weight_grad(): pl.pallas_call(functools.partial(weight_kernel, group, piece), out_shape=...  2.65 us
  transfers between devices with their start and end apart: 24, of which 16 were waited for; matrix products, arithmetic and copies ran while one was open for 1% of the time, Pallas kernels for 21%

profile of v4, /device:TPU:0, one launch (start us, length us, event | category | flops | bytes accessed | tf_op | source)
XLA Modules:
  0.0 113.6 jit_solution(6936041097208059206)
XLA Ops:
  0.6 3.0 %collective-permute-start.1 = (bf16[1024,384]{1,0:T(8,128)(2,1)}, bf16[1024,384]{1,0:T(8,128)(2,1)S(1)}, u32[]{:S(2)}, u32[]{:S(2)}) collective-permute-start(bf16[1024,384]{1,0:T(8,128)(2,1)} %refs_0_.3), channel_id=1, source_target_pairs={{0,2},{1,3},{2,0},{3,1},{4,6},{5,7},{6,4},{7,5},{8,10},{9,11},{10,... | collective-permute-start | bytes 2359304 | tf_op jit(solution)/shard_map/ppermute | solution.py:358
  3.6 1.6 %collective-permute-start.2 = (bf16[256,128]{1,0:T(8,128)(2,1)}, bf16[256,128]{1,0:T(8,128)(2,1)S(1)}, u32[]{:S(2)}, u32[]{:S(2)}) collective-permute-start(bf16[256,128]{1,0:T(8,128)(2,1)} %bitcast.10), channel_id=1, source_target_pairs={{0,8},{4,12},{8,0},{12,4},{16,24},{20,28},{24,16},{28,20},{1,9},{5... | collective-permute-start | bytes 196616 | tf_op jit(solution)/shard_map/ppermute | solution.py:358
  5.2 2.6 %collective-permute-start.3 = (bf16[256,128]{1,0:T(8,128)(2,1)}, bf16[256,128]{1,0:T(8,128)(2,1)S(1)}, u32[]{:S(2)}, u32[]{:S(2)}) collective-permute-start(bf16[256,128]{1,0:T(8,128)(2,1)} %bitcast.11), channel_id=1, source_target_pairs={{0,16},{4,20},{8,24},{12,28},{16,0},{20,4},{24,8},{28,12},{1,17},{... | collective-permute-start | bytes 196616 | tf_op jit(solution)/shard_map/ppermute | solution.py:358
  7.8 0.2 collective-permute-start.4
  8.0 1.6 %copy-done = bf16[1,256,4096]{2,1,0:T(8,128)(2,1)S(1)} copy-done((bf16[1,256,4096]{2,1,0:T(8,128)(2,1)S(1)}, bf16[1,256,4096]{2,1,0:T(8,128)(2,1)}, u32[]{:S(2)}) %copy-start) | copy-done | bytes 2097176
  9.6 2.0 %cut.2 = (bf16[256,1024]{1,0:T(8,128)(2,1)}, bf16[256,1024]{1,0:T(8,128)(2,1)}) custom-call(s32[4]{0:T(128)S(1)} %iota_xor_fusion.1.ids_ref, bf16[256,4096]{1,0:T(8,128)(2,1)S(1)} %bitcast.6), custom_call_target="tpu_custom_call" | custom-call | bytes 2097152 | tf_op jit(solution)/shard_map/cut/pallas_call | solution.py:81
  11.7 0.0 collective-permute-done.2.refs_10_
  11.7 0.7 collective-permute-done.3.refs_11_
  12.4 1.7 %collective-permute-done.4.refs_12_ = bf16[256,128]{1,0:T(8,128)(2,1)S(1)} collective-permute-done((bf16[256,128]{1,0:T(8,128)(2,1)}, bf16[256,128]{1,0:T(8,128)(2,1)S(1)}, u32[]{:S(2)}, u32[]{:S(2)}) %collective-permute-start.4) | collective-permute-done | bytes 65568 | tf_op jit(solution)/shard_map/ppermute | solution.py:358
  14.1 0.9 pad_maximum_fusion.1
  15.0 1.6 %collective-permute-start.5 = (bf16[1024,128]{1,0:T(8,128)(2,1)S(1)}, bf16[1024,128]{1,0:T(8,128)(2,1)S(1)}, u32[]{:S(2)}, u32[]{:S(2)}) collective-permute-start(bf16[1024,128]{1,0:T(8,128)(2,1)S(1)} %pad_maximum_fusion.1), channel_id=1, source_target_pairs={{0,4},{4,0},{8,12},{12,8},{16,20},{20,16},{24,28},{28,24},{1,5},{5... | collective-permute-start | bytes 786440 | tf_op jit(solution)/shard_map/ppermute | solution.py:358
  16.5 0.0 collective-permute-start
  16.5 4.8 %collective-permute-done.5.refs_13_ = bf16[1024,128]{1,0:T(8,128)(2,1)S(1)} collective-permute-done((bf16[1024,128]{1,0:T(8,128)(2,1)S(1)}, bf16[1024,128]{1,0:T(8,128)(2,1)S(1)}, u32[]{:S(2)}, u32[]{:S(2)}) %collective-permute-start.5) | collective-permute-done | bytes 262176 | tf_op jit(solution)/shard_map/ppermute | solution.py:358
  21.4 0.7 copy-done.7
  22.1 0.0 collective-permute-done.1.refs_2_
  22.1 0.0 collective-permute-start.6
  22.1 1.6 %collective-permute-start.10 = (bf16[256,1024]{1,0:T(8,128)(2,1)}, bf16[256,1024]{1,0:T(8,128)(2,1)S(1)}, u32[]{:S(2)}, u32[]{:S(2)}) collective-permute-start(bf16[256,1024]{1,0:T(8,128)(2,1)} %get-tuple-element.23), channel_id=1, source_target_pairs={{0,4},{4,0},{8,12},{12,8},{16,20},{20,16},{24,28},{28,24},{1,5},{5... | collective-permute-start | bytes 1572872 | tf_op jit(solution)/shard_map/ppermute | solution.py:358
  23.7 1.0 collective-permute-start.12
  24.7 0.0 collective-permute-done.refs_1_
  24.7 0.0 collective-permute-done.6.refs_3_
  24.8 0.0 copy-start.2
  24.8 1.1 copy-done.2
  25.9 3.3 %project.1 = (bf16[256,256]{1,0:T(8,128)(2,1)S(1)}, bf16[256,128]{1,0:T(8,128)(2,1)S(1)}) custom-call(s32[4]{0:T(128)S(1)} %iota_xor_fusion.ids_ref.fsdp_ref, bf16[1024,384]{1,0:T(8,128)(2,1)S(1)} %copy-done.2, bf16[1024,384]{1,0:T(8,128)(2,1)} %collective-permute-done.refs_1_, bf16[1024,384]{1,0:T(8,128)(2,1)S(1)} %collective-permute-done.1.refs_2_, ...), custom_call_target="tpu_custom_call" | custom-call | flops 805306368 | bytes 5439488 | tf_op jit(solution)/shard_map/project/pallas_call | solution.py:35
  29.2 0.0 copy-start.4
  29.2 0.0 copy-start.9
  29.2 1.1 collective-permute-start.7
  30.3 2.5 %collective-permute-start.8 = (bf16[256,256]{1,0:T(8,128)(2,1)S(1)}, bf16[256,256]{1,0:T(8,128)(2,1)S(1)}, u32[]{:S(2)}, u32[]{:S(2)}) collective-permute-start(bf16[256,256]{1,0:T(8,128)(2,1)S(1)} %get-tuple-element.33.refs_0_), channel_id=1, source_target_pairs={{0,16},{4,20},{8,24},{12,28},{16,0},{20,4},{24,8},{28,12},{1,17},{... | collective-permute-start | bytes 393224 | tf_op jit(solution)/shard_map/ppermute | solution.py:358
  32.8 0.9 collective-permute-start.9
  33.7 3.0 %collective-permute-done.10.refs_0_ = bf16[256,1024]{1,0:T(8,128)(2,1)S(1)} collective-permute-done((bf16[256,1024]{1,0:T(8,128)(2,1)}, bf16[256,1024]{1,0:T(8,128)(2,1)S(1)}, u32[]{:S(2)}, u32[]{:S(2)}) %collective-permute-start.10) | collective-permute-done | bytes 524320 | tf_op jit(solution)/shard_map/ppermute | solution.py:358
  36.7 1.5 %collective-permute-start.11 = (bf16[256,128]{1,0:T(8,128)(2,1)S(1)}, bf16[256,128]{1,0:T(8,128)(2,1)S(1)}, u32[]{:S(2)}, u32[]{:S(2)}) collective-permute-start(bf16[256,128]{1,0:T(8,128)(2,1)S(1)} %get-tuple-element.32), channel_id=1, source_target_pairs={{0,4},{4,0},{8,12},{12,8},{16,20},{20,16},{24,28},{28,24},{1,5},{5... | collective-permute-start | bytes 196616 | tf_op jit(solution)/shard_map/ppermute | solution.py:358
  38.2 2.7 %collective-permute-done.11 = bf16[256,128]{1,0:T(8,128)(2,1)S(1)} collective-permute-done((bf16[256,128]{1,0:T(8,128)(2,1)S(1)}, bf16[256,128]{1,0:T(8,128)(2,1)S(1)}, u32[]{:S(2)}, u32[]{:S(2)}) %collective-permute-start.11) | collective-permute-done | bytes 65568 | tf_op jit(solution)/shard_map/ppermute | solution.py:358
  40.9 0.7 collective-permute-done.12.refs_1_
  41.6 1.9 %collective-permute-done.7.refs_1_ = bf16[256,256]{1,0:T(8,128)(2,1)S(1)} collective-permute-done((bf16[256,256]{1,0:T(8,128)(2,1)S(1)}, bf16[256,256]{1,0:T(8,128)(2,1)S(1)}, u32[]{:S(2)}, u32[]{:S(2)}) %collective-permute-start.7) | collective-permute-done | bytes 131104 | tf_op jit(solution)/shard_map/ppermute | solution.py:358
  43.5 0.0 collective-permute-done.8.refs_2_
  43.5 4.4 %collective-permute-done.9.refs_3_ = bf16[256,256]{1,0:T(8,128)(2,1)S(1)} collective-permute-done((bf16[256,256]{1,0:T(8,128)(2,1)S(1)}, bf16[256,256]{1,0:T(8,128)(2,1)S(1)}, u32[]{:S(2)}, u32[]{:S(2)}) %collective-permute-start.9) | collective-permute-done | bytes 131104 | tf_op jit(solution)/shard_map/ppermute | solution.py:358
  47.9 0.6 collective-permute-start.13
  48.5 0.0 collective-permute-start.14
  48.5 2.1 %collective-permute-start.15 = (bf16[512,128]{1,0:T(8,128)(2,1)S(1)}, bf16[512,128]{1,0:T(8,128)(2,1)S(1)}, u32[]{:S(2)}, u32[]{:S(2)}) collective-permute-start(bf16[512,128]{1,0:T(8,128)(2,1)S(1)} %constant_dynamic-update-slice_fusion.refs_5_), channel_id=1, source_target_pairs={{0,16},{4,20},{8,24},{12,28},{16,0},{20,4},{24,8},{28,12},{1,17},{... | collective-permute-start | bytes 393224 | tf_op jit(solution)/shard_map/ppermute | solution.py:358
  50.6 2.2 %collective-permute-start.16 = (bf16[512,128]{1,0:T(8,128)(2,1)S(1)}, bf16[512,128]{1,0:T(8,128)(2,1)S(1)}, u32[]{:S(2)}, u32[]{:S(2)}) collective-permute-start(bf16[512,128]{1,0:T(8,128)(2,1)S(1)} %constant_dynamic-update-slice_fusion.refs_5_), channel_id=1, source_target_pairs={{0,24},{4,28},{8,16},{12,20},{16,8},{20,12},{24,0},{28,4},{1,25},{... | collective-permute-start | bytes 393224 | tf_op jit(solution)/shard_map/ppermute | solution.py:358
  52.9 0.8 cut.3
  53.7 1.1 collective-permute-done.14.refs_6_
  54.8 6.2 %collective-permute-done.15.refs_7_ = bf16[512,128]{1,0:T(8,128)(2,1)S(1)} collective-permute-done((bf16[512,128]{1,0:T(8,128)(2,1)S(1)}, bf16[512,128]{1,0:T(8,128)(2,1)S(1)}, u32[]{:S(2)}, u32[]{:S(2)}) %collective-permute-start.15) | collective-permute-done | bytes 131104 | tf_op jit(solution)/shard_map/ppermute | solution.py:358
  60.9 0.0 collective-permute-done.16.refs_8_
  60.9 2.9 %collective-permute-start.17 = (bf16[256,1024]{1,0:T(8,128)(2,1)S(1)}, bf16[256,1024]{1,0:T(8,128)(2,1)S(1)}, u32[]{:S(2)}, u32[]{:S(2)}) collective-permute-start(bf16[256,1024]{1,0:T(8,128)(2,1)S(1)} %cut.3), channel_id=1, source_target_pairs={{0,12},{4,8},{8,4},{12,0},{16,28},{20,24},{24,20},{28,16},{1,13},{... | collective-permute-start | bytes 1572872 | tf_op jit(solution)/shard_map/ppermute | solution.py:358
  63.9 0.0 collective-permute-done.13.refs_4_
  63.9 13.1 %attend.1 = (bf16[1024,384]{1,0:T(8,128)(2,1)S(1)}, bf16[256,384]{1,0:T(8,128)(2,1)S(1)}) custom-call(s32[1]{0:T(128)} %bitcast.block_ref, s32[1,8]{1,0:T(1,128)S(1)} %copy-done.9, bf16[256,256]{1,0:T(8,128)(2,1)S(1)} %get-tuple-element.33.refs_0_, bf16[256,256]{1,0:T(8,128)(2,1)S(1)} %collective-permute-done.7.refs_1_, ...), custom_call_target="tpu_custom_call" | custom-call | flops 5368709120 | bytes 3080192 | tf_op jit(solution)/shard_map/attend/pallas_call | solution.py:35
  77.0 2.7 %weight_grad.1 = (f32[2,256,384]{2,1,0:T(8,128)S(1)}, bf16[2,256,384]{2,1,0:T(8,128)(2,1)S(1)}) custom-call(s32[4]{0:T(128)S(1)} %iota_xor_fusion.1.ids_ref, s32[4]{0:T(128)S(1)} %iota_xor_fusion.ids_ref.fsdp_ref, bf16[1024,384]{1,0:T(8,128)(2,1)S(1)} %get-tuple-element.36.grad_ref, bf16[256,4096]{1,0:T(8,128)(2,1)S(1)} %bitcast.9, ...), custom_call_target="tpu_custom_call" | custom-call | flops 805306368 | bytes 8388608 | tf_op jit(solution)/shard_map/weight_grad/pallas_call | solution.py:321
  79.7 0.0 copy-start.3
  79.7 0.1 collective-permute-start.18
  79.8 1.7 %collective-permute-done.18 = bf16[2,256,384]{2,1,0:T(8,128)(2,1)S(1)} collective-permute-done((bf16[2,256,384]{2,1,0:T(8,128)(2,1)S(1)}, bf16[2,256,384]{2,1,0:T(8,128)(2,1)S(1)}, u32[]{:S(2)}, u32[]{:S(2)}) %collective-permute-start.18) | collective-permute-done | bytes 393248 | tf_op jit(solution)/shard_map/ppermute | solution.py:358
  81.5 0.1 convert_add_fusion
  81.6 0.2 collective-permute-start.19
  81.8 6.8 %collective-permute-done.19 = bf16[1,256,384]{2,1,0:T(8,128)(2,1)S(1)} collective-permute-done((bf16[1,256,384]{2,1,0:T(8,128)(2,1)S(1)}, bf16[1,256,384]{2,1,0:T(8,128)(2,1)S(1)}, u32[]{:S(2)}, u32[]{:S(2)}) %collective-permute-start.19) | collective-permute-done | bytes 196640 | tf_op jit(solution)/shard_map/ppermute | solution.py:358
  88.7 0.1 collective-permute-start.20
  88.8 4.5 %hidden_grad.1 = bf16[256,4096]{1,0:T(8,128)(2,1)} custom-call(s32[4]{0:T(128)S(1)} %iota_xor_fusion.ids_ref.fsdp_ref, bf16[256,384]{1,0:T(8,128)(2,1)S(1)} %get-tuple-element.41.grad_ref, bf16[1024,384]{1,0:T(8,128)(2,1)S(1)} %copy-done.3, bf16[1024,384]{1,0:T(8,128)(2,1)} %collective-permute-done.refs_1_, ...), custom_call_target="tpu_custom_call" | custom-call | flops 805306368 | bytes 5439488 | tf_op jit(solution)/shard_map/hidden_grad/pallas_call | solution.py:35
  93.3 6.2 %collective-permute-done.20 = bf16[256,384]{1,0:T(8,128)(2,1)S(1)} collective-permute-done((bf16[256,384]{1,0:T(8,128)(2,1)S(1)}, bf16[256,384]{1,0:T(8,128)(2,1)S(1)}, u32[]{:S(2)}, u32[]{:S(2)}) %collective-permute-start.20) | collective-permute-done | bytes 196640 | tf_op jit(solution)/shard_map/ppermute | solution.py:358
  99.4 0.1 add_convert_fusion.refs_0_
  99.5 0.6 collective-permute-start.21
  100.1 0.0 collective-permute-start.22
  100.1 3.0 %collective-permute-start.23 = (bf16[256,384]{1,0:T(8,128)(2,1)S(1)}, bf16[256,384]{1,0:T(8,128)(2,1)S(1)}, u32[]{:S(2)}, u32[]{:S(2)}) collective-permute-start(bf16[256,384]{1,0:T(8,128)(2,1)S(1)} %add_convert_fusion.refs_0_), channel_id=1, source_target_pairs={{0,12},{4,8},{8,4},{12,0},{16,28},{20,24},{24,20},{28,16},{1,13},{... | collective-permute-start | bytes 589832 | tf_op jit(solution)/shard_map/ppermute | solution.py:358
  103.1 3.4 %collective-permute-done.21.refs_1_ = bf16[256,384]{1,0:T(8,128)(2,1)S(1)} collective-permute-done((bf16[256,384]{1,0:T(8,128)(2,1)S(1)}, bf16[256,384]{1,0:T(8,128)(2,1)S(1)}, u32[]{:S(2)}, u32[]{:S(2)}) %collective-permute-start.21) | collective-permute-done | bytes 196640 | tf_op jit(solution)/shard_map/ppermute | solution.py:358
  106.5 1.4 %collective-permute-done.22.refs_2_ = bf16[256,384]{1,0:T(8,128)(2,1)S(1)} collective-permute-done((bf16[256,384]{1,0:T(8,128)(2,1)S(1)}, bf16[256,384]{1,0:T(8,128)(2,1)S(1)}, u32[]{:S(2)}, u32[]{:S(2)}) %collective-permute-start.22) | collective-permute-done | bytes 196640 | tf_op jit(solution)/shard_map/ppermute | solution.py:358
  107.9 3.9 %collective-permute-done.23.refs_3_ = bf16[256,384]{1,0:T(8,128)(2,1)S(1)} collective-permute-done((bf16[256,384]{1,0:T(8,128)(2,1)S(1)}, bf16[256,384]{1,0:T(8,128)(2,1)S(1)}, u32[]{:S(2)}, u32[]{:S(2)}) %collective-permute-start.23) | collective-permute-done | bytes 196640 | tf_op jit(solution)/shard_map/ppermute | solution.py:358
  111.8 1.8 %finish.1 = f32[1024,384]{1,0:T(8,128)} custom-call(s32[4]{0:T(128)S(1)} %iota_xor_fusion.1.ids_ref, bf16[256,384]{1,0:T(8,128)(2,1)S(1)} %add_convert_fusion.refs_0_, bf16[256,384]{1,0:T(8,128)(2,1)S(1)} %collective-permute-done.21.refs_1_, bf16[256,384]{1,0:T(8,128)(2,1)S(1)} %collective-permute-done.22.refs_2_, ...), custom_call_target="tpu_custom_call" | custom-call | bytes 2359296 | tf_op jit(solution)/shard_map/finish/pallas_call | solution.py:35
  (21 shorter events, 0.2 us)
Async XLA Ops:
  0.6 21.5 %collective-permute-start.1 = (bf16[1024,384]{1,0:T(8,128)(2,1)}, bf16[1024,384]{1,0:T(8,128)(2,1)S(1)}, u32[]{:S(2)}, u32[]{:S(2)}) collective-permute-start(bf16[1024,384]{1,0:T(8,128)(2,1)} %refs_0_.3), channel_id=1, source_target_pairs={{0,2},{1,3},{2,0},{3,1},{4,6},{5,7},{6,4},{7,5},{8,10},{9,11},{10,... | collective-permute-start | bytes 2359304 | tf_op jit(solution)/shard_map/ppermute | solution.py:358
  3.6 8.0 %collective-permute-start.2 = (bf16[256,128]{1,0:T(8,128)(2,1)}, bf16[256,128]{1,0:T(8,128)(2,1)S(1)}, u32[]{:S(2)}, u32[]{:S(2)}) collective-permute-start(bf16[256,128]{1,0:T(8,128)(2,1)} %bitcast.10), channel_id=1, source_target_pairs={{0,8},{4,12},{8,0},{12,4},{16,24},{20,28},{24,16},{28,20},{1,9},{5... | collective-permute-start | bytes 196616 | tf_op jit(solution)/shard_map/ppermute | solution.py:358
  5.2 7.2 %collective-permute-start.3 = (bf16[256,128]{1,0:T(8,128)(2,1)}, bf16[256,128]{1,0:T(8,128)(2,1)S(1)}, u32[]{:S(2)}, u32[]{:S(2)}) collective-permute-start(bf16[256,128]{1,0:T(8,128)(2,1)} %bitcast.11), channel_id=1, source_target_pairs={{0,16},{4,20},{8,24},{12,28},{16,0},{20,4},{24,8},{28,12},{1,17},{... | collective-permute-start | bytes 196616 | tf_op jit(solution)/shard_map/ppermute | solution.py:358
  7.8 6.3 %collective-permute-start.4 = (bf16[256,128]{1,0:T(8,128)(2,1)}, bf16[256,128]{1,0:T(8,128)(2,1)S(1)}, u32[]{:S(2)}, u32[]{:S(2)}) collective-permute-start(bf16[256,128]{1,0:T(8,128)(2,1)} %bitcast.12), channel_id=1, source_target_pairs={{0,24},{4,28},{8,16},{12,20},{16,8},{20,12},{24,0},{28,4},{1,25},{... | collective-permute-start | bytes 196616 | tf_op jit(solution)/shard_map/ppermute | solution.py:358
  8.0 1.6 %copy-start = (bf16[1,256,4096]{2,1,0:T(8,128)(2,1)S(1)}, bf16[1,256,4096]{2,1,0:T(8,128)(2,1)}, u32[]{:S(2)}) copy-start(bf16[1,256,4096]{2,1,0:T(8,128)(2,1)} %param.4) | copy-start | bytes 6291460
  9.6 15.1 %copy-start.1 = (bf16[1,256,4096]{2,1,0:T(8,128)(2,1)S(1)}, bf16[1,256,4096]{2,1,0:T(8,128)(2,1)}, u32[]{:S(2)}) copy-start(bf16[1,256,4096]{2,1,0:T(8,128)(2,1)} %param.4) | copy-start | bytes 6291460
  14.1 8.0 %copy-start.5 = (bf16[256,128]{1,0:T(8,128)(2,1)}, bf16[256,128]{1,0:T(8,128)(2,1)S(1)}, u32[]{:S(2)}) copy-start(bf16[256,128]{1,0:T(8,128)(2,1)S(1)} %collective-permute-done.4.refs_12_) | copy-start | bytes 196612
  15.0 6.4 %collective-permute-start.5 = (bf16[1024,128]{1,0:T(8,128)(2,1)S(1)}, bf16[1024,128]{1,0:T(8,128)(2,1)S(1)}, u32[]{:S(2)}, u32[]{:S(2)}) collective-permute-start(bf16[1024,128]{1,0:T(8,128)(2,1)S(1)} %pad_maximum_fusion.1), channel_id=1, source_target_pairs={{0,4},{4,0},{8,12},{12,8},{16,20},{20,16},{24,28},{28,24},{1,5},{5... | collective-permute-start | bytes 786440 | tf_op jit(solution)/shard_map/ppermute | solution.py:358
  16.5 8.2 %collective-permute-start = (bf16[1024,384]{1,0:T(8,128)(2,1)}, bf16[1024,384]{1,0:T(8,128)(2,1)}, u32[]{:S(2)}, u32[]{:S(2)}) collective-permute-start(bf16[1024,384]{1,0:T(8,128)(2,1)} %refs_0_.3), channel_id=1, source_target_pairs={{0,1},{1,0},{2,3},{3,2},{4,5},{5,4},{6,7},{7,6},{8,9},{9,8},{10,11... | collective-permute-start | bytes 2359304 | tf_op jit(solution)/shard_map/ppermute | solution.py:358
  21.4 0.7 copy-start.7
  22.1 2.6 %collective-permute-start.6 = (bf16[1024,384]{1,0:T(8,128)(2,1)S(1)}, bf16[1024,384]{1,0:T(8,128)(2,1)}, u32[]{:S(2)}, u32[]{:S(2)}) collective-permute-start(bf16[1024,384]{1,0:T(8,128)(2,1)S(1)} %collective-permute-done.1.refs_2_), channel_id=1, source_target_pairs={{0,1},{1,0},{2,3},{3,2},{4,5},{5,4},{6,7},{7,6},{8,9},{9,8},{10,11... | collective-permute-start | bytes 2359304 | tf_op jit(solution)/shard_map/ppermute | solution.py:358
  22.1 14.5 %collective-permute-start.10 = (bf16[256,1024]{1,0:T(8,128)(2,1)}, bf16[256,1024]{1,0:T(8,128)(2,1)S(1)}, u32[]{:S(2)}, u32[]{:S(2)}) collective-permute-start(bf16[256,1024]{1,0:T(8,128)(2,1)} %get-tuple-element.23), channel_id=1, source_target_pairs={{0,4},{4,0},{8,12},{12,8},{16,20},{20,16},{24,28},{28,24},{1,5},{5... | collective-permute-start | bytes 1572872 | tf_op jit(solution)/shard_map/ppermute | solution.py:358
  23.7 17.9 %collective-permute-start.12 = (bf16[256,1024]{1,0:T(8,128)(2,1)}, bf16[256,1024]{1,0:T(8,128)(2,1)}, u32[]{:S(2)}, u32[]{:S(2)}) collective-permute-start(bf16[256,1024]{1,0:T(8,128)(2,1)} %get-tuple-element.24), channel_id=1, source_target_pairs={{0,8},{4,12},{8,0},{12,4},{16,24},{20,28},{24,16},{28,20},{1,9},{5... | collective-permute-start | bytes 1572872 | tf_op jit(solution)/shard_map/ppermute | solution.py:358
  24.8 1.1 %copy-start.2 = (bf16[1024,384]{1,0:T(8,128)(2,1)S(1)}, bf16[1024,384]{1,0:T(8,128)(2,1)}, u32[]{:S(2)}) copy-start(bf16[1024,384]{1,0:T(8,128)(2,1)} %refs_0_.3) | copy-start | bytes 2359300
  29.2 34.7 %copy-start.4 = (bf16[1,256,128]{2,1,0:T(8,128)(2,1)S(1)}, bf16[1,256,128]{2,1,0:T(8,128)(2,1)}, u32[]{:S(2)}) copy-start(bf16[1,256,128]{2,1,0:T(8,128)(2,1)} %param.6) | copy-start | bytes 196612
  29.2 34.7 %copy-start.6 = (bf16[256,128]{1,0:T(8,128)(2,1)S(1)}, bf16[256,128]{1,0:T(8,128)(2,1)}, u32[]{:S(2)}) copy-start(bf16[256,128]{1,0:T(8,128)(2,1)} %copy-done.5) | copy-start | bytes 196612
  29.2 34.7 %copy-start.8 = (bf16[1024,128]{1,0:T(8,128)(2,1)S(1)}, bf16[1024,128]{1,0:T(8,128)(2,1)}, u32[]{:S(2)}) copy-start(bf16[1024,128]{1,0:T(8,128)(2,1)} %copy-done.7) | copy-start | bytes 786436
  29.2 34.7 %copy-start.9 = (s32[1,8]{1,0:T(1,128)S(1)}, s32[1,8]{1,0:T(1,128)}, u32[]{:S(2)}) copy-start(s32[1,8]{1,0:T(1,128)} %pages_ref.1) | copy-start | bytes 100
  29.2 14.3 %collective-permute-start.7 = (bf16[256,256]{1,0:T(8,128)(2,1)S(1)}, bf16[256,256]{1,0:T(8,128)(2,1)S(1)}, u32[]{:S(2)}, u32[]{:S(2)}) collective-permute-start(bf16[256,256]{1,0:T(8,128)(2,1)S(1)} %get-tuple-element.33.refs_0_), channel_id=1, source_target_pairs={{0,8},{4,12},{8,0},{12,4},{16,24},{20,28},{24,16},{28,20},{1,9},{5... | collective-permute-start | bytes 393224 | tf_op jit(solution)/shard_map/ppermute | solution.py:358
  30.3 13.2 %collective-permute-start.8 = (bf16[256,256]{1,0:T(8,128)(2,1)S(1)}, bf16[256,256]{1,0:T(8,128)(2,1)S(1)}, u32[]{:S(2)}, u32[]{:S(2)}) collective-permute-start(bf16[256,256]{1,0:T(8,128)(2,1)S(1)} %get-tuple-element.33.refs_0_), channel_id=1, source_target_pairs={{0,16},{4,20},{8,24},{12,28},{16,0},{20,4},{24,8},{28,12},{1,17},{... | collective-permute-start | bytes 393224 | tf_op jit(solution)/shard_map/ppermute | solution.py:358
  32.8 15.1 %collective-permute-start.9 = (bf16[256,256]{1,0:T(8,128)(2,1)S(1)}, bf16[256,256]{1,0:T(8,128)(2,1)S(1)}, u32[]{:S(2)}, u32[]{:S(2)}) collective-permute-start(bf16[256,256]{1,0:T(8,128)(2,1)S(1)} %get-tuple-element.33.refs_0_), channel_id=1, source_target_pairs={{0,24},{4,28},{8,16},{12,20},{16,8},{20,12},{24,0},{28,4},{1,25},{... | collective-permute-start | bytes 393224 | tf_op jit(solution)/shard_map/ppermute | solution.py:358
  36.7 4.3 %collective-permute-start.11 = (bf16[256,128]{1,0:T(8,128)(2,1)S(1)}, bf16[256,128]{1,0:T(8,128)(2,1)S(1)}, u32[]{:S(2)}, u32[]{:S(2)}) collective-permute-start(bf16[256,128]{1,0:T(8,128)(2,1)S(1)} %get-tuple-element.32), channel_id=1, source_target_pairs={{0,4},{4,0},{8,12},{12,8},{16,20},{20,16},{24,28},{28,24},{1,5},{5... | collective-permute-start | bytes 196616 | tf_op jit(solution)/shard_map/ppermute | solution.py:358
  47.9 16.0 %collective-permute-start.13 = (bf16[1024,256]{1,0:T(8,128)(2,1)S(1)}, bf16[1024,256]{1,0:T(8,128)(2,1)S(1)}, u32[]{:S(2)}, u32[]{:S(2)}) collective-permute-start(bf16[1024,256]{1,0:T(8,128)(2,1)S(1)} %pad_maximum_fusion), channel_id=1, source_target_pairs={{0,4},{4,0},{8,12},{12,8},{16,20},{20,16},{24,28},{28,24},{1,5},{5... | collective-permute-start | bytes 1572872 | tf_op jit(solution)/shard_map/ppermute | solution.py:358
  48.5 6.3 %collective-permute-start.14 = (bf16[512,128]{1,0:T(8,128)(2,1)S(1)}, bf16[512,128]{1,0:T(8,128)(2,1)S(1)}, u32[]{:S(2)}, u32[]{:S(2)}) collective-permute-start(bf16[512,128]{1,0:T(8,128)(2,1)S(1)} %constant_dynamic-update-slice_fusion.refs_5_), channel_id=1, source_target_pairs={{0,8},{4,12},{8,0},{12,4},{16,24},{20,28},{24,16},{28,20},{1,9},{5... | collective-permute-start | bytes 393224 | tf_op jit(solution)/shard_map/ppermute | solution.py:358
  48.5 12.5 %collective-permute-start.15 = (bf16[512,128]{1,0:T(8,128)(2,1)S(1)}, bf16[512,128]{1,0:T(8,128)(2,1)S(1)}, u32[]{:S(2)}, u32[]{:S(2)}) collective-permute-start(bf16[512,128]{1,0:T(8,128)(2,1)S(1)} %constant_dynamic-update-slice_fusion.refs_5_), channel_id=1, source_target_pairs={{0,16},{4,20},{8,24},{12,28},{16,0},{20,4},{24,8},{28,12},{1,17},{... | collective-permute-start | bytes 393224 | tf_op jit(solution)/shard_map/ppermute | solution.py:358
  50.6 10.3 %collective-permute-start.16 = (bf16[512,128]{1,0:T(8,128)(2,1)S(1)}, bf16[512,128]{1,0:T(8,128)(2,1)S(1)}, u32[]{:S(2)}, u32[]{:S(2)}) collective-permute-start(bf16[512,128]{1,0:T(8,128)(2,1)S(1)} %constant_dynamic-update-slice_fusion.refs_5_), channel_id=1, source_target_pairs={{0,24},{4,28},{8,16},{12,20},{16,8},{20,12},{24,0},{28,4},{1,25},{... | collective-permute-start | bytes 393224 | tf_op jit(solution)/shard_map/ppermute | solution.py:358
  60.9 16.1 %collective-permute-start.17 = (bf16[256,1024]{1,0:T(8,128)(2,1)S(1)}, bf16[256,1024]{1,0:T(8,128)(2,1)S(1)}, u32[]{:S(2)}, u32[]{:S(2)}) collective-permute-start(bf16[256,1024]{1,0:T(8,128)(2,1)S(1)} %cut.3), channel_id=1, source_target_pairs={{0,12},{4,8},{8,4},{12,0},{16,28},{20,24},{24,20},{28,16},{1,13},{... | collective-permute-start | bytes 1572872 | tf_op jit(solution)/shard_map/ppermute | solution.py:358
  79.7 9.1 %copy-start.3 = (bf16[1024,384]{1,0:T(8,128)(2,1)S(1)}, bf16[1024,384]{1,0:T(8,128)(2,1)}, u32[]{:S(2)}) copy-start(bf16[1024,384]{1,0:T(8,128)(2,1)} %refs_0_.3) | copy-start | bytes 2359300
  79.7 1.8 %collective-permute-start.18 = (bf16[2,256,384]{2,1,0:T(8,128)(2,1)S(1)}, bf16[2,256,384]{2,1,0:T(8,128)(2,1)S(1)}, u32[]{:S(2)}, u32[]{:S(2)}) collective-permute-start(bf16[2,256,384]{2,1,0:T(8,128)(2,1)S(1)} %get-tuple-element.40), channel_id=1, source_target_pairs={{0,1},{1,0},{2,3},{3,2},{4,5},{5,4},{6,7},{7,6},{8,9},{9,8},{10,11... | collective-permute-start | bytes 1179656 | tf_op jit(solution)/shard_map/ppermute | solution.py:358
  81.6 7.0 %collective-permute-start.19 = (bf16[1,256,384]{2,1,0:T(8,128)(2,1)S(1)}, bf16[1,256,384]{2,1,0:T(8,128)(2,1)S(1)}, u32[]{:S(2)}, u32[]{:S(2)}) collective-permute-start(bf16[1,256,384]{2,1,0:T(8,128)(2,1)S(1)} %slice.19), channel_id=1, source_target_pairs={{0,2},{1,3},{2,0},{3,1},{4,6},{5,7},{6,4},{7,5},{8,10},{9,11},{10,... | collective-permute-start | bytes 589832 | tf_op jit(solution)/shard_map/ppermute | solution.py:358
  88.7 10.8 %collective-permute-start.20 = (bf16[256,384]{1,0:T(8,128)(2,1)S(1)}, bf16[256,384]{1,0:T(8,128)(2,1)S(1)}, u32[]{:S(2)}, u32[]{:S(2)}) collective-permute-start(bf16[256,384]{1,0:T(8,128)(2,1)S(1)} %fusion.1), channel_id=1, source_target_pairs={{0,16},{4,20},{8,24},{12,28},{16,0},{20,4},{24,8},{28,12},{1,17},{... | collective-permute-start | bytes 589832 | tf_op jit(solution)/shard_map/ppermute | solution.py:358
  99.5 7.0 %collective-permute-start.21 = (bf16[256,384]{1,0:T(8,128)(2,1)S(1)}, bf16[256,384]{1,0:T(8,128)(2,1)S(1)}, u32[]{:S(2)}, u32[]{:S(2)}) collective-permute-start(bf16[256,384]{1,0:T(8,128)(2,1)S(1)} %add_convert_fusion.refs_0_), channel_id=1, source_target_pairs={{0,4},{4,0},{8,12},{12,8},{16,20},{20,16},{24,28},{28,24},{1,5},{5... | collective-permute-start | bytes 589832 | tf_op jit(solution)/shard_map/ppermute | solution.py:358
  100.1 7.8 %collective-permute-start.22 = (bf16[256,384]{1,0:T(8,128)(2,1)S(1)}, bf16[256,384]{1,0:T(8,128)(2,1)S(1)}, u32[]{:S(2)}, u32[]{:S(2)}) collective-permute-start(bf16[256,384]{1,0:T(8,128)(2,1)S(1)} %add_convert_fusion.refs_0_), channel_id=1, source_target_pairs={{0,8},{4,12},{8,0},{12,4},{16,24},{20,28},{24,16},{28,20},{1,9},{5... | collective-permute-start | bytes 589832 | tf_op jit(solution)/shard_map/ppermute | solution.py:358
  100.1 11.7 %collective-permute-start.23 = (bf16[256,384]{1,0:T(8,128)(2,1)S(1)}, bf16[256,384]{1,0:T(8,128)(2,1)S(1)}, u32[]{:S(2)}, u32[]{:S(2)}) collective-permute-start(bf16[256,384]{1,0:T(8,128)(2,1)S(1)} %add_convert_fusion.refs_0_), channel_id=1, source_target_pairs={{0,12},{4,8},{8,4},{12,0},{16,28},{20,24},{24,20},{28,16},{1,13},{... | collective-permute-start | bytes 589832 | tf_op jit(solution)/shard_map/ppermute | solution.py:358

commit v5 on v4

--- a/solution.py
+++ b/solution.py
@@ -331,22 +331,24 @@
 
 
 def finish_kernel(group, piece, ids_ref, *refs):
-    out_ref = refs[group]
-    for k in range(group):
-        for half in range(refs[k].shape[0] // piece):
-            start = pl.multiple_of((half * group + ids_ref[k]) * piece, piece)
-            out_ref[pl.ds(start, piece), :] = refs[k][half * piece : (half + 1) * piece, :].astype(F32)
-
-
-def finish(ids, blocks, piece):
-    group = len(blocks)
+    out_ref = refs[len(refs) - 1]
+    for number, block in enumerate(refs[: len(refs) - 1]):
+        count = block.shape[0] // piece
+        for i in range(count):
+            place = (number // group * count + i) * group + ids_ref[number % group]
+            start = pl.multiple_of(place * piece, piece)
+            out_ref[pl.ds(start, piece), :] = block[i * piece : (i + 1) * piece, :].astype(F32)
+
+
+def finish(ids, blocks, group, piece):
     rows, width = blocks[0].shape
     if piece % 16:
-        order = jnp.take(jnp.stack(blocks), ids, axis=0).reshape(group, rows // piece, piece, width)
-        return order.swapaxes(0, 1).reshape(group * rows, width).astype(F32)
+        order = jnp.stack(blocks).reshape(-1, group, rows // piece, piece, width)
+        order = jnp.take(order, ids, axis=1).swapaxes(1, 2)
+        return order.reshape(len(blocks) * rows, width).astype(F32)
     return pallas(
         functools.partial(finish_kernel, group, piece),
-        shape((group * rows, width), F32),
+        shape((len(blocks) * rows, width), F32),
         [ids],
         blocks,
         "finish",
@@ -418,24 +420,30 @@
     moved[3] = swap(after((late, 0), vs[1:])[0], "ctx", ctx_size, 3)
     block = c.reshape(1).astype(jnp.int32)
     grad_near, grad_own = attend(block, page_tokens, [qks, vs, grads], ctx_size, group)
-    grad_inputs = hidden_grad(fsdp_ids, grad_own, weights, depth)
-
     kept, away = weight_grad(group_ids, fsdp_ids, grad_near, hidden, [moved[k] for k in (1, 2, 3)], piece)
     bit = 1
-    while bit < fsdp_size:
+    while bit < top:
         total = kept + swap(away, "fsdp", fsdp_size, bit).astype(F32)
         bit *= 2
-        if bit < fsdp_size:
-            kept, away = total[0::2], total[1::2].astype(BF16)
-    total = total[0]
+        kept, away = total[0::2], total[1::2].astype(BF16)
+    half = kept.shape[1] // 2
+    first = swap(away[0, :half], "fsdp", fsdp_size, top)
+    second, first = lax.optimization_barrier((away[0, half:], first))
+    second = swap(second, "fsdp", fsdp_size, top)
+    totals = [kept[0, :half] + first.astype(F32)]
+    rest, total = lax.optimization_barrier((kept[0, half:], totals[0].astype(BF16)))
+    grad_own, total = lax.optimization_barrier((grad_own, total))
+    grad_inputs = hidden_grad(fsdp_ids, grad_own, weights, depth)
+    second, grad_inputs = lax.optimization_barrier((second, grad_inputs))
+    totals = [total, rest + second.astype(F32)]
     bit = group
     while bit < ctx_size:
-        half = total.astype(BF16)
-        total = half.astype(F32) + swap(half, "ctx", ctx_size, bit).astype(F32)
+        sent = [total.astype(BF16) for total in totals]
+        totals = [own.astype(F32) + swap(own, "ctx", ctx_size, bit).astype(F32) for own in sent]
         bit *= 2
-    total, grad_inputs = lax.optimization_barrier((total.astype(BF16), grad_inputs))
-    gathered = [swap(total, "ctx", ctx_size, k) if k else total for k in range(group)]
-    grad_weights = finish(group_ids, gathered, depth // (fsdp_size * ctx_size))
+    totals = [total.astype(BF16) for total in totals]
+    gathered = [swap(total, "ctx", ctx_size, k) if k else total for total in totals for k in range(group)]
+    grad_weights = finish(group_ids, gathered, group, piece)
     return grad_inputs[None], grad_weights
 
 

time: 113 us -> 109 us (0.965)
  waiting for transfers between devices: 50.5 us -> 37.5 us
  starting transfers between devices: 29.4 us -> 38.4 us
    ppermute x24 -> x29, waiting for transfers between devices: 50.5 us -> 37.5 us  [swap(): return lax.ppermute(array, axis, [(i, i ^ distance) for i in range(size)])]
    ppermute x24 -> x29, starting transfers between devices: 29.4 us -> 38.4 us  [swap(): return lax.ppermute(array, axis, [(i, i ^ distance) for i in range(size)])]
  transfers between devices with their start and end apart: 24 -> 29, of which waited for: 16 -> 16; matrix products, arithmetic and copies ran while one was open for 1% -> 1% of each run, Pallas kernels for 21% -> 22%
where the time goes in v5:
time: 109 us; the launch traced here: 110 us
  starting transfers between devices  38.4 us (35%)
  waiting for transfers between devices  37.5 us (34%)
  Pallas kernels  28.2 us (26%)
  local copies, waits for them, and re-layouts  3.52 us (3%)
  other arithmetic  1.15 us (1%)
    ppermute x29, starting transfers between devices, swap(): return lax.ppermute(array, axis, [(i, i ^ distance) for i in range(size)])  38.4 us
    ppermute x29, waiting for transfers between devices, swap(): return lax.ppermute(array, axis, [(i, i ^ distance) for i in range(size)])  37.5 us
    pallas_call x4, Pallas kernels, pallas(): pl.pallas_call(kernel, out_shape=out_shape, in_specs=[SMEM] * len(scalars...  22.7 us
    unnamed x21, local copies, waits for them, and re-layouts  3.47 us
    pallas_call x2, Pallas kernels, cut(): pl.pallas_call(functools.partial(cut_kernel, members, group, piece), out_...  2.85 us
    pallas_call x1, Pallas kernels, weight_grad(): pl.pallas_call(functools.partial(weight_kernel, group, piece), out_shape=...  2.65 us
  transfers between devices with their start and end apart: 29, of which 16 were waited for; matrix products, arithmetic and copies ran while one was open for 1% of the time, Pallas kernels for 22%

profile of v5, /device:TPU:0, one launch (start us, length us, event | category | flops | bytes accessed | tf_op | source)
XLA Modules:
  0.0 109.6 jit_solution(15173003144120551185)
XLA Ops:
  0.6 3.0 %collective-permute-start.1 = (bf16[1024,384]{1,0:T(8,128)(2,1)}, bf16[1024,384]{1,0:T(8,128)(2,1)S(1)}, u32[]{:S(2)}, u32[]{:S(2)}) collective-permute-start(bf16[1024,384]{1,0:T(8,128)(2,1)} %refs_0_.3), channel_id=1, source_target_pairs={{0,2},{1,3},{2,0},{3,1},{4,6},{5,7},{6,4},{7,5},{8,10},{9,11},{10,... | collective-permute-start | bytes 2359304 | tf_op jit(solution)/shard_map/ppermute | solution.py:360
  3.6 1.6 %collective-permute-start.2 = (bf16[256,128]{1,0:T(8,128)(2,1)}, bf16[256,128]{1,0:T(8,128)(2,1)S(1)}, u32[]{:S(2)}, u32[]{:S(2)}) collective-permute-start(bf16[256,128]{1,0:T(8,128)(2,1)} %bitcast.20), channel_id=1, source_target_pairs={{0,8},{4,12},{8,0},{12,4},{16,24},{20,28},{24,16},{28,20},{1,9},{5... | collective-permute-start | bytes 196616 | tf_op jit(solution)/shard_map/ppermute | solution.py:360
  5.2 2.6 %collective-permute-start.3 = (bf16[256,128]{1,0:T(8,128)(2,1)}, bf16[256,128]{1,0:T(8,128)(2,1)S(1)}, u32[]{:S(2)}, u32[]{:S(2)}) collective-permute-start(bf16[256,128]{1,0:T(8,128)(2,1)} %bitcast.21), channel_id=1, source_target_pairs={{0,16},{4,20},{8,24},{12,28},{16,0},{20,4},{24,8},{28,12},{1,17},{... | collective-permute-start | bytes 196616 | tf_op jit(solution)/shard_map/ppermute | solution.py:360
  7.8 0.2 collective-permute-start.4
  8.0 1.6 %copy-done = bf16[1,256,4096]{2,1,0:T(8,128)(2,1)S(1)} copy-done((bf16[1,256,4096]{2,1,0:T(8,128)(2,1)S(1)}, bf16[1,256,4096]{2,1,0:T(8,128)(2,1)}, u32[]{:S(2)}) %copy-start) | copy-done | bytes 2097176
  9.6 2.0 %cut.2 = (bf16[256,1024]{1,0:T(8,128)(2,1)}, bf16[256,1024]{1,0:T(8,128)(2,1)}) custom-call(s32[4]{0:T(128)S(1)} %iota_xor_fusion.1.ids_ref, bf16[256,4096]{1,0:T(8,128)(2,1)S(1)} %bitcast.16), custom_call_target="tpu_custom_call" | custom-call | bytes 2097152 | tf_op jit(solution)/shard_map/cut/pallas_call | solution.py:81
  11.7 0.0 collective-permute-done.2.refs_10_
  11.7 0.7 collective-permute-done.3.refs_11_
  12.4 1.7 %collective-permute-done.4.refs_12_ = bf16[256,128]{1,0:T(8,128)(2,1)S(1)} collective-permute-done((bf16[256,128]{1,0:T(8,128)(2,1)}, bf16[256,128]{1,0:T(8,128)(2,1)S(1)}, u32[]{:S(2)}, u32[]{:S(2)}) %collective-permute-start.4) | collective-permute-done | bytes 65568 | tf_op jit(solution)/shard_map/ppermute | solution.py:360
  14.1 0.9 pad_maximum_fusion.1
  15.0 1.6 %collective-permute-start.5 = (bf16[1024,128]{1,0:T(8,128)(2,1)S(1)}, bf16[1024,128]{1,0:T(8,128)(2,1)S(1)}, u32[]{:S(2)}, u32[]{:S(2)}) collective-permute-start(bf16[1024,128]{1,0:T(8,128)(2,1)S(1)} %pad_maximum_fusion.1), channel_id=1, source_target_pairs={{0,4},{4,0},{8,12},{12,8},{16,20},{20,16},{24,28},{28,24},{1,5},{5... | collective-permute-start | bytes 786440 | tf_op jit(solution)/shard_map/ppermute | solution.py:360
  16.5 0.0 collective-permute-start
  16.5 4.8 %collective-permute-done.5.refs_13_ = bf16[1024,128]{1,0:T(8,128)(2,1)S(1)} collective-permute-done((bf16[1024,128]{1,0:T(8,128)(2,1)S(1)}, bf16[1024,128]{1,0:T(8,128)(2,1)S(1)}, u32[]{:S(2)}, u32[]{:S(2)}) %collective-permute-start.5) | collective-permute-done | bytes 262176 | tf_op jit(solution)/shard_map/ppermute | solution.py:360
  21.4 0.7 copy-done.7
  22.1 0.0 collective-permute-done.1.refs_2_
  22.1 1.6 %collective-permute-start.10 = (bf16[256,1024]{1,0:T(8,128)(2,1)}, bf16[256,1024]{1,0:T(8,128)(2,1)S(1)}, u32[]{:S(2)}, u32[]{:S(2)}) collective-permute-start(bf16[256,1024]{1,0:T(8,128)(2,1)} %get-tuple-element.29), channel_id=1, source_target_pairs={{0,4},{4,0},{8,12},{12,8},{16,20},{20,16},{24,28},{28,24},{1,5},{5... | collective-permute-start | bytes 1572872 | tf_op jit(solution)/shard_map/ppermute | solution.py:360
  23.7 1.0 collective-permute-start.12
  24.7 0.0 collective-permute-done.refs_1_
  24.8 0.0 copy-start.2
  24.8 1.1 %copy-done.2 = bf16[1024,384]{1,0:T(8,128)(2,1)S(1)} copy-done((bf16[1024,384]{1,0:T(8,128)(2,1)S(1)}, bf16[1024,384]{1,0:T(8,128)(2,1)}, u32[]{:S(2)}) %copy-start.2) | copy-done | bytes 786456
  25.9 3.3 %project.1 = (bf16[256,256]{1,0:T(8,128)(2,1)S(1)}, bf16[256,128]{1,0:T(8,128)(2,1)S(1)}) custom-call(s32[4]{0:T(128)S(1)} %iota_xor_fusion.ids_ref.fsdp_ref, bf16[1024,384]{1,0:T(8,128)(2,1)S(1)} %copy-done.2, bf16[1024,384]{1,0:T(8,128)(2,1)} %collective-permute-done.refs_1_, bf16[1024,384]{1,0:T(8,128)(2,1)S(1)} %collective-permute-done.1.refs_2_, ...), custom_call_target="tpu_custom_call" | custom-call | flops 805306368 | bytes 5439488 | tf_op jit(solution)/shard_map/project/pallas_call | solution.py:35
  29.2 0.0 copy-start.4
  29.2 0.0 copy-start.9
  29.2 1.1 collective-permute-start.7
  30.3 2.5 %collective-permute-start.8 = (bf16[256,256]{1,0:T(8,128)(2,1)S(1)}, bf16[256,256]{1,0:T(8,128)(2,1)S(1)}, u32[]{:S(2)}, u32[]{:S(2)}) collective-permute-start(bf16[256,256]{1,0:T(8,128)(2,1)S(1)} %get-tuple-element.39.refs_0_), channel_id=1, source_target_pairs={{0,16},{4,20},{8,24},{12,28},{16,0},{20,4},{24,8},{28,12},{1,17},{... | collective-permute-start | bytes 393224 | tf_op jit(solution)/shard_map/ppermute | solution.py:360
  32.8 0.9 collective-permute-start.9
  33.7 3.0 %collective-permute-done.10.refs_0_ = bf16[256,1024]{1,0:T(8,128)(2,1)S(1)} collective-permute-done((bf16[256,1024]{1,0:T(8,128)(2,1)}, bf16[256,1024]{1,0:T(8,128)(2,1)S(1)}, u32[]{:S(2)}, u32[]{:S(2)}) %collective-permute-start.10) | collective-permute-done | bytes 524320 | tf_op jit(solution)/shard_map/ppermute | solution.py:360
  36.7 1.5 %collective-permute-start.11 = (bf16[256,128]{1,0:T(8,128)(2,1)S(1)}, bf16[256,128]{1,0:T(8,128)(2,1)S(1)}, u32[]{:S(2)}, u32[]{:S(2)}) collective-permute-start(bf16[256,128]{1,0:T(8,128)(2,1)S(1)} %get-tuple-element.38), channel_id=1, source_target_pairs={{0,4},{4,0},{8,12},{12,8},{16,20},{20,16},{24,28},{28,24},{1,5},{5... | collective-permute-start | bytes 196616 | tf_op jit(solution)/shard_map/ppermute | solution.py:360
  38.2 2.7 %collective-permute-done.11 = bf16[256,128]{1,0:T(8,128)(2,1)S(1)} collective-permute-done((bf16[256,128]{1,0:T(8,128)(2,1)S(1)}, bf16[256,128]{1,0:T(8,128)(2,1)S(1)}, u32[]{:S(2)}, u32[]{:S(2)}) %collective-permute-start.11) | collective-permute-done | bytes 65568 | tf_op jit(solution)/shard_map/ppermute | solution.py:360
  40.9 0.7 collective-permute-done.12.refs_1_
  41.6 1.9 %collective-permute-done.7.refs_1_ = bf16[256,256]{1,0:T(8,128)(2,1)S(1)} collective-permute-done((bf16[256,256]{1,0:T(8,128)(2,1)S(1)}, bf16[256,256]{1,0:T(8,128)(2,1)S(1)}, u32[]{:S(2)}, u32[]{:S(2)}) %collective-permute-start.7) | collective-permute-done | bytes 131104 | tf_op jit(solution)/shard_map/ppermute | solution.py:360
  43.5 4.4 %collective-permute-done.9.refs_3_ = bf16[256,256]{1,0:T(8,128)(2,1)S(1)} collective-permute-done((bf16[256,256]{1,0:T(8,128)(2,1)S(1)}, bf16[256,256]{1,0:T(8,128)(2,1)S(1)}, u32[]{:S(2)}, u32[]{:S(2)}) %collective-permute-start.9) | collective-permute-done | bytes 131104 | tf_op jit(solution)/shard_map/ppermute | solution.py:360
  47.9 0.6 collective-permute-start.13
  48.5 0.0 collective-permute-start.14
  48.5 2.1 %collective-permute-start.15 = (bf16[512,128]{1,0:T(8,128)(2,1)S(1)}, bf16[512,128]{1,0:T(8,128)(2,1)S(1)}, u32[]{:S(2)}, u32[]{:S(2)}) collective-permute-start(bf16[512,128]{1,0:T(8,128)(2,1)S(1)} %constant_dynamic-update-slice_fusion.refs_5_), channel_id=1, source_target_pairs={{0,16},{4,20},{8,24},{12,28},{16,0},{20,4},{24,8},{28,12},{1,17},{... | collective-permute-start | bytes 393224 | tf_op jit(solution)/shard_map/ppermute | solution.py:360
  50.6 2.2 %collective-permute-start.16 = (bf16[512,128]{1,0:T(8,128)(2,1)S(1)}, bf16[512,128]{1,0:T(8,128)(2,1)S(1)}, u32[]{:S(2)}, u32[]{:S(2)}) collective-permute-start(bf16[512,128]{1,0:T(8,128)(2,1)S(1)} %constant_dynamic-update-slice_fusion.refs_5_), channel_id=1, source_target_pairs={{0,24},{4,28},{8,16},{12,20},{16,8},{20,12},{24,0},{28,4},{1,25},{... | collective-permute-start | bytes 393224 | tf_op jit(solution)/shard_map/ppermute | solution.py:360
  52.9 0.8 cut.3
  53.7 1.1 collective-permute-done.14.refs_6_
  54.8 6.2 %collective-permute-done.15.refs_7_ = bf16[512,128]{1,0:T(8,128)(2,1)S(1)} collective-permute-done((bf16[512,128]{1,0:T(8,128)(2,1)S(1)}, bf16[512,128]{1,0:T(8,128)(2,1)S(1)}, u32[]{:S(2)}, u32[]{:S(2)}) %collective-permute-start.15) | collective-permute-done | bytes 131104 | tf_op jit(solution)/shard_map/ppermute | solution.py:360
  60.9 0.0 collective-permute-done.16.refs_8_
  60.9 2.9 %collective-permute-start.17 = (bf16[256,1024]{1,0:T(8,128)(2,1)S(1)}, bf16[256,1024]{1,0:T(8,128)(2,1)S(1)}, u32[]{:S(2)}, u32[]{:S(2)}) collective-permute-start(bf16[256,1024]{1,0:T(8,128)(2,1)S(1)} %cut.3), channel_id=1, source_target_pairs={{0,12},{4,8},{8,4},{12,0},{16,28},{20,24},{24,20},{28,16},{1,13},{... | collective-permute-start | bytes 1572872 | tf_op jit(solution)/shard_map/ppermute | solution.py:360
  63.9 13.1 %attend.1 = (bf16[1024,384]{1,0:T(8,128)(2,1)S(1)}, bf16[256,384]{1,0:T(8,128)(2,1)S(1)}) custom-call(s32[1]{0:T(128)} %bitcast.block_ref, s32[1,8]{1,0:T(1,128)S(1)} %copy-done.9, bf16[256,256]{1,0:T(8,128)(2,1)S(1)} %get-tuple-element.39.refs_0_, bf16[256,256]{1,0:T(8,128)(2,1)S(1)} %collective-permute-done.7.refs_1_, ...), custom_call_target="tpu_custom_call" | custom-call | flops 5368709120 | bytes 3080192 | tf_op jit(solution)/shard_map/attend/pallas_call | solution.py:35
  77.0 2.7 %weight_grad.1 = (f32[2,256,384]{2,1,0:T(8,128)S(1)}, bf16[2,256,384]{2,1,0:T(8,128)(2,1)S(1)}) custom-call(s32[4]{0:T(128)S(1)} %iota_xor_fusion.1.ids_ref, s32[4]{0:T(128)S(1)} %iota_xor_fusion.ids_ref.fsdp_ref, bf16[1024,384]{1,0:T(8,128)(2,1)S(1)} %get-tuple-element.42.grad_ref, bf16[256,4096]{1,0:T(8,128)(2,1)S(1)} %bitcast.19, ...), custom_call_target="tpu_custom_call" | custom-call | flops 805306368 | bytes 8388608 | tf_op jit(solution)/shard_map/weight_grad/pallas_call | solution.py:321
  79.7 0.0 copy-start.3
  79.7 0.1 collective-permute-start.18
  79.8 1.7 %collective-permute-done.18 = bf16[2,256,384]{2,1,0:T(8,128)(2,1)S(1)} collective-permute-done((bf16[2,256,384]{2,1,0:T(8,128)(2,1)S(1)}, bf16[2,256,384]{2,1,0:T(8,128)(2,1)S(1)}, u32[]{:S(2)}, u32[]{:S(2)}) %collective-permute-start.18) | collective-permute-done | bytes 393248 | tf_op jit(solution)/shard_map/ppermute | solution.py:360
  81.5 0.1 fusion.2
  81.6 1.6 %collective-permute-start.19 = (bf16[128,384]{1,0:T(8,128)(2,1)S(1)}, bf16[128,384]{1,0:T(8,128)(2,1)S(1)}, u32[]{:S(2)}, u32[]{:S(2)}) collective-permute-start(bf16[128,384]{1,0:T(8,128)(2,1)S(1)} %get-tuple-element.58), channel_id=1, source_target_pairs={{0,2},{1,3},{2,0},{3,1},{4,6},{5,7},{6,4},{7,5},{8,10},{9,11},{10,... | collective-permute-start | bytes 294920 | tf_op jit(solution)/shard_map/ppermute | solution.py:360
  83.3 3.3 %collective-permute-done.19 = bf16[128,384]{1,0:T(8,128)(2,1)S(1)} collective-permute-done((bf16[128,384]{1,0:T(8,128)(2,1)S(1)}, bf16[128,384]{1,0:T(8,128)(2,1)S(1)}, u32[]{:S(2)}, u32[]{:S(2)}) %collective-permute-start.19) | collective-permute-done | bytes 98336 | tf_op jit(solution)/shard_map/ppermute | solution.py:360
  86.5 1.5 %collective-permute-start.20 = (bf16[128,384]{1,0:T(8,128)(2,1)S(1)}, bf16[128,384]{1,0:T(8,128)(2,1)S(1)}, u32[]{:S(2)}, u32[]{:S(2)}) collective-permute-start(bf16[128,384]{1,0:T(8,128)(2,1)S(1)} %get-tuple-element.47), channel_id=1, source_target_pairs={{0,2},{1,3},{2,0},{3,1},{4,6},{5,7},{6,4},{7,5},{8,10},{9,11},{10,... | collective-permute-start | bytes 294920 | tf_op jit(solution)/shard_map/ppermute | solution.py:360
  88.1 0.1 collective-permute-start.21
  88.2 4.5 %hidden_grad.1 = bf16[256,4096]{1,0:T(8,128)(2,1)} custom-call(s32[4]{0:T(128)S(1)} %iota_xor_fusion.ids_ref.fsdp_ref, bf16[256,384]{1,0:T(8,128)(2,1)S(1)} %get-tuple-element.51.grad_ref, bf16[1024,384]{1,0:T(8,128)(2,1)S(1)} %copy-done.3, bf16[1024,384]{1,0:T(8,128)(2,1)} %collective-permute-done.refs_1_, ...), custom_call_target="tpu_custom_call" | custom-call | flops 805306368 | bytes 5439488 | tf_op jit(solution)/shard_map/hidden_grad/pallas_call | solution.py:35
  92.8 2.9 %collective-permute-start.25 = (bf16[128,384]{1,0:T(8,128)(2,1)S(1)}, bf16[128,384]{1,0:T(8,128)(2,1)S(1)}, u32[]{:S(2)}, u32[]{:S(2)}) collective-permute-start(bf16[128,384]{1,0:T(8,128)(2,1)S(1)} %add_convert_fusion.1), channel_id=1, source_target_pairs={{0,16},{4,20},{8,24},{12,28},{16,0},{20,4},{24,8},{28,12},{1,17},{... | collective-permute-start | bytes 294920 | tf_op jit(solution)/shard_map/ppermute | solution.py:360
  95.7 0.6 collective-permute-start.22
  96.3 0.1 collective-permute-start.23
  96.4 2.9 %collective-permute-start.24 = (bf16[128,384]{1,0:T(8,128)(2,1)S(1)}, bf16[128,384]{1,0:T(8,128)(2,1)S(1)}, u32[]{:S(2)}, u32[]{:S(2)}) collective-permute-start(bf16[128,384]{1,0:T(8,128)(2,1)S(1)} %add_convert_fusion.2.refs_0_), channel_id=1, source_target_pairs={{0,12},{4,8},{8,4},{12,0},{16,28},{20,24},{24,20},{28,16},{1,13},{... | collective-permute-start | bytes 294920 | tf_op jit(solution)/shard_map/ppermute | solution.py:360
  99.3 0.6 collective-permute-start.26
  99.9 1.9 %collective-permute-start.27 = (bf16[128,384]{1,0:T(8,128)(2,1)S(1)}, bf16[128,384]{1,0:T(8,128)(2,1)S(1)}, u32[]{:S(2)}, u32[]{:S(2)}) collective-permute-start(bf16[128,384]{1,0:T(8,128)(2,1)S(1)} %add_convert_fusion.refs_4_), channel_id=1, source_target_pairs={{0,8},{4,12},{8,0},{12,4},{16,24},{20,28},{24,16},{28,20},{1,9},{5... | collective-permute-start | bytes 294920 | tf_op jit(solution)/shard_map/ppermute | solution.py:360
  101.8 0.4 collective-permute-done.22.refs_1_
  102.3 0.6 collective-permute-start.28
  102.9 2.2 %collective-permute-done.24.refs_3_ = bf16[128,384]{1,0:T(8,128)(2,1)S(1)} collective-permute-done((bf16[128,384]{1,0:T(8,128)(2,1)S(1)}, bf16[128,384]{1,0:T(8,128)(2,1)S(1)}, u32[]{:S(2)}, u32[]{:S(2)}) %collective-permute-start.24) | collective-permute-done | bytes 98336 | tf_op jit(solution)/shard_map/ppermute | solution.py:360
  105.1 0.9 collective-permute-done.26.refs_5_
  106.1 1.7 %collective-permute-done.28.refs_7_ = bf16[128,384]{1,0:T(8,128)(2,1)S(1)} collective-permute-done((bf16[128,384]{1,0:T(8,128)(2,1)S(1)}, bf16[128,384]{1,0:T(8,128)(2,1)S(1)}, u32[]{:S(2)}, u32[]{:S(2)}) %collective-permute-start.28) | collective-permute-done | bytes 98336 | tf_op jit(solution)/shard_map/ppermute | solution.py:360
  107.8 1.8 %finish.1 = f32[1024,384]{1,0:T(8,128)} custom-call(s32[4]{0:T(128)S(1)} %iota_xor_fusion.1.ids_ref, bf16[128,384]{1,0:T(8,128)(2,1)S(1)} %add_convert_fusion.2.refs_0_, bf16[128,384]{1,0:T(8,128)(2,1)S(1)} %collective-permute-done.22.refs_1_, bf16[128,384]{1,0:T(8,128)(2,1)S(1)} %collective-permute-done.23.refs_2_, ...), custom_call_target="tpu_custom_call" | custom-call | bytes 2359296 | tf_op jit(solution)/shard_map/finish/pallas_call | solution.py:35
  (34 shorter events, 0.3 us)
Async XLA Ops:
  0.6 21.5 %collective-permute-start.1 = (bf16[1024,384]{1,0:T(8,128)(2,1)}, bf16[1024,384]{1,0:T(8,128)(2,1)S(1)}, u32[]{:S(2)}, u32[]{:S(2)}) collective-permute-start(bf16[1024,384]{1,0:T(8,128)(2,1)} %refs_0_.3), channel_id=1, source_target_pairs={{0,2},{1,3},{2,0},{3,1},{4,6},{5,7},{6,4},{7,5},{8,10},{9,11},{10,... | collective-permute-start | bytes 2359304 | tf_op jit(solution)/shard_map/ppermute | solution.py:360
  3.6 8.0 %collective-permute-start.2 = (bf16[256,128]{1,0:T(8,128)(2,1)}, bf16[256,128]{1,0:T(8,128)(2,1)S(1)}, u32[]{:S(2)}, u32[]{:S(2)}) collective-permute-start(bf16[256,128]{1,0:T(8,128)(2,1)} %bitcast.20), channel_id=1, source_target_pairs={{0,8},{4,12},{8,0},{12,4},{16,24},{20,28},{24,16},{28,20},{1,9},{5... | collective-permute-start | bytes 196616 | tf_op jit(solution)/shard_map/ppermute | solution.py:360
  5.2 7.2 %collective-permute-start.3 = (bf16[256,128]{1,0:T(8,128)(2,1)}, bf16[256,128]{1,0:T(8,128)(2,1)S(1)}, u32[]{:S(2)}, u32[]{:S(2)}) collective-permute-start(bf16[256,128]{1,0:T(8,128)(2,1)} %bitcast.21), channel_id=1, source_target_pairs={{0,16},{4,20},{8,24},{12,28},{16,0},{20,4},{24,8},{28,12},{1,17},{... | collective-permute-start | bytes 196616 | tf_op jit(solution)/shard_map/ppermute | solution.py:360
  7.8 6.3 %collective-permute-start.4 = (bf16[256,128]{1,0:T(8,128)(2,1)}, bf16[256,128]{1,0:T(8,128)(2,1)S(1)}, u32[]{:S(2)}, u32[]{:S(2)}) collective-permute-start(bf16[256,128]{1,0:T(8,128)(2,1)} %bitcast.22), channel_id=1, source_target_pairs={{0,24},{4,28},{8,16},{12,20},{16,8},{20,12},{24,0},{28,4},{1,25},{... | collective-permute-start | bytes 196616 | tf_op jit(solution)/shard_map/ppermute | solution.py:360
  8.0 1.6 %copy-start = (bf16[1,256,4096]{2,1,0:T(8,128)(2,1)S(1)}, bf16[1,256,4096]{2,1,0:T(8,128)(2,1)}, u32[]{:S(2)}) copy-start(bf16[1,256,4096]{2,1,0:T(8,128)(2,1)} %param.4) | copy-start | bytes 6291460
  9.6 15.1 %copy-start.1 = (bf16[1,256,4096]{2,1,0:T(8,128)(2,1)S(1)}, bf16[1,256,4096]{2,1,0:T(8,128)(2,1)}, u32[]{:S(2)}) copy-start(bf16[1,256,4096]{2,1,0:T(8,128)(2,1)} %param.4) | copy-start | bytes 6291460
  14.1 8.0 %copy-start.5 = (bf16[256,128]{1,0:T(8,128)(2,1)}, bf16[256,128]{1,0:T(8,128)(2,1)S(1)}, u32[]{:S(2)}) copy-start(bf16[256,128]{1,0:T(8,128)(2,1)S(1)} %collective-permute-done.4.refs_12_) | copy-start | bytes 196612
  15.0 6.4 %collective-permute-start.5 = (bf16[1024,128]{1,0:T(8,128)(2,1)S(1)}, bf16[1024,128]{1,0:T(8,128)(2,1)S(1)}, u32[]{:S(2)}, u32[]{:S(2)}) collective-permute-start(bf16[1024,128]{1,0:T(8,128)(2,1)S(1)} %pad_maximum_fusion.1), channel_id=1, source_target_pairs={{0,4},{4,0},{8,12},{12,8},{16,20},{20,16},{24,28},{28,24},{1,5},{5... | collective-permute-start | bytes 786440 | tf_op jit(solution)/shard_map/ppermute | solution.py:360
  16.5 8.2 %collective-permute-start = (bf16[1024,384]{1,0:T(8,128)(2,1)}, bf16[1024,384]{1,0:T(8,128)(2,1)}, u32[]{:S(2)}, u32[]{:S(2)}) collective-permute-start(bf16[1024,384]{1,0:T(8,128)(2,1)} %refs_0_.3), channel_id=1, source_target_pairs={{0,1},{1,0},{2,3},{3,2},{4,5},{5,4},{6,7},{7,6},{8,9},{9,8},{10,11... | collective-permute-start | bytes 2359304 | tf_op jit(solution)/shard_map/ppermute | solution.py:360
  21.4 0.7 copy-start.7
  22.1 2.6 %collective-permute-start.6 = (bf16[1024,384]{1,0:T(8,128)(2,1)S(1)}, bf16[1024,384]{1,0:T(8,128)(2,1)}, u32[]{:S(2)}, u32[]{:S(2)}) collective-permute-start(bf16[1024,384]{1,0:T(8,128)(2,1)S(1)} %collective-permute-done.1.refs_2_), channel_id=1, source_target_pairs={{0,1},{1,0},{2,3},{3,2},{4,5},{5,4},{6,7},{7,6},{8,9},{9,8},{10,11... | collective-permute-start | bytes 2359304 | tf_op jit(solution)/shard_map/ppermute | solution.py:360
  22.1 14.5 %collective-permute-start.10 = (bf16[256,1024]{1,0:T(8,128)(2,1)}, bf16[256,1024]{1,0:T(8,128)(2,1)S(1)}, u32[]{:S(2)}, u32[]{:S(2)}) collective-permute-start(bf16[256,1024]{1,0:T(8,128)(2,1)} %get-tuple-element.29), channel_id=1, source_target_pairs={{0,4},{4,0},{8,12},{12,8},{16,20},{20,16},{24,28},{28,24},{1,5},{5... | collective-permute-start | bytes 1572872 | tf_op jit(solution)/shard_map/ppermute | solution.py:360
  23.7 17.9 %collective-permute-start.12 = (bf16[256,1024]{1,0:T(8,128)(2,1)}, bf16[256,1024]{1,0:T(8,128)(2,1)}, u32[]{:S(2)}, u32[]{:S(2)}) collective-permute-start(bf16[256,1024]{1,0:T(8,128)(2,1)} %get-tuple-element.30), channel_id=1, source_target_pairs={{0,8},{4,12},{8,0},{12,4},{16,24},{20,28},{24,16},{28,20},{1,9},{5... | collective-permute-start | bytes 1572872 | tf_op jit(solution)/shard_map/ppermute | solution.py:360
  24.8 1.1 %copy-start.2 = (bf16[1024,384]{1,0:T(8,128)(2,1)S(1)}, bf16[1024,384]{1,0:T(8,128)(2,1)}, u32[]{:S(2)}) copy-start(bf16[1024,384]{1,0:T(8,128)(2,1)} %refs_0_.3) | copy-start | bytes 2359300
  29.2 34.7 %copy-start.4 = (bf16[1,256,128]{2,1,0:T(8,128)(2,1)S(1)}, bf16[1,256,128]{2,1,0:T(8,128)(2,1)}, u32[]{:S(2)}) copy-start(bf16[1,256,128]{2,1,0:T(8,128)(2,1)} %param.6) | copy-start | bytes 196612
  29.2 34.7 %copy-start.6 = (bf16[256,128]{1,0:T(8,128)(2,1)S(1)}, bf16[256,128]{1,0:T(8,128)(2,1)}, u32[]{:S(2)}) copy-start(bf16[256,128]{1,0:T(8,128)(2,1)} %copy-done.5) | copy-start | bytes 196612
  29.2 34.7 %copy-start.8 = (bf16[1024,128]{1,0:T(8,128)(2,1)S(1)}, bf16[1024,128]{1,0:T(8,128)(2,1)}, u32[]{:S(2)}) copy-start(bf16[1024,128]{1,0:T(8,128)(2,1)} %copy-done.7) | copy-start | bytes 786436
  29.2 34.7 %copy-start.9 = (s32[1,8]{1,0:T(1,128)S(1)}, s32[1,8]{1,0:T(1,128)}, u32[]{:S(2)}) copy-start(s32[1,8]{1,0:T(1,128)} %pages_ref.1) | copy-start | bytes 100
  29.2 14.3 %collective-permute-start.7 = (bf16[256,256]{1,0:T(8,128)(2,1)S(1)}, bf16[256,256]{1,0:T(8,128)(2,1)S(1)}, u32[]{:S(2)}, u32[]{:S(2)}) collective-permute-start(bf16[256,256]{1,0:T(8,128)(2,1)S(1)} %get-tuple-element.39.refs_0_), channel_id=1, source_target_pairs={{0,8},{4,12},{8,0},{12,4},{16,24},{20,28},{24,16},{28,20},{1,9},{5... | collective-permute-start | bytes 393224 | tf_op jit(solution)/shard_map/ppermute | solution.py:360
  30.3 13.2 %collective-permute-start.8 = (bf16[256,256]{1,0:T(8,128)(2,1)S(1)}, bf16[256,256]{1,0:T(8,128)(2,1)S(1)}, u32[]{:S(2)}, u32[]{:S(2)}) collective-permute-start(bf16[256,256]{1,0:T(8,128)(2,1)S(1)} %get-tuple-element.39.refs_0_), channel_id=1, source_target_pairs={{0,16},{4,20},{8,24},{12,28},{16,0},{20,4},{24,8},{28,12},{1,17},{... | collective-permute-start | bytes 393224 | tf_op jit(solution)/shard_map/ppermute | solution.py:360
  32.8 15.1 %collective-permute-start.9 = (bf16[256,256]{1,0:T(8,128)(2,1)S(1)}, bf16[256,256]{1,0:T(8,128)(2,1)S(1)}, u32[]{:S(2)}, u32[]{:S(2)}) collective-permute-start(bf16[256,256]{1,0:T(8,128)(2,1)S(1)} %get-tuple-element.39.refs_0_), channel_id=1, source_target_pairs={{0,24},{4,28},{8,16},{12,20},{16,8},{20,12},{24,0},{28,4},{1,25},{... | collective-permute-start | bytes 393224 | tf_op jit(solution)/shard_map/ppermute | solution.py:360
  36.7 4.3 %collective-permute-start.11 = (bf16[256,128]{1,0:T(8,128)(2,1)S(1)}, bf16[256,128]{1,0:T(8,128)(2,1)S(1)}, u32[]{:S(2)}, u32[]{:S(2)}) collective-permute-start(bf16[256,128]{1,0:T(8,128)(2,1)S(1)} %get-tuple-element.38), channel_id=1, source_target_pairs={{0,4},{4,0},{8,12},{12,8},{16,20},{20,16},{24,28},{28,24},{1,5},{5... | collective-permute-start | bytes 196616 | tf_op jit(solution)/shard_map/ppermute | solution.py:360
  47.9 16.0 %collective-permute-start.13 = (bf16[1024,256]{1,0:T(8,128)(2,1)S(1)}, bf16[1024,256]{1,0:T(8,128)(2,1)S(1)}, u32[]{:S(2)}, u32[]{:S(2)}) collective-permute-start(bf16[1024,256]{1,0:T(8,128)(2,1)S(1)} %pad_maximum_fusion), channel_id=1, source_target_pairs={{0,4},{4,0},{8,12},{12,8},{16,20},{20,16},{24,28},{28,24},{1,5},{5... | collective-permute-start | bytes 1572872 | tf_op jit(solution)/shard_map/ppermute | solution.py:360
  48.5 6.3 %collective-permute-start.14 = (bf16[512,128]{1,0:T(8,128)(2,1)S(1)}, bf16[512,128]{1,0:T(8,128)(2,1)S(1)}, u32[]{:S(2)}, u32[]{:S(2)}) collective-permute-start(bf16[512,128]{1,0:T(8,128)(2,1)S(1)} %constant_dynamic-update-slice_fusion.refs_5_), channel_id=1, source_target_pairs={{0,8},{4,12},{8,0},{12,4},{16,24},{20,28},{24,16},{28,20},{1,9},{5... | collective-permute-start | bytes 393224 | tf_op jit(solution)/shard_map/ppermute | solution.py:360
  48.5 12.4 %collective-permute-start.15 = (bf16[512,128]{1,0:T(8,128)(2,1)S(1)}, bf16[512,128]{1,0:T(8,128)(2,1)S(1)}, u32[]{:S(2)}, u32[]{:S(2)}) collective-permute-start(bf16[512,128]{1,0:T(8,128)(2,1)S(1)} %constant_dynamic-update-slice_fusion.refs_5_), channel_id=1, source_target_pairs={{0,16},{4,20},{8,24},{12,28},{16,0},{20,4},{24,8},{28,12},{1,17},{... | collective-permute-start | bytes 393224 | tf_op jit(solution)/shard_map/ppermute | solution.py:360
  50.6 10.3 %collective-permute-start.16 = (bf16[512,128]{1,0:T(8,128)(2,1)S(1)}, bf16[512,128]{1,0:T(8,128)(2,1)S(1)}, u32[]{:S(2)}, u32[]{:S(2)}) collective-permute-start(bf16[512,128]{1,0:T(8,128)(2,1)S(1)} %constant_dynamic-update-slice_fusion.refs_5_), channel_id=1, source_target_pairs={{0,24},{4,28},{8,16},{12,20},{16,8},{20,12},{24,0},{28,4},{1,25},{... | collective-permute-start | bytes 393224 | tf_op jit(solution)/shard_map/ppermute | solution.py:360
  60.9 16.1 %collective-permute-start.17 = (bf16[256,1024]{1,0:T(8,128)(2,1)S(1)}, bf16[256,1024]{1,0:T(8,128)(2,1)S(1)}, u32[]{:S(2)}, u32[]{:S(2)}) collective-permute-start(bf16[256,1024]{1,0:T(8,128)(2,1)S(1)} %cut.3), channel_id=1, source_target_pairs={{0,12},{4,8},{8,4},{12,0},{16,28},{20,24},{24,20},{28,16},{1,13},{... | collective-permute-start | bytes 1572872 | tf_op jit(solution)/shard_map/ppermute | solution.py:360
  79.7 8.5 %copy-start.3 = (bf16[1024,384]{1,0:T(8,128)(2,1)S(1)}, bf16[1024,384]{1,0:T(8,128)(2,1)}, u32[]{:S(2)}) copy-start(bf16[1024,384]{1,0:T(8,128)(2,1)} %refs_0_.3) | copy-start | bytes 2359300
  79.7 1.8 %collective-permute-start.18 = (bf16[2,256,384]{2,1,0:T(8,128)(2,1)S(1)}, bf16[2,256,384]{2,1,0:T(8,128)(2,1)S(1)}, u32[]{:S(2)}, u32[]{:S(2)}) collective-permute-start(bf16[2,256,384]{2,1,0:T(8,128)(2,1)S(1)} %get-tuple-element.46), channel_id=1, source_target_pairs={{0,1},{1,0},{2,3},{3,2},{4,5},{5,4},{6,7},{7,6},{8,9},{9,8},{10,11... | collective-permute-start | bytes 1179656 | tf_op jit(solution)/shard_map/ppermute | solution.py:360
  81.6 4.9 %collective-permute-start.19 = (bf16[128,384]{1,0:T(8,128)(2,1)S(1)}, bf16[128,384]{1,0:T(8,128)(2,1)S(1)}, u32[]{:S(2)}, u32[]{:S(2)}) collective-permute-start(bf16[128,384]{1,0:T(8,128)(2,1)S(1)} %get-tuple-element.58), channel_id=1, source_target_pairs={{0,2},{1,3},{2,0},{3,1},{4,6},{5,7},{6,4},{7,5},{8,10},{9,11},{10,... | collective-permute-start | bytes 294920 | tf_op jit(solution)/shard_map/ppermute | solution.py:360
  86.5 6.2 %collective-permute-start.20 = (bf16[128,384]{1,0:T(8,128)(2,1)S(1)}, bf16[128,384]{1,0:T(8,128)(2,1)S(1)}, u32[]{:S(2)}, u32[]{:S(2)}) collective-permute-start(bf16[128,384]{1,0:T(8,128)(2,1)S(1)} %get-tuple-element.47), channel_id=1, source_target_pairs={{0,2},{1,3},{2,0},{3,1},{4,6},{5,7},{6,4},{7,5},{8,10},{9,11},{10,... | collective-permute-start | bytes 294920 | tf_op jit(solution)/shard_map/ppermute | solution.py:360
  88.1 7.6 %collective-permute-start.21 = (bf16[128,384]{1,0:T(8,128)(2,1)S(1)}, bf16[128,384]{1,0:T(8,128)(2,1)S(1)}, u32[]{:S(2)}, u32[]{:S(2)}) collective-permute-start(bf16[128,384]{1,0:T(8,128)(2,1)S(1)} %fusion.1), channel_id=1, source_target_pairs={{0,16},{4,20},{8,24},{12,28},{16,0},{20,4},{24,8},{28,12},{1,17},{... | collective-permute-start | bytes 294920 | tf_op jit(solution)/shard_map/ppermute | solution.py:360
  92.8 6.5 %collective-permute-start.25 = (bf16[128,384]{1,0:T(8,128)(2,1)S(1)}, bf16[128,384]{1,0:T(8,128)(2,1)S(1)}, u32[]{:S(2)}, u32[]{:S(2)}) collective-permute-start(bf16[128,384]{1,0:T(8,128)(2,1)S(1)} %add_convert_fusion.1), channel_id=1, source_target_pairs={{0,16},{4,20},{8,24},{12,28},{16,0},{20,4},{24,8},{28,12},{1,17},{... | collective-permute-start | bytes 294920 | tf_op jit(solution)/shard_map/ppermute | solution.py:360
  95.7 6.5 %collective-permute-start.22 = (bf16[128,384]{1,0:T(8,128)(2,1)S(1)}, bf16[128,384]{1,0:T(8,128)(2,1)S(1)}, u32[]{:S(2)}, u32[]{:S(2)}) collective-permute-start(bf16[128,384]{1,0:T(8,128)(2,1)S(1)} %add_convert_fusion.2.refs_0_), channel_id=1, source_target_pairs={{0,4},{4,0},{8,12},{12,8},{16,20},{20,16},{24,28},{28,24},{1,5},{5... | collective-permute-start | bytes 294920 | tf_op jit(solution)/shard_map/ppermute | solution.py:360
  96.3 6.6 %collective-permute-start.23 = (bf16[128,384]{1,0:T(8,128)(2,1)S(1)}, bf16[128,384]{1,0:T(8,128)(2,1)S(1)}, u32[]{:S(2)}, u32[]{:S(2)}) collective-permute-start(bf16[128,384]{1,0:T(8,128)(2,1)S(1)} %add_convert_fusion.2.refs_0_), channel_id=1, source_target_pairs={{0,8},{4,12},{8,0},{12,4},{16,24},{20,28},{24,16},{28,20},{1,9},{5... | collective-permute-start | bytes 294920 | tf_op jit(solution)/shard_map/ppermute | solution.py:360
  96.4 8.7 %collective-permute-start.24 = (bf16[128,384]{1,0:T(8,128)(2,1)S(1)}, bf16[128,384]{1,0:T(8,128)(2,1)S(1)}, u32[]{:S(2)}, u32[]{:S(2)}) collective-permute-start(bf16[128,384]{1,0:T(8,128)(2,1)S(1)} %add_convert_fusion.2.refs_0_), channel_id=1, source_target_pairs={{0,12},{4,8},{8,4},{12,0},{16,28},{20,24},{24,20},{28,16},{1,13},{... | collective-permute-start | bytes 294920 | tf_op jit(solution)/shard_map/ppermute | solution.py:360
  99.3 6.7 %collective-permute-start.26 = (bf16[128,384]{1,0:T(8,128)(2,1)S(1)}, bf16[128,384]{1,0:T(8,128)(2,1)S(1)}, u32[]{:S(2)}, u32[]{:S(2)}) collective-permute-start(bf16[128,384]{1,0:T(8,128)(2,1)S(1)} %add_convert_fusion.refs_4_), channel_id=1, source_target_pairs={{0,4},{4,0},{8,12},{12,8},{16,20},{20,16},{24,28},{28,24},{1,5},{5... | collective-permute-start | bytes 294920 | tf_op jit(solution)/shard_map/ppermute | solution.py:360
  99.9 6.2 %collective-permute-start.27 = (bf16[128,384]{1,0:T(8,128)(2,1)S(1)}, bf16[128,384]{1,0:T(8,128)(2,1)S(1)}, u32[]{:S(2)}, u32[]{:S(2)}) collective-permute-start(bf16[128,384]{1,0:T(8,128)(2,1)S(1)} %add_convert_fusion.refs_4_), channel_id=1, source_target_pairs={{0,8},{4,12},{8,0},{12,4},{16,24},{20,28},{24,16},{28,20},{1,9},{5... | collective-permute-start | bytes 294920 | tf_op jit(solution)/shard_map/ppermute | solution.py:360
  102.3 5.5 %collective-permute-start.28 = (bf16[128,384]{1,0:T(8,128)(2,1)S(1)}, bf16[128,384]{1,0:T(8,128)(2,1)S(1)}, u32[]{:S(2)}, u32[]{:S(2)}) collective-permute-start(bf16[128,384]{1,0:T(8,128)(2,1)S(1)} %add_convert_fusion.refs_4_), channel_id=1, source_target_pairs={{0,12},{4,8},{8,4},{12,0},{16,28},{20,24},{24,20},{28,16},{1,13},{... | collective-permute-start | bytes 294920 | tf_op jit(solution)/shard_map/ppermute | solution.py:360

commit v6 on v5

--- a/solution.py
+++ b/solution.py
@@ -52,10 +52,10 @@
 
 def cut_copies(members, outs, group, piece, ids_ref, hidden_ref, sems):
     copies = []
-    for k, out in zip(members, outs):
+    for (k, first), out in zip(members, outs):
         for block in range(out.shape[1] // piece):
             start = pl.multiple_of((block * group + ids_ref[k]) * piece, piece)
-            source = hidden_ref.at[:, pl.ds(start, piece)]
+            source = hidden_ref.at[pl.ds(first, out.shape[0]), pl.ds(start, piece)]
             target = out.at[:, pl.ds(block * piece, piece)]
             copies.append(pltpu.make_async_copy(source, target, sems.at[len(copies)]))
             copies[len(copies) - 1].start()
@@ -74,20 +74,24 @@
 
 
 def cut(ids, hidden, members, group, piece):
-    rows, depth = hidden.shape
+    depth = hidden.shape[1]
     if piece % 128:
-        return [cut_plain(ids, hidden, k, group, piece) for k in members]
-    count = len(members)
+        return [cut_plain(ids, hidden[first : first + count], k, group, piece) for k, first, count in members]
+    number = len(members)
     return pl.pallas_call(
-        functools.partial(cut_kernel, members, group, piece),
-        out_shape=tuple(shape((rows, depth // group)) for _ in members),
+        functools.partial(cut_kernel, [(k, first) for k, first, _ in members], group, piece),
+        out_shape=tuple(shape((count, depth // group)) for *_, count in members),
         in_specs=[SMEM, ANY],
-        out_specs=(VMEM,) * count,
-        scratch_shapes=[pltpu.SemaphoreType.DMA((count * depth // (group * piece),))],
+        out_specs=(VMEM,) * number,
+        scratch_shapes=[pltpu.SemaphoreType.DMA((number * depth // (group * piece),))],
         compiler_params=pltpu.CompilerParams(vmem_limit_bytes=8 * MIB),
-        cost_estimate=pl.CostEstimate(flops=0, bytes_accessed=hidden.size * count, transcendentals=0),
+        cost_estimate=pl.CostEstimate(flops=0, bytes_accessed=hidden.size * number, transcendentals=0),
         name="cut",
-    )(ids, hidden)
+    )(ids, in_hbm(hidden))
+
+
+def in_hbm(array):
+    return pltpu.with_memory_space_constraint(array, pltpu.HBM)
 
 
 def fetch(sources, slots):
@@ -98,37 +102,43 @@
     return copies
 
 
-def project_kernel(places, ids_ref, *refs):
-    count = len(places)
-    slots = refs[len(refs) - 2 * (count + 1) :]
-    copies = fetch(refs[: count + 1], slots)
-    hidden = slots[count]
-    size = sum(slots[i].shape[0] for i in range(count) if places[i][0] == 0)
-    copies[count].wait()
-    total = None
-    for i, (part, first) in enumerate(places):
-        rows = slots[i].shape[0]
-        start = pl.multiple_of(ids_ref[part] * size + first, rows)
-        copies[i].wait()
-        term = nn(hidden[:, pl.ds(start, rows)], slots[i][...])
+def project_kernel(parts, carried, ids_ref, hidden_ref, *refs):
+    weights, (slots, sems) = refs[: len(parts)], refs[len(refs) - 2 :]
+    size = weights[0].shape[0]
+    copies = []
+    for number, part in enumerate(parts):
+        start = pl.multiple_of(ids_ref[part] * size, size)
+        source = hidden_ref.at[:, pl.ds(start, size)]
+        copies.append(pltpu.make_async_copy(source, slots.at[number], sems.at[number]))
+        copies[number].start()
+    total = refs[len(parts)][...] if carried else None
+    for number, weight in enumerate(weights):
+        copies[number].wait()
+        term = nn(slots[number], weight[...])
         total = term if total is None else total + term
     first = 0
-    for out in refs[count + 1 : len(refs) - 2 * (count + 1)]:
+    for out in refs[len(parts) + carried : len(refs) - 2]:
         width = out.shape[1]
-        out[...] = total[:, first : first + width].astype(BF16)
+        out[...] = total[:, first : first + width].astype(out.dtype)
         first += width
 
 
-def project(ids, hidden, weights, widths):
-    return pallas(
-        functools.partial(project_kernel, [place for _, *place in weights]),
-        tuple(shape((hidden.shape[0], width)) for width in widths),
-        [ids],
-        [],
-        "project",
-        2 * hidden.size * sum(widths),
-        far=[*[array for array, *_ in weights], hidden],
-    )
+def project(ids, hidden, weights, total, widths, dtype):
+    rows, size = hidden.shape[0], weights[0][0].shape[0]
+    arrays = [array for array, *_ in weights] + total
+    parts = [part for _, part, _ in weights]
+    return pl.pallas_call(
+        functools.partial(project_kernel, parts, len(total)),
+        out_shape=tuple(shape((rows, width), dtype) for width in widths),
+        in_specs=[SMEM, ANY] + [VMEM] * len(arrays),
+        out_specs=(VMEM,) * len(widths),
+        scratch_shapes=[pltpu.VMEM((len(parts), rows, size), BF16), pltpu.SemaphoreType.DMA((len(parts),))],
+        compiler_params=pltpu.CompilerParams(vmem_limit_bytes=16 * MIB),
+        cost_estimate=pl.CostEstimate(
+            flops=2 * rows * size * len(parts) * sum(widths), bytes_accessed=4 * MIB, transcendentals=0
+        ),
+        name="project",
+    )(ids, in_hbm(hidden), *arrays)
 
 
 def hidden_kernel(places, ids_ref, grad_ref, *refs):
@@ -288,9 +298,9 @@
     )
 
 
-def weight_kernel(group, piece, ids_ref, fsdp_ref, grad_ref, hidden_ref, *refs):
-    parts, (kept_ref, away_ref, own_ref, sems) = refs[: group - 1], refs[group - 1 :]
-    copies = cut_copies([0], [own_ref], group, piece, ids_ref, hidden_ref, sems)
+def weight_kernel(group, piece, places, ids_ref, fsdp_ref, grad_ref, hidden_ref, *refs):
+    parts, (kept_ref, away_ref, own_ref, sems) = refs[: len(places)], refs[len(places) :]
+    copies = cut_copies([(0, 0)], [own_ref], group, piece, ids_ref, hidden_ref, sems)
     rows, width = own_ref.shape
     fsdp_size = 2 * kept_ref.shape[0]
     size = width // fsdp_size
@@ -299,35 +309,39 @@
     for j in range(fsdp_size):
         columns = pl.ds(pl.multiple_of(fsdp_ref[j] * size, size), size)
         total = None
-        for k, part in enumerate((own_ref, *parts)):
-            here = pl.ds(pl.multiple_of(ids_ref[k] * rows, rows), rows)
+        for (k, first), part in zip([(0, 0), *places], (own_ref, *parts)):
+            count = part.shape[0]
+            here = pl.ds(pl.multiple_of(ids_ref[k] * rows + first, math.gcd(rows, first)), count)
             term = tn(part[:, columns], grad_ref[here, :])
             total = term if total is None else total + term
         out = away_ref if j % 2 else kept_ref
         out[j // 2] = total.astype(out.dtype)
 
 
-def weight_grad(ids, fsdp_ids, grad, hidden, parts, piece):
-    group, fsdp_size, width = len(parts) + 1, fsdp_ids.shape[0], grad.shape[1]
-    rows, columns = parts[0].shape
+def weight_grad(ids, fsdp_ids, grad, hidden, parts, group, piece):
+    fsdp_size, width = fsdp_ids.shape[0], grad.shape[1]
+    rows, columns = hidden.shape[0], parts[0][0].shape[1]
     size = columns // fsdp_size
     half = (fsdp_size // 2, size, width)
     if piece % 128:
-        parts = [cut_plain(ids, hidden, 0, group, piece), *parts]
-        total = sum(tn(parts[k], lax.dynamic_slice_in_dim(grad, ids[k] * rows, rows, 0)) for k in range(group))
+        parts = [(cut_plain(ids, hidden, 0, group, piece), 0, 0), *parts]
+        total = sum(
+            tn(array, lax.dynamic_slice_in_dim(grad, ids[k] * rows + first, array.shape[0], 0))
+            for array, k, first in parts
+        )
         both = jnp.take(total.reshape(fsdp_size, size, width), fsdp_ids, axis=0)
         both = both.reshape(fsdp_size // 2, 2, size, width)
         return both[:, 0], both[:, 1].astype(BF16)
     return pl.pallas_call(
-        functools.partial(weight_kernel, group, piece),
+        functools.partial(weight_kernel, group, piece, [(k, first) for _, k, first in parts]),
         out_shape=(shape(half, F32), shape(half)),
-        in_specs=[SMEM, SMEM, VMEM, ANY] + [VMEM] * (group - 1),
+        in_specs=[SMEM, SMEM, VMEM, ANY] + [VMEM] * len(parts),
         out_specs=(VMEM, VMEM),
         scratch_shapes=[pltpu.VMEM((rows, columns), BF16), pltpu.SemaphoreType.DMA((columns // piece,))],
         compiler_params=pltpu.CompilerParams(vmem_limit_bytes=20 * MIB),
         cost_estimate=pl.CostEstimate(flops=2 * grad.size * columns, bytes_accessed=8 * MIB, transcendentals=0),
         name="weight_grad",
-    )(ids, fsdp_ids, grad, hidden, *parts)
+    )(ids, fsdp_ids, grad, hidden, *[array for array, *_ in parts])
 
 
 def finish_kernel(group, piece, ids_ref, *refs):
@@ -388,39 +402,44 @@
     piece = depth // (fsdp_size * ctx_size)
     top = fsdp_size // 2
     weights = {0: [w_qkv], top: [swap(w_qkv, "fsdp", fsdp_size, top)]}
-    chunks = dict(zip((1, 2), cut(group_ids, hidden, (1, 2), group, piece)))
+    near = rows * 3 // 4
+    members = [(1, 0, rows), (2, 0, near), (2, near, rows - near)]
+    chunks = cut(group_ids, hidden, members, group, piece)
     grads = [(grad_out, [0])]
     grads += spread(grads[0], ctx_size)
-    moved = {k: swap(chunks[k], "ctx", ctx_size, k) for k in (1, 2)}
+    moved = [swap(chunk, "ctx", ctx_size, k) for chunk, (k, *_) in zip(chunks[:2], members)]
     arrays, _ = lax.optimization_barrier(([array for array, _ in grads], chunks))
     grads = [(array, distances) for array, (_, distances) in zip(arrays, grads)]
     whole = jnp.concatenate([array for array, _ in grads], axis=0)
     array, distances = widen([(whole, [d for _, distances in grads for d in distances])], ctx_size)
-    weights[top], array = lax.optimization_barrier((weights[top], array))
+    weights[1] = [swap(w_qkv, "fsdp", fsdp_size, 1)]
+    early = [(weights[k][0], k, 0) for k in (0, 1)]
+    (total,) = project(fsdp_ids, hidden, early, [], (3 * hd,), F32)
+    weights[top], array, total = lax.optimization_barrier((weights[top], array, total))
     grads.append((array, distances))
     bit = top // 2
     while bit:
         for k in list(weights):
-            halves = weights[k]
-            weights[k ^ bit] = [swap(half, "fsdp", fsdp_size, bit) for half in halves]
+            if k ^ bit not in weights:
+                weights[k ^ bit] = [swap(weights[k][0], "fsdp", fsdp_size, bit)]
         bit //= 2
-    size = w_qkv.shape[0]
-    weights = [
-        (array, k, number * (size // len(weights[k]))) for k in range(fsdp_size) for number, array in enumerate(weights[k])
-    ]
-
-    qk, v = project(fsdp_ids, hidden, weights, (2 * hd, hd))
+    weights = [(weights[k][0], k, 0) for k in range(fsdp_size)]
+
+    qk, v = project(fsdp_ids, hidden, weights[2:], [total], (2 * hd, hd), BF16)
     qks = [(qk, [0])]
     qks += spread(qks[0], ctx_size)
-    v_pair = [(v, [0]), widen([after((v, [0]), [(moved[1], 0)])], ctx_size)]
+    v_pair = [(v, [0]), widen([after((v, [0]), [(moved[0], 0)])], ctx_size)]
     pair = jnp.concatenate([array for array, _ in v_pair], axis=0), [0, 1]
     vs = [pair, *spread(after(pair, qks[1:]), ctx_size)]
-    qks.append(widen([after(qks[0], [pair, (moved[1], 0), (moved[2], 0)]), *qks[1:]], ctx_size))
-    (late,) = cut(group_ids, after((hidden, 0), [(qk, 0)])[0], (3,), group, piece)
-    moved[3] = swap(after((late, 0), vs[1:])[0], "ctx", ctx_size, 3)
+    qks.append(widen([after(qks[0], [pair, (moved[0], 0), (moved[1], 0)]), *qks[1:]], ctx_size))
+    moved.append(swap(after((chunks[2], 0), qks[1 : ctx_size // 2])[0], "ctx", ctx_size, 2))
+    members.append((3, 0, rows))
+    (late,) = cut(group_ids, after((hidden, 0), [(qk, 0)])[0], members[3:], group, piece)
+    moved.append(swap(after((late, 0), [qks[-1], vs[1]])[0], "ctx", ctx_size, 3))
     block = c.reshape(1).astype(jnp.int32)
     grad_near, grad_own = attend(block, page_tokens, [qks, vs, grads], ctx_size, group)
-    kept, away = weight_grad(group_ids, fsdp_ids, grad_near, hidden, [moved[k] for k in (1, 2, 3)], piece)
+    parts = [(array, k, first) for array, (k, first, _) in zip(moved, members)]
+    kept, away = weight_grad(group_ids, fsdp_ids, grad_near, hidden, parts, group, piece)
     bit = 1
     while bit < top:
         total = kept + swap(away, "fsdp", fsdp_size, bit).astype(F32)

time: 109 us -> 106 us (0.972)
  local copies, waits for them, and re-layouts: 3.52 us -> 0.73 us
  waiting for transfers between devices: 37.5 us -> 35.3 us
    pallas_call x3 -> x5, Pallas kernels: 5.5 us -> 10.9 us  [the longest x2 4.93 us: project(): pl.pallas_call(functools.partial(project_kernel, parts, len(total)), out_...]
    pallas_call x4 -> x3, Pallas kernels: 22.7 us -> 18.2 us  [pallas(): pl.pallas_call(kernel, out_shape=out_shape, in_specs=[SMEM] * len(scalars...]
    unnamed x21 -> x13, local copies, waits for them, and re-layouts: 3.47 us -> 0.68 us
    ppermute x29 -> x30, waiting for transfers between devices: 37.5 us -> 35.3 us  [swap(): return lax.ppermute(array, axis, [(i, i ^ distance) for i in range(size)])]
    ppermute x29 -> x30, starting transfers between devices: 38.4 us -> 39.4 us  [swap(): return lax.ppermute(array, axis, [(i, i ^ distance) for i in range(size)])]
  transfers between devices with their start and end apart: 29 -> 30, of which waited for: 16 -> 17; matrix products, arithmetic and copies ran while one was open for 1% -> 1% of each run, Pallas kernels for 22% -> 23%
where the time goes in v6:
time: 106 us
  starting transfers between devices  39.4 us (37%)
  waiting for transfers between devices  35.3 us (33%)
  Pallas kernels  29.2 us (28%)
    ppermute x30, starting transfers between devices, swap(): return lax.ppermute(array, axis, [(i, i ^ distance) for i in range(size)])  39.4 us
    ppermute x30, waiting for transfers between devices, swap(): return lax.ppermute(array, axis, [(i, i ^ distance) for i in range(size)])  35.3 us
    pallas_call x3, Pallas kernels, pallas(): pl.pallas_call(kernel, out_shape=out_shape, in_specs=[SMEM] * len(scalars...  18.2 us
    pallas_call x2, Pallas kernels, project(): pl.pallas_call(functools.partial(project_kernel, parts, len(total)), out_...  4.93 us
    pallas_call x2, Pallas kernels, cut(): pl.pallas_call(functools.partial(cut_kernel, [(k, first) for k, first, _...  3.64 us
    pallas_call x1, Pallas kernels, weight_grad(): pl.pallas_call(functools.partial(weight_kernel, group, piece, [(k, first)...  2.36 us
  transfers between devices with their start and end apart: 30, of which 17 were waited for; matrix products, arithmetic and copies ran while one was open for 1% of the time, Pallas kernels for 23%

profile of v6, /device:TPU:0, one launch (start us, length us, event | category | flops | bytes accessed | tf_op | source)
XLA Modules:
  0.0 106.5 jit_solution(15673347638248140019)
XLA Ops:
  0.6 0.5 collective-permute-start.5
  1.2 2.6 %collective-permute-start = (bf16[1024,384]{1,0:T(8,128)(2,1)}, bf16[1024,384]{1,0:T(8,128)(2,1)S(1)}, u32[]{:S(2)}, u32[]{:S(2)}) collective-permute-start(bf16[1024,384]{1,0:T(8,128)(2,1)} %refs_0_.3), channel_id=1, source_target_pairs={{0,2},{1,3},{2,0},{3,1},{4,6},{5,7},{6,4},{7,5},{8,10},{9,11},{10,... | collective-permute-start | bytes 2359304 | tf_op jit(solution)/shard_map/ppermute | solution.py:374
  3.7 1.6 %collective-permute-start.1 = (bf16[256,128]{1,0:T(8,128)(2,1)}, bf16[256,128]{1,0:T(8,128)(2,1)S(1)}, u32[]{:S(2)}, u32[]{:S(2)}) collective-permute-start(bf16[256,128]{1,0:T(8,128)(2,1)} %bitcast.21), channel_id=1, source_target_pairs={{0,8},{4,12},{8,0},{12,4},{16,24},{20,28},{24,16},{28,20},{1,9},{5... | collective-permute-start | bytes 196616 | tf_op jit(solution)/shard_map/ppermute | solution.py:374
  5.3 2.6 %collective-permute-start.2 = (bf16[256,128]{1,0:T(8,128)(2,1)}, bf16[256,128]{1,0:T(8,128)(2,1)S(1)}, u32[]{:S(2)}, u32[]{:S(2)}) collective-permute-start(bf16[256,128]{1,0:T(8,128)(2,1)} %bitcast.22), channel_id=1, source_target_pairs={{0,16},{4,20},{8,24},{12,28},{16,0},{20,4},{24,8},{28,12},{1,17},{... | collective-permute-start | bytes 196616 | tf_op jit(solution)/shard_map/ppermute | solution.py:374
  7.9 0.2 collective-permute-start.3
  8.1 1.9 %cut.2 = (bf16[256,1024]{1,0:T(8,128)(2,1)S(1)}, bf16[192,1024]{1,0:T(8,128)(2,1)S(1)}, bf16[64,1024]{1,0:T(8,128)(2,1)S(1)}) custom-call(s32[4]{0:T(128)S(1)} %iota_xor_fusion.1.ids_ref, bf16[256,4096]{1,0:T(8,128)(2,1)} %bitcast.16), custom_call_target="tpu_custom_call" | custom-call | bytes 3145728 | tf_op jit(solution)/shard_map/cut/pallas_call | solution.py:81
  10.1 0.0 copy-start.3
  10.1 0.6 copy-done.3
  10.7 2.3 %collective-permute-done.2.refs_11_ = bf16[256,128]{1,0:T(8,128)(2,1)S(1)} collective-permute-done((bf16[256,128]{1,0:T(8,128)(2,1)}, bf16[256,128]{1,0:T(8,128)(2,1)S(1)}, u32[]{:S(2)}, u32[]{:S(2)}) %collective-permute-start.2) | collective-permute-done | bytes 65568 | tf_op jit(solution)/shard_map/ppermute | solution.py:374
  13.1 1.2 %collective-permute-done.3.refs_12_ = bf16[256,128]{1,0:T(8,128)(2,1)S(1)} collective-permute-done((bf16[256,128]{1,0:T(8,128)(2,1)}, bf16[256,128]{1,0:T(8,128)(2,1)S(1)}, u32[]{:S(2)}, u32[]{:S(2)}) %collective-permute-start.3) | collective-permute-done | bytes 65568 | tf_op jit(solution)/shard_map/ppermute | solution.py:374
  14.3 0.7 pad_maximum_fusion.1
  15.0 1.5 %collective-permute-start.4 = (bf16[1024,128]{1,0:T(8,128)(2,1)}, bf16[1024,128]{1,0:T(8,128)(2,1)}, u32[]{:S(2)}, u32[]{:S(2)}) collective-permute-start(bf16[1024,128]{1,0:T(8,128)(2,1)} %pad_maximum_fusion.1), channel_id=1, source_target_pairs={{0,4},{4,0},{8,12},{12,8},{16,20},{20,16},{24,28},{28,24},{1,5},{5... | collective-permute-start | bytes 786440 | tf_op jit(solution)/shard_map/ppermute | solution.py:374
  16.5 0.0 collective-permute-done.5.refs_1_
  16.5 2.5 %project.2.refs_2_ = f32[256,384]{1,0:T(8,128)S(1)} custom-call(s32[4]{0:T(128)S(1)} %iota_xor_fusion.ids_ref.fsdp_ref, bf16[256,4096]{1,0:T(8,128)(2,1)} %bitcast.17, bf16[1024,384]{1,0:T(8,128)(2,1)S(1)} %copy-done.1, bf16[1024,384]{1,0:T(8,128)(2,1)S(1)} %collective-permute-done.5.refs_1_), custom_call_target="tpu_custom_call" | custom-call | flops 402653184 | bytes 4194304 | tf_op jit(solution)/shard_map/project/pallas_call | solution.py:130
  19.0 3.0 %collective-permute-done.4.refs_13_ = bf16[1024,128]{1,0:T(8,128)(2,1)} collective-permute-done((bf16[1024,128]{1,0:T(8,128)(2,1)}, bf16[1024,128]{1,0:T(8,128)(2,1)}, u32[]{:S(2)}, u32[]{:S(2)}) %collective-permute-start.4) | collective-permute-done | bytes 262176 | tf_op jit(solution)/shard_map/ppermute | solution.py:374
  22.0 0.1 collective-permute-done.refs_0_.refs_2_
  22.1 1.8 %collective-permute-start.10 = (bf16[256,1024]{1,0:T(8,128)(2,1)S(1)}, bf16[256,1024]{1,0:T(8,128)(2,1)S(1)}, u32[]{:S(2)}, u32[]{:S(2)}) collective-permute-start(bf16[256,1024]{1,0:T(8,128)(2,1)S(1)} %get-tuple-element.32), channel_id=1, source_target_pairs={{0,4},{4,0},{8,12},{12,8},{16,20},{20,16},{24,28},{28,24},{1,5},{5... | collective-permute-start | bytes 1572872 | tf_op jit(solution)/shard_map/ppermute | solution.py:374
  23.9 1.6 %collective-permute-start.12 = (bf16[192,1024]{1,0:T(8,128)(2,1)S(1)}, bf16[192,1024]{1,0:T(8,128)(2,1)S(1)}, u32[]{:S(2)}, u32[]{:S(2)}) collective-permute-start(bf16[192,1024]{1,0:T(8,128)(2,1)S(1)} %get-tuple-element.33), channel_id=1, source_target_pairs={{0,8},{4,12},{8,0},{12,4},{16,24},{20,28},{24,16},{28,20},{1,9},{5... | collective-permute-start | bytes 1179656 | tf_op jit(solution)/shard_map/ppermute | solution.py:374
  25.4 0.0 collective-permute-done.6.refs_1_.refs_3_
  25.4 2.5 %project.3 = (bf16[256,256]{1,0:T(8,128)(2,1)S(1)}, bf16[256,128]{1,0:T(8,128)(2,1)S(1)}) custom-call(s32[4]{0:T(128)S(1)} %iota_xor_fusion.ids_ref.fsdp_ref, bf16[256,4096]{1,0:T(8,128)(2,1)} %bitcast.18, bf16[1024,384]{1,0:T(8,128)(2,1)S(1)} %collective-permute-done.refs_0_.refs_2_, bf16[1024,384]{1,0:T(8,128)(2,1)S(1)} %collective-permute-done.6.refs_1_.refs_3_, ...), custom_call_target="tpu_custom_call" | custom-call | flops 402653184 | bytes 4194304 | tf_op jit(solution)/shard_map/project/pallas_call | solution.py:130
  27.9 0.0 copy-start.4
  27.9 0.0 copy-start.5
  27.9 0.8 collective-permute-start.7
  28.8 2.6 %collective-permute-start.8 = (bf16[256,256]{1,0:T(8,128)(2,1)S(1)}, bf16[256,256]{1,0:T(8,128)(2,1)S(1)}, u32[]{:S(2)}, u32[]{:S(2)}) collective-permute-start(bf16[256,256]{1,0:T(8,128)(2,1)S(1)} %get-tuple-element.44.refs_0_), channel_id=1, source_target_pairs={{0,16},{4,20},{8,24},{12,28},{16,0},{20,4},{24,8},{28,12},{1,17},{... | collective-permute-start | bytes 393224 | tf_op jit(solution)/shard_map/ppermute | solution.py:374
  31.4 1.0 collective-permute-start.9
  32.4 4.1 %collective-permute-done.10.refs_0_ = bf16[256,1024]{1,0:T(8,128)(2,1)S(1)} collective-permute-done((bf16[256,1024]{1,0:T(8,128)(2,1)S(1)}, bf16[256,1024]{1,0:T(8,128)(2,1)S(1)}, u32[]{:S(2)}, u32[]{:S(2)}) %collective-permute-start.10) | collective-permute-done | bytes 524320 | tf_op jit(solution)/shard_map/ppermute | solution.py:374
  36.5 1.7 %collective-permute-start.11 = (bf16[256,128]{1,0:T(8,128)(2,1)S(1)}, bf16[256,128]{1,0:T(8,128)(2,1)S(1)}, u32[]{:S(2)}, u32[]{:S(2)}) collective-permute-start(bf16[256,128]{1,0:T(8,128)(2,1)S(1)} %get-tuple-element.43), channel_id=1, source_target_pairs={{0,4},{4,0},{8,12},{12,8},{16,20},{20,16},{24,28},{28,24},{1,5},{5... | collective-permute-start | bytes 196616 | tf_op jit(solution)/shard_map/ppermute | solution.py:374
  38.2 2.5 %collective-permute-done.11 = bf16[256,128]{1,0:T(8,128)(2,1)S(1)} collective-permute-done((bf16[256,128]{1,0:T(8,128)(2,1)S(1)}, bf16[256,128]{1,0:T(8,128)(2,1)S(1)}, u32[]{:S(2)}, u32[]{:S(2)}) %collective-permute-start.11) | collective-permute-done | bytes 65568 | tf_op jit(solution)/shard_map/ppermute | solution.py:374
  40.7 0.0 collective-permute-done.12.refs_1_
  40.8 0.0 collective-permute-done.7.refs_1_
  40.8 4.8 %collective-permute-done.9.refs_3_ = bf16[256,256]{1,0:T(8,128)(2,1)S(1)} collective-permute-done((bf16[256,256]{1,0:T(8,128)(2,1)S(1)}, bf16[256,256]{1,0:T(8,128)(2,1)S(1)}, u32[]{:S(2)}, u32[]{:S(2)}) %collective-permute-start.9) | collective-permute-done | bytes 131104 | tf_op jit(solution)/shard_map/ppermute | solution.py:374
  45.6 0.6 collective-permute-start.13
  46.2 2.1 %collective-permute-start.15 = (bf16[512,128]{1,0:T(8,128)(2,1)S(1)}, bf16[512,128]{1,0:T(8,128)(2,1)S(1)}, u32[]{:S(2)}, u32[]{:S(2)}) collective-permute-start(bf16[512,128]{1,0:T(8,128)(2,1)S(1)} %constant_dynamic-update-slice_fusion.refs_5_), channel_id=1, source_target_pairs={{0,16},{4,20},{8,24},{12,28},{16,0},{20,4},{24,8},{28,12},{1,17},{... | collective-permute-start | bytes 393224 | tf_op jit(solution)/shard_map/ppermute | solution.py:374
  48.3 2.2 %collective-permute-start.16 = (bf16[512,128]{1,0:T(8,128)(2,1)S(1)}, bf16[512,128]{1,0:T(8,128)(2,1)S(1)}, u32[]{:S(2)}, u32[]{:S(2)}) collective-permute-start(bf16[512,128]{1,0:T(8,128)(2,1)S(1)} %constant_dynamic-update-slice_fusion.refs_5_), channel_id=1, source_target_pairs={{0,24},{4,28},{8,16},{12,20},{16,8},{20,12},{24,0},{28,4},{1,25},{... | collective-permute-start | bytes 393224 | tf_op jit(solution)/shard_map/ppermute | solution.py:374
  50.6 1.7 %cut.3 = bf16[256,1024]{1,0:T(8,128)(2,1)S(1)} custom-call(s32[4]{0:T(128)S(1)} %iota_xor_fusion.1.ids_ref, bf16[256,4096]{1,0:T(8,128)(2,1)} %bitcast.19), custom_call_target="tpu_custom_call" | custom-call | bytes 1048576 | tf_op jit(solution)/shard_map/cut/pallas_call | solution.py:81
  52.3 0.3 collective-permute-done.14.refs_6_
  52.5 6.4 %collective-permute-done.13.refs_4_ = bf16[1024,256]{1,0:T(8,128)(2,1)S(1)} collective-permute-done((bf16[1024,256]{1,0:T(8,128)(2,1)S(1)}, bf16[1024,256]{1,0:T(8,128)(2,1)S(1)}, u32[]{:S(2)}, u32[]{:S(2)}) %collective-permute-start.13) | collective-permute-done | bytes 524320 | tf_op jit(solution)/shard_map/ppermute | solution.py:374
  58.9 2.0 %collective-permute-start.17 = (bf16[64,1024]{1,0:T(8,128)(2,1)S(1)}, bf16[64,1024]{1,0:T(8,128)(2,1)S(1)}, u32[]{:S(2)}, u32[]{:S(2)}) collective-permute-start(bf16[64,1024]{1,0:T(8,128)(2,1)S(1)} %copy-done.4), channel_id=1, source_target_pairs={{0,8},{4,12},{8,0},{12,4},{16,24},{20,28},{24,16},{28,20},{1,9},{5... | collective-permute-start | bytes 393224 | tf_op jit(solution)/shard_map/ppermute | solution.py:374
  60.9 0.0 copy-start
  60.9 12.4 %attend.1 = (bf16[1024,384]{1,0:T(8,128)(2,1)S(1)}, bf16[256,384]{1,0:T(8,128)(2,1)S(1)}) custom-call(s32[1]{0:T(128)} %bitcast.block_ref, s32[1,8]{1,0:T(1,128)S(1)} %copy-done.5, bf16[256,256]{1,0:T(8,128)(2,1)S(1)} %get-tuple-element.44.refs_0_, bf16[256,256]{1,0:T(8,128)(2,1)S(1)} %collective-permute-done.7.refs_1_, ...), custom_call_target="tpu_custom_call" | custom-call | flops 5368709120 | bytes 3080192 | tf_op jit(solution)/shard_map/attend/pallas_call | solution.py:35
  73.4 0.6 collective-permute-done.17.refs_2_
  74.0 2.4 %weight_grad.1 = (f32[2,256,384]{2,1,0:T(8,128)S(1)}, bf16[2,256,384]{2,1,0:T(8,128)(2,1)S(1)}) custom-call(s32[4]{0:T(128)S(1)} %iota_xor_fusion.1.ids_ref, s32[4]{0:T(128)S(1)} %iota_xor_fusion.ids_ref.fsdp_ref, bf16[1024,384]{1,0:T(8,128)(2,1)S(1)} %get-tuple-element.47.grad_ref, bf16[256,4096]{1,0:T(8,128)(2,1)S(1)} %bitcast.20, ...), custom_call_target="tpu_custom_call" | custom-call | flops 805306368 | bytes 8388608 | tf_op jit(solution)/shard_map/weight_grad/pallas_call | solution.py:335
  76.4 0.1 collective-permute-start.19
  76.4 1.7 %collective-permute-done.19 = bf16[2,256,384]{2,1,0:T(8,128)(2,1)S(1)} collective-permute-done((bf16[2,256,384]{2,1,0:T(8,128)(2,1)S(1)}, bf16[2,256,384]{2,1,0:T(8,128)(2,1)S(1)}, u32[]{:S(2)}, u32[]{:S(2)}) %collective-permute-start.19) | collective-permute-done | bytes 393248 | tf_op jit(solution)/shard_map/ppermute | solution.py:374
  78.1 0.1 fusion.2
  78.3 2.3 %collective-permute-start.20 = (bf16[128,384]{1,0:T(8,128)(2,1)S(1)}, bf16[128,384]{1,0:T(8,128)(2,1)S(1)}, u32[]{:S(2)}, u32[]{:S(2)}) collective-permute-start(bf16[128,384]{1,0:T(8,128)(2,1)S(1)} %get-tuple-element.64), channel_id=1, source_target_pairs={{0,2},{1,3},{2,0},{3,1},{4,6},{5,7},{6,4},{7,5},{8,10},{9,11},{10,... | collective-permute-start | bytes 294920 | tf_op jit(solution)/shard_map/ppermute | solution.py:374
  80.6 3.1 %collective-permute-done.20 = bf16[128,384]{1,0:T(8,128)(2,1)S(1)} collective-permute-done((bf16[128,384]{1,0:T(8,128)(2,1)S(1)}, bf16[128,384]{1,0:T(8,128)(2,1)S(1)}, u32[]{:S(2)}, u32[]{:S(2)}) %collective-permute-start.20) | collective-permute-done | bytes 98336 | tf_op jit(solution)/shard_map/ppermute | solution.py:374
  83.7 1.7 %collective-permute-start.21 = (bf16[128,384]{1,0:T(8,128)(2,1)S(1)}, bf16[128,384]{1,0:T(8,128)(2,1)S(1)}, u32[]{:S(2)}, u32[]{:S(2)}) collective-permute-start(bf16[128,384]{1,0:T(8,128)(2,1)S(1)} %get-tuple-element.53), channel_id=1, source_target_pairs={{0,2},{1,3},{2,0},{3,1},{4,6},{5,7},{6,4},{7,5},{8,10},{9,11},{10,... | collective-permute-start | bytes 294920 | tf_op jit(solution)/shard_map/ppermute | solution.py:374
  85.5 0.1 collective-permute-start.22
  85.6 4.0 %hidden_grad.1 = bf16[256,4096]{1,0:T(8,128)(2,1)} custom-call(s32[4]{0:T(128)S(1)} %iota_xor_fusion.ids_ref.fsdp_ref, bf16[256,384]{1,0:T(8,128)(2,1)S(1)} %get-tuple-element.57.grad_ref, bf16[1024,384]{1,0:T(8,128)(2,1)S(1)} %copy-done.1, bf16[1024,384]{1,0:T(8,128)(2,1)S(1)} %collective-permute-done.5.refs_1_, ...), custom_call_target="tpu_custom_call" | custom-call | flops 805306368 | bytes 5439488 | tf_op jit(solution)/shard_map/hidden_grad/pallas_call | solution.py:35
  89.6 3.0 %collective-permute-start.26 = (bf16[128,384]{1,0:T(8,128)(2,1)S(1)}, bf16[128,384]{1,0:T(8,128)(2,1)S(1)}, u32[]{:S(2)}, u32[]{:S(2)}) collective-permute-start(bf16[128,384]{1,0:T(8,128)(2,1)S(1)} %add_convert_fusion.1), channel_id=1, source_target_pairs={{0,16},{4,20},{8,24},{12,28},{16,0},{20,4},{24,8},{28,12},{1,17},{... | collective-permute-start | bytes 294920 | tf_op jit(solution)/shard_map/ppermute | solution.py:374
  92.6 1.6 %collective-permute-start.23 = (bf16[128,384]{1,0:T(8,128)(2,1)S(1)}, bf16[128,384]{1,0:T(8,128)(2,1)S(1)}, u32[]{:S(2)}, u32[]{:S(2)}) collective-permute-start(bf16[128,384]{1,0:T(8,128)(2,1)S(1)} %add_convert_fusion.2.refs_0_), channel_id=1, source_target_pairs={{0,4},{4,0},{8,12},{12,8},{16,20},{20,16},{24,28},{28,24},{1,5},{5... | collective-permute-start | bytes 294920 | tf_op jit(solution)/shard_map/ppermute | solution.py:374
  94.2 0.0 collective-permute-start.24
  94.2 1.9 %collective-permute-start.25 = (bf16[128,384]{1,0:T(8,128)(2,1)S(1)}, bf16[128,384]{1,0:T(8,128)(2,1)S(1)}, u32[]{:S(2)}, u32[]{:S(2)}) collective-permute-start(bf16[128,384]{1,0:T(8,128)(2,1)S(1)} %add_convert_fusion.2.refs_0_), channel_id=1, source_target_pairs={{0,12},{4,8},{8,4},{12,0},{16,28},{20,24},{24,20},{28,16},{1,13},{... | collective-permute-start | bytes 294920 | tf_op jit(solution)/shard_map/ppermute | solution.py:374
  96.2 1.6 %collective-permute-start.27 = (bf16[128,384]{1,0:T(8,128)(2,1)S(1)}, bf16[128,384]{1,0:T(8,128)(2,1)S(1)}, u32[]{:S(2)}, u32[]{:S(2)}) collective-permute-start(bf16[128,384]{1,0:T(8,128)(2,1)S(1)} %add_convert_fusion.refs_4_), channel_id=1, source_target_pairs={{0,4},{4,0},{8,12},{12,8},{16,20},{20,16},{24,28},{28,24},{1,5},{5... | collective-permute-start | bytes 294920 | tf_op jit(solution)/shard_map/ppermute | solution.py:374
  97.8 1.0 collective-permute-start.28
  98.8 0.3 collective-permute-done.23.refs_1_
  99.2 0.6 collective-permute-start.29
  99.8 0.1 collective-permute-done.24.refs_2_
  99.9 2.2 %collective-permute-done.25.refs_3_ = bf16[128,384]{1,0:T(8,128)(2,1)S(1)} collective-permute-done((bf16[128,384]{1,0:T(8,128)(2,1)S(1)}, bf16[128,384]{1,0:T(8,128)(2,1)S(1)}, u32[]{:S(2)}, u32[]{:S(2)}) %collective-permute-start.25) | collective-permute-done | bytes 98336 | tf_op jit(solution)/shard_map/ppermute | solution.py:374
  102.1 0.9 collective-permute-done.27.refs_5_
  103.0 0.0 collective-permute-done.28.refs_6_
  103.0 1.6 %collective-permute-done.29.refs_7_ = bf16[128,384]{1,0:T(8,128)(2,1)S(1)} collective-permute-done((bf16[128,384]{1,0:T(8,128)(2,1)S(1)}, bf16[128,384]{1,0:T(8,128)(2,1)S(1)}, u32[]{:S(2)}, u32[]{:S(2)}) %collective-permute-start.29) | collective-permute-done | bytes 98336 | tf_op jit(solution)/shard_map/ppermute | solution.py:374
  104.7 1.8 %finish.1 = f32[1024,384]{1,0:T(8,128)} custom-call(s32[4]{0:T(128)S(1)} %iota_xor_fusion.1.ids_ref, bf16[128,384]{1,0:T(8,128)(2,1)S(1)} %add_convert_fusion.2.refs_0_, bf16[128,384]{1,0:T(8,128)(2,1)S(1)} %collective-permute-done.23.refs_1_, bf16[128,384]{1,0:T(8,128)(2,1)S(1)} %collective-permute-done.24.refs_2_, ...), custom_call_target="tpu_custom_call" | custom-call | bytes 2359296 | tf_op jit(solution)/shard_map/finish/pallas_call | solution.py:35
  (29 shorter events, 0.2 us)
Async XLA Ops:
  0.6 15.9 %copy-start.1 = (bf16[1024,384]{1,0:T(8,128)(2,1)S(1)}, bf16[1024,384]{1,0:T(8,128)(2,1)}, u32[]{:S(2)}) copy-start(bf16[1024,384]{1,0:T(8,128)(2,1)} %refs_0_.3) | copy-start | bytes 2359300
  0.6 13.6 %copy-start.2 = (bf16[1,256,128]{2,1,0:T(8,128)(2,1)S(1)}, bf16[1,256,128]{2,1,0:T(8,128)(2,1)}, u32[]{:S(2)}) copy-start(bf16[1,256,128]{2,1,0:T(8,128)(2,1)} %param.6) | copy-start | bytes 196612
  0.6 15.9 %collective-permute-start.5 = (bf16[1024,384]{1,0:T(8,128)(2,1)}, bf16[1024,384]{1,0:T(8,128)(2,1)S(1)}, u32[]{:S(2)}, u32[]{:S(2)}) collective-permute-start(bf16[1024,384]{1,0:T(8,128)(2,1)} %refs_0_.3), channel_id=1, source_target_pairs={{0,1},{1,0},{2,3},{3,2},{4,5},{5,4},{6,7},{7,6},{8,9},{9,8},{10,11... | collective-permute-start | bytes 2359304 | tf_op jit(solution)/shard_map/ppermute | solution.py:374
  1.2 20.9 %collective-permute-start = (bf16[1024,384]{1,0:T(8,128)(2,1)}, bf16[1024,384]{1,0:T(8,128)(2,1)S(1)}, u32[]{:S(2)}, u32[]{:S(2)}) collective-permute-start(bf16[1024,384]{1,0:T(8,128)(2,1)} %refs_0_.3), channel_id=1, source_target_pairs={{0,2},{1,3},{2,0},{3,1},{4,6},{5,7},{6,4},{7,5},{8,10},{9,11},{10,... | collective-permute-start | bytes 2359304 | tf_op jit(solution)/shard_map/ppermute | solution.py:374
  3.7 7.0 %collective-permute-start.1 = (bf16[256,128]{1,0:T(8,128)(2,1)}, bf16[256,128]{1,0:T(8,128)(2,1)S(1)}, u32[]{:S(2)}, u32[]{:S(2)}) collective-permute-start(bf16[256,128]{1,0:T(8,128)(2,1)} %bitcast.21), channel_id=1, source_target_pairs={{0,8},{4,12},{8,0},{12,4},{16,24},{20,28},{24,16},{28,20},{1,9},{5... | collective-permute-start | bytes 196616 | tf_op jit(solution)/shard_map/ppermute | solution.py:374
  5.3 7.8 %collective-permute-start.2 = (bf16[256,128]{1,0:T(8,128)(2,1)}, bf16[256,128]{1,0:T(8,128)(2,1)S(1)}, u32[]{:S(2)}, u32[]{:S(2)}) collective-permute-start(bf16[256,128]{1,0:T(8,128)(2,1)} %bitcast.22), channel_id=1, source_target_pairs={{0,16},{4,20},{8,24},{12,28},{16,0},{20,4},{24,8},{28,12},{1,17},{... | collective-permute-start | bytes 196616 | tf_op jit(solution)/shard_map/ppermute | solution.py:374
  7.9 6.4 %collective-permute-start.3 = (bf16[256,128]{1,0:T(8,128)(2,1)}, bf16[256,128]{1,0:T(8,128)(2,1)S(1)}, u32[]{:S(2)}, u32[]{:S(2)}) collective-permute-start(bf16[256,128]{1,0:T(8,128)(2,1)} %bitcast.23), channel_id=1, source_target_pairs={{0,24},{4,28},{8,16},{12,20},{16,8},{20,12},{24,0},{28,4},{1,25},{... | collective-permute-start | bytes 196616 | tf_op jit(solution)/shard_map/ppermute | solution.py:374
  10.1 0.7 copy-start.3
  15.0 7.0 %collective-permute-start.4 = (bf16[1024,128]{1,0:T(8,128)(2,1)}, bf16[1024,128]{1,0:T(8,128)(2,1)}, u32[]{:S(2)}, u32[]{:S(2)}) collective-permute-start(bf16[1024,128]{1,0:T(8,128)(2,1)} %pad_maximum_fusion.1), channel_id=1, source_target_pairs={{0,4},{4,0},{8,12},{12,8},{16,20},{20,16},{24,28},{28,24},{1,5},{5... | collective-permute-start | bytes 786440 | tf_op jit(solution)/shard_map/ppermute | solution.py:374
  22.1 3.4 %collective-permute-start.6 = (bf16[1024,384]{1,0:T(8,128)(2,1)S(1)}, bf16[1024,384]{1,0:T(8,128)(2,1)S(1)}, u32[]{:S(2)}, u32[]{:S(2)}) collective-permute-start(bf16[1024,384]{1,0:T(8,128)(2,1)S(1)} %collective-permute-done.refs_0_.refs_2_), channel_id=1, source_target_pairs={{0,1},{1,0},{2,3},{3,2},{4,5},{5,4},{6,7},{7,6},{8,9},{9,8},{10,11... | collective-permute-start | bytes 2359304 | tf_op jit(solution)/shard_map/ppermute | solution.py:374
  22.1 14.4 %collective-permute-start.10 = (bf16[256,1024]{1,0:T(8,128)(2,1)S(1)}, bf16[256,1024]{1,0:T(8,128)(2,1)S(1)}, u32[]{:S(2)}, u32[]{:S(2)}) collective-permute-start(bf16[256,1024]{1,0:T(8,128)(2,1)S(1)} %get-tuple-element.32), channel_id=1, source_target_pairs={{0,4},{4,0},{8,12},{12,8},{16,20},{20,16},{24,28},{28,24},{1,5},{5... | collective-permute-start | bytes 1572872 | tf_op jit(solution)/shard_map/ppermute | solution.py:374
  23.9 16.9 %collective-permute-start.12 = (bf16[192,1024]{1,0:T(8,128)(2,1)S(1)}, bf16[192,1024]{1,0:T(8,128)(2,1)S(1)}, u32[]{:S(2)}, u32[]{:S(2)}) collective-permute-start(bf16[192,1024]{1,0:T(8,128)(2,1)S(1)} %get-tuple-element.33), channel_id=1, source_target_pairs={{0,8},{4,12},{8,0},{12,4},{16,24},{20,28},{24,16},{28,20},{1,9},{5... | collective-permute-start | bytes 1179656 | tf_op jit(solution)/shard_map/ppermute | solution.py:374
  27.9 31.0 %copy-start.4 = (bf16[64,1024]{1,0:T(8,128)(2,1)S(1)}, bf16[64,1024]{1,0:T(8,128)(2,1)}, u32[]{:S(2)}) copy-start(bf16[64,1024]{1,0:T(8,128)(2,1)} %copy-done.3) | copy-start | bytes 393220
  27.9 33.0 %copy-start.5 = (s32[1,8]{1,0:T(1,128)S(1)}, s32[1,8]{1,0:T(1,128)}, u32[]{:S(2)}) copy-start(s32[1,8]{1,0:T(1,128)} %pages_ref.1) | copy-start | bytes 100
  27.9 12.8 %collective-permute-start.7 = (bf16[256,256]{1,0:T(8,128)(2,1)S(1)}, bf16[256,256]{1,0:T(8,128)(2,1)S(1)}, u32[]{:S(2)}, u32[]{:S(2)}) collective-permute-start(bf16[256,256]{1,0:T(8,128)(2,1)S(1)} %get-tuple-element.44.refs_0_), channel_id=1, source_target_pairs={{0,8},{4,12},{8,0},{12,4},{16,24},{20,28},{24,16},{28,20},{1,9},{5... | collective-permute-start | bytes 393224 | tf_op jit(solution)/shard_map/ppermute | solution.py:374
  28.8 12.0 %collective-permute-start.8 = (bf16[256,256]{1,0:T(8,128)(2,1)S(1)}, bf16[256,256]{1,0:T(8,128)(2,1)S(1)}, u32[]{:S(2)}, u32[]{:S(2)}) collective-permute-start(bf16[256,256]{1,0:T(8,128)(2,1)S(1)} %get-tuple-element.44.refs_0_), channel_id=1, source_target_pairs={{0,16},{4,20},{8,24},{12,28},{16,0},{20,4},{24,8},{28,12},{1,17},{... | collective-permute-start | bytes 393224 | tf_op jit(solution)/shard_map/ppermute | solution.py:374
  31.4 14.2 %collective-permute-start.9 = (bf16[256,256]{1,0:T(8,128)(2,1)S(1)}, bf16[256,256]{1,0:T(8,128)(2,1)S(1)}, u32[]{:S(2)}, u32[]{:S(2)}) collective-permute-start(bf16[256,256]{1,0:T(8,128)(2,1)S(1)} %get-tuple-element.44.refs_0_), channel_id=1, source_target_pairs={{0,24},{4,28},{8,16},{12,20},{16,8},{20,12},{24,0},{28,4},{1,25},{... | collective-permute-start | bytes 393224 | tf_op jit(solution)/shard_map/ppermute | solution.py:374
  36.5 4.3 %collective-permute-start.11 = (bf16[256,128]{1,0:T(8,128)(2,1)S(1)}, bf16[256,128]{1,0:T(8,128)(2,1)S(1)}, u32[]{:S(2)}, u32[]{:S(2)}) collective-permute-start(bf16[256,128]{1,0:T(8,128)(2,1)S(1)} %get-tuple-element.43), channel_id=1, source_target_pairs={{0,4},{4,0},{8,12},{12,8},{16,20},{20,16},{24,28},{28,24},{1,5},{5... | collective-permute-start | bytes 196616 | tf_op jit(solution)/shard_map/ppermute | solution.py:374
  45.6 13.3 %collective-permute-start.13 = (bf16[1024,256]{1,0:T(8,128)(2,1)S(1)}, bf16[1024,256]{1,0:T(8,128)(2,1)S(1)}, u32[]{:S(2)}, u32[]{:S(2)}) collective-permute-start(bf16[1024,256]{1,0:T(8,128)(2,1)S(1)} %pad_maximum_fusion), channel_id=1, source_target_pairs={{0,4},{4,0},{8,12},{12,8},{16,20},{20,16},{24,28},{28,24},{1,5},{5... | collective-permute-start | bytes 1572872 | tf_op jit(solution)/shard_map/ppermute | solution.py:374
  46.2 6.3 %collective-permute-start.14 = (bf16[512,128]{1,0:T(8,128)(2,1)S(1)}, bf16[512,128]{1,0:T(8,128)(2,1)S(1)}, u32[]{:S(2)}, u32[]{:S(2)}) collective-permute-start(bf16[512,128]{1,0:T(8,128)(2,1)S(1)} %constant_dynamic-update-slice_fusion.refs_5_), channel_id=1, source_target_pairs={{0,8},{4,12},{8,0},{12,4},{16,24},{20,28},{24,16},{28,20},{1,9},{5... | collective-permute-start | bytes 393224 | tf_op jit(solution)/shard_map/ppermute | solution.py:374
  46.2 14.7 %collective-permute-start.15 = (bf16[512,128]{1,0:T(8,128)(2,1)S(1)}, bf16[512,128]{1,0:T(8,128)(2,1)S(1)}, u32[]{:S(2)}, u32[]{:S(2)}) collective-permute-start(bf16[512,128]{1,0:T(8,128)(2,1)S(1)} %constant_dynamic-update-slice_fusion.refs_5_), channel_id=1, source_target_pairs={{0,16},{4,20},{8,24},{12,28},{16,0},{20,4},{24,8},{28,12},{1,17},{... | collective-permute-start | bytes 393224 | tf_op jit(solution)/shard_map/ppermute | solution.py:374
  48.3 12.6 %collective-permute-start.16 = (bf16[512,128]{1,0:T(8,128)(2,1)S(1)}, bf16[512,128]{1,0:T(8,128)(2,1)S(1)}, u32[]{:S(2)}, u32[]{:S(2)}) collective-permute-start(bf16[512,128]{1,0:T(8,128)(2,1)S(1)} %constant_dynamic-update-slice_fusion.refs_5_), channel_id=1, source_target_pairs={{0,24},{4,28},{8,16},{12,20},{16,8},{20,12},{24,0},{28,4},{1,25},{... | collective-permute-start | bytes 393224 | tf_op jit(solution)/shard_map/ppermute | solution.py:374
  58.9 15.1 %collective-permute-start.18 = (bf16[256,1024]{1,0:T(8,128)(2,1)S(1)}, bf16[256,1024]{1,0:T(8,128)(2,1)S(1)}, u32[]{:S(2)}, u32[]{:S(2)}) collective-permute-start(bf16[256,1024]{1,0:T(8,128)(2,1)S(1)} %cut.3), channel_id=1, source_target_pairs={{0,12},{4,8},{8,4},{12,0},{16,28},{20,24},{24,20},{28,16},{1,13},{... | collective-permute-start | bytes 1572872 | tf_op jit(solution)/shard_map/ppermute | solution.py:374
  58.9 15.1 %collective-permute-start.17 = (bf16[64,1024]{1,0:T(8,128)(2,1)S(1)}, bf16[64,1024]{1,0:T(8,128)(2,1)S(1)}, u32[]{:S(2)}, u32[]{:S(2)}) collective-permute-start(bf16[64,1024]{1,0:T(8,128)(2,1)S(1)} %copy-done.4), channel_id=1, source_target_pairs={{0,8},{4,12},{8,0},{12,4},{16,24},{20,28},{24,16},{28,20},{1,9},{5... | collective-permute-start | bytes 393224 | tf_op jit(solution)/shard_map/ppermute | solution.py:374
  60.9 13.1 %copy-start = (bf16[1,256,4096]{2,1,0:T(8,128)(2,1)S(1)}, bf16[1,256,4096]{2,1,0:T(8,128)(2,1)}, u32[]{:S(2)}) copy-start(bf16[1,256,4096]{2,1,0:T(8,128)(2,1)} %param.4) | copy-start | bytes 6291460
  76.4 1.8 %collective-permute-start.19 = (bf16[2,256,384]{2,1,0:T(8,128)(2,1)S(1)}, bf16[2,256,384]{2,1,0:T(8,128)(2,1)S(1)}, u32[]{:S(2)}, u32[]{:S(2)}) collective-permute-start(bf16[2,256,384]{2,1,0:T(8,128)(2,1)S(1)} %get-tuple-element.52), channel_id=1, source_target_pairs={{0,1},{1,0},{2,3},{3,2},{4,5},{5,4},{6,7},{7,6},{8,9},{9,8},{10,11... | collective-permute-start | bytes 1179656 | tf_op jit(solution)/shard_map/ppermute | solution.py:374
  78.3 5.4 %collective-permute-start.20 = (bf16[128,384]{1,0:T(8,128)(2,1)S(1)}, bf16[128,384]{1,0:T(8,128)(2,1)S(1)}, u32[]{:S(2)}, u32[]{:S(2)}) collective-permute-start(bf16[128,384]{1,0:T(8,128)(2,1)S(1)} %get-tuple-element.64), channel_id=1, source_target_pairs={{0,2},{1,3},{2,0},{3,1},{4,6},{5,7},{6,4},{7,5},{8,10},{9,11},{10,... | collective-permute-start | bytes 294920 | tf_op jit(solution)/shard_map/ppermute | solution.py:374
  83.7 5.9 %collective-permute-start.21 = (bf16[128,384]{1,0:T(8,128)(2,1)S(1)}, bf16[128,384]{1,0:T(8,128)(2,1)S(1)}, u32[]{:S(2)}, u32[]{:S(2)}) collective-permute-start(bf16[128,384]{1,0:T(8,128)(2,1)S(1)} %get-tuple-element.53), channel_id=1, source_target_pairs={{0,2},{1,3},{2,0},{3,1},{4,6},{5,7},{6,4},{7,5},{8,10},{9,11},{10,... | collective-permute-start | bytes 294920 | tf_op jit(solution)/shard_map/ppermute | solution.py:374
  85.5 7.1 %collective-permute-start.22 = (bf16[128,384]{1,0:T(8,128)(2,1)S(1)}, bf16[128,384]{1,0:T(8,128)(2,1)S(1)}, u32[]{:S(2)}, u32[]{:S(2)}) collective-permute-start(bf16[128,384]{1,0:T(8,128)(2,1)S(1)} %fusion.1), channel_id=1, source_target_pairs={{0,16},{4,20},{8,24},{12,28},{16,0},{20,4},{24,8},{28,12},{1,17},{... | collective-permute-start | bytes 294920 | tf_op jit(solution)/shard_map/ppermute | solution.py:374
  89.6 6.6 %collective-permute-start.26 = (bf16[128,384]{1,0:T(8,128)(2,1)S(1)}, bf16[128,384]{1,0:T(8,128)(2,1)S(1)}, u32[]{:S(2)}, u32[]{:S(2)}) collective-permute-start(bf16[128,384]{1,0:T(8,128)(2,1)S(1)} %add_convert_fusion.1), channel_id=1, source_target_pairs={{0,16},{4,20},{8,24},{12,28},{16,0},{20,4},{24,8},{28,12},{1,17},{... | collective-permute-start | bytes 294920 | tf_op jit(solution)/shard_map/ppermute | solution.py:374
  92.6 6.5 %collective-permute-start.23 = (bf16[128,384]{1,0:T(8,128)(2,1)S(1)}, bf16[128,384]{1,0:T(8,128)(2,1)S(1)}, u32[]{:S(2)}, u32[]{:S(2)}) collective-permute-start(bf16[128,384]{1,0:T(8,128)(2,1)S(1)} %add_convert_fusion.2.refs_0_), channel_id=1, source_target_pairs={{0,4},{4,0},{8,12},{12,8},{16,20},{20,16},{24,28},{28,24},{1,5},{5... | collective-permute-start | bytes 294920 | tf_op jit(solution)/shard_map/ppermute | solution.py:374
  94.2 5.7 %collective-permute-start.24 = (bf16[128,384]{1,0:T(8,128)(2,1)S(1)}, bf16[128,384]{1,0:T(8,128)(2,1)S(1)}, u32[]{:S(2)}, u32[]{:S(2)}) collective-permute-start(bf16[128,384]{1,0:T(8,128)(2,1)S(1)} %add_convert_fusion.2.refs_0_), channel_id=1, source_target_pairs={{0,8},{4,12},{8,0},{12,4},{16,24},{20,28},{24,16},{28,20},{1,9},{5... | collective-permute-start | bytes 294920 | tf_op jit(solution)/shard_map/ppermute | solution.py:374
  94.2 7.9 %collective-permute-start.25 = (bf16[128,384]{1,0:T(8,128)(2,1)S(1)}, bf16[128,384]{1,0:T(8,128)(2,1)S(1)}, u32[]{:S(2)}, u32[]{:S(2)}) collective-permute-start(bf16[128,384]{1,0:T(8,128)(2,1)S(1)} %add_convert_fusion.2.refs_0_), channel_id=1, source_target_pairs={{0,12},{4,8},{8,4},{12,0},{16,28},{20,24},{24,20},{28,16},{1,13},{... | collective-permute-start | bytes 294920 | tf_op jit(solution)/shard_map/ppermute | solution.py:374
  96.2 6.8 %collective-permute-start.27 = (bf16[128,384]{1,0:T(8,128)(2,1)S(1)}, bf16[128,384]{1,0:T(8,128)(2,1)S(1)}, u32[]{:S(2)}, u32[]{:S(2)}) collective-permute-start(bf16[128,384]{1,0:T(8,128)(2,1)S(1)} %add_convert_fusion.refs_4_), channel_id=1, source_target_pairs={{0,4},{4,0},{8,12},{12,8},{16,20},{20,16},{24,28},{28,24},{1,5},{5... | collective-permute-start | bytes 294920 | tf_op jit(solution)/shard_map/ppermute | solution.py:374
  97.8 5.3 %collective-permute-start.28 = (bf16[128,384]{1,0:T(8,128)(2,1)S(1)}, bf16[128,384]{1,0:T(8,128)(2,1)S(1)}, u32[]{:S(2)}, u32[]{:S(2)}) collective-permute-start(bf16[128,384]{1,0:T(8,128)(2,1)S(1)} %add_convert_fusion.refs_4_), channel_id=1, source_target_pairs={{0,8},{4,12},{8,0},{12,4},{16,24},{20,28},{24,16},{28,20},{1,9},{5... | collective-permute-start | bytes 294920 | tf_op jit(solution)/shard_map/ppermute | solution.py:374
  99.2 5.5 %collective-permute-start.29 = (bf16[128,384]{1,0:T(8,128)(2,1)S(1)}, bf16[128,384]{1,0:T(8,128)(2,1)S(1)}, u32[]{:S(2)}, u32[]{:S(2)}) collective-permute-start(bf16[128,384]{1,0:T(8,128)(2,1)S(1)} %add_convert_fusion.refs_4_), channel_id=1, source_target_pairs={{0,12},{4,8},{8,4},{12,0},{16,28},{20,24},{24,20},{28,16},{1,13},{... | collective-permute-start | bytes 294920 | tf_op jit(solution)/shard_map/ppermute | solution.py:374

commit v7 on v6

--- a/solution.py
+++ b/solution.py
@@ -344,14 +344,20 @@
     )(ids, fsdp_ids, grad, hidden, *[array for array, *_ in parts])
 
 
-def finish_kernel(group, piece, ids_ref, *refs):
-    out_ref = refs[len(refs) - 1]
-    for number, block in enumerate(refs[: len(refs) - 1]):
+def finish_kernel(group, piece, turn, ids_ref, *refs):
+    blocks, (out_ref, wide_ref, sems) = refs[:group], refs[len(refs) - 3 :]
+    copies = []
+    for number, block in enumerate(blocks):
         count = block.shape[0] // piece
         for i in range(count):
-            place = (number // group * count + i) * group + ids_ref[number % group]
-            start = pl.multiple_of(place * piece, piece)
-            out_ref[pl.ds(start, piece), :] = block[i * piece : (i + 1) * piece, :].astype(F32)
+            place = (turn * count + i) * group + ids_ref[number]
+            here = pl.ds(pl.multiple_of(place * piece, piece), piece)
+            slot = wide_ref.at[len(copies)]
+            slot[...] = block[i * piece : (i + 1) * piece, :].astype(F32)
+            copies.append(pltpu.make_async_copy(slot, out_ref.at[here, :], sems.at[len(copies)]))
+            copies[len(copies) - 1].start()
+    for copy in copies:
+        copy.wait()
 
 
 def finish(ids, blocks, group, piece):
@@ -360,14 +366,21 @@
         order = jnp.stack(blocks).reshape(-1, group, rows // piece, piece, width)
         order = jnp.take(order, ids, axis=1).swapaxes(1, 2)
         return order.reshape(len(blocks) * rows, width).astype(F32)
-    return pallas(
-        functools.partial(finish_kernel, group, piece),
-        shape((len(blocks) * rows, width), F32),
-        [ids],
-        blocks,
-        "finish",
-        0,
-    )
+    out = []
+    for turn in range(len(blocks) // group):
+        number = group * rows // piece
+        out = pl.pallas_call(
+            functools.partial(finish_kernel, group, piece, turn),
+            out_shape=shape((len(blocks) * rows, width), F32),
+            in_specs=[SMEM] + [VMEM] * group + [ANY] * (turn > 0),
+            out_specs=ANY,
+            input_output_aliases={group + 1: 0} if turn else {},
+            scratch_shapes=[pltpu.VMEM((number, piece, width), F32), pltpu.SemaphoreType.DMA((number,))],
+            compiler_params=pltpu.CompilerParams(vmem_limit_bytes=12 * MIB),
+            cost_estimate=pl.CostEstimate(flops=0, bytes_accessed=3 * MIB, transcendentals=0),
+            name="finish",
+        )(ids, *blocks[turn * group : (turn + 1) * group], *([out] if turn else []))
+    return out
 
 
 def swap(array, axis, size, distance):
@@ -402,7 +415,7 @@
     piece = depth // (fsdp_size * ctx_size)
     top = fsdp_size // 2
     weights = {0: [w_qkv], top: [swap(w_qkv, "fsdp", fsdp_size, top)]}
-    near = rows * 3 // 4
+    near = rows * 5 // 8
     members = [(1, 0, rows), (2, 0, near), (2, near, rows - near)]
     chunks = cut(group_ids, hidden, members, group, piece)
     grads = [(grad_out, [0])]

time: 106 us -> 106 us (level); the launches traced: 106 us -> 105 us
  waiting for transfers between devices: 35.3 us -> 32 us
  Pallas kernels: 29.2 us -> 31.7 us
    ppermute x30, waiting for transfers between devices: 35.3 us -> 32 us  [swap(): return lax.ppermute(array, axis, [(i, i ^ distance) for i in range(size)])]
    pallas_call x0 -> x2, Pallas kernels: none -> 2.91 us  [finish(): pl.pallas_call(functools.partial(finish_kernel, group, piece, turn), out_...]
    pallas_call x3 -> x2, Pallas kernels: 18.2 us -> 17.8 us  [pallas(): pl.pallas_call(kernel, out_shape=out_shape, in_specs=[SMEM] * len(scalars...]
  transfers between devices with their start and end apart: 30 -> 30, of which waited for: 17 -> 17; matrix products, arithmetic and copies ran while one was open for 1% -> 1% of each run, Pallas kernels for 23% -> 26%
where the time goes in v7:
time: 106 us; the launch traced here: 105 us
  starting transfers between devices  38.9 us (37%)
  waiting for transfers between devices  32 us (30%)
  Pallas kernels  31.7 us (30%)
    ppermute x30, starting transfers between devices, swap(): return lax.ppermute(array, axis, [(i, i ^ distance) for i in range(size)])  38.9 us
    ppermute x30, waiting for transfers between devices, swap(): return lax.ppermute(array, axis, [(i, i ^ distance) for i in range(size)])  32 us
    pallas_call x2, Pallas kernels, pallas(): pl.pallas_call(kernel, out_shape=out_shape, in_specs=[SMEM] * len(scalars...  17.8 us
    pallas_call x2, Pallas kernels, project(): pl.pallas_call(functools.partial(project_kernel, parts, len(total)), out_...  4.93 us
    pallas_call x2, Pallas kernels, cut(): pl.pallas_call(functools.partial(cut_kernel, [(k, first) for k, first, _...  3.63 us
    pallas_call x2, Pallas kernels, finish(): pl.pallas_call(functools.partial(finish_kernel, group, piece, turn), out_...  2.91 us
    pallas_call x1, Pallas kernels, weight_grad(): pl.pallas_call(functools.partial(weight_kernel, group, piece, [(k, first)...  2.34 us
  transfers between devices with their start and end apart: 30, of which 17 were waited for; matrix products, arithmetic and copies ran while one was open for 1% of the time, Pallas kernels for 26%

profile of v7, /device:TPU:0, one launch (start us, length us, event | category | flops | bytes accessed | tf_op | source)
XLA Modules:
  0.0 105.3 jit_solution(7298138501383135538)
XLA Ops:
  0.6 0.5 collective-permute-start.5
  1.2 2.6 %collective-permute-start = (bf16[1024,384]{1,0:T(8,128)(2,1)}, bf16[1024,384]{1,0:T(8,128)(2,1)S(1)}, u32[]{:S(2)}, u32[]{:S(2)}) collective-permute-start(bf16[1024,384]{1,0:T(8,128)(2,1)} %refs_0_.3), channel_id=1, source_target_pairs={{0,2},{1,3},{2,0},{3,1},{4,6},{5,7},{6,4},{7,5},{8,10},{9,11},{10,... | collective-permute-start | bytes 2359304 | tf_op jit(solution)/shard_map/ppermute | solution.py:387
  3.7 1.6 %collective-permute-start.1 = (bf16[256,128]{1,0:T(8,128)(2,1)}, bf16[256,128]{1,0:T(8,128)(2,1)S(1)}, u32[]{:S(2)}, u32[]{:S(2)}) collective-permute-start(bf16[256,128]{1,0:T(8,128)(2,1)} %bitcast.21), channel_id=1, source_target_pairs={{0,8},{4,12},{8,0},{12,4},{16,24},{20,28},{24,16},{28,20},{1,9},{5... | collective-permute-start | bytes 196616 | tf_op jit(solution)/shard_map/ppermute | solution.py:387
  5.3 2.6 %collective-permute-start.2 = (bf16[256,128]{1,0:T(8,128)(2,1)}, bf16[256,128]{1,0:T(8,128)(2,1)S(1)}, u32[]{:S(2)}, u32[]{:S(2)}) collective-permute-start(bf16[256,128]{1,0:T(8,128)(2,1)} %bitcast.22), channel_id=1, source_target_pairs={{0,16},{4,20},{8,24},{12,28},{16,0},{20,4},{24,8},{28,12},{1,17},{... | collective-permute-start | bytes 196616 | tf_op jit(solution)/shard_map/ppermute | solution.py:387
  7.9 0.2 collective-permute-start.3
  8.1 1.9 %cut.2 = (bf16[256,1024]{1,0:T(8,128)(2,1)S(1)}, bf16[160,1024]{1,0:T(8,128)(2,1)S(1)}, bf16[96,1024]{1,0:T(8,128)(2,1)S(1)}) custom-call(s32[4]{0:T(128)S(1)} %iota_xor_fusion.1.ids_ref, bf16[256,4096]{1,0:T(8,128)(2,1)} %bitcast.16), custom_call_target="tpu_custom_call" | custom-call | bytes 3145728 | tf_op jit(solution)/shard_map/cut/pallas_call | solution.py:81
  10.1 0.0 copy-start.3
  10.1 0.7 copy-done.3
  10.8 2.3 %collective-permute-done.2.refs_11_ = bf16[256,128]{1,0:T(8,128)(2,1)S(1)} collective-permute-done((bf16[256,128]{1,0:T(8,128)(2,1)}, bf16[256,128]{1,0:T(8,128)(2,1)S(1)}, u32[]{:S(2)}, u32[]{:S(2)}) %collective-permute-start.2) | collective-permute-done | bytes 65568 | tf_op jit(solution)/shard_map/ppermute | solution.py:387
  13.1 1.2 %collective-permute-done.3.refs_12_ = bf16[256,128]{1,0:T(8,128)(2,1)S(1)} collective-permute-done((bf16[256,128]{1,0:T(8,128)(2,1)}, bf16[256,128]{1,0:T(8,128)(2,1)S(1)}, u32[]{:S(2)}, u32[]{:S(2)}) %collective-permute-start.3) | collective-permute-done | bytes 65568 | tf_op jit(solution)/shard_map/ppermute | solution.py:387
  14.3 0.7 pad_maximum_fusion.1
  15.0 1.5 %collective-permute-start.4 = (bf16[1024,128]{1,0:T(8,128)(2,1)}, bf16[1024,128]{1,0:T(8,128)(2,1)}, u32[]{:S(2)}, u32[]{:S(2)}) collective-permute-start(bf16[1024,128]{1,0:T(8,128)(2,1)} %pad_maximum_fusion.1), channel_id=1, source_target_pairs={{0,4},{4,0},{8,12},{12,8},{16,20},{20,16},{24,28},{28,24},{1,5},{5... | collective-permute-start | bytes 786440 | tf_op jit(solution)/shard_map/ppermute | solution.py:387
  16.5 2.5 %project.2.refs_2_ = f32[256,384]{1,0:T(8,128)S(1)} custom-call(s32[4]{0:T(128)S(1)} %iota_xor_fusion.ids_ref.fsdp_ref, bf16[256,4096]{1,0:T(8,128)(2,1)} %bitcast.17, bf16[1024,384]{1,0:T(8,128)(2,1)S(1)} %copy-done.1, bf16[1024,384]{1,0:T(8,128)(2,1)S(1)} %collective-permute-done.5.refs_1_), custom_call_target="tpu_custom_call" | custom-call | flops 402653184 | bytes 4194304 | tf_op jit(solution)/shard_map/project/pallas_call | solution.py:130
  19.0 3.0 %collective-permute-done.4.refs_13_ = bf16[1024,128]{1,0:T(8,128)(2,1)} collective-permute-done((bf16[1024,128]{1,0:T(8,128)(2,1)}, bf16[1024,128]{1,0:T(8,128)(2,1)}, u32[]{:S(2)}, u32[]{:S(2)}) %collective-permute-start.4) | collective-permute-done | bytes 262176 | tf_op jit(solution)/shard_map/ppermute | solution.py:387
  22.0 0.1 collective-permute-done.refs_0_.refs_2_
  22.1 0.0 collective-permute-start.6
  22.1 1.8 %collective-permute-start.10 = (bf16[256,1024]{1,0:T(8,128)(2,1)S(1)}, bf16[256,1024]{1,0:T(8,128)(2,1)S(1)}, u32[]{:S(2)}, u32[]{:S(2)}) collective-permute-start(bf16[256,1024]{1,0:T(8,128)(2,1)S(1)} %get-tuple-element.32), channel_id=1, source_target_pairs={{0,4},{4,0},{8,12},{12,8},{16,20},{20,16},{24,28},{28,24},{1,5},{5... | collective-permute-start | bytes 1572872 | tf_op jit(solution)/shard_map/ppermute | solution.py:387
  23.9 1.6 %collective-permute-start.12 = (bf16[160,1024]{1,0:T(8,128)(2,1)S(1)}, bf16[160,1024]{1,0:T(8,128)(2,1)S(1)}, u32[]{:S(2)}, u32[]{:S(2)}) collective-permute-start(bf16[160,1024]{1,0:T(8,128)(2,1)S(1)} %get-tuple-element.33), channel_id=1, source_target_pairs={{0,8},{4,12},{8,0},{12,4},{16,24},{20,28},{24,16},{28,20},{1,9},{5... | collective-permute-start | bytes 983048 | tf_op jit(solution)/shard_map/ppermute | solution.py:387
  25.4 0.0 collective-permute-done.6.refs_1_.refs_3_
  25.4 2.5 %project.3 = (bf16[256,256]{1,0:T(8,128)(2,1)S(1)}, bf16[256,128]{1,0:T(8,128)(2,1)S(1)}) custom-call(s32[4]{0:T(128)S(1)} %iota_xor_fusion.ids_ref.fsdp_ref, bf16[256,4096]{1,0:T(8,128)(2,1)} %bitcast.18, bf16[1024,384]{1,0:T(8,128)(2,1)S(1)} %collective-permute-done.refs_0_.refs_2_, bf16[1024,384]{1,0:T(8,128)(2,1)S(1)} %collective-permute-done.6.refs_1_.refs_3_, ...), custom_call_target="tpu_custom_call" | custom-call | flops 402653184 | bytes 4194304 | tf_op jit(solution)/shard_map/project/pallas_call | solution.py:130
  27.9 0.0 copy-start.4
  27.9 0.0 copy-start.5
  27.9 0.8 collective-permute-start.7
  28.8 2.6 %collective-permute-start.8 = (bf16[256,256]{1,0:T(8,128)(2,1)S(1)}, bf16[256,256]{1,0:T(8,128)(2,1)S(1)}, u32[]{:S(2)}, u32[]{:S(2)}) collective-permute-start(bf16[256,256]{1,0:T(8,128)(2,1)S(1)} %get-tuple-element.44.refs_0_), channel_id=1, source_target_pairs={{0,16},{4,20},{8,24},{12,28},{16,0},{20,4},{24,8},{28,12},{1,17},{... | collective-permute-start | bytes 393224 | tf_op jit(solution)/shard_map/ppermute | solution.py:387
  31.4 1.0 collective-permute-start.9
  32.4 4.1 %collective-permute-done.10.refs_0_ = bf16[256,1024]{1,0:T(8,128)(2,1)S(1)} collective-permute-done((bf16[256,1024]{1,0:T(8,128)(2,1)S(1)}, bf16[256,1024]{1,0:T(8,128)(2,1)S(1)}, u32[]{:S(2)}, u32[]{:S(2)}) %collective-permute-start.10) | collective-permute-done | bytes 524320 | tf_op jit(solution)/shard_map/ppermute | solution.py:387
  36.5 1.7 %collective-permute-start.11 = (bf16[256,128]{1,0:T(8,128)(2,1)S(1)}, bf16[256,128]{1,0:T(8,128)(2,1)S(1)}, u32[]{:S(2)}, u32[]{:S(2)}) collective-permute-start(bf16[256,128]{1,0:T(8,128)(2,1)S(1)} %get-tuple-element.43), channel_id=1, source_target_pairs={{0,4},{4,0},{8,12},{12,8},{16,20},{20,16},{24,28},{28,24},{1,5},{5... | collective-permute-start | bytes 196616 | tf_op jit(solution)/shard_map/ppermute | solution.py:387
  38.2 2.5 %collective-permute-done.11 = bf16[256,128]{1,0:T(8,128)(2,1)S(1)} collective-permute-done((bf16[256,128]{1,0:T(8,128)(2,1)S(1)}, bf16[256,128]{1,0:T(8,128)(2,1)S(1)}, u32[]{:S(2)}, u32[]{:S(2)}) %collective-permute-start.11) | collective-permute-done | bytes 65568 | tf_op jit(solution)/shard_map/ppermute | solution.py:387
  40.8 0.0 collective-permute-done.8.refs_2_
  40.8 3.4 %collective-permute-done.9.refs_3_ = bf16[256,256]{1,0:T(8,128)(2,1)S(1)} collective-permute-done((bf16[256,256]{1,0:T(8,128)(2,1)S(1)}, bf16[256,256]{1,0:T(8,128)(2,1)S(1)}, u32[]{:S(2)}, u32[]{:S(2)}) %collective-permute-start.9) | collective-permute-done | bytes 131104 | tf_op jit(solution)/shard_map/ppermute | solution.py:387
  44.2 0.7 collective-permute-start.13
  44.9 0.7 collective-permute-start.14
  45.6 1.3 %collective-permute-start.15 = (bf16[512,128]{1,0:T(8,128)(2,1)S(1)}, bf16[512,128]{1,0:T(8,128)(2,1)S(1)}, u32[]{:S(2)}, u32[]{:S(2)}) collective-permute-start(bf16[512,128]{1,0:T(8,128)(2,1)S(1)} %constant_dynamic-update-slice_fusion.refs_5_), channel_id=1, source_target_pairs={{0,16},{4,20},{8,24},{12,28},{16,0},{20,4},{24,8},{28,12},{1,17},{... | collective-permute-start | bytes 393224 | tf_op jit(solution)/shard_map/ppermute | solution.py:387
  46.9 2.3 %collective-permute-start.16 = (bf16[512,128]{1,0:T(8,128)(2,1)S(1)}, bf16[512,128]{1,0:T(8,128)(2,1)S(1)}, u32[]{:S(2)}, u32[]{:S(2)}) collective-permute-start(bf16[512,128]{1,0:T(8,128)(2,1)S(1)} %constant_dynamic-update-slice_fusion.refs_5_), channel_id=1, source_target_pairs={{0,24},{4,28},{8,16},{12,20},{16,8},{20,12},{24,0},{28,4},{1,25},{... | collective-permute-start | bytes 393224 | tf_op jit(solution)/shard_map/ppermute | solution.py:387
  49.3 1.7 %cut.3 = bf16[256,1024]{1,0:T(8,128)(2,1)S(1)} custom-call(s32[4]{0:T(128)S(1)} %iota_xor_fusion.1.ids_ref, bf16[256,4096]{1,0:T(8,128)(2,1)} %bitcast.19), custom_call_target="tpu_custom_call" | custom-call | bytes 1048576 | tf_op jit(solution)/shard_map/cut/pallas_call | solution.py:81
  51.0 0.4 collective-permute-done.14.refs_6_
  51.4 6.1 %collective-permute-done.13.refs_4_ = bf16[1024,256]{1,0:T(8,128)(2,1)S(1)} collective-permute-done((bf16[1024,256]{1,0:T(8,128)(2,1)S(1)}, bf16[1024,256]{1,0:T(8,128)(2,1)S(1)}, u32[]{:S(2)}, u32[]{:S(2)}) %collective-permute-start.13) | collective-permute-done | bytes 524320 | tf_op jit(solution)/shard_map/ppermute | solution.py:387
  57.5 0.0 collective-permute-start.18
  57.5 2.0 %collective-permute-start.17 = (bf16[96,1024]{1,0:T(8,128)(2,1)S(1)}, bf16[96,1024]{1,0:T(8,128)(2,1)S(1)}, u32[]{:S(2)}, u32[]{:S(2)}) collective-permute-start(bf16[96,1024]{1,0:T(8,128)(2,1)S(1)} %copy-done.4), channel_id=1, source_target_pairs={{0,8},{4,12},{8,0},{12,4},{16,24},{20,28},{24,16},{28,20},{1,9},{5... | collective-permute-start | bytes 589832 | tf_op jit(solution)/shard_map/ppermute | solution.py:387
  59.5 0.0 copy-start
  59.5 13.8 %attend.1 = (bf16[1024,384]{1,0:T(8,128)(2,1)S(1)}, bf16[256,384]{1,0:T(8,128)(2,1)S(1)}) custom-call(s32[1]{0:T(128)} %bitcast.block_ref, s32[1,8]{1,0:T(1,128)S(1)} %copy-done.5, bf16[256,256]{1,0:T(8,128)(2,1)S(1)} %get-tuple-element.44.refs_0_, bf16[256,256]{1,0:T(8,128)(2,1)S(1)} %collective-permute-done.7.refs_1_, ...), custom_call_target="tpu_custom_call" | custom-call | flops 5368709120 | bytes 3080192 | tf_op jit(solution)/shard_map/attend/pallas_call | solution.py:35
  73.4 0.6 collective-permute-done.17.refs_2_
  74.0 2.3 %weight_grad.1 = (f32[2,256,384]{2,1,0:T(8,128)S(1)}, bf16[2,256,384]{2,1,0:T(8,128)(2,1)S(1)}) custom-call(s32[4]{0:T(128)S(1)} %iota_xor_fusion.1.ids_ref, s32[4]{0:T(128)S(1)} %iota_xor_fusion.ids_ref.fsdp_ref, bf16[1024,384]{1,0:T(8,128)(2,1)S(1)} %get-tuple-element.47.grad_ref, bf16[256,4096]{1,0:T(8,128)(2,1)S(1)} %bitcast.20, ...), custom_call_target="tpu_custom_call" | custom-call | flops 805306368 | bytes 8388608 | tf_op jit(solution)/shard_map/weight_grad/pallas_call | solution.py:335
  76.3 0.1 collective-permute-start.19
  76.4 1.7 %collective-permute-done.19 = bf16[2,256,384]{2,1,0:T(8,128)(2,1)S(1)} collective-permute-done((bf16[2,256,384]{2,1,0:T(8,128)(2,1)S(1)}, bf16[2,256,384]{2,1,0:T(8,128)(2,1)S(1)}, u32[]{:S(2)}, u32[]{:S(2)}) %collective-permute-start.19) | collective-permute-done | bytes 393248 | tf_op jit(solution)/shard_map/ppermute | solution.py:387
  78.1 0.1 fusion.2
  78.3 1.6 %collective-permute-start.20 = (bf16[128,384]{1,0:T(8,128)(2,1)S(1)}, bf16[128,384]{1,0:T(8,128)(2,1)S(1)}, u32[]{:S(2)}, u32[]{:S(2)}) collective-permute-start(bf16[128,384]{1,0:T(8,128)(2,1)S(1)} %get-tuple-element.64), channel_id=1, source_target_pairs={{0,2},{1,3},{2,0},{3,1},{4,6},{5,7},{6,4},{7,5},{8,10},{9,11},{10,... | collective-permute-start | bytes 294920 | tf_op jit(solution)/shard_map/ppermute | solution.py:387
  79.8 3.3 %collective-permute-done.20 = bf16[128,384]{1,0:T(8,128)(2,1)S(1)} collective-permute-done((bf16[128,384]{1,0:T(8,128)(2,1)S(1)}, bf16[128,384]{1,0:T(8,128)(2,1)S(1)}, u32[]{:S(2)}, u32[]{:S(2)}) %collective-permute-start.20) | collective-permute-done | bytes 98336 | tf_op jit(solution)/shard_map/ppermute | solution.py:387
  83.2 1.5 %collective-permute-start.21 = (bf16[128,384]{1,0:T(8,128)(2,1)S(1)}, bf16[128,384]{1,0:T(8,128)(2,1)S(1)}, u32[]{:S(2)}, u32[]{:S(2)}) collective-permute-start(bf16[128,384]{1,0:T(8,128)(2,1)S(1)} %get-tuple-element.53), channel_id=1, source_target_pairs={{0,2},{1,3},{2,0},{3,1},{4,6},{5,7},{6,4},{7,5},{8,10},{9,11},{10,... | collective-permute-start | bytes 294920 | tf_op jit(solution)/shard_map/ppermute | solution.py:387
  84.7 1.1 %collective-permute-start.26 = (bf16[128,384]{1,0:T(8,128)(2,1)S(1)}, bf16[128,384]{1,0:T(8,128)(2,1)S(1)}, u32[]{:S(2)}, u32[]{:S(2)}) collective-permute-start(bf16[128,384]{1,0:T(8,128)(2,1)S(1)} %fusion.1), channel_id=1, source_target_pairs={{0,16},{4,20},{8,24},{12,28},{16,0},{20,4},{24,8},{28,12},{1,17},{... | collective-permute-start | bytes 294920 | tf_op jit(solution)/shard_map/ppermute | solution.py:387
  85.8 4.0 %hidden_grad.1 = bf16[256,4096]{1,0:T(8,128)(2,1)} custom-call(s32[4]{0:T(128)S(1)} %iota_xor_fusion.ids_ref.fsdp_ref, bf16[256,384]{1,0:T(8,128)(2,1)S(1)} %get-tuple-element.57.grad_ref, bf16[1024,384]{1,0:T(8,128)(2,1)S(1)} %copy-done.1, bf16[1024,384]{1,0:T(8,128)(2,1)S(1)} %collective-permute-done.5.refs_1_, ...), custom_call_target="tpu_custom_call" | custom-call | flops 805306368 | bytes 5439488 | tf_op jit(solution)/shard_map/hidden_grad/pallas_call | solution.py:35
  89.9 1.9 %collective-permute-start.22 = (bf16[128,384]{1,0:T(8,128)(2,1)S(1)}, bf16[128,384]{1,0:T(8,128)(2,1)S(1)}, u32[]{:S(2)}, u32[]{:S(2)}) collective-permute-start(bf16[128,384]{1,0:T(8,128)(2,1)S(1)} %add_convert_fusion.2), channel_id=1, source_target_pairs={{0,16},{4,20},{8,24},{12,28},{16,0},{20,4},{24,8},{28,12},{1,17},{... | collective-permute-start | bytes 294920 | tf_op jit(solution)/shard_map/ppermute | solution.py:387
  91.8 1.6 %collective-permute-start.27 = (bf16[128,384]{1,0:T(8,128)(2,1)S(1)}, bf16[128,384]{1,0:T(8,128)(2,1)S(1)}, u32[]{:S(2)}, u32[]{:S(2)}) collective-permute-start(bf16[128,384]{1,0:T(8,128)(2,1)S(1)} %add_convert_fusion.refs_0_), channel_id=1, source_target_pairs={{0,4},{4,0},{8,12},{12,8},{16,20},{20,16},{24,28},{28,24},{1,5},{5... | collective-permute-start | bytes 294920 | tf_op jit(solution)/shard_map/ppermute | solution.py:387
  93.4 2.0 %collective-permute-start.29 = (bf16[128,384]{1,0:T(8,128)(2,1)S(1)}, bf16[128,384]{1,0:T(8,128)(2,1)S(1)}, u32[]{:S(2)}, u32[]{:S(2)}) collective-permute-start(bf16[128,384]{1,0:T(8,128)(2,1)S(1)} %add_convert_fusion.refs_0_), channel_id=1, source_target_pairs={{0,12},{4,8},{8,4},{12,0},{16,28},{20,24},{24,20},{28,16},{1,13},{... | collective-permute-start | bytes 294920 | tf_op jit(solution)/shard_map/ppermute | solution.py:387
  95.4 1.0 collective-permute-done.22
  96.4 0.6 collective-permute-start.23
  97.0 1.2 %collective-permute-start.24 = (bf16[128,384]{1,0:T(8,128)(2,1)S(1)}, bf16[128,384]{1,0:T(8,128)(2,1)S(1)}, u32[]{:S(2)}, u32[]{:S(2)}) collective-permute-start(bf16[128,384]{1,0:T(8,128)(2,1)S(1)} %add_convert_fusion.1.refs_0_), channel_id=1, source_target_pairs={{0,8},{4,12},{8,0},{12,4},{16,24},{20,28},{24,16},{28,20},{1,9},{5... | collective-permute-start | bytes 294920 | tf_op jit(solution)/shard_map/ppermute | solution.py:387
  98.2 1.8 %collective-permute-start.25 = (bf16[128,384]{1,0:T(8,128)(2,1)S(1)}, bf16[128,384]{1,0:T(8,128)(2,1)S(1)}, u32[]{:S(2)}, u32[]{:S(2)}) collective-permute-start(bf16[128,384]{1,0:T(8,128)(2,1)S(1)} %add_convert_fusion.1.refs_0_), channel_id=1, source_target_pairs={{0,12},{4,8},{8,4},{12,0},{16,28},{20,24},{24,20},{28,16},{1,13},{... | collective-permute-start | bytes 294920 | tf_op jit(solution)/shard_map/ppermute | solution.py:387
  100.0 1.0 collective-permute-done.29.refs_3_
  101.0 1.5 %finish.2.refs_4_ = f32[1024,384]{1,0:T(8,128)} custom-call(s32[4]{0:T(128)S(1)} %iota_xor_fusion.1.ids_ref, bf16[128,384]{1,0:T(8,128)(2,1)S(1)} %add_convert_fusion.refs_0_, bf16[128,384]{1,0:T(8,128)(2,1)S(1)} %collective-permute-done.27.refs_1_, bf16[128,384]{1,0:T(8,128)(2,1)S(1)} %collective-permute-done.28.refs_2_, ...), custom_call_target="tpu_custom_call" | custom-call | bytes 3145728 | tf_op jit(solution)/shard_map/finish/pallas_call | solution.py:372
  102.5 0.1 collective-permute-done.23.refs_1_
  102.6 0.2 collective-permute-done.24.refs_2_
  102.8 0.9 collective-permute-done.25.refs_3_
  103.7 1.5 %finish.3 = f32[1024,384]{1,0:T(8,128)} custom-call(s32[4]{0:T(128)S(1)} %iota_xor_fusion.1.ids_ref, bf16[128,384]{1,0:T(8,128)(2,1)S(1)} %add_convert_fusion.1.refs_0_, bf16[128,384]{1,0:T(8,128)(2,1)S(1)} %collective-permute-done.23.refs_1_, bf16[128,384]{1,0:T(8,128)(2,1)S(1)} %collective-permute-done.24.refs_2_, ...), custom_call_target="tpu_custom_call", output_to_operand_aliasing={{}: (5, {})} | custom-call | bytes 3145728 | tf_op jit(solution)/shard_map/finish/pallas_call | solution.py:372
  (30 shorter events, 0.2 us)
Async XLA Ops:
  0.6 15.9 %copy-start.1 = (bf16[1024,384]{1,0:T(8,128)(2,1)S(1)}, bf16[1024,384]{1,0:T(8,128)(2,1)}, u32[]{:S(2)}) copy-start(bf16[1024,384]{1,0:T(8,128)(2,1)} %refs_0_.3) | copy-start | bytes 2359300
  0.6 13.6 %copy-start.2 = (bf16[1,256,128]{2,1,0:T(8,128)(2,1)S(1)}, bf16[1,256,128]{2,1,0:T(8,128)(2,1)}, u32[]{:S(2)}) copy-start(bf16[1,256,128]{2,1,0:T(8,128)(2,1)} %param.6) | copy-start | bytes 196612
  0.6 15.9 %collective-permute-start.5 = (bf16[1024,384]{1,0:T(8,128)(2,1)}, bf16[1024,384]{1,0:T(8,128)(2,1)S(1)}, u32[]{:S(2)}, u32[]{:S(2)}) collective-permute-start(bf16[1024,384]{1,0:T(8,128)(2,1)} %refs_0_.3), channel_id=1, source_target_pairs={{0,1},{1,0},{2,3},{3,2},{4,5},{5,4},{6,7},{7,6},{8,9},{9,8},{10,11... | collective-permute-start | bytes 2359304 | tf_op jit(solution)/shard_map/ppermute | solution.py:387
  1.2 20.9 %collective-permute-start = (bf16[1024,384]{1,0:T(8,128)(2,1)}, bf16[1024,384]{1,0:T(8,128)(2,1)S(1)}, u32[]{:S(2)}, u32[]{:S(2)}) collective-permute-start(bf16[1024,384]{1,0:T(8,128)(2,1)} %refs_0_.3), channel_id=1, source_target_pairs={{0,2},{1,3},{2,0},{3,1},{4,6},{5,7},{6,4},{7,5},{8,10},{9,11},{10,... | collective-permute-start | bytes 2359304 | tf_op jit(solution)/shard_map/ppermute | solution.py:387
  3.7 7.0 %collective-permute-start.1 = (bf16[256,128]{1,0:T(8,128)(2,1)}, bf16[256,128]{1,0:T(8,128)(2,1)S(1)}, u32[]{:S(2)}, u32[]{:S(2)}) collective-permute-start(bf16[256,128]{1,0:T(8,128)(2,1)} %bitcast.21), channel_id=1, source_target_pairs={{0,8},{4,12},{8,0},{12,4},{16,24},{20,28},{24,16},{28,20},{1,9},{5... | collective-permute-start | bytes 196616 | tf_op jit(solution)/shard_map/ppermute | solution.py:387
  5.3 7.8 %collective-permute-start.2 = (bf16[256,128]{1,0:T(8,128)(2,1)}, bf16[256,128]{1,0:T(8,128)(2,1)S(1)}, u32[]{:S(2)}, u32[]{:S(2)}) collective-permute-start(bf16[256,128]{1,0:T(8,128)(2,1)} %bitcast.22), channel_id=1, source_target_pairs={{0,16},{4,20},{8,24},{12,28},{16,0},{20,4},{24,8},{28,12},{1,17},{... | collective-permute-start | bytes 196616 | tf_op jit(solution)/shard_map/ppermute | solution.py:387
  7.9 6.4 %collective-permute-start.3 = (bf16[256,128]{1,0:T(8,128)(2,1)}, bf16[256,128]{1,0:T(8,128)(2,1)S(1)}, u32[]{:S(2)}, u32[]{:S(2)}) collective-permute-start(bf16[256,128]{1,0:T(8,128)(2,1)} %bitcast.23), channel_id=1, source_target_pairs={{0,24},{4,28},{8,16},{12,20},{16,8},{20,12},{24,0},{28,4},{1,25},{... | collective-permute-start | bytes 196616 | tf_op jit(solution)/shard_map/ppermute | solution.py:387
  10.1 0.7 copy-start.3
  15.0 7.0 %collective-permute-start.4 = (bf16[1024,128]{1,0:T(8,128)(2,1)}, bf16[1024,128]{1,0:T(8,128)(2,1)}, u32[]{:S(2)}, u32[]{:S(2)}) collective-permute-start(bf16[1024,128]{1,0:T(8,128)(2,1)} %pad_maximum_fusion.1), channel_id=1, source_target_pairs={{0,4},{4,0},{8,12},{12,8},{16,20},{20,16},{24,28},{28,24},{1,5},{5... | collective-permute-start | bytes 786440 | tf_op jit(solution)/shard_map/ppermute | solution.py:387
  22.1 3.4 %collective-permute-start.6 = (bf16[1024,384]{1,0:T(8,128)(2,1)S(1)}, bf16[1024,384]{1,0:T(8,128)(2,1)S(1)}, u32[]{:S(2)}, u32[]{:S(2)}) collective-permute-start(bf16[1024,384]{1,0:T(8,128)(2,1)S(1)} %collective-permute-done.refs_0_.refs_2_), channel_id=1, source_target_pairs={{0,1},{1,0},{2,3},{3,2},{4,5},{5,4},{6,7},{7,6},{8,9},{9,8},{10,11... | collective-permute-start | bytes 2359304 | tf_op jit(solution)/shard_map/ppermute | solution.py:387
  22.1 14.4 %collective-permute-start.10 = (bf16[256,1024]{1,0:T(8,128)(2,1)S(1)}, bf16[256,1024]{1,0:T(8,128)(2,1)S(1)}, u32[]{:S(2)}, u32[]{:S(2)}) collective-permute-start(bf16[256,1024]{1,0:T(8,128)(2,1)S(1)} %get-tuple-element.32), channel_id=1, source_target_pairs={{0,4},{4,0},{8,12},{12,8},{16,20},{20,16},{24,28},{28,24},{1,5},{5... | collective-permute-start | bytes 1572872 | tf_op jit(solution)/shard_map/ppermute | solution.py:387
  23.9 16.9 %collective-permute-start.12 = (bf16[160,1024]{1,0:T(8,128)(2,1)S(1)}, bf16[160,1024]{1,0:T(8,128)(2,1)S(1)}, u32[]{:S(2)}, u32[]{:S(2)}) collective-permute-start(bf16[160,1024]{1,0:T(8,128)(2,1)S(1)} %get-tuple-element.33), channel_id=1, source_target_pairs={{0,8},{4,12},{8,0},{12,4},{16,24},{20,28},{24,16},{28,20},{1,9},{5... | collective-permute-start | bytes 983048 | tf_op jit(solution)/shard_map/ppermute | solution.py:387
  27.9 29.6 %copy-start.4 = (bf16[96,1024]{1,0:T(8,128)(2,1)S(1)}, bf16[96,1024]{1,0:T(8,128)(2,1)}, u32[]{:S(2)}) copy-start(bf16[96,1024]{1,0:T(8,128)(2,1)} %copy-done.3) | copy-start | bytes 589828
  27.9 31.6 %copy-start.5 = (s32[1,8]{1,0:T(1,128)S(1)}, s32[1,8]{1,0:T(1,128)}, u32[]{:S(2)}) copy-start(s32[1,8]{1,0:T(1,128)} %pages_ref.1) | copy-start | bytes 100
  27.9 12.8 %collective-permute-start.7 = (bf16[256,256]{1,0:T(8,128)(2,1)S(1)}, bf16[256,256]{1,0:T(8,128)(2,1)S(1)}, u32[]{:S(2)}, u32[]{:S(2)}) collective-permute-start(bf16[256,256]{1,0:T(8,128)(2,1)S(1)} %get-tuple-element.44.refs_0_), channel_id=1, source_target_pairs={{0,8},{4,12},{8,0},{12,4},{16,24},{20,28},{24,16},{28,20},{1,9},{5... | collective-permute-start | bytes 393224 | tf_op jit(solution)/shard_map/ppermute | solution.py:387
  28.8 12.0 %collective-permute-start.8 = (bf16[256,256]{1,0:T(8,128)(2,1)S(1)}, bf16[256,256]{1,0:T(8,128)(2,1)S(1)}, u32[]{:S(2)}, u32[]{:S(2)}) collective-permute-start(bf16[256,256]{1,0:T(8,128)(2,1)S(1)} %get-tuple-element.44.refs_0_), channel_id=1, source_target_pairs={{0,16},{4,20},{8,24},{12,28},{16,0},{20,4},{24,8},{28,12},{1,17},{... | collective-permute-start | bytes 393224 | tf_op jit(solution)/shard_map/ppermute | solution.py:387
  31.4 12.8 %collective-permute-start.9 = (bf16[256,256]{1,0:T(8,128)(2,1)S(1)}, bf16[256,256]{1,0:T(8,128)(2,1)S(1)}, u32[]{:S(2)}, u32[]{:S(2)}) collective-permute-start(bf16[256,256]{1,0:T(8,128)(2,1)S(1)} %get-tuple-element.44.refs_0_), channel_id=1, source_target_pairs={{0,24},{4,28},{8,16},{12,20},{16,8},{20,12},{24,0},{28,4},{1,25},{... | collective-permute-start | bytes 393224 | tf_op jit(solution)/shard_map/ppermute | solution.py:387
  36.5 4.3 %collective-permute-start.11 = (bf16[256,128]{1,0:T(8,128)(2,1)S(1)}, bf16[256,128]{1,0:T(8,128)(2,1)S(1)}, u32[]{:S(2)}, u32[]{:S(2)}) collective-permute-start(bf16[256,128]{1,0:T(8,128)(2,1)S(1)} %get-tuple-element.43), channel_id=1, source_target_pairs={{0,4},{4,0},{8,12},{12,8},{16,20},{20,16},{24,28},{28,24},{1,5},{5... | collective-permute-start | bytes 196616 | tf_op jit(solution)/shard_map/ppermute | solution.py:387
  44.2 13.3 %collective-permute-start.13 = (bf16[1024,256]{1,0:T(8,128)(2,1)S(1)}, bf16[1024,256]{1,0:T(8,128)(2,1)S(1)}, u32[]{:S(2)}, u32[]{:S(2)}) collective-permute-start(bf16[1024,256]{1,0:T(8,128)(2,1)S(1)} %pad_maximum_fusion), channel_id=1, source_target_pairs={{0,4},{4,0},{8,12},{12,8},{16,20},{20,16},{24,28},{28,24},{1,5},{5... | collective-permute-start | bytes 1572872 | tf_op jit(solution)/shard_map/ppermute | solution.py:387
  44.9 6.5 %collective-permute-start.14 = (bf16[512,128]{1,0:T(8,128)(2,1)S(1)}, bf16[512,128]{1,0:T(8,128)(2,1)S(1)}, u32[]{:S(2)}, u32[]{:S(2)}) collective-permute-start(bf16[512,128]{1,0:T(8,128)(2,1)S(1)} %constant_dynamic-update-slice_fusion.refs_5_), channel_id=1, source_target_pairs={{0,8},{4,12},{8,0},{12,4},{16,24},{20,28},{24,16},{28,20},{1,9},{5... | collective-permute-start | bytes 393224 | tf_op jit(solution)/shard_map/ppermute | solution.py:387
  45.6 13.9 %collective-permute-start.15 = (bf16[512,128]{1,0:T(8,128)(2,1)S(1)}, bf16[512,128]{1,0:T(8,128)(2,1)S(1)}, u32[]{:S(2)}, u32[]{:S(2)}) collective-permute-start(bf16[512,128]{1,0:T(8,128)(2,1)S(1)} %constant_dynamic-update-slice_fusion.refs_5_), channel_id=1, source_target_pairs={{0,16},{4,20},{8,24},{12,28},{16,0},{20,4},{24,8},{28,12},{1,17},{... | collective-permute-start | bytes 393224 | tf_op jit(solution)/shard_map/ppermute | solution.py:387
  46.9 12.6 %collective-permute-start.16 = (bf16[512,128]{1,0:T(8,128)(2,1)S(1)}, bf16[512,128]{1,0:T(8,128)(2,1)S(1)}, u32[]{:S(2)}, u32[]{:S(2)}) collective-permute-start(bf16[512,128]{1,0:T(8,128)(2,1)S(1)} %constant_dynamic-update-slice_fusion.refs_5_), channel_id=1, source_target_pairs={{0,24},{4,28},{8,16},{12,20},{16,8},{20,12},{24,0},{28,4},{1,25},{... | collective-permute-start | bytes 393224 | tf_op jit(solution)/shard_map/ppermute | solution.py:387
  57.5 16.5 %collective-permute-start.18 = (bf16[256,1024]{1,0:T(8,128)(2,1)S(1)}, bf16[256,1024]{1,0:T(8,128)(2,1)S(1)}, u32[]{:S(2)}, u32[]{:S(2)}) collective-permute-start(bf16[256,1024]{1,0:T(8,128)(2,1)S(1)} %cut.3), channel_id=1, source_target_pairs={{0,12},{4,8},{8,4},{12,0},{16,28},{20,24},{24,20},{28,16},{1,13},{... | collective-permute-start | bytes 1572872 | tf_op jit(solution)/shard_map/ppermute | solution.py:387
  57.5 16.4 %collective-permute-start.17 = (bf16[96,1024]{1,0:T(8,128)(2,1)S(1)}, bf16[96,1024]{1,0:T(8,128)(2,1)S(1)}, u32[]{:S(2)}, u32[]{:S(2)}) collective-permute-start(bf16[96,1024]{1,0:T(8,128)(2,1)S(1)} %copy-done.4), channel_id=1, source_target_pairs={{0,8},{4,12},{8,0},{12,4},{16,24},{20,28},{24,16},{28,20},{1,9},{5... | collective-permute-start | bytes 589832 | tf_op jit(solution)/shard_map/ppermute | solution.py:387
  59.5 14.4 %copy-start = (bf16[1,256,4096]{2,1,0:T(8,128)(2,1)S(1)}, bf16[1,256,4096]{2,1,0:T(8,128)(2,1)}, u32[]{:S(2)}) copy-start(bf16[1,256,4096]{2,1,0:T(8,128)(2,1)} %param.4) | copy-start | bytes 6291460
  76.3 1.8 %collective-permute-start.19 = (bf16[2,256,384]{2,1,0:T(8,128)(2,1)S(1)}, bf16[2,256,384]{2,1,0:T(8,128)(2,1)S(1)}, u32[]{:S(2)}, u32[]{:S(2)}) collective-permute-start(bf16[2,256,384]{2,1,0:T(8,128)(2,1)S(1)} %get-tuple-element.52), channel_id=1, source_target_pairs={{0,1},{1,0},{2,3},{3,2},{4,5},{5,4},{6,7},{7,6},{8,9},{9,8},{10,11... | collective-permute-start | bytes 1179656 | tf_op jit(solution)/shard_map/ppermute | solution.py:387
  78.3 4.9 %collective-permute-start.20 = (bf16[128,384]{1,0:T(8,128)(2,1)S(1)}, bf16[128,384]{1,0:T(8,128)(2,1)S(1)}, u32[]{:S(2)}, u32[]{:S(2)}) collective-permute-start(bf16[128,384]{1,0:T(8,128)(2,1)S(1)} %get-tuple-element.64), channel_id=1, source_target_pairs={{0,2},{1,3},{2,0},{3,1},{4,6},{5,7},{6,4},{7,5},{8,10},{9,11},{10,... | collective-permute-start | bytes 294920 | tf_op jit(solution)/shard_map/ppermute | solution.py:387
  83.2 6.7 %collective-permute-start.21 = (bf16[128,384]{1,0:T(8,128)(2,1)S(1)}, bf16[128,384]{1,0:T(8,128)(2,1)S(1)}, u32[]{:S(2)}, u32[]{:S(2)}) collective-permute-start(bf16[128,384]{1,0:T(8,128)(2,1)S(1)} %get-tuple-element.53), channel_id=1, source_target_pairs={{0,2},{1,3},{2,0},{3,1},{4,6},{5,7},{6,4},{7,5},{8,10},{9,11},{10,... | collective-permute-start | bytes 294920 | tf_op jit(solution)/shard_map/ppermute | solution.py:387
  84.7 7.1 %collective-permute-start.26 = (bf16[128,384]{1,0:T(8,128)(2,1)S(1)}, bf16[128,384]{1,0:T(8,128)(2,1)S(1)}, u32[]{:S(2)}, u32[]{:S(2)}) collective-permute-start(bf16[128,384]{1,0:T(8,128)(2,1)S(1)} %fusion.1), channel_id=1, source_target_pairs={{0,16},{4,20},{8,24},{12,28},{16,0},{20,4},{24,8},{28,12},{1,17},{... | collective-permute-start | bytes 294920 | tf_op jit(solution)/shard_map/ppermute | solution.py:387
  89.9 6.5 %collective-permute-start.22 = (bf16[128,384]{1,0:T(8,128)(2,1)S(1)}, bf16[128,384]{1,0:T(8,128)(2,1)S(1)}, u32[]{:S(2)}, u32[]{:S(2)}) collective-permute-start(bf16[128,384]{1,0:T(8,128)(2,1)S(1)} %add_convert_fusion.2), channel_id=1, source_target_pairs={{0,16},{4,20},{8,24},{12,28},{16,0},{20,4},{24,8},{28,12},{1,17},{... | collective-permute-start | bytes 294920 | tf_op jit(solution)/shard_map/ppermute | solution.py:387
  91.8 6.3 %collective-permute-start.27 = (bf16[128,384]{1,0:T(8,128)(2,1)S(1)}, bf16[128,384]{1,0:T(8,128)(2,1)S(1)}, u32[]{:S(2)}, u32[]{:S(2)}) collective-permute-start(bf16[128,384]{1,0:T(8,128)(2,1)S(1)} %add_convert_fusion.refs_0_), channel_id=1, source_target_pairs={{0,4},{4,0},{8,12},{12,8},{16,20},{20,16},{24,28},{28,24},{1,5},{5... | collective-permute-start | bytes 294920 | tf_op jit(solution)/shard_map/ppermute | solution.py:387
  93.4 6.6 %collective-permute-start.28 = (bf16[128,384]{1,0:T(8,128)(2,1)S(1)}, bf16[128,384]{1,0:T(8,128)(2,1)S(1)}, u32[]{:S(2)}, u32[]{:S(2)}) collective-permute-start(bf16[128,384]{1,0:T(8,128)(2,1)S(1)} %add_convert_fusion.refs_0_), channel_id=1, source_target_pairs={{0,8},{4,12},{8,0},{12,4},{16,24},{20,28},{24,16},{28,20},{1,9},{5... | collective-permute-start | bytes 294920 | tf_op jit(solution)/shard_map/ppermute | solution.py:387
  93.4 7.6 %collective-permute-start.29 = (bf16[128,384]{1,0:T(8,128)(2,1)S(1)}, bf16[128,384]{1,0:T(8,128)(2,1)S(1)}, u32[]{:S(2)}, u32[]{:S(2)}) collective-permute-start(bf16[128,384]{1,0:T(8,128)(2,1)S(1)} %add_convert_fusion.refs_0_), channel_id=1, source_target_pairs={{0,12},{4,8},{8,4},{12,0},{16,28},{20,24},{24,20},{28,16},{1,13},{... | collective-permute-start | bytes 294920 | tf_op jit(solution)/shard_map/ppermute | solution.py:387
  96.4 6.2 %collective-permute-start.23 = (bf16[128,384]{1,0:T(8,128)(2,1)S(1)}, bf16[128,384]{1,0:T(8,128)(2,1)S(1)}, u32[]{:S(2)}, u32[]{:S(2)}) collective-permute-start(bf16[128,384]{1,0:T(8,128)(2,1)S(1)} %add_convert_fusion.1.refs_0_), channel_id=1, source_target_pairs={{0,4},{4,0},{8,12},{12,8},{16,20},{20,16},{24,28},{28,24},{1,5},{5... | collective-permute-start | bytes 294920 | tf_op jit(solution)/shard_map/ppermute | solution.py:387
  97.0 5.8 %collective-permute-start.24 = (bf16[128,384]{1,0:T(8,128)(2,1)S(1)}, bf16[128,384]{1,0:T(8,128)(2,1)S(1)}, u32[]{:S(2)}, u32[]{:S(2)}) collective-permute-start(bf16[128,384]{1,0:T(8,128)(2,1)S(1)} %add_convert_fusion.1.refs_0_), channel_id=1, source_target_pairs={{0,8},{4,12},{8,0},{12,4},{16,24},{20,28},{24,16},{28,20},{1,9},{5... | collective-permute-start | bytes 294920 | tf_op jit(solution)/shard_map/ppermute | solution.py:387
  98.2 5.5 %collective-permute-start.25 = (bf16[128,384]{1,0:T(8,128)(2,1)S(1)}, bf16[128,384]{1,0:T(8,128)(2,1)S(1)}, u32[]{:S(2)}, u32[]{:S(2)}) collective-permute-start(bf16[128,384]{1,0:T(8,128)(2,1)S(1)} %add_convert_fusion.1.refs_0_), channel_id=1, source_target_pairs={{0,12},{4,8},{8,4},{12,0},{16,28},{20,24},{24,20},{28,16},{1,13},{... | collective-permute-start | bytes 294920 | tf_op jit(solution)/shard_map/ppermute | solution.py:387

commit v8 on v7

--- a/solution.py
+++ b/solution.py
@@ -417,7 +417,7 @@
     weights = {0: [w_qkv], top: [swap(w_qkv, "fsdp", fsdp_size, top)]}
     near = rows * 5 // 8
     members = [(1, 0, rows), (2, 0, near), (2, near, rows - near)]
-    chunks = cut(group_ids, hidden, members, group, piece)
+    chunks = cut(group_ids, hidden, members[:2], group, piece)
     grads = [(grad_out, [0])]
     grads += spread(grads[0], ctx_size)
     moved = [swap(chunk, "ctx", ctx_size, k) for chunk, (k, *_) in zip(chunks[:2], members)]
@@ -445,9 +445,9 @@
     pair = jnp.concatenate([array for array, _ in v_pair], axis=0), [0, 1]
     vs = [pair, *spread(after(pair, qks[1:]), ctx_size)]
     qks.append(widen([after(qks[0], [pair, (moved[0], 0), (moved[1], 0)]), *qks[1:]], ctx_size))
-    moved.append(swap(after((chunks[2], 0), qks[1 : ctx_size // 2])[0], "ctx", ctx_size, 2))
     members.append((3, 0, rows))
-    (late,) = cut(group_ids, after((hidden, 0), [(qk, 0)])[0], members[3:], group, piece)
+    middle, late = cut(group_ids, after((hidden, 0), [(qk, 0)])[0], members[2:], group, piece)
+    moved.append(swap(after((middle, 0), qks[1 : ctx_size // 2])[0], "ctx", ctx_size, 2))
     moved.append(swap(after((late, 0), [qks[-1], vs[1]])[0], "ctx", ctx_size, 3))
     block = c.reshape(1).astype(jnp.int32)
     grad_near, grad_own = attend(block, page_tokens, [qks, vs, grads], ctx_size, group)

time: 106 us -> 105 us (level)
  transfers between devices with their start and end apart: 30 -> 30, of which waited for: 17 -> 16; matrix products, arithmetic and copies ran while one was open for 1% -> 1% of each run, Pallas kernels for 26% -> 27%
where the time goes in v8:
time: 105 us
  starting transfers between devices  39.5 us (38%)
  Pallas kernels  31.7 us (30%)
  waiting for transfers between devices  31.7 us (30%)
    ppermute x30, starting transfers between devices, swap(): return lax.ppermute(array, axis, [(i, i ^ distance) for i in range(size)])  39.5 us
    ppermute x30, waiting for transfers between devices, swap(): return lax.ppermute(array, axis, [(i, i ^ distance) for i in range(size)])  31.7 us
    pallas_call x2, Pallas kernels, pallas(): pl.pallas_call(kernel, out_shape=out_shape, in_specs=[SMEM] * len(scalars...  17.8 us
    pallas_call x2, Pallas kernels, project(): pl.pallas_call(functools.partial(project_kernel, parts, len(total)), out_...  4.93 us
    pallas_call x2, Pallas kernels, cut(): pl.pallas_call(functools.partial(cut_kernel, [(k, first) for k, first, _...  3.7 us
    pallas_call x2, Pallas kernels, finish(): pl.pallas_call(functools.partial(finish_kernel, group, piece, turn), out_...  2.91 us
    pallas_call x1, Pallas kernels, weight_grad(): pl.pallas_call(functools.partial(weight_kernel, group, piece, [(k, first)...  2.34 us
  transfers between devices with their start and end apart: 30, of which 16 were waited for; matrix products, arithmetic and copies ran while one was open for 1% of the time, Pallas kernels for 27%

profile of v8, /device:TPU:0, one launch (start us, length us, event | category | flops | bytes accessed | tf_op | source)
XLA Modules:
  0.0 104.9 jit_solution(1017556707241014870)
XLA Ops:
  0.6 0.5 collective-permute-start.5
  1.2 2.6 %collective-permute-start = (bf16[1024,384]{1,0:T(8,128)(2,1)}, bf16[1024,384]{1,0:T(8,128)(2,1)S(1)}, u32[]{:S(2)}, u32[]{:S(2)}) collective-permute-start(bf16[1024,384]{1,0:T(8,128)(2,1)} %refs_0_.3), channel_id=1, source_target_pairs={{0,2},{1,3},{2,0},{3,1},{4,6},{5,7},{6,4},{7,5},{8,10},{9,11},{10,... | collective-permute-start | bytes 2359304 | tf_op jit(solution)/shard_map/ppermute | solution.py:387
  3.7 3.6 %collective-permute-start.3 = (bf16[256,128]{1,0:T(8,128)(2,1)}, bf16[256,128]{1,0:T(8,128)(2,1)S(1)}, u32[]{:S(2)}, u32[]{:S(2)}) collective-permute-start(bf16[256,128]{1,0:T(8,128)(2,1)} %bitcast.21), channel_id=1, source_target_pairs={{0,24},{4,28},{8,16},{12,20},{16,8},{20,12},{24,0},{28,4},{1,25},{... | collective-permute-start | bytes 196616 | tf_op jit(solution)/shard_map/ppermute | solution.py:387
  7.3 0.8 collective-permute-start.1
  8.1 1.8 %cut.2 = (bf16[256,1024]{1,0:T(8,128)(2,1)S(1)}, bf16[160,1024]{1,0:T(8,128)(2,1)S(1)}) custom-call(s32[4]{0:T(128)S(1)} %iota_xor_fusion.1.ids_ref, bf16[256,4096]{1,0:T(8,128)(2,1)} %bitcast.16), custom_call_target="tpu_custom_call" | custom-call | bytes 2097152 | tf_op jit(solution)/shard_map/cut/pallas_call | solution.py:81
  10.0 0.3 collective-permute-done.3.refs_12_
  10.2 3.2 %collective-permute-done.2.refs_11_ = bf16[256,128]{1,0:T(8,128)(2,1)S(1)} collective-permute-done((bf16[256,128]{1,0:T(8,128)(2,1)}, bf16[256,128]{1,0:T(8,128)(2,1)S(1)}, u32[]{:S(2)}, u32[]{:S(2)}) %collective-permute-start.2) | collective-permute-done | bytes 65568 | tf_op jit(solution)/shard_map/ppermute | solution.py:387
  13.4 0.0 collective-permute-done.1.refs_10_
  13.4 0.7 pad_maximum_fusion.1
  14.2 1.5 %collective-permute-start.4 = (bf16[1024,128]{1,0:T(8,128)(2,1)}, bf16[1024,128]{1,0:T(8,128)(2,1)}, u32[]{:S(2)}, u32[]{:S(2)}) collective-permute-start(bf16[1024,128]{1,0:T(8,128)(2,1)} %pad_maximum_fusion.1), channel_id=1, source_target_pairs={{0,4},{4,0},{8,12},{12,8},{16,20},{20,16},{24,28},{28,24},{1,5},{5... | collective-permute-start | bytes 786440 | tf_op jit(solution)/shard_map/ppermute | solution.py:387
  15.7 0.0 collective-permute-done.5.refs_1_
  15.7 2.5 %project.2.refs_2_ = f32[256,384]{1,0:T(8,128)S(1)} custom-call(s32[4]{0:T(128)S(1)} %iota_xor_fusion.ids_ref.fsdp_ref, bf16[256,4096]{1,0:T(8,128)(2,1)} %bitcast.17, bf16[1024,384]{1,0:T(8,128)(2,1)S(1)} %copy-done.1, bf16[1024,384]{1,0:T(8,128)(2,1)S(1)} %collective-permute-done.5.refs_1_), custom_call_target="tpu_custom_call" | custom-call | flops 402653184 | bytes 4194304 | tf_op jit(solution)/shard_map/project/pallas_call | solution.py:130
  18.2 4.2 %collective-permute-done.4.refs_13_ = bf16[1024,128]{1,0:T(8,128)(2,1)} collective-permute-done((bf16[1024,128]{1,0:T(8,128)(2,1)}, bf16[1024,128]{1,0:T(8,128)(2,1)}, u32[]{:S(2)}, u32[]{:S(2)}) %collective-permute-start.4) | collective-permute-done | bytes 262176 | tf_op jit(solution)/shard_map/ppermute | solution.py:387
  22.4 0.0 collective-permute-done.refs_0_.refs_2_
  22.4 1.5 %collective-permute-start.10 = (bf16[256,1024]{1,0:T(8,128)(2,1)S(1)}, bf16[256,1024]{1,0:T(8,128)(2,1)S(1)}, u32[]{:S(2)}, u32[]{:S(2)}) collective-permute-start(bf16[256,1024]{1,0:T(8,128)(2,1)S(1)} %get-tuple-element.33), channel_id=1, source_target_pairs={{0,4},{4,0},{8,12},{12,8},{16,20},{20,16},{24,28},{28,24},{1,5},{5... | collective-permute-start | bytes 1572872 | tf_op jit(solution)/shard_map/ppermute | solution.py:387
  23.9 1.5 %collective-permute-start.12 = (bf16[160,1024]{1,0:T(8,128)(2,1)S(1)}, bf16[160,1024]{1,0:T(8,128)(2,1)S(1)}, u32[]{:S(2)}, u32[]{:S(2)}) collective-permute-start(bf16[160,1024]{1,0:T(8,128)(2,1)S(1)} %get-tuple-element.34), channel_id=1, source_target_pairs={{0,8},{4,12},{8,0},{12,4},{16,24},{20,28},{24,16},{28,20},{1,9},{5... | collective-permute-start | bytes 983048 | tf_op jit(solution)/shard_map/ppermute | solution.py:387
  25.4 0.0 collective-permute-done.6.refs_1_.refs_3_
  25.4 2.5 %project.3 = (bf16[256,256]{1,0:T(8,128)(2,1)S(1)}, bf16[256,128]{1,0:T(8,128)(2,1)S(1)}) custom-call(s32[4]{0:T(128)S(1)} %iota_xor_fusion.ids_ref.fsdp_ref, bf16[256,4096]{1,0:T(8,128)(2,1)} %bitcast.18, bf16[1024,384]{1,0:T(8,128)(2,1)S(1)} %collective-permute-done.refs_0_.refs_2_, bf16[1024,384]{1,0:T(8,128)(2,1)S(1)} %collective-permute-done.6.refs_1_.refs_3_, ...), custom_call_target="tpu_custom_call" | custom-call | flops 402653184 | bytes 4194304 | tf_op jit(solution)/shard_map/project/pallas_call | solution.py:130
  27.9 0.0 copy-start.3
  27.9 2.8 %collective-permute-start.9 = (bf16[256,256]{1,0:T(8,128)(2,1)S(1)}, bf16[256,256]{1,0:T(8,128)(2,1)S(1)}, u32[]{:S(2)}, u32[]{:S(2)}) collective-permute-start(bf16[256,256]{1,0:T(8,128)(2,1)S(1)} %get-tuple-element.44.refs_0_), channel_id=1, source_target_pairs={{0,24},{4,28},{8,16},{12,20},{16,8},{20,12},{24,0},{28,4},{1,25},{... | collective-permute-start | bytes 393224 | tf_op jit(solution)/shard_map/ppermute | solution.py:387
  30.8 1.6 %collective-permute-start.7 = (bf16[256,256]{1,0:T(8,128)(2,1)S(1)}, bf16[256,256]{1,0:T(8,128)(2,1)S(1)}, u32[]{:S(2)}, u32[]{:S(2)}) collective-permute-start(bf16[256,256]{1,0:T(8,128)(2,1)S(1)} %get-tuple-element.44.refs_0_), channel_id=1, source_target_pairs={{0,8},{4,12},{8,0},{12,4},{16,24},{20,28},{24,16},{28,20},{1,9},{5... | collective-permute-start | bytes 393224 | tf_op jit(solution)/shard_map/ppermute | solution.py:387
  32.4 4.4 %collective-permute-done.10.refs_0_ = bf16[256,1024]{1,0:T(8,128)(2,1)S(1)} collective-permute-done((bf16[256,1024]{1,0:T(8,128)(2,1)S(1)}, bf16[256,1024]{1,0:T(8,128)(2,1)S(1)}, u32[]{:S(2)}, u32[]{:S(2)}) %collective-permute-start.10) | collective-permute-done | bytes 524320 | tf_op jit(solution)/shard_map/ppermute | solution.py:387
  36.7 1.5 %collective-permute-start.11 = (bf16[256,128]{1,0:T(8,128)(2,1)S(1)}, bf16[256,128]{1,0:T(8,128)(2,1)S(1)}, u32[]{:S(2)}, u32[]{:S(2)}) collective-permute-start(bf16[256,128]{1,0:T(8,128)(2,1)S(1)} %get-tuple-element.43), channel_id=1, source_target_pairs={{0,4},{4,0},{8,12},{12,8},{16,20},{20,16},{24,28},{28,24},{1,5},{5... | collective-permute-start | bytes 196616 | tf_op jit(solution)/shard_map/ppermute | solution.py:387
  38.3 2.7 %collective-permute-done.11 = bf16[256,128]{1,0:T(8,128)(2,1)S(1)} collective-permute-done((bf16[256,128]{1,0:T(8,128)(2,1)S(1)}, bf16[256,128]{1,0:T(8,128)(2,1)S(1)}, u32[]{:S(2)}, u32[]{:S(2)}) %collective-permute-start.11) | collective-permute-done | bytes 65568 | tf_op jit(solution)/shard_map/ppermute | solution.py:387
  41.0 0.0 collective-permute-done.12.refs_1_
  41.0 0.0 collective-permute-done.9.refs_3_
  41.0 1.6 %collective-permute-done.8.refs_2_ = bf16[256,256]{1,0:T(8,128)(2,1)S(1)} collective-permute-done((bf16[256,256]{1,0:T(8,128)(2,1)S(1)}, bf16[256,256]{1,0:T(8,128)(2,1)S(1)}, u32[]{:S(2)}, u32[]{:S(2)}) %collective-permute-start.8) | collective-permute-done | bytes 131104 | tf_op jit(solution)/shard_map/ppermute | solution.py:387
  42.7 0.0 collective-permute-done.7.refs_1_
  42.7 1.5 %collective-permute-start.13 = (bf16[1024,256]{1,0:T(8,128)(2,1)S(1)}, bf16[1024,256]{1,0:T(8,128)(2,1)S(1)}, u32[]{:S(2)}, u32[]{:S(2)}) collective-permute-start(bf16[1024,256]{1,0:T(8,128)(2,1)S(1)} %pad_maximum_fusion), channel_id=1, source_target_pairs={{0,4},{4,0},{8,12},{12,8},{16,20},{20,16},{24,28},{28,24},{1,5},{5... | collective-permute-start | bytes 1572872 | tf_op jit(solution)/shard_map/ppermute | solution.py:387
  44.2 0.2 collective-permute-start.14
  44.4 2.4 %collective-permute-start.16 = (bf16[512,128]{1,0:T(8,128)(2,1)S(1)}, bf16[512,128]{1,0:T(8,128)(2,1)S(1)}, u32[]{:S(2)}, u32[]{:S(2)}) collective-permute-start(bf16[512,128]{1,0:T(8,128)(2,1)S(1)} %constant_dynamic-update-slice_fusion.refs_5_), channel_id=1, source_target_pairs={{0,24},{4,28},{8,16},{12,20},{16,8},{20,12},{24,0},{28,4},{1,25},{... | collective-permute-start | bytes 393224 | tf_op jit(solution)/shard_map/ppermute | solution.py:387
  46.8 0.9 collective-permute-start.15
  47.7 1.9 %cut.3 = (bf16[96,1024]{1,0:T(8,128)(2,1)S(1)}, bf16[256,1024]{1,0:T(8,128)(2,1)S(1)}) custom-call(s32[4]{0:T(128)S(1)} %iota_xor_fusion.1.ids_ref, bf16[256,4096]{1,0:T(8,128)(2,1)} %bitcast.19), custom_call_target="tpu_custom_call" | custom-call | bytes 2097152 | tf_op jit(solution)/shard_map/cut/pallas_call | solution.py:81
  49.5 1.1 %collective-permute-done.14.refs_6_ = bf16[512,128]{1,0:T(8,128)(2,1)S(1)} collective-permute-done((bf16[512,128]{1,0:T(8,128)(2,1)S(1)}, bf16[512,128]{1,0:T(8,128)(2,1)S(1)}, u32[]{:S(2)}, u32[]{:S(2)}) %collective-permute-start.14) | collective-permute-done | bytes 131104 | tf_op jit(solution)/shard_map/ppermute | solution.py:387
  50.6 5.1 %collective-permute-done.13.refs_4_ = bf16[1024,256]{1,0:T(8,128)(2,1)S(1)} collective-permute-done((bf16[1024,256]{1,0:T(8,128)(2,1)S(1)}, bf16[1024,256]{1,0:T(8,128)(2,1)S(1)}, u32[]{:S(2)}, u32[]{:S(2)}) %collective-permute-start.13) | collective-permute-done | bytes 524320 | tf_op jit(solution)/shard_map/ppermute | solution.py:387
  55.8 1.3 %collective-permute-start.18 = (bf16[256,1024]{1,0:T(8,128)(2,1)S(1)}, bf16[256,1024]{1,0:T(8,128)(2,1)S(1)}, u32[]{:S(2)}, u32[]{:S(2)}) collective-permute-start(bf16[256,1024]{1,0:T(8,128)(2,1)S(1)} %get-tuple-element.52), channel_id=1, source_target_pairs={{0,12},{4,8},{8,4},{12,0},{16,28},{20,24},{24,20},{28,16},{1,13},{... | collective-permute-start | bytes 1572872 | tf_op jit(solution)/shard_map/ppermute | solution.py:387
  57.0 1.9 %collective-permute-start.17 = (bf16[96,1024]{1,0:T(8,128)(2,1)S(1)}, bf16[96,1024]{1,0:T(8,128)(2,1)S(1)}, u32[]{:S(2)}, u32[]{:S(2)}) collective-permute-start(bf16[96,1024]{1,0:T(8,128)(2,1)S(1)} %get-tuple-element.50), channel_id=1, source_target_pairs={{0,8},{4,12},{8,0},{12,4},{16,24},{20,28},{24,16},{28,20},{1,9},{5... | collective-permute-start | bytes 589832 | tf_op jit(solution)/shard_map/ppermute | solution.py:387
  59.0 0.0 collective-permute-done.16.refs_8_
  59.0 0.0 copy-start
  59.0 13.8 %attend.1 = (bf16[1024,384]{1,0:T(8,128)(2,1)S(1)}, bf16[256,384]{1,0:T(8,128)(2,1)S(1)}) custom-call(s32[1]{0:T(128)} %bitcast.block_ref, s32[1,8]{1,0:T(1,128)S(1)} %copy-done.3, bf16[256,256]{1,0:T(8,128)(2,1)S(1)} %get-tuple-element.44.refs_0_, bf16[256,256]{1,0:T(8,128)(2,1)S(1)} %collective-permute-done.7.refs_1_, ...), custom_call_target="tpu_custom_call" | custom-call | flops 5368709120 | bytes 3080192 | tf_op jit(solution)/shard_map/attend/pallas_call | solution.py:35
  72.8 1.0 collective-permute-done.17.refs_2_
  73.9 0.0 collective-permute-done.18.refs_3_
  73.9 2.3 %weight_grad.1 = (f32[2,256,384]{2,1,0:T(8,128)S(1)}, bf16[2,256,384]{2,1,0:T(8,128)(2,1)S(1)}) custom-call(s32[4]{0:T(128)S(1)} %iota_xor_fusion.1.ids_ref, s32[4]{0:T(128)S(1)} %iota_xor_fusion.ids_ref.fsdp_ref, bf16[1024,384]{1,0:T(8,128)(2,1)S(1)} %get-tuple-element.47.grad_ref, bf16[256,4096]{1,0:T(8,128)(2,1)S(1)} %bitcast.20, ...), custom_call_target="tpu_custom_call" | custom-call | flops 805306368 | bytes 8388608 | tf_op jit(solution)/shard_map/weight_grad/pallas_call | solution.py:335
  76.2 0.1 collective-permute-start.19
  76.3 1.7 %collective-permute-done.19 = bf16[2,256,384]{2,1,0:T(8,128)(2,1)S(1)} collective-permute-done((bf16[2,256,384]{2,1,0:T(8,128)(2,1)S(1)}, bf16[2,256,384]{2,1,0:T(8,128)(2,1)S(1)}, u32[]{:S(2)}, u32[]{:S(2)}) %collective-permute-start.19) | collective-permute-done | bytes 393248 | tf_op jit(solution)/shard_map/ppermute | solution.py:387
  78.0 0.1 fusion.2
  78.1 1.6 %collective-permute-start.20 = (bf16[128,384]{1,0:T(8,128)(2,1)S(1)}, bf16[128,384]{1,0:T(8,128)(2,1)S(1)}, u32[]{:S(2)}, u32[]{:S(2)}) collective-permute-start(bf16[128,384]{1,0:T(8,128)(2,1)S(1)} %get-tuple-element.66), channel_id=1, source_target_pairs={{0,2},{1,3},{2,0},{3,1},{4,6},{5,7},{6,4},{7,5},{8,10},{9,11},{10,... | collective-permute-start | bytes 294920 | tf_op jit(solution)/shard_map/ppermute | solution.py:387
  79.7 3.3 %collective-permute-done.20 = bf16[128,384]{1,0:T(8,128)(2,1)S(1)} collective-permute-done((bf16[128,384]{1,0:T(8,128)(2,1)S(1)}, bf16[128,384]{1,0:T(8,128)(2,1)S(1)}, u32[]{:S(2)}, u32[]{:S(2)}) %collective-permute-start.20) | collective-permute-done | bytes 98336 | tf_op jit(solution)/shard_map/ppermute | solution.py:387
  83.0 1.5 %collective-permute-start.21 = (bf16[128,384]{1,0:T(8,128)(2,1)S(1)}, bf16[128,384]{1,0:T(8,128)(2,1)S(1)}, u32[]{:S(2)}, u32[]{:S(2)}) collective-permute-start(bf16[128,384]{1,0:T(8,128)(2,1)S(1)} %get-tuple-element.55), channel_id=1, source_target_pairs={{0,2},{1,3},{2,0},{3,1},{4,6},{5,7},{6,4},{7,5},{8,10},{9,11},{10,... | collective-permute-start | bytes 294920 | tf_op jit(solution)/shard_map/ppermute | solution.py:387
  84.6 0.7 collective-permute-start.26
  85.3 4.0 %hidden_grad.1 = bf16[256,4096]{1,0:T(8,128)(2,1)} custom-call(s32[4]{0:T(128)S(1)} %iota_xor_fusion.ids_ref.fsdp_ref, bf16[256,384]{1,0:T(8,128)(2,1)S(1)} %get-tuple-element.59.grad_ref, bf16[1024,384]{1,0:T(8,128)(2,1)S(1)} %copy-done.1, bf16[1024,384]{1,0:T(8,128)(2,1)S(1)} %collective-permute-done.5.refs_1_, ...), custom_call_target="tpu_custom_call" | custom-call | flops 805306368 | bytes 5439488 | tf_op jit(solution)/shard_map/hidden_grad/pallas_call | solution.py:35
  89.3 2.3 %collective-permute-start.22 = (bf16[128,384]{1,0:T(8,128)(2,1)S(1)}, bf16[128,384]{1,0:T(8,128)(2,1)S(1)}, u32[]{:S(2)}, u32[]{:S(2)}) collective-permute-start(bf16[128,384]{1,0:T(8,128)(2,1)S(1)} %add_convert_fusion.2), channel_id=1, source_target_pairs={{0,16},{4,20},{8,24},{12,28},{16,0},{20,4},{24,8},{28,12},{1,17},{... | collective-permute-start | bytes 294920 | tf_op jit(solution)/shard_map/ppermute | solution.py:387
  91.7 0.7 collective-permute-start.29
  92.4 1.7 %collective-permute-start.28 = (bf16[128,384]{1,0:T(8,128)(2,1)S(1)}, bf16[128,384]{1,0:T(8,128)(2,1)S(1)}, u32[]{:S(2)}, u32[]{:S(2)}) collective-permute-start(bf16[128,384]{1,0:T(8,128)(2,1)S(1)} %add_convert_fusion.refs_0_), channel_id=1, source_target_pairs={{0,8},{4,12},{8,0},{12,4},{16,24},{20,28},{24,16},{28,20},{1,9},{5... | collective-permute-start | bytes 294920 | tf_op jit(solution)/shard_map/ppermute | solution.py:387
  94.1 1.2 %collective-permute-start.27 = (bf16[128,384]{1,0:T(8,128)(2,1)S(1)}, bf16[128,384]{1,0:T(8,128)(2,1)S(1)}, u32[]{:S(2)}, u32[]{:S(2)}) collective-permute-start(bf16[128,384]{1,0:T(8,128)(2,1)S(1)} %add_convert_fusion.refs_0_), channel_id=1, source_target_pairs={{0,4},{4,0},{8,12},{12,8},{16,20},{20,16},{24,28},{28,24},{1,5},{5... | collective-permute-start | bytes 294920 | tf_op jit(solution)/shard_map/ppermute | solution.py:387
  95.3 3.1 %collective-permute-start.25 = (bf16[128,384]{1,0:T(8,128)(2,1)S(1)}, bf16[128,384]{1,0:T(8,128)(2,1)S(1)}, u32[]{:S(2)}, u32[]{:S(2)}) collective-permute-start(bf16[128,384]{1,0:T(8,128)(2,1)S(1)} %add_convert_fusion.1.refs_0_), channel_id=1, source_target_pairs={{0,12},{4,8},{8,4},{12,0},{16,28},{20,24},{24,20},{28,16},{1,13},{... | collective-permute-start | bytes 294920 | tf_op jit(solution)/shard_map/ppermute | solution.py:387
  98.4 0.1 collective-permute-done.29.refs_3_
  98.5 0.6 collective-permute-start.23
  99.1 0.3 collective-permute-done.28.refs_2_
  99.4 2.0 %collective-permute-done.27.refs_1_ = bf16[128,384]{1,0:T(8,128)(2,1)S(1)} collective-permute-done((bf16[128,384]{1,0:T(8,128)(2,1)S(1)}, bf16[128,384]{1,0:T(8,128)(2,1)S(1)}, u32[]{:S(2)}, u32[]{:S(2)}) %collective-permute-start.27) | collective-permute-done | bytes 98336 | tf_op jit(solution)/shard_map/ppermute | solution.py:387
  101.4 1.5 %finish.2.refs_4_ = f32[1024,384]{1,0:T(8,128)} custom-call(s32[4]{0:T(128)S(1)} %iota_xor_fusion.1.ids_ref, bf16[128,384]{1,0:T(8,128)(2,1)S(1)} %add_convert_fusion.refs_0_, bf16[128,384]{1,0:T(8,128)(2,1)S(1)} %collective-permute-done.27.refs_1_, bf16[128,384]{1,0:T(8,128)(2,1)S(1)} %collective-permute-done.28.refs_2_, ...), custom_call_target="tpu_custom_call" | custom-call | bytes 3145728 | tf_op jit(solution)/shard_map/finish/pallas_call | solution.py:372
  102.9 0.1 collective-permute-done.24.refs_2_
  103.0 0.4 collective-permute-done.23.refs_1_
  103.3 1.5 %finish.3 = f32[1024,384]{1,0:T(8,128)} custom-call(s32[4]{0:T(128)S(1)} %iota_xor_fusion.1.ids_ref, bf16[128,384]{1,0:T(8,128)(2,1)S(1)} %add_convert_fusion.1.refs_0_, bf16[128,384]{1,0:T(8,128)(2,1)S(1)} %collective-permute-done.23.refs_1_, bf16[128,384]{1,0:T(8,128)(2,1)S(1)} %collective-permute-done.24.refs_2_, ...), custom_call_target="tpu_custom_call", output_to_operand_aliasing={{}: (5, {})} | custom-call | bytes 3145728 | tf_op jit(solution)/shard_map/finish/pallas_call | solution.py:372
  (26 shorter events, 0.2 us)
Async XLA Ops:
  0.6 15.1 %copy-start.1 = (bf16[1024,384]{1,0:T(8,128)(2,1)S(1)}, bf16[1024,384]{1,0:T(8,128)(2,1)}, u32[]{:S(2)}) copy-start(bf16[1024,384]{1,0:T(8,128)(2,1)} %refs_0_.3) | copy-start | bytes 2359300
  0.6 12.8 %copy-start.2 = (bf16[1,256,128]{2,1,0:T(8,128)(2,1)S(1)}, bf16[1,256,128]{2,1,0:T(8,128)(2,1)}, u32[]{:S(2)}) copy-start(bf16[1,256,128]{2,1,0:T(8,128)(2,1)} %param.6) | copy-start | bytes 196612
  0.6 15.0 %collective-permute-start.5 = (bf16[1024,384]{1,0:T(8,128)(2,1)}, bf16[1024,384]{1,0:T(8,128)(2,1)S(1)}, u32[]{:S(2)}, u32[]{:S(2)}) collective-permute-start(bf16[1024,384]{1,0:T(8,128)(2,1)} %refs_0_.3), channel_id=1, source_target_pairs={{0,1},{1,0},{2,3},{3,2},{4,5},{5,4},{6,7},{7,6},{8,9},{9,8},{10,11... | collective-permute-start | bytes 2359304 | tf_op jit(solution)/shard_map/ppermute | solution.py:387
  1.2 21.2 %collective-permute-start = (bf16[1024,384]{1,0:T(8,128)(2,1)}, bf16[1024,384]{1,0:T(8,128)(2,1)S(1)}, u32[]{:S(2)}, u32[]{:S(2)}) collective-permute-start(bf16[1024,384]{1,0:T(8,128)(2,1)} %refs_0_.3), channel_id=1, source_target_pairs={{0,2},{1,3},{2,0},{3,1},{4,6},{5,7},{6,4},{7,5},{8,10},{9,11},{10,... | collective-permute-start | bytes 2359304 | tf_op jit(solution)/shard_map/ppermute | solution.py:387
  3.7 6.5 %collective-permute-start.3 = (bf16[256,128]{1,0:T(8,128)(2,1)}, bf16[256,128]{1,0:T(8,128)(2,1)S(1)}, u32[]{:S(2)}, u32[]{:S(2)}) collective-permute-start(bf16[256,128]{1,0:T(8,128)(2,1)} %bitcast.21), channel_id=1, source_target_pairs={{0,24},{4,28},{8,16},{12,20},{16,8},{20,12},{24,0},{28,4},{1,25},{... | collective-permute-start | bytes 196616 | tf_op jit(solution)/shard_map/ppermute | solution.py:387
  7.3 6.1 %collective-permute-start.2 = (bf16[256,128]{1,0:T(8,128)(2,1)}, bf16[256,128]{1,0:T(8,128)(2,1)S(1)}, u32[]{:S(2)}, u32[]{:S(2)}) collective-permute-start(bf16[256,128]{1,0:T(8,128)(2,1)} %bitcast.22), channel_id=1, source_target_pairs={{0,16},{4,20},{8,24},{12,28},{16,0},{20,4},{24,8},{28,12},{1,17},{... | collective-permute-start | bytes 196616 | tf_op jit(solution)/shard_map/ppermute | solution.py:387
  7.3 6.1 %collective-permute-start.1 = (bf16[256,128]{1,0:T(8,128)(2,1)}, bf16[256,128]{1,0:T(8,128)(2,1)S(1)}, u32[]{:S(2)}, u32[]{:S(2)}) collective-permute-start(bf16[256,128]{1,0:T(8,128)(2,1)} %bitcast.23), channel_id=1, source_target_pairs={{0,8},{4,12},{8,0},{12,4},{16,24},{20,28},{24,16},{28,20},{1,9},{5... | collective-permute-start | bytes 196616 | tf_op jit(solution)/shard_map/ppermute | solution.py:387
  14.2 8.2 %collective-permute-start.4 = (bf16[1024,128]{1,0:T(8,128)(2,1)}, bf16[1024,128]{1,0:T(8,128)(2,1)}, u32[]{:S(2)}, u32[]{:S(2)}) collective-permute-start(bf16[1024,128]{1,0:T(8,128)(2,1)} %pad_maximum_fusion.1), channel_id=1, source_target_pairs={{0,4},{4,0},{8,12},{12,8},{16,20},{20,16},{24,28},{28,24},{1,5},{5... | collective-permute-start | bytes 786440 | tf_op jit(solution)/shard_map/ppermute | solution.py:387
  22.4 3.0 %collective-permute-start.6 = (bf16[1024,384]{1,0:T(8,128)(2,1)S(1)}, bf16[1024,384]{1,0:T(8,128)(2,1)S(1)}, u32[]{:S(2)}, u32[]{:S(2)}) collective-permute-start(bf16[1024,384]{1,0:T(8,128)(2,1)S(1)} %collective-permute-done.refs_0_.refs_2_), channel_id=1, source_target_pairs={{0,1},{1,0},{2,3},{3,2},{4,5},{5,4},{6,7},{7,6},{8,9},{9,8},{10,11... | collective-permute-start | bytes 2359304 | tf_op jit(solution)/shard_map/ppermute | solution.py:387
  22.4 14.3 %collective-permute-start.10 = (bf16[256,1024]{1,0:T(8,128)(2,1)S(1)}, bf16[256,1024]{1,0:T(8,128)(2,1)S(1)}, u32[]{:S(2)}, u32[]{:S(2)}) collective-permute-start(bf16[256,1024]{1,0:T(8,128)(2,1)S(1)} %get-tuple-element.33), channel_id=1, source_target_pairs={{0,4},{4,0},{8,12},{12,8},{16,20},{20,16},{24,28},{28,24},{1,5},{5... | collective-permute-start | bytes 1572872 | tf_op jit(solution)/shard_map/ppermute | solution.py:387
  23.9 17.1 %collective-permute-start.12 = (bf16[160,1024]{1,0:T(8,128)(2,1)S(1)}, bf16[160,1024]{1,0:T(8,128)(2,1)S(1)}, u32[]{:S(2)}, u32[]{:S(2)}) collective-permute-start(bf16[160,1024]{1,0:T(8,128)(2,1)S(1)} %get-tuple-element.34), channel_id=1, source_target_pairs={{0,8},{4,12},{8,0},{12,4},{16,24},{20,28},{24,16},{28,20},{1,9},{5... | collective-permute-start | bytes 983048 | tf_op jit(solution)/shard_map/ppermute | solution.py:387
  27.9 31.1 %copy-start.3 = (s32[1,8]{1,0:T(1,128)S(1)}, s32[1,8]{1,0:T(1,128)}, u32[]{:S(2)}) copy-start(s32[1,8]{1,0:T(1,128)} %pages_ref.1) | copy-start | bytes 100
  27.9 13.1 %collective-permute-start.9 = (bf16[256,256]{1,0:T(8,128)(2,1)S(1)}, bf16[256,256]{1,0:T(8,128)(2,1)S(1)}, u32[]{:S(2)}, u32[]{:S(2)}) collective-permute-start(bf16[256,256]{1,0:T(8,128)(2,1)S(1)} %get-tuple-element.44.refs_0_), channel_id=1, source_target_pairs={{0,24},{4,28},{8,16},{12,20},{16,8},{20,12},{24,0},{28,4},{1,25},{... | collective-permute-start | bytes 393224 | tf_op jit(solution)/shard_map/ppermute | solution.py:387
  30.8 11.9 %collective-permute-start.8 = (bf16[256,256]{1,0:T(8,128)(2,1)S(1)}, bf16[256,256]{1,0:T(8,128)(2,1)S(1)}, u32[]{:S(2)}, u32[]{:S(2)}) collective-permute-start(bf16[256,256]{1,0:T(8,128)(2,1)S(1)} %get-tuple-element.44.refs_0_), channel_id=1, source_target_pairs={{0,16},{4,20},{8,24},{12,28},{16,0},{20,4},{24,8},{28,12},{1,17},{... | collective-permute-start | bytes 393224 | tf_op jit(solution)/shard_map/ppermute | solution.py:387
  30.8 11.9 %collective-permute-start.7 = (bf16[256,256]{1,0:T(8,128)(2,1)S(1)}, bf16[256,256]{1,0:T(8,128)(2,1)S(1)}, u32[]{:S(2)}, u32[]{:S(2)}) collective-permute-start(bf16[256,256]{1,0:T(8,128)(2,1)S(1)} %get-tuple-element.44.refs_0_), channel_id=1, source_target_pairs={{0,8},{4,12},{8,0},{12,4},{16,24},{20,28},{24,16},{28,20},{1,9},{5... | collective-permute-start | bytes 393224 | tf_op jit(solution)/shard_map/ppermute | solution.py:387
  36.7 4.3 %collective-permute-start.11 = (bf16[256,128]{1,0:T(8,128)(2,1)S(1)}, bf16[256,128]{1,0:T(8,128)(2,1)S(1)}, u32[]{:S(2)}, u32[]{:S(2)}) collective-permute-start(bf16[256,128]{1,0:T(8,128)(2,1)S(1)} %get-tuple-element.43), channel_id=1, source_target_pairs={{0,4},{4,0},{8,12},{12,8},{16,20},{20,16},{24,28},{28,24},{1,5},{5... | collective-permute-start | bytes 196616 | tf_op jit(solution)/shard_map/ppermute | solution.py:387
  42.7 13.1 %collective-permute-start.13 = (bf16[1024,256]{1,0:T(8,128)(2,1)S(1)}, bf16[1024,256]{1,0:T(8,128)(2,1)S(1)}, u32[]{:S(2)}, u32[]{:S(2)}) collective-permute-start(bf16[1024,256]{1,0:T(8,128)(2,1)S(1)} %pad_maximum_fusion), channel_id=1, source_target_pairs={{0,4},{4,0},{8,12},{12,8},{16,20},{20,16},{24,28},{28,24},{1,5},{5... | collective-permute-start | bytes 1572872 | tf_op jit(solution)/shard_map/ppermute | solution.py:387
  44.2 6.5 %collective-permute-start.14 = (bf16[512,128]{1,0:T(8,128)(2,1)S(1)}, bf16[512,128]{1,0:T(8,128)(2,1)S(1)}, u32[]{:S(2)}, u32[]{:S(2)}) collective-permute-start(bf16[512,128]{1,0:T(8,128)(2,1)S(1)} %constant_dynamic-update-slice_fusion.refs_5_), channel_id=1, source_target_pairs={{0,8},{4,12},{8,0},{12,4},{16,24},{20,28},{24,16},{28,20},{1,9},{5... | collective-permute-start | bytes 393224 | tf_op jit(solution)/shard_map/ppermute | solution.py:387
  44.4 14.6 %collective-permute-start.16 = (bf16[512,128]{1,0:T(8,128)(2,1)S(1)}, bf16[512,128]{1,0:T(8,128)(2,1)S(1)}, u32[]{:S(2)}, u32[]{:S(2)}) collective-permute-start(bf16[512,128]{1,0:T(8,128)(2,1)S(1)} %constant_dynamic-update-slice_fusion.refs_5_), channel_id=1, source_target_pairs={{0,24},{4,28},{8,16},{12,20},{16,8},{20,12},{24,0},{28,4},{1,25},{... | collective-permute-start | bytes 393224 | tf_op jit(solution)/shard_map/ppermute | solution.py:387
  46.8 12.2 %collective-permute-start.15 = (bf16[512,128]{1,0:T(8,128)(2,1)S(1)}, bf16[512,128]{1,0:T(8,128)(2,1)S(1)}, u32[]{:S(2)}, u32[]{:S(2)}) collective-permute-start(bf16[512,128]{1,0:T(8,128)(2,1)S(1)} %constant_dynamic-update-slice_fusion.refs_5_), channel_id=1, source_target_pairs={{0,16},{4,20},{8,24},{12,28},{16,0},{20,4},{24,8},{28,12},{1,17},{... | collective-permute-start | bytes 393224 | tf_op jit(solution)/shard_map/ppermute | solution.py:387
  55.8 18.1 %collective-permute-start.18 = (bf16[256,1024]{1,0:T(8,128)(2,1)S(1)}, bf16[256,1024]{1,0:T(8,128)(2,1)S(1)}, u32[]{:S(2)}, u32[]{:S(2)}) collective-permute-start(bf16[256,1024]{1,0:T(8,128)(2,1)S(1)} %get-tuple-element.52), channel_id=1, source_target_pairs={{0,12},{4,8},{8,4},{12,0},{16,28},{20,24},{24,20},{28,16},{1,13},{... | collective-permute-start | bytes 1572872 | tf_op jit(solution)/shard_map/ppermute | solution.py:387
  57.0 16.8 %collective-permute-start.17 = (bf16[96,1024]{1,0:T(8,128)(2,1)S(1)}, bf16[96,1024]{1,0:T(8,128)(2,1)S(1)}, u32[]{:S(2)}, u32[]{:S(2)}) collective-permute-start(bf16[96,1024]{1,0:T(8,128)(2,1)S(1)} %get-tuple-element.50), channel_id=1, source_target_pairs={{0,8},{4,12},{8,0},{12,4},{16,24},{20,28},{24,16},{28,20},{1,9},{5... | collective-permute-start | bytes 589832 | tf_op jit(solution)/shard_map/ppermute | solution.py:387
  59.0 14.9 %copy-start = (bf16[1,256,4096]{2,1,0:T(8,128)(2,1)S(1)}, bf16[1,256,4096]{2,1,0:T(8,128)(2,1)}, u32[]{:S(2)}) copy-start(bf16[1,256,4096]{2,1,0:T(8,128)(2,1)} %param.4) | copy-start | bytes 6291460
  76.2 1.8 %collective-permute-start.19 = (bf16[2,256,384]{2,1,0:T(8,128)(2,1)S(1)}, bf16[2,256,384]{2,1,0:T(8,128)(2,1)S(1)}, u32[]{:S(2)}, u32[]{:S(2)}) collective-permute-start(bf16[2,256,384]{2,1,0:T(8,128)(2,1)S(1)} %get-tuple-element.54), channel_id=1, source_target_pairs={{0,1},{1,0},{2,3},{3,2},{4,5},{5,4},{6,7},{7,6},{8,9},{9,8},{10,11... | collective-permute-start | bytes 1179656 | tf_op jit(solution)/shard_map/ppermute | solution.py:387
  78.1 4.9 %collective-permute-start.20 = (bf16[128,384]{1,0:T(8,128)(2,1)S(1)}, bf16[128,384]{1,0:T(8,128)(2,1)S(1)}, u32[]{:S(2)}, u32[]{:S(2)}) collective-permute-start(bf16[128,384]{1,0:T(8,128)(2,1)S(1)} %get-tuple-element.66), channel_id=1, source_target_pairs={{0,2},{1,3},{2,0},{3,1},{4,6},{5,7},{6,4},{7,5},{8,10},{9,11},{10,... | collective-permute-start | bytes 294920 | tf_op jit(solution)/shard_map/ppermute | solution.py:387
  83.0 6.3 %collective-permute-start.21 = (bf16[128,384]{1,0:T(8,128)(2,1)S(1)}, bf16[128,384]{1,0:T(8,128)(2,1)S(1)}, u32[]{:S(2)}, u32[]{:S(2)}) collective-permute-start(bf16[128,384]{1,0:T(8,128)(2,1)S(1)} %get-tuple-element.55), channel_id=1, source_target_pairs={{0,2},{1,3},{2,0},{3,1},{4,6},{5,7},{6,4},{7,5},{8,10},{9,11},{10,... | collective-permute-start | bytes 294920 | tf_op jit(solution)/shard_map/ppermute | solution.py:387
  84.6 7.1 %collective-permute-start.26 = (bf16[128,384]{1,0:T(8,128)(2,1)S(1)}, bf16[128,384]{1,0:T(8,128)(2,1)S(1)}, u32[]{:S(2)}, u32[]{:S(2)}) collective-permute-start(bf16[128,384]{1,0:T(8,128)(2,1)S(1)} %fusion.1), channel_id=1, source_target_pairs={{0,16},{4,20},{8,24},{12,28},{16,0},{20,4},{24,8},{28,12},{1,17},{... | collective-permute-start | bytes 294920 | tf_op jit(solution)/shard_map/ppermute | solution.py:387
  89.3 5.9 %collective-permute-start.22 = (bf16[128,384]{1,0:T(8,128)(2,1)S(1)}, bf16[128,384]{1,0:T(8,128)(2,1)S(1)}, u32[]{:S(2)}, u32[]{:S(2)}) collective-permute-start(bf16[128,384]{1,0:T(8,128)(2,1)S(1)} %add_convert_fusion.2), channel_id=1, source_target_pairs={{0,16},{4,20},{8,24},{12,28},{16,0},{20,4},{24,8},{28,12},{1,17},{... | collective-permute-start | bytes 294920 | tf_op jit(solution)/shard_map/ppermute | solution.py:387
  91.7 6.8 %collective-permute-start.29 = (bf16[128,384]{1,0:T(8,128)(2,1)S(1)}, bf16[128,384]{1,0:T(8,128)(2,1)S(1)}, u32[]{:S(2)}, u32[]{:S(2)}) collective-permute-start(bf16[128,384]{1,0:T(8,128)(2,1)S(1)} %add_convert_fusion.refs_0_), channel_id=1, source_target_pairs={{0,12},{4,8},{8,4},{12,0},{16,28},{20,24},{24,20},{28,16},{1,13},{... | collective-permute-start | bytes 294920 | tf_op jit(solution)/shard_map/ppermute | solution.py:387
  92.4 6.9 %collective-permute-start.28 = (bf16[128,384]{1,0:T(8,128)(2,1)S(1)}, bf16[128,384]{1,0:T(8,128)(2,1)S(1)}, u32[]{:S(2)}, u32[]{:S(2)}) collective-permute-start(bf16[128,384]{1,0:T(8,128)(2,1)S(1)} %add_convert_fusion.refs_0_), channel_id=1, source_target_pairs={{0,8},{4,12},{8,0},{12,4},{16,24},{20,28},{24,16},{28,20},{1,9},{5... | collective-permute-start | bytes 294920 | tf_op jit(solution)/shard_map/ppermute | solution.py:387
  94.1 7.3 %collective-permute-start.27 = (bf16[128,384]{1,0:T(8,128)(2,1)S(1)}, bf16[128,384]{1,0:T(8,128)(2,1)S(1)}, u32[]{:S(2)}, u32[]{:S(2)}) collective-permute-start(bf16[128,384]{1,0:T(8,128)(2,1)S(1)} %add_convert_fusion.refs_0_), channel_id=1, source_target_pairs={{0,4},{4,0},{8,12},{12,8},{16,20},{20,16},{24,28},{28,24},{1,5},{5... | collective-permute-start | bytes 294920 | tf_op jit(solution)/shard_map/ppermute | solution.py:387
  95.3 7.6 %collective-permute-start.25 = (bf16[128,384]{1,0:T(8,128)(2,1)S(1)}, bf16[128,384]{1,0:T(8,128)(2,1)S(1)}, u32[]{:S(2)}, u32[]{:S(2)}) collective-permute-start(bf16[128,384]{1,0:T(8,128)(2,1)S(1)} %add_convert_fusion.1.refs_0_), channel_id=1, source_target_pairs={{0,12},{4,8},{8,4},{12,0},{16,28},{20,24},{24,20},{28,16},{1,13},{... | collective-permute-start | bytes 294920 | tf_op jit(solution)/shard_map/ppermute | solution.py:387
  98.4 4.6 %collective-permute-start.24 = (bf16[128,384]{1,0:T(8,128)(2,1)S(1)}, bf16[128,384]{1,0:T(8,128)(2,1)S(1)}, u32[]{:S(2)}, u32[]{:S(2)}) collective-permute-start(bf16[128,384]{1,0:T(8,128)(2,1)S(1)} %add_convert_fusion.1.refs_0_), channel_id=1, source_target_pairs={{0,8},{4,12},{8,0},{12,4},{16,24},{20,28},{24,16},{28,20},{1,9},{5... | collective-permute-start | bytes 294920 | tf_op jit(solution)/shard_map/ppermute | solution.py:387
  98.5 4.8 %collective-permute-start.23 = (bf16[128,384]{1,0:T(8,128)(2,1)S(1)}, bf16[128,384]{1,0:T(8,128)(2,1)S(1)}, u32[]{:S(2)}, u32[]{:S(2)}) collective-permute-start(bf16[128,384]{1,0:T(8,128)(2,1)S(1)} %add_convert_fusion.1.refs_0_), channel_id=1, source_target_pairs={{0,4},{4,0},{8,12},{12,8},{16,20},{20,16},{24,28},{28,24},{1,5},{5... | collective-permute-start | bytes 294920 | tf_op jit(solution)/shard_map/ppermute | solution.py:387
